TPU v7x, 32 devices: a whole 2x2x4 slice. The times are simulated.
32 devices in a mesh: fsdp: 8 (over z, y), dp: 4 (over x, core).
Axes of the slice: x: 2, y: 2, z: 4, core: 2. Of those that a mesh axis runs over, the one named last changes fastest.
Arguments:
- features: bfloat16 [4, 32, 192, 2048], P('dp', 'fsdp'), may hold values from -6 to 6
- crop_scale: int32 [8], replicated, may hold values from 2 to 8, as said below
- crop_group: int32 [8], replicated, may hold values from 0 to 3, as said below
- labels: int32 [3, 4, 32, 192], P(None, 'dp', 'fsdp'), may hold values from 0 to 20
- w_reduce: bfloat16 [2048, 512], P('fsdp'), may hold values from -0.125 to 0.125
- gain_reduce: float32 [512], replicated, may hold values from 0.5 to 1.5
- bias_reduce: float32 [512], replicated, may hold values from -2 to 2
- w_middle: bfloat16 [512, 9, 512], P('fsdp'), may hold values from -0.09375 to 0.09375
- gain_middle: float32 [512], replicated, may hold values from 0.5 to 1.5
- bias_middle: float32 [512], replicated, may hold values from -2 to 2
- w_expand: bfloat16 [512, 2048], P('fsdp'), may hold values from -0.25 to 0.25
- gain_expand: float32 [2048], replicated, may hold values from 0.5 to 1.5
- bias_expand: float32 [2048], replicated, may hold values from -2 to 2
- w_heads: bfloat16 [2048, 3, 9, 256], P('fsdp'), may hold values from -0.046875 to 0.046875
- gain_heads: float32 [3, 256], replicated, may hold values from 0.5 to 1.5
- bias_heads: float32 [3, 256], replicated, may hold values from -2 to 2
- w_class: bfloat16 [3, 256, 21], replicated, may hold values from -0.75 to 0.75
- b_class: float32 [3, 21], replicated, may hold values from -3 to 3
Outputs:
- grad_features: float32 [4, 32, 192, 2048], P('dp', 'fsdp')
- grad_reduce: float32 [2048, 512], P('fsdp')
- grad_middle: float32 [512, 9, 512], P('fsdp')
- grad_expand: float32 [512, 2048], P('fsdp')
- grad_heads: float32 [2048, 3, 9, 256], P('fsdp')
- grad_gain_reduce: float32 [512], replicated
- grad_bias_reduce: float32 [512], replicated
- grad_gain_middle: float32 [512], replicated
- grad_bias_middle: float32 [512], replicated
- grad_gain_expand: float32 [2048], replicated
- grad_bias_expand: float32 [2048], replicated
- grad_gain_heads: float32 [3, 256], replicated
- grad_bias_heads: float32 [3, 256], replicated
- grad_class: float32 [3, 256, 21], replicated
- grad_class_bias: float32 [3, 21], replicated
- task_weights: float32 [3], replicated
Inputs may be any that keep to these rules, and one draw needn't show every extreme that they name: `crop_group`: every index of dp receives exactly 2 crops. `crop_scale`: code 8 occurs in every draw.
All inputs are finite; a program needn't handle non-finite values.
Results may differ from a plain program's by a relative error of at most 0.02.
Values may be sent and summed in bfloat16 or wider, within the bound.
No kernel may reach another device: no remote copies, remote signals or barrier semaphores. Data moves between devices by JAX's collectives and lax.ppermute only.
A program may use at most 320 MiB of HBM per device.

v0:
```python
import jax
import jax.numpy as jnp
from jax import lax
from jax.sharding import PartitionSpec as P

W_UNIT = 12


eps = 1e-05
mid_rate = 2
head_rates = (12, 24, 36)


def shifted(value, axis, steps):
    count = lax.axis_size(axis)
    first, last = (max(0, -steps), min(count, count - steps))
    return lax.ppermute(value, axis, [(source, source + steps) for source in range(first, last)])


def with_halo(x, sides, width):
    for axis, dim in sides:
        size, length = (lax.axis_size(axis), x.shape[dim])
        up = [(i, (i + 1) % size) for i in range(size - 1)]
        down = [(j, i) for i, j in up]
        last = lax.slice_in_dim(x, length - width, length, axis=dim)
        first = lax.slice_in_dim(x, 0, width, axis=dim)
        before = lax.ppermute(last, axis, up)
        after = lax.ppermute(first, axis, down)
        x = jnp.concatenate([before, x, after], axis=dim)
    return x


def along(value, offset, axis):
    size = value.shape[axis]
    if offset == 0:
        return value
    widths = [(0, 0)] * value.ndim
    if offset > 0:
        widths[axis] = (0, offset)
        return lax.slice_in_dim(jnp.pad(value, widths), offset, offset + size, axis=axis)
    widths[axis] = (-offset, 0)
    return lax.slice_in_dim(jnp.pad(value, widths), 0, size, axis=axis)


def crop_table(crop_scale, crop_group, group, unit, cols):
    mine = (crop_group == group).astype(jnp.int32)
    widths = crop_scale * unit * mine
    ends = jnp.cumsum(widths)
    starts = ends - widths
    column = jnp.arange(cols, dtype=jnp.int32)[:, None]
    return ((column >= starts[None, :]) & (column < ends[None, :])).astype(jnp.float32)


def same_crop(inside, offset):
    return jnp.sum(inside * along(inside, offset, 0), axis=1)


def silu_slope(value):
    sigma = jax.nn.sigmoid(value)
    return sigma * (1.0 + value * (1.0 - sigma))


def norm_forward(value, gain, bias, count):
    total, square = lax.psum(
        (jnp.sum(value, axis=0), jnp.sum(value * value, axis=0)), ("fsdp", "dp")
    )
    mean = total / count
    scale = lax.rsqrt(square / count - mean * mean + eps)
    normed = (value - mean) * scale
    return (normed, scale, normed * gain + bias)


def norm_backward(grad, normed, scale, gain, valid, count):
    dgain, dbias = lax.psum((jnp.sum(grad * normed, axis=0), jnp.sum(grad, axis=0)), ("fsdp", "dp"))
    dvalue = valid * (gain * scale) * (grad - dbias / count - normed * (dgain / count))
    return (dvalue, dgain, dbias)


def middle_stack(padded, inside, sign):
    rows = padded.shape[0] - 2 * mid_rate
    pieces = []
    for ir in range(3):
        for ic in range(3):
            drow = sign * (ir - 1) * mid_rate
            dcol = sign * (ic - 1) * mid_rate
            piece = padded[mid_rate + drow : mid_rate + drow + rows]
            mask = same_crop(inside, dcol).astype(padded.dtype)
            pieces.append(along(piece, dcol, 1) * mask[None, :, None])
    stacked = jnp.stack(pieces, axis=2)
    return stacked.reshape(rows * padded.shape[1], -1)


def head_stack(grid, inside, rate):
    pieces = []
    for ic in range(3):
        dcol = (ic - 1) * rate
        mask = same_crop(inside, dcol).astype(grid.dtype)
        pieces.append(along(grid, dcol, 1) * mask[None, :, None])
    stacked = jnp.stack(pieces, axis=2)
    return stacked.reshape(grid.shape[0] * grid.shape[1], -1)


def head_matrix(weight):
    depth = weight.shape[0]
    width = weight.shape[2]
    return weight.reshape(depth, 3, 3, width).transpose(2, 0, 1, 3).reshape(3 * depth, 3 * width)


def head_unstack(grad, inside, rate, rows, cols):
    depth = grad.shape[1] // 3
    parts = grad.reshape(rows, cols, 3, depth)
    total = jnp.zeros((rows, cols, depth), jnp.float32)
    for ic in range(3):
        dcol = (ic - 1) * rate
        mask = same_crop(inside, dcol)
        total = total + along(parts[:, :, ic] * mask[None, :, None], -dcol, 1)
    return total.reshape(rows * cols, depth)


def rows_forward(value, hop):
    if abs(hop) >= lax.axis_size("fsdp"):
        return jnp.zeros_like(value)
    return shifted(value, "fsdp", hop)


def rows_backward(value, hop):
    if abs(hop) >= lax.axis_size("fsdp"):
        return jnp.zeros_like(value)
    return shifted(value, "fsdp", hop)


def task_scales(gram):
    norms = jnp.sqrt(jnp.stack([gram[0, 0], gram[1, 1], gram[2, 2]]) + 1e-12)
    corr = gram / (norms[:, None] * norms[None, :]) + 0.1 * jnp.eye(3, dtype=jnp.float32)
    adjugate = jnp.stack(
        [
            jnp.cross(corr[:, 1], corr[:, 2]),
            jnp.cross(corr[:, 2], corr[:, 0]),
            jnp.cross(corr[:, 0], corr[:, 1]),
        ]
    )
    weights = jnp.sum(adjugate, axis=1)
    return 3.0 * weights * jnp.mean(norms) / (norms * jnp.sum(weights))


def on_device(
    features,
    crop_scale,
    crop_group,
    labels,
    w_reduce,
    gain_reduce,
    bias_reduce,
    w_middle,
    gain_middle,
    bias_middle,
    w_expand,
    gain_expand,
    bias_expand,
    w_heads,
    gain_heads,
    bias_heads,
    w_class,
    b_class,
):
    rows = features.shape[1]
    cols = features.shape[2]
    depth = features.shape[3]
    pixels = rows * cols
    inside = crop_table(crop_scale, crop_group, lax.axis_index("dp"), W_UNIT, cols)
    valid = jnp.tile(jnp.sum(inside, axis=1), rows)[:, None]
    valid_heads = valid[:, :, None]
    count = jnp.sum(crop_scale).astype(jnp.float32) * float(W_UNIT * rows * lax.axis_size("fsdp"))
    crops = float(crop_scale.shape[0])
    source = features.reshape(pixels, depth) * valid.astype(jnp.bfloat16)
    red_all, mid_all, exp_all = (
        lax.all_gather(w_reduce, "fsdp", axis=0, tiled=True),
        lax.all_gather(w_middle, "fsdp", axis=0, tiled=True),
        lax.all_gather(w_expand, "fsdp", axis=0, tiled=True),
    )
    heads_all = lax.all_gather(w_heads, "fsdp", axis=0, tiled=True)
    width = red_all.shape[1]
    tasks = heads_all.shape[1]
    head_width = heads_all.shape[3]
    classes = w_class.shape[2]
    reduced = jnp.dot(source, red_all, preferred_element_type=jnp.float32)
    normed1, scale1, out1 = norm_forward(reduced, gain_reduce, bias_reduce, count)
    hidden1 = (jax.nn.silu(out1) * valid).astype(jnp.bfloat16)
    padded1 = with_halo(hidden1.reshape(rows, cols, width), (("fsdp", 0),), mid_rate)
    stack1 = middle_stack(padded1, inside, 1)
    middled = jnp.dot(
        stack1,
        mid_all.transpose(1, 0, 2).reshape(9 * width, width),
        preferred_element_type=jnp.float32,
    )
    normed2, scale2, out2 = norm_forward(middled, gain_middle, bias_middle, count)
    hidden2 = (jax.nn.silu(out2) * valid).astype(jnp.bfloat16)
    expanded = jnp.dot(hidden2, exp_all, preferred_element_type=jnp.float32)
    normed3, scale3, out3 = norm_forward(expanded, gain_expand, bias_expand, count)
    before = out3 + source.astype(jnp.float32)
    grid = (jax.nn.silu(before) * valid).astype(jnp.bfloat16).reshape(rows, cols, depth)
    stacks = []
    matrices = []
    mixed_list = []
    for task in range(tasks):
        rate = head_rates[task]
        hop = rate // rows
        stack = head_stack(grid, inside, rate)
        matrix = head_matrix(heads_all[:, task])
        terms = jnp.dot(stack, matrix, preferred_element_type=jnp.float32).reshape(
            pixels, 3, head_width
        )
        upper = rows_forward(terms[:, 0].astype(jnp.bfloat16), hop)
        lower = rows_forward(terms[:, 2].astype(jnp.bfloat16), -hop)
        mixed_list.append(terms[:, 1] + upper.astype(jnp.float32) + lower.astype(jnp.float32))
        stacks.append(stack)
        matrices.append(matrix)
    mixed = jnp.stack(mixed_list, axis=1)
    normed_h, scale_h, out_h = norm_forward(mixed, gain_heads, bias_heads, count)
    activ = (jax.nn.silu(out_h) * valid_heads).astype(jnp.bfloat16)
    logits = (
        jnp.einsum("pkh,khc->pkc", activ, w_class, preferred_element_type=jnp.float32) + b_class
    )
    picked = labels.reshape(tasks, pixels).T
    onehot = (picked[:, :, None] == jnp.arange(classes, dtype=jnp.int32)[None, None, :]).astype(
        jnp.float32
    )
    dlogits = ((jax.nn.softmax(logits, axis=-1) - onehot) * valid_heads / crops).astype(
        jnp.bfloat16
    )
    class_part = jnp.einsum("pkh,pkc->khc", activ, dlogits, preferred_element_type=jnp.float32)
    class_bias_part = jnp.sum(dlogits.astype(jnp.float32), axis=0)
    dactiv = jnp.einsum("pkc,khc->pkh", dlogits, w_class, preferred_element_type=jnp.float32)
    dout_h = dactiv * valid_heads * silu_slope(out_h)
    dmixed, dgain_h, dbias_h = norm_backward(
        dout_h, normed_h, scale_h, gain_heads, valid_heads, count
    )
    dmixed_low = dmixed.astype(jnp.bfloat16)
    red_back, mid_back, exp_back = (
        lax.all_gather(w_reduce, "fsdp", axis=0, tiled=True),
        lax.all_gather(w_middle, "fsdp", axis=0, tiled=True),
        lax.all_gather(w_expand, "fsdp", axis=0, tiled=True),
    )
    heads_back = lax.all_gather(w_heads, "fsdp", axis=0, tiled=True)
    back_matrices = [head_matrix(heads_back[:, task]) for task in range(tasks)]
    task_grads = []
    head_grad_list = []
    for task in range(tasks):
        rate = head_rates[task]
        hop = rate // rows
        center = dmixed_low[:, task]
        from_above = rows_backward(center, -hop)
        from_below = rows_backward(center, hop)
        dterms = jnp.stack([from_above, center, from_below], axis=1).reshape(pixels, 3 * head_width)
        grad_matrix = jnp.dot(stacks[task].T, dterms, preferred_element_type=jnp.float32)
        head_grad_list.append(
            grad_matrix.reshape(3, depth, 3, head_width)
            .transpose(1, 2, 0, 3)
            .reshape(depth, 9, head_width)
        )
        dstack = jnp.dot(dterms, back_matrices[task].T, preferred_element_type=jnp.float32)
        task_grads.append(head_unstack(dstack, inside, rate, rows, cols))
    grad_heads_full = jnp.stack(head_grad_list, axis=1)
    partial_gram = jnp.stack(
        [jnp.stack([jnp.sum(first * second) for second in task_grads]) for first in task_grads]
    )
    gram, grad_class, grad_class_bias = lax.psum(
        (partial_gram, class_part, class_bias_part), ("fsdp", "dp")
    )
    task_weights = task_scales(gram)
    combined = task_weights[0] * task_grads[0]
    for task in range(1, tasks):
        combined = combined + task_weights[task] * task_grads[task]
    dbefore = combined * valid * silu_slope(before)
    dexpanded, dgain3, dbias3 = norm_backward(dbefore, normed3, scale3, gain_expand, valid, count)
    dexpanded_low = dexpanded.astype(jnp.bfloat16)
    grad_expand_full = jnp.dot(hidden2.T, dexpanded_low, preferred_element_type=jnp.float32)
    dhidden2 = jnp.dot(dexpanded_low, exp_back.T, preferred_element_type=jnp.float32)
    dout2 = dhidden2 * valid * silu_slope(out2)
    dmiddled, dgain2, dbias2 = norm_backward(dout2, normed2, scale2, gain_middle, valid, count)
    dmiddled_low = dmiddled.astype(jnp.bfloat16)
    grad_middle_full = (
        jnp.dot(stack1.T, dmiddled_low, preferred_element_type=jnp.float32)
        .reshape(9, width, width)
        .transpose(1, 0, 2)
    )
    padded_back = with_halo(dmiddled_low.reshape(rows, cols, width), (("fsdp", 0),), mid_rate)
    stack_back = middle_stack(padded_back, inside, -1)
    dhidden1 = jnp.dot(
        stack_back,
        mid_back.transpose(1, 2, 0).reshape(9 * width, width),
        preferred_element_type=jnp.float32,
    )
    dout1 = dhidden1 * valid * silu_slope(out1)
    dreduced, dgain1, dbias1 = norm_backward(dout1, normed1, scale1, gain_reduce, valid, count)
    dreduced_low = dreduced.astype(jnp.bfloat16)
    grad_reduce_full = jnp.dot(source.T, dreduced_low, preferred_element_type=jnp.float32)
    dfeatures = dbefore + jnp.dot(dreduced_low, red_back.T, preferred_element_type=jnp.float32)
    red_shard, mid_shard, exp_shard, head_shard = (
        lax.psum_scatter(
            grad_reduce_full.astype(jnp.bfloat16), "fsdp", scatter_dimension=0, tiled=True
        ).astype(jnp.float32),
        lax.psum_scatter(
            grad_middle_full.astype(jnp.bfloat16), "fsdp", scatter_dimension=0, tiled=True
        ).astype(jnp.float32),
        lax.psum_scatter(
            grad_expand_full.astype(jnp.bfloat16), "fsdp", scatter_dimension=0, tiled=True
        ).astype(jnp.float32),
        lax.psum_scatter(
            grad_heads_full.astype(jnp.bfloat16), "fsdp", scatter_dimension=0, tiled=True
        ).astype(jnp.float32),
    )
    red_out, mid_out, exp_out, head_out = (
        lax.psum(red_shard.astype(jnp.bfloat16), "dp").astype(jnp.float32),
        lax.psum(mid_shard.astype(jnp.bfloat16), "dp").astype(jnp.float32),
        lax.psum(exp_shard.astype(jnp.bfloat16), "dp").astype(jnp.float32),
        lax.psum(head_shard.astype(jnp.bfloat16), "dp").astype(jnp.float32),
    )
    return (
        dfeatures.reshape(1, rows, cols, depth),
        red_out,
        mid_out,
        exp_out,
        head_out,
        dgain1,
        dbias1,
        dgain2,
        dbias2,
        dgain3,
        dbias3,
        dgain_h,
        dbias_h,
        grad_class,
        grad_class_bias,
        task_weights,
    )


def solution(mesh):
    in_specs = (
        P("dp", "fsdp", None, None),
        P(),
        P(),
        P(None, "dp", "fsdp", None),
        P("fsdp", None),
        P(),
        P(),
        P("fsdp", None, None),
        P(),
        P(),
        P("fsdp", None),
        P(),
        P(),
        P("fsdp", None, None, None),
        P(),
        P(),
        P(),
        P(),
    )
    out_specs = (
        P("dp", "fsdp", None, None),
        P("fsdp", None),
        P("fsdp", None, None),
        P("fsdp", None),
        P("fsdp", None, None, None),
        P(),
        P(),
        P(),
        P(),
        P(),
        P(),
        P(),
        P(),
        P(),
        P(),
        P(),
    )
    return jax.shard_map(
        on_device, mesh=mesh, in_specs=in_specs, out_specs=out_specs, check_vma=False
    )
```

profile of v0, /device:TPU:0, one launch (start us, length us, event | category | flops | bytes accessed | tf_op | source)
XLA Modules:
  0.0 2444.5 jit_solution(16772327610601244157)
XLA Ops:
  14.3 48.0 %all-gather.5.cloned.1.call-done = bf16[2048,512]{1,0:T(8,128)(2,1)} async-done(((bf16[256,512]{1,0:T(8,128)(2,1)}), bf16[2048,512]{1,0:T(8,128)(2,1)}) %all-gather.5.cloned.1.call-update) | async-done | bytes 2097168 | tf_op jit(solution)/shard_map/all_gather | solution.py:177
  66.6 40.1 %all-reduce.39 = (f32[512]{0:T(512)S(1)}, f32[512]{0:T(512)S(1)}) all-reduce(f32[512]{0:T(512)S(1)} %get-tuple-element.38, f32[512]{0:T(512)S(1)} %get-tuple-element.37), channel_id=1, replica_groups=mesh['fsdp'=8,'dp'=4] {'fsdp','dp'}, use_global_device_ids=true, to_apply=%region_6.7 | all-reduce | flops 1024 | bytes 8192 | tf_op jit(solution)/shard_map/psum | solution.py:64
  115.2 23.8 collective-permute-done
  149.6 14.6 copy.205
  164.2 16.6 reshape.342
  190.2 75.7 %all-reduce.38 = (f32[512]{0:T(512)S(1)}, f32[512]{0:T(512)S(1)}) all-reduce(f32[512]{0:T(512)S(1)} %get-tuple-element.36, f32[512]{0:T(512)S(1)} %get-tuple-element.35), channel_id=1, replica_groups=mesh['fsdp'=8,'dp'=4] {'fsdp','dp'}, use_global_device_ids=true, to_apply=%region_13.14 | all-reduce | flops 1024 | bytes 8192 | tf_op jit(solution)/shard_map/psum | solution.py:64
  273.5 52.2 %all-reduce.37 = (f32[2048]{0:T(1024)S(1)}, f32[2048]{0:T(1024)S(1)}) all-reduce(f32[2048]{0:T(1024)S(1)} %get-tuple-element.26, f32[2048]{0:T(1024)S(1)} %get-tuple-element.25), channel_id=1, replica_groups=mesh['fsdp'=8,'dp'=4] {'fsdp','dp'}, use_global_device_ids=true, to_apply=%region_15.16 | all-reduce | flops 4096 | bytes 32768 | tf_op jit(solution)/shard_map/psum | solution.py:64
  348.2 30.2 %copy.206 = bf16[4,192,3,2048]{3,2,1,0:T(4,128)(2,1)} copy(bf16[4,192,3,2048]{3,1,0,2:T(8,128)(2,1)S(1)} %get-tuple-element.103) | data formatting | bytes 18874368 | tf_op jit(solution)/shard_map/stack | solution.py:99
  378.4 25.9 %reshape.361 = bf16[768,6144,1]{1,0,2:T(8,128)(2,1)} reshape(bf16[4,192,3,2048]{3,2,1,0:T(4,128)(2,1)} %copy.206) | data formatting | bytes 18874368 | tf_op jit(solution)/shard_map/reshape | solution.py:100
  404.3 14.7 copy.209
  419.0 25.9 %reshape.362 = bf16[768,6144,1]{1,0,2:T(8,128)(2,1)} reshape(bf16[4,192,3,2048]{3,2,1,0:T(4,128)(2,1)} %copy.209) | data formatting | bytes 18874368 | tf_op jit(solution)/shard_map/reshape | solution.py:100
  444.9 14.7 copy.212
  459.5 25.9 %reshape.363 = bf16[768,6144,1]{1,0,2:T(8,128)(2,1)} reshape(bf16[4,192,3,2048]{3,2,1,0:T(4,128)(2,1)} %copy.212) | data formatting | bytes 18874368 | tf_op jit(solution)/shard_map/reshape | solution.py:100
  485.4 267.5 %all-gather.11.cloned.1.call-done = bf16[2048,3,9,256]{3,0,2,1:T(8,128)(2,1)} async-done(((bf16[256,3,9,256]{3,0,2,1:T(8,128)(2,1)}), bf16[2048,3,9,256]{3,0,2,1:T(8,128)(2,1)}) %all-gather.11.cloned.1.call-update) | async-done | bytes 28311568 | tf_op jit(solution)/shard_map/all_gather | solution.py:181
  752.9 17.2 fusion.120
  770.1 49.7 %copy.213 = bf16[3,2048,3,256]{3,2,1,0:T(4,128)(2,1)} copy(bf16[3,2048,3,256]{3,1,0,2:T(8,128)(2,1)S(1)} %bitcast.405) | data formatting | bytes 18874368 | tf_op jit(solution)/shard_map/transpose | solution.py:106
  830.8 12.7 copy.214
  843.5 14.7 copy.210
  881.7 14.9 copy.207
  907.5 12.7 copy.208
  920.3 14.2 fusion.131
  973.6 12.7 copy.228
  986.4 12.7 copy.222
  999.1 12.7 copy.217
  1016.6 39.9 %all-reduce.36 = (f32[3,256]{1,0:T(4,128)S(1)}, f32[3,256]{1,0:T(4,128)S(1)}) all-reduce(f32[3,256]{1,0:T(4,128)S(1)} %get-tuple-element.30, f32[3,256]{1,0:T(4,128)S(1)} %get-tuple-element.29), channel_id=1, replica_groups=mesh['fsdp'=8,'dp'=4] {'fsdp','dp'}, use_global_device_ids=true, to_apply=%region_25.26 | all-reduce | flops 1536 | bytes 12288 | tf_op jit(solution)/shard_map/psum | solution.py:64
  1064.0 41.6 %all-reduce.35 = (f32[3,256]{1,0:T(4,128)S(1)}, f32[3,256]{1,0:T(4,128)S(1)}) all-reduce(f32[3,256]{1,0:T(4,128)S(1)} %get-tuple-element.28, f32[3,256]{1,0:T(4,128)S(1)} %get-tuple-element.27), channel_id=1, replica_groups=mesh['fsdp'=8,'dp'=4] {'fsdp','dp'}, use_global_device_ids=true, to_apply=%region_33.34 | all-reduce | flops 1536 | bytes 12288 | tf_op jit(solution)/shard_map/psum | solution.py:74
  1127.5 14.4 fusion.40
  1161.1 14.4 fusion.42
  1187.6 14.6 fusion.33
  1214.3 24.1 multiply_reduce_fusion.6
  1244.2 41.2 %psum.171 = f32[3,3]{1,0:T(4,128)S(1)} all-reduce(f32[3,3]{1,0:T(4,128)S(1)} %pad_maximum_fusion.12), channel_id=1, replica_groups=mesh['fsdp'=8,'dp'=4] {'fsdp','dp'}, use_global_device_ids=true, to_apply=%region_40.41 | all-reduce | flops 9 | bytes 72 | tf_op jit(solution)/shard_map/psum | solution.py:267
  1318.4 14.2 multiply_add_fusion
  1342.2 42.2 %all-reduce.34 = (f32[2048]{0:T(1024)S(1)}, f32[2048]{0:T(1024)S(1)}) all-reduce(f32[2048]{0:T(1024)S(1)} %get-tuple-element.18, f32[2048]{0:T(1024)S(1)} %get-tuple-element.17), channel_id=1, replica_groups=mesh['fsdp'=8,'dp'=4] {'fsdp','dp'}, use_global_device_ids=true, to_apply=%region_49.51 | all-reduce | flops 4096 | bytes 32768 | tf_op jit(solution)/shard_map/psum | solution.py:74
  1394.6 38.1 %all-reduce.33 = (f32[512]{0:T(512)S(1)}, f32[512]{0:T(512)S(1)}) all-reduce(f32[512]{0:T(512)S(1)} %get-tuple-element.34, f32[512]{0:T(512)S(1)} %get-tuple-element.33), channel_id=1, replica_groups=mesh['fsdp'=8,'dp'=4] {'fsdp','dp'}, use_global_device_ids=true, to_apply=%region_53.55 | all-reduce | flops 1024 | bytes 8192 | tf_op jit(solution)/shard_map/psum | solution.py:74
  1468.3 14.7 copy.240
  1483.1 16.7 reshape.355
  1516.3 115.9 %all-reduce.44.cloned.1.call-done = (f32[512]{0:T(512)}, f32[512]{0:T(512)}, f32[3,256,21]{1,2,0:T(8,128)}, f32[3,21]{1,0:T(4,128)}) async-done(((f32[512]{0:T(512)}, f32[512]{0:T(512)}, f32[3,256,21]{1,2,0:T(8,128)}, f32[3,21]{1,0:T(4,128)}), (f32[512]{0:T(512)}, f32[512]{0:T(512)}, f32[3,256,21]{1,2,0:T(8,128)}, f32[3,21]{1,0:T(4,128)})) %all-reduce.44.cloned.1.call-update) | async-done | bytes 68876 | tf_op jit(solution)/shard_map/psum | solution.py:74
  1647.9 19.2 copy.275
  1667.1 12.8 copy.242
  1679.9 19.2 copy.276
  1699.1 12.9 copy.244
  1712.0 19.3 copy.277
  1731.3 13.1 copy.246
  1744.4 13.7 convert_bitcast_fusion
  1807.3 19.8 pad_maximum_fusion
  1827.3 47.1 %reduce-scatter.7.cloned.1.call-done = bf16[64,9,512]{2,0,1:T(8,128)(2,1)} async-done(((bf16[512,9,512]{2,0,1:T(8,128)(2,1)}), bf16[64,9,512]{2,0,1:T(8,128)(2,1)}) %reduce-scatter.7.cloned.1.call-update) | async-done | bytes 589840 | tf_op jit(solution)/shard_map/reduce_scatter | solution.py:303
  1874.4 453.8 %reduce-scatter.11.cloned.1.call-done = bf16[256,3,9,256]{3,0,2,1:T(8,128)(2,1)} async-done(((bf16[2048,3,9,256]{3,0,2,1:T(8,128)(2,1)}), bf16[256,3,9,256]{3,0,2,1:T(8,128)(2,1)}) %reduce-scatter.11.cloned.1.call-update) | async-done | bytes 3538960 | tf_op jit(solution)/shard_map/reduce_scatter | solution.py:309
  2335.7 87.7 %all-reduce.46.cloned.1.call-done = (bf16[256,512]{1,0:T(8,128)(2,1)}, bf16[64,9,512]{2,0,1:T(8,128)(2,1)}, bf16[64,2048]{1,0:T(8,128)(2,1)}, bf16[256,3,9,256]{3,0,2,1:T(8,128)(2,1)}) async-done(((bf16[256,512]{1,0:T(8,128)(2,1)}, bf16[64,9,512]{2,0,1:T(8,128)(2,1)}, bf16[64,2048]{1,0:T(8,128)(2,1)}, bf16[256,3,9,256]{3,0,2,1:T(8,128)(2,1)}), (bf16[256,512]{1,0:T(8,128)(2,1)}, ...) | async-done | bytes 4653072 | tf_op jit(solution)/shard_map/psum | solution.py:314
  (388 shorter events, 403.0 us)
Async XLA Ops:
  7.2 1051.6 %copy-start = (bf16[3,256,21]{1,2,0:T(8,128)(2,1)S(1)}, bf16[3,256,21]{1,2,0:T(8,128)(2,1)}, u32[]{:S(2)}) copy-start(bf16[3,256,21]{1,2,0:T(8,128)(2,1)} %param.36) | copy-start | bytes 96772
  7.2 55.0 %all-gather.5.cloned.1.call-start = ((), (), s32[]{:S(2)}) async-start(), calls=%async_computation.4 | async-start | bytes 2359296 | tf_op jit(solution)/shard_map/all_gather | solution.py:177
  8.0 172.8 %all-gather.7.cloned.1.call-start = ((), (), s32[]{:S(2)}) async-start(), calls=%async_computation.5 | async-start | bytes 5308416 | tf_op jit(solution)/shard_map/all_gather | solution.py:178
  8.7 257.7 %all-gather.9.cloned.1.call-start = ((), (), s32[]{:S(2)}) async-start(), calls=%async_computation.6 | async-start | bytes 2359296 | tf_op jit(solution)/shard_map/all_gather | solution.py:179
  9.4 743.4 %all-gather.11.cloned.1.call-start = ((), (), s32[]{:S(2)}) async-start(), calls=%async_computation.7 | async-start | bytes 31850496 | tf_op jit(solution)/shard_map/all_gather | solution.py:181
  10.0 1622.2 %all-reduce.44.cloned.1.call-start = ((), (), s32[]{:S(2)}) async-start(), calls=%async_computation.12 | async-start | bytes 159744 | tf_op jit(solution)/shard_map/psum | solution.py:74
  11.8 102.5 %copy-start.63 = (f32[192]{0:T(256)}, f32[192]{0:T(256)S(1)}, u32[]{:S(2)}) copy-start(f32[192]{0:T(256)S(1)} %get-tuple-element.50) | copy-start | bytes 2308
  11.8 102.6 %copy-start.65 = (f32[192]{0:T(256)}, f32[192]{0:T(256)S(1)}, u32[]{:S(2)}) copy-start(f32[192]{0:T(256)S(1)} %get-tuple-element.39) | copy-start | bytes 2308
  11.8 102.6 %copy-start.69 = (f32[192]{0:T(256)}, f32[192]{0:T(256)S(1)}, u32[]{:S(2)}) copy-start(f32[192]{0:T(256)S(1)} %get-tuple-element.40) | copy-start | bytes 2308
  11.8 102.6 %copy-start.71 = (f32[192]{0:T(256)}, f32[192]{0:T(256)S(1)}, u32[]{:S(2)}) copy-start(f32[192]{0:T(256)S(1)} %get-tuple-element.41) | copy-start | bytes 2308
  11.8 102.6 %copy-start.67 = (f32[192]{0:T(256)}, f32[192]{0:T(256)S(1)}, u32[]{:S(2)}) copy-start(f32[192]{0:T(256)S(1)} %get-tuple-element.42) | copy-start | bytes 2308
  11.8 102.6 %copy-start.73 = (f32[192]{0:T(256)}, f32[192]{0:T(256)S(1)}, u32[]{:S(2)}) copy-start(f32[192]{0:T(256)S(1)} %get-tuple-element.44) | copy-start | bytes 2308
  11.8 102.6 %copy-start.75 = (f32[192]{0:T(256)}, f32[192]{0:T(256)S(1)}, u32[]{:S(2)}) copy-start(f32[192]{0:T(256)S(1)} %get-tuple-element.46) | copy-start | bytes 2308
  11.8 134.3 %copy-start.39 = (bf16[192]{0:T(256)(128)(2,1)}, bf16[192]{0:T(256)(128)(2,1)S(1)}, u32[]{:S(2)}) copy-start(bf16[192]{0:T(256)(128)(2,1)S(1)} %get-tuple-element.45) | copy-start | bytes 1156
  11.8 136.5 %copy-start.41 = (bf16[192]{0:T(256)(128)(2,1)}, bf16[192]{0:T(256)(128)(2,1)S(1)}, u32[]{:S(2)}) copy-start(bf16[192]{0:T(256)(128)(2,1)S(1)} %get-tuple-element.43) | copy-start | bytes 1156
  11.9 314.4 %copy-start.21 = (f32[768]{0:T(1024)}, f32[768]{0:T(1024)S(1)}, u32[]{:S(2)}) copy-start(f32[768]{0:T(1024)S(1)} %mul.763) | copy-start | bytes 9220
  11.9 314.4 %copy-start.34 = (bf16[768]{0:T(1024)(128)(2,1)}, bf16[768]{0:T(1024)(128)(2,1)S(1)}, u32[]{:S(2)}) copy-start(bf16[768]{0:T(1024)(128)(2,1)S(1)} %convert_element_type.268) | copy-start | bytes 4612
  14.3 92.4 %copy-start.50 = (f32[512]{0:T(512)S(1)}, f32[512]{0:T(512)}, u32[]{:S(2)}) copy-start(f32[512]{0:T(512)} %param.25) | copy-start | bytes 6148
  14.3 93.0 %copy-start.80 = (f32[512]{0:T(512)S(1)}, f32[512]{0:T(512)}, u32[]{:S(2)}) copy-start(f32[512]{0:T(512)} %param.26) | copy-start | bytes 6148
  66.6 72.6 %copy-start.6 = (f32[768,512]{1,0:T(8,128)}, f32[768,512]{1,0:T(8,128)S(1)}, u32[]{:S(2)}) copy-start(f32[768,512]{1,0:T(8,128)S(1)} %get-tuple-element.149) | copy-start | bytes 4718596
  108.8 30.2 %collective-permute-start = (bf16[2,192,512]{2,1,0:T(8,128)(2,1)}, bf16[2,192,512]{2,1,0:T(8,128)(2,1)S(1)}, u32[]{:S(2)}, u32[]{:S(2)}) collective-permute-start(bf16[2,192,512]{2,1,0:T(8,128)(2,1)} %bitcast.3), channel_id=1, source_target_pairs={{0,4},{4,8},{8,12},{12,16},{16,20},{20,24},{24,28},{1,5},{5,9},{9,... | collective-permute-start | bytes 1179656 | tf_op jit(solution)/shard_map/ppermute | solution.py:27
  113.0 26.0 %collective-permute-start.1 = (bf16[2,192,512]{2,1,0:T(8,128)(2,1)}, bf16[2,192,512]{2,1,0:T(8,128)(2,1)S(1)}, u32[]{:S(2)}, u32[]{:S(2)}) collective-permute-start(bf16[2,192,512]{2,1,0:T(8,128)(2,1)} %bitcast.12), channel_id=1, source_target_pairs={{4,0},{8,4},{12,8},{16,12},{20,16},{24,20},{28,24},{5,1},{9,5},{13... | collective-permute-start | bytes 1179656 | tf_op jit(solution)/shard_map/ppermute | solution.py:28
  114.3 217.7 %copy-start.37 = (bf16[192]{0:T(256)(128)(2,1)}, bf16[192]{0:T(256)(128)(2,1)S(1)}, u32[]{:S(2)}) copy-start(bf16[192]{0:T(256)(128)(2,1)S(1)} %convert_element_type.272) | copy-start | bytes 1156
  180.8 85.0 %copy-start.82 = (f32[512]{0:T(512)S(1)}, f32[512]{0:T(512)}, u32[]{:S(2)}) copy-start(f32[512]{0:T(512)} %param.28) | copy-start | bytes 6148
  180.8 85.6 %copy-start.91 = (f32[512]{0:T(512)S(1)}, f32[512]{0:T(512)}, u32[]{:S(2)}) copy-start(f32[512]{0:T(512)} %param.29) | copy-start | bytes 6148
  266.4 59.3 %copy-start.29 = (f32[2048]{0:T(1024)S(1)}, f32[2048]{0:T(1024)}, u32[]{:S(2)}) copy-start(f32[2048]{0:T(1024)} %param.31) | copy-start | bytes 24580
  266.4 59.9 %copy-start.4 = (bf16[1,4,192,2048]{3,2,1,0:T(8,128)(2,1)S(1)}, bf16[1,4,192,2048]{3,2,1,0:T(8,128)(2,1)}, u32[]{:S(2)}) copy-start(bf16[1,4,192,2048]{3,2,1,0:T(8,128)(2,1)} %param.20) | copy-start | bytes 9437188
  266.4 59.9 %copy-start.32 = (f32[2048]{0:T(1024)S(1)}, f32[2048]{0:T(1024)}, u32[]{:S(2)}) copy-start(f32[2048]{0:T(1024)} %param.32) | copy-start | bytes 24580
  770.1 49.7 %copy-start.2 = (bf16[2048,1,9,256]{3,0,2,1:T(8,128)(2,1)}, bf16[2048,1,9,256]{3,0,2,1:T(8,128)(2,1)S(1)}, u32[]{:S(2)}) copy-start(bf16[2048,1,9,256]{3,0,2,1:T(8,128)(2,1)S(1)} %get-tuple-element.95) | copy-start | bytes 28311556
  936.6 75.2 %collective-permute-start.2 = (bf16[768,256]{0,1:T(8,128)(2,1)}, bf16[768,256]{0,1:T(8,128)(2,1)S(1)}, u32[]{:S(2)}, u32[]{:S(2)}) collective-permute-start(bf16[768,256]{0,1:T(8,128)(2,1)} %get-tuple-element.117), channel_id=1, source_target_pairs={{0,12},{4,16},{8,20},{12,24},{16,28},{1,13},{5,17},{9,21},{13,25},... | collective-permute-start | bytes 1179656 | tf_op jit(solution)/shard_map/ppermute | solution.py:17
  940.0 71.8 %collective-permute-start.3 = (bf16[768,256]{0,1:T(8,128)(2,1)}, bf16[768,256]{0,1:T(8,128)(2,1)}, u32[]{:S(2)}, u32[]{:S(2)}) collective-permute-start(bf16[768,256]{0,1:T(8,128)(2,1)} %get-tuple-element.118), channel_id=1, source_target_pairs={{12,0},{16,4},{20,8},{24,12},{28,16},{13,1},{17,5},{21,9},{25,13},... | collective-permute-start | bytes 1179656 | tf_op jit(solution)/shard_map/ppermute | solution.py:17
  955.6 58.5 %collective-permute-start.4 = (bf16[768,256]{0,1:T(8,128)(2,1)}, bf16[768,256]{0,1:T(8,128)(2,1)S(1)}, u32[]{:S(2)}, u32[]{:S(2)}) collective-permute-start(bf16[768,256]{0,1:T(8,128)(2,1)} %get-tuple-element.119), channel_id=1, source_target_pairs={{0,24},{4,28},{1,25},{5,29},{2,26},{6,30},{3,27},{7,31}} | collective-permute-start | bytes 1179656 | tf_op jit(solution)/shard_map/ppermute | solution.py:17
  964.4 49.6 %collective-permute-start.5 = (bf16[768,256]{0,1:T(8,128)(2,1)S(1)}, bf16[768,256]{0,1:T(8,128)(2,1)S(1)}, u32[]{:S(2)}, u32[]{:S(2)}) collective-permute-start(bf16[768,256]{0,1:T(8,128)(2,1)S(1)} %get-tuple-element.120), channel_id=1, source_target_pairs={{24,0},{28,4},{25,1},{29,5},{26,2},{30,6},{27,3},{31,7}} | collective-permute-start | bytes 1179656 | tf_op jit(solution)/shard_map/ppermute | solution.py:17
  1109.3 48.1 %copy-start.12 = (bf16[768,1,256]{0,2,1:T(8,128)(2,1)}, bf16[768,1,256]{0,2,1:T(8,128)(2,1)S(1)}, u32[]{:S(2)}) copy-start(bf16[768,1,256]{0,2,1:T(8,128)(2,1)S(1)} %get-tuple-element.115) | copy-start | bytes 1179652
  1109.3 44.5 %collective-permute-start.7 = (bf16[768,256]{0,1:T(8,128)(2,1)}, bf16[768,256]{0,1:T(8,128)(2,1)}, u32[]{:S(2)}, u32[]{:S(2)}) collective-permute-start(bf16[768,256]{0,1:T(8,128)(2,1)} %get-tuple-element.113), channel_id=1, source_target_pairs={{0,12},{4,16},{8,20},{12,24},{16,28},{1,13},{5,17},{9,21},{13,25},... | collective-permute-start | bytes 1179656 | tf_op jit(solution)/shard_map/ppermute | solution.py:17
  1113.6 40.2 %collective-permute-start.6 = (bf16[768,256]{0,1:T(8,128)(2,1)}, bf16[768,256]{0,1:T(8,128)(2,1)}, u32[]{:S(2)}, u32[]{:S(2)}) collective-permute-start(bf16[768,256]{0,1:T(8,128)(2,1)} %get-tuple-element.113), channel_id=1, source_target_pairs={{12,0},{16,4},{20,8},{24,12},{28,16},{13,1},{17,5},{21,9},{25,13},... | collective-permute-start | bytes 1179656 | tf_op jit(solution)/shard_map/ppermute | solution.py:17
  1114.9 42.5 %collective-permute-start.9 = (bf16[768,256]{0,1:T(8,128)(2,1)}, bf16[768,256]{0,1:T(8,128)(2,1)}, u32[]{:S(2)}, u32[]{:S(2)}) collective-permute-start(bf16[768,256]{0,1:T(8,128)(2,1)} %get-tuple-element.114), channel_id=1, source_target_pairs={{0,24},{4,28},{1,25},{5,29},{2,26},{6,30},{3,27},{7,31}} | collective-permute-start | bytes 1179656 | tf_op jit(solution)/shard_map/ppermute | solution.py:17
  1122.6 34.8 %collective-permute-start.8 = (bf16[768,256]{0,1:T(8,128)(2,1)}, bf16[768,256]{0,1:T(8,128)(2,1)}, u32[]{:S(2)}, u32[]{:S(2)}) collective-permute-start(bf16[768,256]{0,1:T(8,128)(2,1)} %get-tuple-element.114), channel_id=1, source_target_pairs={{24,0},{28,4},{25,1},{29,5},{26,2},{30,6},{27,3},{31,7}} | collective-permute-start | bytes 1179656 | tf_op jit(solution)/shard_map/ppermute | solution.py:17
  1332.7 52.3 %copy-start.36 = (f32[2048]{0:T(1024)S(1)}, f32[2048]{0:T(1024)}, u32[]{:S(2)}) copy-start(f32[2048]{0:T(1024)} %get-tuple-element.78) | copy-start | bytes 24580
  1436.0 14.1 collective-permute-start.10
  1437.3 20.3 collective-permute-start.11
  1510.4 123.4 %copy-start.52 = (f32[512]{0:T(512)S(1)}, f32[512]{0:T(512)}, u32[]{:S(2)}) copy-start(f32[512]{0:T(512)} %get-tuple-element.74) | copy-start | bytes 6148
  1510.4 316.8 %reduce-scatter.9.cloned.1.call-start = ((), (), s32[]{:S(2)}) async-start(), calls=%async_computation.10 | async-start | bytes 2359296 | tf_op jit(solution)/shard_map/reduce_scatter | solution.py:306
  1516.2 311.0 %reduce-scatter.5.cloned.1.call-start = ((), (), s32[]{:S(2)}) async-start(), calls=%async_computation.8 | async-start | bytes 2359296 | tf_op jit(solution)/shard_map/reduce_scatter | solution.py:300
  1638.9 235.4 %reduce-scatter.7.cloned.1.call-start = ((), (), s32[]{:S(2)}) async-start(), calls=%async_computation.9 | async-start | bytes 5308416 | tf_op jit(solution)/shard_map/reduce_scatter | solution.py:303
  1647.9 680.3 %reduce-scatter.11.cloned.1.call-start = ((), (), s32[]{:S(2)}) async-start(), calls=%async_computation.11 | async-start | bytes 31850496 | tf_op jit(solution)/shard_map/reduce_scatter | solution.py:309
  1827.1 501.1 %copy-start.11 = (bf16[2048,512]{1,0:T(8,128)(2,1)S(1)}, bf16[2048,512]{1,0:T(8,128)(2,1)}, u32[]{:S(2)}) copy-start(bf16[2048,512]{1,0:T(8,128)(2,1)} %all-gather.5.cloned.1.call-done) | copy-start | bytes 6291460
  1827.2 596.3 %all-reduce.46.cloned.1.call-start = ((), (), s32[]{:S(2)}) async-start(), calls=%async_computation.13 | async-start | bytes 9306112 | tf_op jit(solution)/shard_map/psum | solution.py:314
  (78 other events, 1243.9 us)
Sparse Core Ops, SparseCore 0:
  10.2 51.9 all-gather.4
  64.4 96.7 all-gather.6
  163.3 48.1 all-gather.8
  212.8 540.0 all-gather.10
  1510.5 121.6 all-reduce.43
  1635.6 69.4 reduce-scatter.8
  1708.7 66.7 reduce-scatter.4
  1779.7 94.6 reduce-scatter.6
  1878.3 449.7 reduce-scatter.10
  2330.8 92.5 all-reduce.45
where the time goes:
time: 2460 us; the launch traced here: 2440 us
  waiting for transfers between devices  1050 us (43%)
  local copies, waits for them, and re-layouts  558 us (23%)
  blocking collectives  371 us (15%)
  other arithmetic  196 us (8%)
  matrix products  182 us (7%)
  starting transfers between devices  42.5 us (2%)
  between operations  41.2 us (2%)
    reduce_scatter x1, waiting for transfers between devices, on_device(): lax.psum_scatter(grad_heads_full.astype(jnp.bfloat16), 'fsdp', scatter_di...  454 us
    all_gather x1, waiting for transfers between devices, on_device(): heads_all = lax.all_gather(w_heads, 'fsdp', axis=0, tiled=True)  267 us
    psum x4, blocking collectives, norm_forward(): lax.psum((jnp.sum(value, axis=0), jnp.sum(value * value, axis=0)), ('fsdp...  208 us
    psum x3, blocking collectives, norm_backward(): lax.psum((jnp.sum(grad * normed, axis=0), jnp.sum(grad, axis=0)), ('fsdp'...  122 us
    transpose x6, local copies, waits for them, and re-layouts, head_matrix(): weight.reshape(depth, 3, 3, width).transpose(2, 0, 1, 3)  117 us
    psum x1, waiting for transfers between devices, norm_backward(): lax.psum((jnp.sum(grad * normed, axis=0), jnp.sum(grad, axis=0)), ('fsdp'...  116 us
    unnamed x218, local copies, waits for them, and re-layouts  97.3 us
    psum x1, waiting for transfers between devices, on_device(): lax.psum(red_shard.astype(jnp.bfloat16), 'dp').astype(jnp.float32)  87.7 us
  transfers between devices with their start and end apart: 22, of which 8 were waited for; matrix products, arithmetic and copies ran while one was open for 22% of the time, Pallas kernels for 0%

commit v1 on v0

v1 whole, which is shorter than its diff:
```python
import itertools

import jax
import jax.numpy as jnp
import numpy as np
from jax import lax
from jax.sharding import Mesh
from jax.sharding import PartitionSpec as P

W_UNIT = 12


eps = 1e-05
mid_rate = 2
head_rates = (12, 24, 36)
AXES = ("z", "y", "x", "c")
LINE = ("z", "y")
low = jnp.bfloat16
full = jnp.float32


def coords(names):
    return list(itertools.product(*[range(lax.axis_size(name)) for name in names]))


def flip(value, moves):
    moves = sorted(moves, key=lambda move: AXES.index(move[0]))
    names = tuple(name for name, _ in moves)
    places = coords(names)
    index = {place: i for i, place in enumerate(places)}
    pairs = [
        (i, index[tuple(at ^ bit for at, (_, bit) in zip(place, moves))])
        for i, place in enumerate(places)
    ]
    return lax.ppermute(value, names, pairs)


def all_sum(value):
    moves = []
    for name in ("y", "x", "z"):
        bit = 1
        while bit < lax.axis_size(name):
            moves.append((name, bit))
            bit *= 2
    value = value + flip(value, [("c", 1)])
    while moves:
        if len(moves) == 1:
            value = value + flip(value, moves)
            break
        first, second = moves[:2]
        moves = moves[2:]
        both = [(first[0], first[1] | second[1])] if first[0] == second[0] else [first, second]
        one, two, three = flip(value, [first]), flip(value, [second]), flip(value, both)
        value = (value + one) + (two + three)
    return value


def rows_to(value, pairs):
    if not pairs:
        return jnp.zeros_like(value)
    return lax.ppermute(value, LINE, pairs)


def line_size():
    return lax.axis_size("z") * lax.axis_size("y")


def half_of(value, axis, core):
    size = value.shape[axis] // 2
    return lax.dynamic_slice_in_dim(value, core * size, size, axis=axis)


def both_halves(mine, other, core, axis):
    first = jnp.where(core == 0, mine, other)
    second = jnp.where(core == 0, other, mine)
    return jnp.stack([first, second], axis=axis)


def gather_rows(shard, axis):
    core = lax.axis_index("c")
    mine = lax.all_gather(half_of(shard, axis, core), LINE, axis=0, tiled=False)
    other = flip(mine, [("c", 1)])
    return both_halves(mine, other, core, axis + 1)


def scatter_rows(partial, axis):
    core = lax.axis_index("c")
    mine = half_of(partial, axis + 1, core)
    other = flip(half_of(partial, axis + 1, 1 - core), [("c", 1)])
    summed = (mine.astype(full) + other.astype(full)).astype(low)
    own = lax.psum_scatter(summed, LINE, scatter_dimension=0, tiled=False)
    bit = 1
    while bit < lax.axis_size("x"):
        own = (own.astype(full) + flip(own, [("x", bit)]).astype(full)).astype(low)
        bit *= 2
    other = flip(own, [("c", 1)])
    whole = both_halves(own, other, core, axis)
    return whole.reshape(own.shape[:axis] + (-1,) + own.shape[axis + 1 :]).astype(full)


def along(value, offset, axis):
    size = value.shape[axis]
    if offset == 0:
        return value
    widths = [(0, 0)] * value.ndim
    if offset > 0:
        widths[axis] = (0, offset)
        return lax.slice_in_dim(jnp.pad(value, widths), offset, offset + size, axis=axis)
    widths[axis] = (-offset, 0)
    return lax.slice_in_dim(jnp.pad(value, widths), 0, size, axis=axis)


def crop_table(crop_scale, crop_group, group, unit, cols):
    mine = (crop_group == group).astype(jnp.int32)
    widths = crop_scale * unit * mine
    ends = jnp.cumsum(widths)
    starts = ends - widths
    column = jnp.arange(cols, dtype=jnp.int32)[:, None]
    return ((column >= starts[None, :]) & (column < ends[None, :])).astype(full)


def silu_slope(value):
    sigma = jax.nn.sigmoid(value)
    return sigma * (1.0 + value * (1.0 - sigma))


def norm_scale(value, count):
    sums = all_sum(jnp.stack([jnp.sum(value, axis=0), jnp.sum(value * value, axis=0)]))
    mean = sums[0] / count
    return mean, lax.rsqrt(sums[1] / count - mean * mean + eps)


def head_plan(rows):
    line = line_size()
    terms = []
    for task, rate in enumerate(head_rates):
        hop = rate // rows
        for side in (-1, 1):
            if hop < line:
                terms.append((task, side, hop))
    last = lax.axis_size("y")
    planes = []
    for z in range(lax.axis_size("z")):
        need = []
        for e, (task, side, hop) in enumerate(terms):
            if any(0 <= z * last + y - side * hop < line for y in range(last)):
                need.append(e)
        planes.append(need)
    slots = max(len(need) for need in planes)
    table = np.zeros((slots, line), np.int32)
    for z, need in enumerate(planes):
        rest = [e for e in range(len(terms)) if e not in need]
        for s, e in enumerate((need + rest)[:slots]):
            table[s, z * last : (z + 1) * last] = e
    return terms, table


def task_scales(gram):
    norms = jnp.sqrt(jnp.stack([gram[0, 0], gram[1, 1], gram[2, 2]]) + 1e-12)
    corr = gram / (norms[:, None] * norms[None, :]) + 0.1 * jnp.eye(3, dtype=full)
    adjugate = jnp.stack(
        [
            jnp.cross(corr[:, 1], corr[:, 2]),
            jnp.cross(corr[:, 2], corr[:, 0]),
            jnp.cross(corr[:, 0], corr[:, 1]),
        ]
    )
    weights = jnp.sum(adjugate, axis=1)
    return 3.0 * weights * jnp.mean(norms) / (norms * jnp.sum(weights))


def dot(a, b):
    return jnp.dot(a, b, preferred_element_type=full)


def dot_nt(a, b):
    return lax.dot_general(a, b, (((1,), (1,)), ((), ())), preferred_element_type=full)


def dot_tn(a, b):
    return lax.dot_general(a, b, (((0,), (0,)), ((), ())), preferred_element_type=full)


def on_device(
    features,
    crop_scale,
    crop_group,
    labels,
    w_reduce,
    gain_reduce,
    bias_reduce,
    w_middle,
    gain_middle,
    bias_middle,
    w_expand,
    gain_expand,
    bias_expand,
    w_heads,
    gain_heads,
    bias_heads,
    w_class,
    b_class,
):
    rows = features.shape[1]
    cols = features.shape[2]
    depth = features.shape[3]
    width = w_reduce.shape[1]
    tasks = w_heads.shape[1]
    head = w_heads.shape[3]
    own = w_heads.shape[0]
    classes = w_class.shape[2]
    pixels = rows * cols
    line = line_size()
    place = lax.axis_index(LINE)
    group = lax.axis_index(("x", "c"))
    inside = crop_table(crop_scale, crop_group, group, W_UNIT, cols)

    def same(offset):
        return jnp.tile(jnp.sum(inside * along(inside, offset, 0), axis=1), rows)[:, None]

    valid = same(0)
    count = jnp.sum(crop_scale).astype(full) * float(W_UNIT * rows * line)
    crops = float(crop_scale.shape[0])

    red_all = gather_rows(w_reduce, 0).reshape(depth, width)
    mid_own = w_middle.reshape(-1, 3, 3, width).transpose(1, 0, 2, 3).reshape(3, -1, 3 * width)
    mid_all = gather_rows(mid_own, 1)
    mid_all = mid_all.transpose(1, 0, 2, 3, 4).reshape(3 * width, 3 * width)
    exp_all = gather_rows(w_expand, 0).reshape(width, depth)
    terms, table = head_plan(rows)
    slots = table.shape[0]
    by_term = w_heads.reshape(own, tasks, 3, 3, head).transpose(1, 2, 0, 3, 4)
    by_term = by_term.reshape(tasks, 3, own, 3 * head)
    parts = [by_term[t, 1] for t in range(tasks)] + [by_term[t, s + 1] for t, s, _ in terms]
    heads_all = gather_rows(jnp.stack(parts), 1)
    heads_all = heads_all.transpose(1, 0, 2, 3, 4).reshape(len(parts), depth, 3 * head)
    picked_term = [jnp.asarray(table[s])[place] for s in range(slots)]

    def slot_weight(s):
        if (table[s] == table[s][0]).all():
            return heads_all[tasks + int(table[s][0])]
        return lax.dynamic_index_in_dim(heads_all, tasks + picked_term[s], 0, keepdims=False)

    source = features.reshape(pixels, depth) * valid.astype(low)
    reduced = dot(source, red_all)
    mean1, scale1 = norm_scale(reduced, count)
    normed1 = (reduced - mean1) * scale1
    out1 = normed1 * gain_reduce + bias_reduce
    hidden1 = (jax.nn.silu(out1) * valid).astype(low)
    edge = mid_rate * cols
    down = [(i, i + 1) for i in range(line - 1)]
    up = [(i + 1, i) for i in range(line - 1)]
    before1 = rows_to(hidden1[pixels - edge :], down)
    after1 = rows_to(hidden1[:edge], up)
    tall = jnp.concatenate([before1, hidden1, after1], axis=0)
    wide1 = jnp.concatenate([tall[i * edge : i * edge + pixels] for i in range(3)], axis=1)
    spread = dot(wide1, mid_all)
    mid_masks = [same((k - 1) * mid_rate) for k in range(3)]
    middled = sum(
        along(spread[:, k * width : (k + 1) * width], (k - 1) * mid_rate, 0) * mid_masks[k]
        for k in range(3)
    )
    mean2, scale2 = norm_scale(middled, count)
    normed2 = (middled - mean2) * scale2
    out2 = normed2 * gain_middle + bias_middle
    hidden2 = (jax.nn.silu(out2) * valid).astype(low)
    expanded = dot(hidden2, exp_all)
    mean3, scale3 = norm_scale(expanded, count)
    normed3 = (expanded - mean3) * scale3
    before = normed3 * gain_expand + bias_expand + source.astype(full)
    grid = (jax.nn.silu(before) * valid).astype(low)

    masks = [[same((k - 1) * rate) for k in range(3)] for rate in head_rates]

    def gathered(spread, task):
        rate = head_rates[task]
        return sum(
            along(spread[:, k * head : (k + 1) * head], (k - 1) * rate, 0) * masks[task][k]
            for k in range(3)
        )

    def choose(s, by_task):
        tasks_of = [terms[e][0] for e in table[s]]
        chosen = by_task(tasks_of[0])
        for task in sorted(set(tasks_of) - {tasks_of[0]}):
            here = jnp.asarray(np.array([t == task for t in tasks_of]))[place]
            chosen = jnp.where(here, by_task(task), chosen)
        return chosen

    side_terms = []
    for s in range(slots):
        spread = dot(grid, slot_weight(s))
        side_terms.append(choose(s, lambda task: gathered(spread, task)).astype(low))
    moved = [None] * tasks
    for e, (task, side, hop) in enumerate(terms):
        pairs = [(f, f - side * hop) for f in range(line) if 0 <= f - side * hop < line]
        using = [s for s in range(slots) if any(table[s, f] == e for f, _ in pairs)]
        sent = side_terms[using[0]]
        for s in using[1:]:
            sent = jnp.where(picked_term[s] == e, side_terms[s], sent)
        got = rows_to(sent, pairs).astype(full)
        moved[task] = got if moved[task] is None else moved[task] + got
    mixed = []
    for task in range(tasks):
        center = gathered(dot(grid, heads_all[task]), task)
        mixed.append(center if moved[task] is None else center + moved[task])
    mixed = jnp.concatenate(mixed, axis=1)
    gain_h, bias_h = gain_heads.reshape(-1), bias_heads.reshape(-1)
    mean_h, scale_h = norm_scale(mixed, count)
    normed_h = (mixed - mean_h) * scale_h
    out_h = normed_h * gain_h + bias_h
    activ = (jax.nn.silu(out_h) * valid).astype(low)
    marks = labels.reshape(tasks, pixels)
    class_part, class_bias_part, dactiv = [], [], []
    for task in range(tasks):
        act = activ[:, task * head : (task + 1) * head]
        logits = dot(act, w_class[task]) + b_class[task]
        onehot = (marks[task][:, None] == jnp.arange(classes, dtype=jnp.int32)[None, :]).astype(full)
        dlogits = ((jax.nn.softmax(logits, axis=-1) - onehot) * valid / crops).astype(low)
        class_part.append(dot_tn(act, dlogits))
        class_bias_part.append(jnp.sum(dlogits.astype(full), axis=0))
        dactiv.append(dot_nt(dlogits, w_class[task]))
    dout_h = jnp.concatenate(dactiv, axis=1) * valid * silu_slope(out_h)
    sums_h = all_sum(jnp.stack([jnp.sum(dout_h * normed_h, axis=0), jnp.sum(dout_h, axis=0)]))
    dgain_h, dbias_h = sums_h[0], sums_h[1]
    dmixed = valid * (gain_h * scale_h) * (dout_h - dbias_h / count - normed_h * (dgain_h / count))
    dmixed = dmixed.astype(low)

    def spread_back(grad, task):
        rate = head_rates[task]
        return jnp.concatenate(
            [along(grad * masks[task][k].astype(low), -(k - 1) * rate, 0) for k in range(3)], axis=1
        )

    back = []
    for task, side, hop in terms:
        pairs = [(f, f + side * hop) for f in range(line) if 0 <= f + side * hop < line]
        back.append(rows_to(dmixed[:, task * head : (task + 1) * head], pairs))
    shared_grads, head_parts = [], [None] * len(parts)
    for task in range(tasks):
        dspread = spread_back(dmixed[:, task * head : (task + 1) * head], task)
        shared_grads.append(dot_nt(dspread, heads_all[task]))
        head_parts[task] = dot_tn(grid, dspread).astype(low)
    for s in range(slots):
        dside = back[table[s][0]]
        for e in sorted(set(table[s].tolist()) - {int(table[s][0])}):
            dside = jnp.where(picked_term[s] == e, back[e], dside)
        dspread = choose(s, lambda task: spread_back(dside, task))
        dshared = dot_nt(dspread, slot_weight(s))
        dweight = dot_tn(grid, dspread).astype(low)
        tasks_of = np.array([terms[e][0] for e in table[s]])
        for task in sorted(set(tasks_of.tolist())):
            here = jnp.asarray((tasks_of == task).astype(np.float32))[place]
            shared_grads[task] = shared_grads[task] + here * dshared
        for e in sorted(set(table[s].tolist())):
            here = jnp.asarray((table[s] == e).astype(np.float32))[place].astype(low)
            part = here * dweight
            held = head_parts[tasks + e]
            head_parts[tasks + e] = part if held is None else held + part
    slope3 = valid * silu_slope(before)
    sums = []
    for task in range(tasks):
        part = shared_grads[task] * slope3
        sums += [jnp.sum(part * normed3, axis=0), jnp.sum(part, axis=0)]
    gram_part = jnp.stack(
        [jnp.sum(shared_grads[t] * shared_grads[u]) for t in range(tasks) for u in range(tasks)]
    )
    class_part = jnp.stack(class_part).reshape(-1)
    class_bias_part = jnp.stack(class_bias_part).reshape(-1)
    small = jnp.concatenate([class_part, class_bias_part, gram_part])
    short = -small.shape[0] % depth
    small = jnp.pad(small, (0, short)).reshape(-1, depth)
    summed = all_sum(jnp.concatenate([jnp.stack(sums), small], axis=0))
    sums3 = summed[: 2 * tasks].reshape(tasks, 2, depth)
    small = summed[2 * tasks :].reshape(-1)
    size = tasks * head * classes
    grad_class = small[:size].reshape(tasks, head, classes)
    grad_class_bias = small[size : size + tasks * classes].reshape(tasks, classes)
    gram = small[size + tasks * classes :][: tasks * tasks].reshape(tasks, tasks)
    task_weights = task_scales(gram)
    head_full = jnp.stack(head_parts).reshape(len(parts), line, own, 3 * head).transpose(1, 0, 2, 3)
    head_own = scatter_rows(head_full, 1)

    combined = sum(task_weights[t] * shared_grads[t] for t in range(tasks))
    dgain3, dbias3 = (
        sum(task_weights[t] * sums3[t, j] for t in range(tasks)) for j in range(2)
    )
    dbefore = combined * slope3
    dexpanded = valid * (gain_expand * scale3) * (
        dbefore - dbias3 / count - normed3 * (dgain3 / count)
    )
    dexpanded = dexpanded.astype(low)
    dhidden2 = dot_nt(dexpanded, exp_all)
    dout2 = dhidden2 * valid * silu_slope(out2)
    sums2 = all_sum(jnp.stack([jnp.sum(dout2 * normed2, axis=0), jnp.sum(dout2, axis=0)]))
    dgain2, dbias2 = sums2[0], sums2[1]
    exp_own = scatter_rows(dot_tn(hidden2, dexpanded).astype(low).reshape(line, -1, depth), 0)
    dmiddled = valid * (gain_middle * scale2) * (
        dout2 - dbias2 / count - normed2 * (dgain2 / count)
    )
    dmiddled = dmiddled.astype(low)
    dspread = jnp.concatenate(
        [along(dmiddled * mid_masks[k].astype(low), -(k - 1) * mid_rate, 0) for k in range(3)],
        axis=1,
    )
    dwide = dot_nt(dspread, mid_all)
    from_below = rows_to(dwide[:edge, :width].astype(low), up).astype(full)
    from_above = rows_to(dwide[pixels - edge :, 2 * width :].astype(low), down).astype(full)
    dhidden1 = (
        dwide[:, width : 2 * width]
        + jnp.concatenate([dwide[edge:, :width], from_below], axis=0)
        + jnp.concatenate([from_above, dwide[: pixels - edge, 2 * width :]], axis=0)
    )
    dout1 = dhidden1 * valid * silu_slope(out1)
    sums1 = all_sum(jnp.stack([jnp.sum(dout1 * normed1, axis=0), jnp.sum(dout1, axis=0)]))
    dgain1, dbias1 = sums1[0], sums1[1]
    mid_part = dot_tn(wide1, dspread).astype(low).reshape(3, line, -1, 3 * width)
    mid_sum = scatter_rows(mid_part.transpose(1, 0, 2, 3), 1)
    mid_sum = mid_sum.reshape(3, -1, 3, width).transpose(1, 0, 2, 3).reshape(w_middle.shape)
    dreduced = valid * (gain_reduce * scale1) * (
        dout1 - dbias1 / count - normed1 * (dgain1 / count)
    )
    dreduced = dreduced.astype(low)
    red_own = scatter_rows(dot_tn(source, dreduced).astype(low).reshape(line, -1, width), 0)
    dfeatures = dbefore + dot_nt(dreduced, red_all)

    zero = jnp.zeros((own, 3 * head), full)
    ordered = [[zero, head_own[t], zero] for t in range(tasks)]
    for e, (task, side, _) in enumerate(terms):
        ordered[task][side + 1] = head_own[tasks + e]
    heads_out = jnp.stack([part for row in ordered for part in row])
    heads_out = heads_out.reshape(tasks, 3, own, 3, head).transpose(2, 0, 1, 3, 4)
    return (
        dfeatures.reshape(1, rows, cols, depth),
        red_own,
        mid_sum,
        exp_own,
        heads_out.reshape(w_heads.shape),
        dgain1,
        dbias1,
        dgain2,
        dbias2,
        dgain3,
        dbias3,
        dgain_h.reshape(tasks, head),
        dbias_h.reshape(tasks, head),
        grad_class,
        grad_class_bias,
        task_weights,
    )


def solution(mesh):
    line, groups = mesh.shape["fsdp"], mesh.shape["dp"]
    fine = Mesh(mesh.devices.reshape(line // 2, 2, groups // 2, 2), AXES)
    dp = ("x", "c")
    rows = P(LINE)
    in_specs = (
        P(dp, LINE, None, None),
        P(),
        P(),
        P(None, dp, LINE, None),
        rows,
        P(),
        P(),
        rows,
        P(),
        P(),
        rows,
        P(),
        P(),
        rows,
        P(),
        P(),
        P(),
        P(),
    )
    out_specs = (P(dp, LINE, None, None),) + (rows,) * 4 + (P(),) * 11
    return jax.shard_map(
        on_device, mesh=fine, in_specs=in_specs, out_specs=out_specs, check_vma=False
    )
```

time: 2460 us -> 1150 us (0.47)
  local copies, waits for them, and re-layouts: 558 us -> 113 us
  waiting for transfers between devices: 1050 us -> 632 us
  blocking collectives: 371 us -> 0 us
  other arithmetic: 196 us -> 108 us
  starting transfers between devices: 42.5 us -> 111 us
  matrix products: 182 us -> 128 us
    psum x8 -> x0, blocking collectives: 371 us -> none  [the longest x4 208 us: norm_forward(): lax.psum((jnp.sum(value, axis=0), jnp.sum(value * value, axis=0)), ('fsdp...]
    reduce_scatter x4, waiting for transfers between devices: 501 us -> 275 us  [scatter_rows(): own = lax.psum_scatter(summed, LINE, scatter_dimension=0, tiled=False)]
    psum x2 -> x0, waiting for transfers between devices: 204 us -> none  [the longest x1 116 us: norm_backward(): lax.psum((jnp.sum(grad * normed, axis=0), jnp.sum(grad, axis=0)), ('fsdp'...]
    transpose x10 -> x2, local copies, waits for them, and re-layouts: 148 us -> 8.18 us  [the longest x1 7.67 us: on_device(): heads_all.transpose(1, 0, 2, 3, 4).reshape(len(parts), depth, 3 * head)]
    reshape x6 -> x11, local copies, waits for them, and re-layouts: 112 us -> 7.97 us  [the longest x2 3.32 us: on_device(): mid_sum.reshape(3, -1, 3, width).transpose(1, 0, 2, 3)]
    dot_general x11 -> x0, local copies, waits for them, and re-layouts: 84 us -> none  [the longest x3 38.8 us: on_device(): jnp.dot(stacks[task].T, dterms, preferred_element_type=jnp.float32)]
    ppermute x12 -> x84, waiting for transfers between devices: 31.3 us -> 111 us  [the longest x72 80.8 us: flip(): return lax.ppermute(value, names, pairs)]
    another operation x7 -> x20, local copies, waits for them, and re-layouts: 88.9 us -> 11.6 us  [the longest x2 8.94 us: on_device(): heads_out = jnp.stack([part for row in ordered for part in row])]
  transfers between devices with their start and end apart: 22 -> 92, of which waited for: 8 -> 58; matrix products, arithmetic and copies ran while one was open for 22% -> 19% of each run, Pallas kernels for 0% -> 0%
where the time goes in v1:
time: 1150 us; the launch traced here: 1140 us
  waiting for transfers between devices  632 us (55%)
  matrix products  128 us (11%)
  local copies, waits for them, and re-layouts  113 us (10%)
  starting transfers between devices  111 us (10%)
  other arithmetic  108 us (9%)
  between operations  48.2 us (4%)
    reduce_scatter x4, waiting for transfers between devices, scatter_rows(): own = lax.psum_scatter(summed, LINE, scatter_dimension=0, tiled=False)  275 us
    all_gather x4, waiting for transfers between devices, gather_rows(): mine = lax.all_gather(half_of(shard, axis, core), LINE, axis=0, tiled=False)  246 us
    ppermute x72, waiting for transfers between devices, flip(): return lax.ppermute(value, names, pairs)  80.8 us
    ppermute x72, starting transfers between devices, flip(): return lax.ppermute(value, names, pairs)  72.1 us
    dot_general x11, matrix products, dot_nt(): lax.dot_general(a, b, (((1,), (1,)), ((), ())), preferred_element_type=full)  64.9 us
    unnamed x250, local copies, waits for them, and re-layouts  53.4 us
    ppermute x12, starting transfers between devices, rows_to(): return lax.ppermute(value, LINE, pairs)  38 us
    dot_general x11, matrix products, dot_tn(): lax.dot_general(a, b, (((0,), (0,)), ((), ())), preferred_element_type=full)  33.9 us
  transfers between devices with their start and end apart: 92, of which 58 were waited for; matrix products, arithmetic and copies ran while one was open for 19% of the time, Pallas kernels for 0%

profile of v1, /device:TPU:0, one launch (start us, length us, event | category | flops | bytes accessed | tf_op | source)
XLA Modules:
  0.0 1139.1 jit_solution(5608299086180602053)
XLA Ops:
  12.1 5.7 copy.169
  30.1 23.5 %all-gather.9.cloned.1.call-done = bf16[1024,512]{1,0:T(8,128)(2,1)} async-done(((bf16[128,512]{1,0:T(8,128)(2,1)}), bf16[1024,512]{1,0:T(8,128)(2,1)}) %all-gather.9.cloned.1.call-update) | async-done | bytes 1048592 | tf_op jit(solution)/shard_map/all_gather | solution.py:81
  56.4 50.8 %all-gather.11.cloned.1.call-done = bf16[24,32,1536]{2,1,0:T(8,128)(2,1)} async-done(((bf16[3,32,1536]{2,1,0:T(8,128)(2,1)}), bf16[24,32,1536]{2,1,0:T(8,128)(2,1)}) %all-gather.11.cloned.1.call-update) | async-done | bytes 2359312 | tf_op jit(solution)/shard_map/all_gather | solution.py:81
  107.2 158.6 %all-gather.15.cloned.1.call-done = bf16[56,128,768]{2,1,0:T(8,128)(2,1)} async-done(((bf16[7,128,768]{2,1,0:T(8,128)(2,1)}), bf16[56,128,768]{2,1,0:T(8,128)(2,1)}) %all-gather.15.cloned.1.call-update) | async-done | bytes 11010064 | tf_op jit(solution)/shard_map/all_gather | solution.py:81
  272.6 10.2 collective-permute-done.1
  293.3 13.5 %all-gather.13.cloned.1.call-done = bf16[256,2048]{1,0:T(8,128)(2,1)} async-done(((bf16[32,2048]{1,0:T(8,128)(2,1)}), bf16[256,2048]{1,0:T(8,128)(2,1)}) %all-gather.13.cloned.1.call-update) | async-done | bytes 1048592 | tf_op jit(solution)/shard_map/all_gather | solution.py:81
  308.9 4.6 collective-permute-start.8
  316.5 4.4 collective-permute-done.9
  320.9 7.4 collective-permute-done.8
  328.3 3.8 fusion.72
  349.2 4.9 fusion.126
  371.1 7.2 multiply_convert_fusion.1
  378.3 12.3 %select_bitcast_fusion.1 = (bf16[8,7,1,128,768]{4,3,1,0,2:T(8,128)(2,1)S(1)}, bf16[8,7,1,128,768]{4,3,1,0,2:T(8,128)(2,1)}) fusion(bf16[8,7,128,768]{3,2,1,0:T(8,128)(2,1)} %bitcast.333, bf16[8,7,128,768]{3,2,1,0:T(8,128)(2,1)} %collective-permute-done.26, pred[]{:T(512)S(6)} %eq.93), kind=kLoop, calls=%fused_computation.5 | loop fusion | flops 11010048 | bytes 44040192 | tf_op jit(solution)/shard_map/stack | solution.py:76
  390.5 8.8 maximum_bitcast_fusion
  399.3 7.7 copy.172
  407.7 5.4 fusion.7
  415.0 4.5 fusion.4
  423.0 6.4 collective-permute-start.29
  436.7 5.5 collective-permute-start.27
  453.1 4.0 collective-permute-start.34
  461.5 6.1 collective-permute-start.37
  502.5 8.3 collective-permute-start.47
  526.0 4.6 fusion.57
  532.2 4.1 convolution_convert_fusion.2
  536.4 7.5 fusion.2
  543.9 12.5 %broadcast_multiply_fusion.1 = (bf16[2048,768]{1,0:T(8,128)(2,1)S(1)}, bf16[2048,768]{1,0:T(8,128)(2,1)}, bf16[2048,768]{1,0:T(8,128)(2,1)}, bf16[2048,768]{1,0:T(8,128)(2,1)}) fusion(bf16[]{:T(256)} %bitcast.137, bf16[]{:T(256)} %bitcast.141, bf16[]{:T(256)} %bitcast.138, bf16[2048,768]{1,0:T(8,128)(2,1)} %convolution_convert_fusion.2, bf16[]{:T(256)} %bitcast.134, ...), kind=kOutput, calls=%fused_computation.89 | convolution fusion | flops 2434007040 | bytes 20840456 | tf_op jit(solution)/shard_map/dot_general | solution.py:181
  561.6 5.5 dynamic-slice_bitcast_fusion
  567.1 7.3 copy-done.3
  574.5 7.8 multiply_add_fusion
  582.5 6.8 multiply_add_fusion.1
  589.4 19.0 %multiply_reduce_fusion.6 = (f32[2048]{0:T(1024)S(1)}, f32[2048]{0:T(1024)S(1)}, f32[2048]{0:T(1024)S(1)}, f32[]{:T(128)}, f32[]{:T(128)}, /*index=5*/f32[]{:T(1...) fusion(f32[2048]{0:T(1024)S(1)} %bitcast.381, ...), kind=kOutput, calls=%fused_computation.15 | convolution fusion | flops 2479214592 | bytes 39013400 | tf_op jit(solution)/shard_map/dot_general | solution.py:177
  608.4 5.9 concatenate.72
  631.0 8.4 collective-permute-done.54
  675.5 17.5 %multiply_convert_fusion = (bf16[768,2048]{1,0:T(8,128)(2,1)S(1)}, f32[768,2048]{1,0:T(8,128)}) fusion(f32[2048]{0:T(1024)S(1)} %broadcast_divide_fusion, f32[2048]{0:T(1024)S(1)} %broadcast_divide_fusion.1, f32[2048]{0:T(1024)S(1)} %mul.1134, f32[768]{0:T(1024)S(1)} %mul.956, f32[2048]{0:T(1024)S(1)} %bitcast.383, f32[768,2048]{1,0:T(8,128)} %get-tuple-element.291, ...), kind=kLoop, calls=%fused_computation.7 | loop fusion | flops 22020096 | bytes 40938508 | tf_op jit(solution)/shard_map/convert_element_type | solution.py:392
  699.5 13.9 %fusion = bf16[8,7,128,768]{3,2,1,0:T(8,128)(2,1)} fusion(bf16[8,7,128,768]{3,2,1,0:T(8,128)(2,1)} %collective-permute-done.81, bf16[7,8,256,768]{3,2,0,1:T(8,128)(2,1)} %copy-done.3, s32[]{:T(128)S(6)} %select_n.180), kind=kLoop, calls=%fused_computation.2 | loop fusion | flops 22020096 | bytes 33030148 | tf_op jit(solution)/shard_map/convert_element_type | solution.py:90
  713.5 5.0 multiply_reduce_fusion.16
  735.3 5.8 fusion.161
  746.2 14.2 %collective-permute-done.64 = bf16[384,512]{1,0:T(8,128)(2,1)S(1)} collective-permute-done((bf16[384,512]{1,0:T(8,128)(2,1)S(1)}, bf16[384,512]{1,0:T(8,128)(2,1)S(1)}, u32[]{:S(2)}, u32[]{:S(2)}) %collective-permute-start.64) | collective-permute-done | bytes 393248 | tf_op jit(solution)/shard_map/ppermute | solution.py:61
  774.2 3.9 convolution_convert_fusion
  789.1 3.9 fusion.1
  800.1 7.4 convolution_add_fusion
  807.6 145.2 %reduce-scatter.11.cloned.1.call-done = bf16[1,7,128,768]{3,2,1,0:T(8,128)(2,1)} async-done(((bf16[8,7,128,768]{3,2,1,0:T(8,128)(2,1)}), bf16[1,7,128,768]{3,2,1,0:T(8,128)(2,1)}) %reduce-scatter.11.cloned.1.call-update) | async-done | bytes 1376272 | tf_op jit(solution)/shard_map/reduce_scatter | solution.py:91
  954.3 65.4 %reduce-scatter.5.cloned.1.call-done = bf16[1,128,512]{2,1,0:T(8,128)(2,1)} async-done(((bf16[8,128,512]{2,1,0:T(8,128)(2,1)}), bf16[1,128,512]{2,1,0:T(8,128)(2,1)}) %reduce-scatter.5.cloned.1.call-update) | async-done | bytes 131088 | tf_op jit(solution)/shard_map/reduce_scatter | solution.py:91
  1021.2 3.7 collective-permute-done.73
  1027.2 64.4 %reduce-scatter.7.cloned.1.call-done = bf16[1,3,32,1536]{3,2,1,0:T(8,128)(2,1)} async-done(((bf16[8,3,32,1536]{3,2,1,0:T(8,128)(2,1)}), bf16[1,3,32,1536]{3,2,1,0:T(8,128)(2,1)}) %reduce-scatter.7.cloned.1.call-update) | async-done | bytes 294928 | tf_op jit(solution)/shard_map/reduce_scatter | solution.py:91
  1094.8 4.7 collective-permute-done.76
  1115.8 8.0 copy.191
  1123.8 8.0 copy.192
  (655 shorter events, 267.0 us)
Async XLA Ops:
  7.2 46.4 %all-gather.9.cloned.1.call-start = ((), (), s32[]{:S(2)}) async-start(), calls=%async_computation.8 | async-start | bytes 1179648 | tf_op jit(solution)/shard_map/all_gather | solution.py:81
  8.8 98.4 %all-gather.11.cloned.1.call-start = ((), (), s32[]{:S(2)}) async-start(), calls=%async_computation.9 | async-start | bytes 2654208 | tf_op jit(solution)/shard_map/all_gather | solution.py:81
  12.1 253.7 %all-gather.15.cloned.1.call-start = ((), (), s32[]{:S(2)}) async-start(), calls=%async_computation.11 | async-start | bytes 12386304 | tf_op jit(solution)/shard_map/all_gather | solution.py:81
  29.1 277.6 %all-gather.13.cloned.1.call-start = ((), (), s32[]{:S(2)}) async-start(), calls=%async_computation.10 | async-start | bytes 1179648 | tf_op jit(solution)/shard_map/all_gather | solution.py:81
  29.9 763.1 %reduce-scatter.9.cloned.1.call-start = ((), (), s32[]{:S(2)}) async-start(), calls=%async_computation.6 | async-start | bytes 1179648 | tf_op jit(solution)/shard_map/reduce_scatter | solution.py:91
  53.6 212.2 %collective-permute-start = (bf16[8,128,512]{2,1,0:T(8,128)(2,1)}, bf16[8,128,512]{2,1,0:T(8,128)(2,1)}, u32[]{:S(2)}, u32[]{:S(2)}) collective-permute-start(bf16[8,128,512]{2,1,0:T(8,128)(2,1)} %bitcast.373), channel_id=1, source_target_pairs={{0,1},{1,0},{2,3},{3,2},{4,5},{5,4},{6,7},{7,6},{8,9},{9,8},{10,11... | collective-permute-start | bytes 3145736 | tf_op jit(solution)/shard_map/ppermute | solution.py:35
  107.2 206.3 %collective-permute-start.10 = (bf16[8,3,32,1536]{3,2,1,0:T(8,128)(2,1)}, bf16[8,3,32,1536]{3,2,1,0:T(8,128)(2,1)}, u32[]{:S(2)}, u32[]{:S(2)}) collective-permute-start(bf16[8,3,32,1536]{3,2,1,0:T(8,128)(2,1)} %bitcast.361), channel_id=1, source_target_pairs={{0,1},{1,0},{2,3},{3,2},{4,5},{5,4},{6,7},{7,6},{8,9},{9,8},{10,11... | collective-permute-start | bytes 7077896 | tf_op jit(solution)/shard_map/ppermute | solution.py:35
  265.8 112.5 %collective-permute-start.26 = (bf16[8,7,128,768]{3,2,1,0:T(8,128)(2,1)}, bf16[8,7,128,768]{3,2,1,0:T(8,128)(2,1)}, u32[]{:S(2)}, u32[]{:S(2)}) collective-permute-start(bf16[8,7,128,768]{3,2,1,0:T(8,128)(2,1)} %bitcast.332), channel_id=1, source_target_pairs={{0,1},{1,0},{2,3},{3,2},{4,5},{5,4},{6,7},{7,6},{8,9},{9,8},{10,11... | collective-permute-start | bytes 33030152 | tf_op jit(solution)/shard_map/ppermute | solution.py:35
  272.0 10.7 collective-permute-start.1
  288.8 17.9 %collective-permute-start.6 = (f32[2,512]{1,0:T(2,128)S(1)}, f32[2,512]{1,0:T(2,128)S(1)}, u32[]{:S(2)}, u32[]{:S(2)}) collective-permute-start(f32[2,512]{1,0:T(2,128)S(1)} %add_add_fusion.15), channel_id=1, source_target_pairs={{0,16},{8,24},{16,0},{24,8},{1,17},{9,25},{17,1},{25,9},{2,18},{10... | collective-permute-start | bytes 12296 | tf_op jit(solution)/shard_map/ppermute | solution.py:35
  290.4 16.4 %collective-permute-start.7 = (f32[2,512]{1,0:T(2,128)S(1)}, f32[2,512]{1,0:T(2,128)S(1)}, u32[]{:S(2)}, u32[]{:S(2)}) collective-permute-start(f32[2,512]{1,0:T(2,128)S(1)} %add_add_fusion.15), channel_id=1, source_target_pairs={{0,24},{8,16},{16,8},{24,0},{1,25},{9,17},{17,9},{25,1},{2,26},{10... | collective-permute-start | bytes 12296 | tf_op jit(solution)/shard_map/ppermute | solution.py:35
  290.9 15.9 %collective-permute-start.5 = (f32[2,512]{1,0:T(2,128)S(1)}, f32[2,512]{1,0:T(2,128)S(1)}, u32[]{:S(2)}, u32[]{:S(2)}) collective-permute-start(f32[2,512]{1,0:T(2,128)S(1)} %add_add_fusion.15), channel_id=1, source_target_pairs={{0,8},{8,0},{16,24},{24,16},{1,9},{9,1},{17,25},{25,17},{2,10},{10... | collective-permute-start | bytes 12296 | tf_op jit(solution)/shard_map/ppermute | solution.py:35
  306.7 32.1 %collective-permute-start.18 = (bf16[8,32,2048]{2,1,0:T(8,128)(2,1)}, bf16[8,32,2048]{2,1,0:T(8,128)(2,1)S(1)}, u32[]{:S(2)}, u32[]{:S(2)}) collective-permute-start(bf16[8,32,2048]{2,1,0:T(8,128)(2,1)} %bitcast.371), channel_id=1, source_target_pairs={{0,1},{1,0},{2,3},{3,2},{4,5},{5,4},{6,7},{7,6},{8,9},{9,8},{10,11... | collective-permute-start | bytes 3145736 | tf_op jit(solution)/shard_map/ppermute | solution.py:35
  307.5 13.4 %collective-permute-start.9 = (bf16[384,512]{1,0:T(8,128)(2,1)S(1)}, bf16[384,512]{1,0:T(8,128)(2,1)S(1)}, u32[]{:S(2)}, u32[]{:S(2)}) collective-permute-start(bf16[384,512]{1,0:T(8,128)(2,1)S(1)} %get-tuple-element.234), channel_id=1, source_target_pairs={{4,0},{8,4},{12,8},{16,12},{20,16},{24,20},{28,24},{5,1},{9,5},{13... | collective-permute-start | bytes 1179656 | tf_op jit(solution)/shard_map/ppermute | solution.py:61
  308.9 19.4 %collective-permute-start.8 = (bf16[384,512]{1,0:T(8,128)(2,1)S(1)}, bf16[384,512]{1,0:T(8,128)(2,1)S(1)}, u32[]{:S(2)}, u32[]{:S(2)}) collective-permute-start(bf16[384,512]{1,0:T(8,128)(2,1)S(1)} %get-tuple-element.233), channel_id=1, source_target_pairs={{0,4},{4,8},{8,12},{12,16},{16,20},{20,24},{24,28},{1,5},{5,9},{9,... | collective-permute-start | bytes 1179656 | tf_op jit(solution)/shard_map/ppermute | solution.py:61
  361.8 9.2 collective-permute-start.24
  362.5 8.4 collective-permute-start.25
  364.8 6.1 collective-permute-start.23
  421.7 27.6 %collective-permute-start.30 = (bf16[768,256]{1,0:T(8,128)(2,1)S(1)}, bf16[768,256]{1,0:T(8,128)(2,1)S(1)}, u32[]{:S(2)}, u32[]{:S(2)}) collective-permute-start(bf16[768,256]{1,0:T(8,128)(2,1)S(1)} %get-tuple-element.170), channel_id=1, source_target_pairs={{24,0},{28,4},{25,1},{29,5},{26,2},{30,6},{27,3},{31,7}} | collective-permute-start | bytes 1179656 | tf_op jit(solution)/shard_map/ppermute | solution.py:61
  423.0 26.3 %collective-permute-start.29 = (bf16[768,256]{1,0:T(8,128)(2,1)S(1)}, bf16[768,256]{1,0:T(8,128)(2,1)S(1)}, u32[]{:S(2)}, u32[]{:S(2)}) collective-permute-start(bf16[768,256]{1,0:T(8,128)(2,1)S(1)} %get-tuple-element.170), channel_id=1, source_target_pairs={{0,24},{4,28},{1,25},{5,29},{2,26},{6,30},{3,27},{7,31}} | collective-permute-start | bytes 1179656 | tf_op jit(solution)/shard_map/ppermute | solution.py:61
  435.4 11.0 collective-permute-start.28
  436.7 12.6 %collective-permute-start.27 = (bf16[768,256]{1,0:T(8,128)(2,1)S(1)}, bf16[768,256]{1,0:T(8,128)(2,1)S(1)}, u32[]{:S(2)}, u32[]{:S(2)}) collective-permute-start(bf16[768,256]{1,0:T(8,128)(2,1)S(1)} %get-tuple-element.169), channel_id=1, source_target_pairs={{0,12},{4,16},{8,20},{12,24},{16,28},{1,13},{5,17},{9,21},{13,25},... | collective-permute-start | bytes 1179656 | tf_op jit(solution)/shard_map/ppermute | solution.py:61
  460.7 12.7 %collective-permute-start.36 = (f32[2,768]{1,0:T(2,128)S(1)}, f32[2,768]{1,0:T(2,128)S(1)}, u32[]{:S(2)}, u32[]{:S(2)}) collective-permute-start(f32[2,768]{1,0:T(2,128)S(1)} %add_add_fusion.7), channel_id=1, source_target_pairs={{0,16},{8,24},{16,0},{24,8},{1,17},{9,25},{17,1},{25,9},{2,18},{10... | collective-permute-start | bytes 18440 | tf_op jit(solution)/shard_map/ppermute | solution.py:35
  461.5 11.9 %collective-permute-start.37 = (f32[2,768]{1,0:T(2,128)S(1)}, f32[2,768]{1,0:T(2,128)S(1)}, u32[]{:S(2)}, u32[]{:S(2)}) collective-permute-start(f32[2,768]{1,0:T(2,128)S(1)} %add_add_fusion.7), channel_id=1, source_target_pairs={{0,24},{8,16},{16,8},{24,0},{1,25},{9,17},{17,9},{25,1},{2,26},{10... | collective-permute-start | bytes 18440 | tf_op jit(solution)/shard_map/ppermute | solution.py:35
  467.6 5.9 collective-permute-start.35
  499.4 31.2 %collective-permute-start.45 = (bf16[768,256]{1,0:T(8,128)(2,1)S(1)}, bf16[768,256]{1,0:T(8,128)(2,1)S(1)}, u32[]{:S(2)}, u32[]{:S(2)}) collective-permute-start(bf16[768,256]{1,0:T(8,128)(2,1)S(1)} %get-tuple-element.230), channel_id=1, source_target_pairs={{0,12},{4,16},{8,20},{12,24},{16,28},{1,13},{5,17},{9,21},{13,25},... | collective-permute-start | bytes 1179656 | tf_op jit(solution)/shard_map/ppermute | solution.py:61
  501.2 29.4 %collective-permute-start.46 = (bf16[768,256]{1,0:T(8,128)(2,1)S(1)}, bf16[768,256]{1,0:T(8,128)(2,1)S(1)}, u32[]{:S(2)}, u32[]{:S(2)}) collective-permute-start(bf16[768,256]{1,0:T(8,128)(2,1)S(1)} %get-tuple-element.230), channel_id=1, source_target_pairs={{12,0},{16,4},{20,8},{24,12},{28,16},{13,1},{17,5},{21,9},{25,13},... | collective-permute-start | bytes 1179656 | tf_op jit(solution)/shard_map/ppermute | solution.py:61
  502.5 28.2 %collective-permute-start.47 = (bf16[768,256]{1,0:T(8,128)(2,1)S(1)}, bf16[768,256]{1,0:T(8,128)(2,1)S(1)}, u32[]{:S(2)}, u32[]{:S(2)}) collective-permute-start(bf16[768,256]{1,0:T(8,128)(2,1)S(1)} %get-tuple-element.229), channel_id=1, source_target_pairs={{0,24},{4,28},{1,25},{5,29},{2,26},{6,30},{3,27},{7,31}} | collective-permute-start | bytes 1179656 | tf_op jit(solution)/shard_map/ppermute | solution.py:61
  510.8 19.8 %collective-permute-start.48 = (bf16[768,256]{1,0:T(8,128)(2,1)S(1)}, bf16[768,256]{1,0:T(8,128)(2,1)S(1)}, u32[]{:S(2)}, u32[]{:S(2)}) collective-permute-start(bf16[768,256]{1,0:T(8,128)(2,1)S(1)} %get-tuple-element.229), channel_id=1, source_target_pairs={{24,0},{28,4},{25,1},{29,5},{26,2},{30,6},{27,3},{31,7}} | collective-permute-start | bytes 1179656 | tf_op jit(solution)/shard_map/ppermute | solution.py:61
  574.5 125.0 %collective-permute-start.81 = (bf16[8,7,128,768]{3,2,1,0:T(8,128)(2,1)}, bf16[8,7,128,768]{3,2,1,0:T(8,128)(2,1)}, u32[]{:S(2)}, u32[]{:S(2)}) collective-permute-start(bf16[8,7,128,768]{3,2,1,0:T(8,128)(2,1)} %dynamic-slice_bitcast_fusion), channel_id=1, source_target_pairs={{0,1},{1,0},{2,3},{3,2},{4,5},{5,4},{6,7},{7,6},{8,9},{9,8},{10,11... | collective-permute-start | bytes 33030152 | tf_op jit(solution)/shard_map/ppermute | solution.py:35
  616.1 6.4 collective-permute-start.51
  617.0 9.1 collective-permute-start.52
  619.5 8.0 collective-permute-start.50
  627.5 12.0 %collective-permute-start.54 = (f32[14,2048]{1,0:T(8,128)S(1)}, f32[14,2048]{1,0:T(8,128)S(1)}, u32[]{:S(2)}, u32[]{:S(2)}) collective-permute-start(f32[14,2048]{1,0:T(8,128)S(1)} %add_add_fusion.1), channel_id=1, source_target_pairs={{0,16},{8,24},{16,0},{24,8},{1,17},{9,25},{17,1},{25,9},{2,18},{10... | collective-permute-start | bytes 344072 | tf_op jit(solution)/shard_map/ppermute | solution.py:35
  627.6 11.9 %collective-permute-start.55 = (f32[14,2048]{1,0:T(8,128)S(1)}, f32[14,2048]{1,0:T(8,128)S(1)}, u32[]{:S(2)}, u32[]{:S(2)}) collective-permute-start(f32[14,2048]{1,0:T(8,128)S(1)} %add_add_fusion.1), channel_id=1, source_target_pairs={{0,24},{8,16},{16,8},{24,0},{1,25},{9,17},{17,9},{25,1},{2,26},{10... | collective-permute-start | bytes 344072 | tf_op jit(solution)/shard_map/ppermute | solution.py:35
  630.5 9.5 collective-permute-start.53
  699.4 253.4 %reduce-scatter.11.cloned.1.call-start = ((), (), s32[]{:S(2)}) async-start(), calls=%async_computation.7 | async-start | bytes 12386304 | tf_op jit(solution)/shard_map/reduce_scatter | solution.py:91
  713.4 306.3 %reduce-scatter.5.cloned.1.call-start = ((), (), s32[]{:S(2)}) async-start(), calls=%async_computation.4 | async-start | bytes 1179648 | tf_op jit(solution)/shard_map/reduce_scatter | solution.py:91
  741.1 19.3 %collective-permute-start.64 = (bf16[384,512]{1,0:T(8,128)(2,1)S(1)}, bf16[384,512]{1,0:T(8,128)(2,1)S(1)}, u32[]{:S(2)}, u32[]{:S(2)}) collective-permute-start(bf16[384,512]{1,0:T(8,128)(2,1)S(1)} %get-tuple-element.205), channel_id=1, source_target_pairs={{0,4},{4,8},{8,12},{12,16},{16,20},{20,24},{24,28},{1,5},{5,9},{9,... | collective-permute-start | bytes 1179656 | tf_op jit(solution)/shard_map/ppermute | solution.py:61
  744.5 16.0 %collective-permute-start.63 = (bf16[384,512]{1,0:T(8,128)(2,1)S(1)}, bf16[384,512]{1,0:T(8,128)(2,1)S(1)}, u32[]{:S(2)}, u32[]{:S(2)}) collective-permute-start(bf16[384,512]{1,0:T(8,128)(2,1)S(1)} %get-tuple-element.204), channel_id=1, source_target_pairs={{4,0},{8,4},{12,8},{16,12},{20,16},{24,20},{28,24},{5,1},{9,5},{13... | collective-permute-start | bytes 1179656 | tf_op jit(solution)/shard_map/ppermute | solution.py:61
  770.6 7.5 collective-permute-start.70
  770.7 7.4 collective-permute-start.71
  785.9 305.7 %reduce-scatter.7.cloned.1.call-start = ((), (), s32[]{:S(2)}) async-start(), calls=%async_computation.5 | async-start | bytes 2654208 | tf_op jit(solution)/shard_map/reduce_scatter | solution.py:91
  793.0 6.1 collective-permute-start.79
  800.0 154.2 %collective-permute-start.80 = (bf16[32,2048]{1,0:T(8,128)(2,1)S(1)}, bf16[32,2048]{1,0:T(8,128)(2,1)S(1)}, u32[]{:S(2)}, u32[]{:S(2)}) collective-permute-start(bf16[32,2048]{1,0:T(8,128)(2,1)S(1)} %add_convert_fusion.4), channel_id=1, source_target_pairs={{0,1},{1,0},{2,3},{3,2},{4,5},{5,4},{6,7},{7,6},{8,9},{9,8},{10,11... | collective-permute-start | bytes 393224 | tf_op jit(solution)/shard_map/ppermute | solution.py:35
  952.8 140.3 %collective-permute-start.82 = (bf16[7,128,768]{2,1,0:T(8,128)(2,1)}, bf16[7,128,768]{2,1,0:T(8,128)(2,1)}, u32[]{:S(2)}, u32[]{:S(2)}) collective-permute-start(bf16[7,128,768]{2,1,0:T(8,128)(2,1)} %bitcast.369), channel_id=1, source_target_pairs={{0,2},{2,0},{1,3},{3,1},{4,6},{6,4},{5,7},{7,5},{8,10},{10,8},{9,1... | collective-permute-start | bytes 4128776 | tf_op jit(solution)/shard_map/ppermute | solution.py:35
  1091.6 7.9 collective-permute-start.76
  1094.7 11.0 collective-permute-start.83
  (156 other events, 1647.8 us)
Sparse Core Ops, SparseCore 0:
  10.7 42.8 all-gather.8
  56.4 50.8 all-gather.10
  110.0 155.7 all-gather.14
  268.4 38.3 all-gather.12
  699.5 62.9 reduce-scatter.8
  766.4 186.2 reduce-scatter.10
  957.1 62.4 reduce-scatter.4
  1023.7 67.8 reduce-scatter.6

commit v2 on v1

--- a/solution.py
+++ b/solution.py
@@ -4,6 +4,8 @@
 import jax.numpy as jnp
 import numpy as np
 from jax import lax
+from jax.experimental import pallas as pl
+from jax.experimental.pallas import tpu as pltpu
 from jax.sharding import Mesh
 from jax.sharding import PartitionSpec as P
 
@@ -76,26 +78,28 @@
     return jnp.stack([first, second], axis=axis)
 
 
-def gather_rows(shard, axis):
+def between_cores(partial):
     core = lax.axis_index("c")
-    mine = lax.all_gather(half_of(shard, axis, core), LINE, axis=0, tiled=False)
-    other = flip(mine, [("c", 1)])
-    return both_halves(mine, other, core, axis + 1)
-
-
-def scatter_rows(partial, axis):
-    core = lax.axis_index("c")
-    mine = half_of(partial, axis + 1, core)
-    other = flip(half_of(partial, axis + 1, 1 - core), [("c", 1)])
-    summed = (mine.astype(full) + other.astype(full)).astype(low)
-    own = lax.psum_scatter(summed, LINE, scatter_dimension=0, tiled=False)
+    mine = half_of(partial, 1, core)
+    other = flip(half_of(partial, 1, 1 - core), [("c", 1)])
+    return (mine.astype(full) + other.astype(full)).astype(low)
+
+
+def over_groups(own):
     bit = 1
     while bit < lax.axis_size("x"):
         own = (own.astype(full) + flip(own, [("x", bit)]).astype(full)).astype(low)
         bit *= 2
-    other = flip(own, [("c", 1)])
-    whole = both_halves(own, other, core, axis)
-    return whole.reshape(own.shape[:axis] + (-1,) + own.shape[axis + 1 :]).astype(full)
+    return own, flip(own, [("c", 1)])
+
+
+def scatter_halves(summed):
+    return over_groups(lax.psum_scatter(summed, LINE, scatter_dimension=0, tiled=False))
+
+
+def scatter_few(summed):
+    arrived = lax.all_to_all(summed, LINE, 0, 0, tiled=True)
+    return over_groups(jnp.sum(arrived.astype(full), axis=0).astype(low))
 
 
 def along(value, offset, axis):
@@ -155,18 +159,17 @@
     return terms, table
 
 
-def task_scales(gram):
-    norms = jnp.sqrt(jnp.stack([gram[0, 0], gram[1, 1], gram[2, 2]]) + 1e-12)
-    corr = gram / (norms[:, None] * norms[None, :]) + 0.1 * jnp.eye(3, dtype=full)
-    adjugate = jnp.stack(
-        [
-            jnp.cross(corr[:, 1], corr[:, 2]),
-            jnp.cross(corr[:, 2], corr[:, 0]),
-            jnp.cross(corr[:, 0], corr[:, 1]),
-        ]
-    )
-    weights = jnp.sum(adjugate, axis=1)
-    return 3.0 * weights * jnp.mean(norms) / (norms * jnp.sum(weights))
+def task_scales(products):
+    g00, g01, g02, g11, g12, g22 = products
+    n0, n1, n2 = (jnp.sqrt(g + 1e-12) for g in (g00, g11, g22))
+    c00, c11, c22 = (g / (n * n) + 0.1 for g, n in ((g00, n0), (g11, n1), (g22, n2)))
+    c01, c02, c12 = g01 / (n0 * n1), g02 / (n0 * n2), g12 / (n1 * n2)
+    w0 = (c11 * c22 - c12 * c12) + (c12 * c02 - c01 * c22) + (c01 * c12 - c11 * c02)
+    w1 = (c12 * c02 - c22 * c01) + (c22 * c00 - c02 * c02) + (c02 * c01 - c12 * c00)
+    w2 = (c01 * c12 - c02 * c11) + (c02 * c01 - c00 * c12) + (c00 * c11 - c01 * c01)
+    top = n0 + n1 + n2
+    total = w0 + w1 + w2
+    return [w * top / (n * total) for w, n in ((w0, n0), (w1, n1), (w2, n2))]
 
 
 def dot(a, b):
@@ -179,6 +182,327 @@
 
 def dot_tn(a, b):
     return lax.dot_general(a, b, (((0,), (0,)), ((), ())), preferred_element_type=full)
+
+
+def spec(shape, index):
+    return pl.BlockSpec(shape, index)
+
+
+def params(mib=56):
+    return pltpu.CompilerParams(vmem_limit_bytes=mib * 2**20)
+
+
+def cost(flops, moved):
+    return pl.CostEstimate(flops=flops, bytes_accessed=moved, transcendentals=0)
+
+
+def terms_kernel(picked_ref, task_ref, x_ref, w_ref, mask_ref, out_ref):
+    at = pl.program_id(0)
+    spread = jnp.dot(x_ref[...], w_ref[...], preferred_element_type=full)
+    pixels, head = out_ref.shape
+    for task, rate in enumerate(head_rates):
+
+        @pl.when(task_ref[at] == task)
+        def _():
+            total = spread[:, head : 2 * head]
+            for k, shift in ((0, rate), (2, pixels - rate)):
+                piece = pltpu.roll(spread[:, k * head : (k + 1) * head], shift, 0)
+                total = total + piece * mask_ref[:, 3 * task + k : 3 * task + k + 1]
+            out_ref[...] = total.astype(out_ref.dtype)
+
+
+def head_terms(grid, heads_all, masks, picked, task_of, head, dtype):
+    pixels, depth = grid.shape
+    items = picked.shape[0]
+    return pl.pallas_call(
+        terms_kernel,
+        out_shape=jax.ShapeDtypeStruct((pixels, items * head), dtype),
+        grid_spec=pltpu.PrefetchScalarGridSpec(
+            num_scalar_prefetch=2,
+            grid=(items,),
+            in_specs=[
+                spec((pixels, depth), lambda i, p, t: (0, 0)),
+                spec((depth, 3 * head), lambda i, p, t: (0, p[i])),
+                spec(masks.shape, lambda i, p, t: (0, 0)),
+            ],
+            out_specs=spec((pixels, head), lambda i, p, t: (0, i)),
+        ),
+        compiler_params=params(),
+        cost_estimate=cost(
+            2 * pixels * depth * 3 * head * items, 2 * items * depth * 3 * head + 2 * pixels * depth
+        ),
+    )(picked, task_of, grid, heads_all, masks)
+
+
+def spread_kernel(task_ref, d_ref, mask_ref, out_ref):
+    at = pl.program_id(0)
+    pixels, head = d_ref.shape
+    for task, rate in enumerate(head_rates):
+
+        @pl.when(task_ref[at] == task)
+        def _():
+            grad = d_ref[...].astype(full)
+            out_ref[:, head : 2 * head] = d_ref[...]
+            for k, shift in ((0, pixels - rate), (2, rate)):
+                piece = grad * mask_ref[:, 3 * task + k : 3 * task + k + 1]
+                out_ref[:, k * head : (k + 1) * head] = pltpu.roll(piece, shift, 0).astype(low)
+
+
+def spread_back(grads, masks, task_of, head):
+    pixels = grads.shape[0]
+    items = grads.shape[1] // head
+    return pl.pallas_call(
+        spread_kernel,
+        out_shape=jax.ShapeDtypeStruct((pixels, 3 * head * items), low),
+        grid_spec=pltpu.PrefetchScalarGridSpec(
+            num_scalar_prefetch=1,
+            grid=(items,),
+            in_specs=[
+                spec((pixels, head), lambda i, t: (0, i)),
+                spec(masks.shape, lambda i, t: (0, 0)),
+            ],
+            out_specs=spec((pixels, 3 * head), lambda i, t: (0, i)),
+        ),
+        compiler_params=params(),
+        cost_estimate=cost(10 * pixels * head * items * 3, 8 * pixels * head * items),
+    )(task_of, grads, masks)
+
+
+def shared_back_kernel(tasks, side_tasks, *refs):
+    slots = len(side_tasks)
+    picked_ref, here_ref = refs[:2]
+    dy_ref = refs[2]
+    w_refs = refs[3 : 3 + tasks + slots]
+    wide_ref, source_ref, vec_ref, mask_ref = refs[3 + tasks + slots : 7 + tasks + slots]
+    out_refs = refs[7 + tasks + slots : -1]
+    sums_ref = refs[-1]
+    three = w_refs[0].shape[1]
+
+    def back(i):
+        return lax.dot_general(
+            dy_ref[:, i * three : (i + 1) * three],
+            w_refs[i][...],
+            (((1,), (1,)), ((), ())),
+            preferred_element_type=full,
+        )
+
+    grads = [back(t) for t in range(tasks)]
+    for s, choices in enumerate(side_tasks):
+        side = back(tasks + s)
+        for t in choices:
+            grads[t] = grads[t] + (side if len(choices) == 1 else side * here_ref[s * tasks + t])
+    normed = (wide_ref[...].astype(full) - vec_ref[0:1]) * vec_ref[1:2]
+    value = normed * vec_ref[2:3] + vec_ref[3:4] + source_ref[...].astype(full)
+    slope = silu_slope(value) * mask_ref[:, 1:2]
+    rows = []
+    for t in range(tasks):
+        out_refs[t][...] = grads[t].astype(low)
+        part = grads[t] * slope
+        rows += [jnp.sum(part * normed, axis=0), jnp.sum(part, axis=0)]
+    for t in range(tasks):
+        for u in range(t, tasks):
+            rows.append(jnp.sum(grads[t] * grads[u], axis=0))
+    sums_ref[...] = jnp.zeros_like(sums_ref)
+    for i, row in enumerate(rows):
+        sums_ref[i, :] = row
+
+
+def shared_back(dys, heads_all, picked, here, side_tasks, tasks, wide, source, vecs, masks, block):
+    pixels, depth = wide.shape
+    items = tasks + len(side_tasks)
+    three = dys.shape[1] // items
+    weights = [
+        spec((block, three), (lambda j, p, h, i=i: (j, i)) if i < tasks else (lambda j, p, h, i=i: (j, p[i])))
+        for i in range(items)
+    ]
+    column = lambda j, p, h: (0, j)
+    return pl.pallas_call(
+        lambda *refs: shared_back_kernel(tasks, side_tasks, *refs),
+        out_shape=[jax.ShapeDtypeStruct((pixels, depth), low)] * tasks
+        + [jax.ShapeDtypeStruct((16, depth), full)],
+        grid_spec=pltpu.PrefetchScalarGridSpec(
+            num_scalar_prefetch=2,
+            grid=(depth // block,),
+            in_specs=[spec(dys.shape, lambda j, p, h: (0, 0))]
+            + weights
+            + [
+                spec((pixels, block), column),
+                spec((pixels, block), column),
+                spec((8, block), column),
+                spec(masks.shape, lambda j, p, h: (0, 0)),
+            ],
+            out_specs=[spec((pixels, block), column)] * tasks + [spec((16, block), column)],
+        ),
+        compiler_params=params(),
+        cost_estimate=cost(
+            2 * pixels * depth * three * items, 2 * items * depth * three + 12 * pixels * depth
+        ),
+    )(picked, here, dys, *([heads_all] * items), wide, source, vecs, masks)
+
+
+def expand_back_kernel(tasks, blocks, *refs):
+    weight_ref = refs[0]
+    grad_refs = refs[1 : 1 + tasks]
+    wide_ref, source_ref, vec_ref, mask_ref, hidden_ref, w_ref, mid_ref, mid_vec_ref = refs[
+        1 + tasks : 9 + tasks
+    ]
+    dbefore_ref, dweight_ref, dout_ref, sums_ref, total_ref = refs[9 + tasks :]
+    at = pl.program_id(0)
+    combined = grad_refs[0][...].astype(full) * weight_ref[0]
+    for t in range(1, tasks):
+        combined = combined + grad_refs[t][...].astype(full) * weight_ref[t]
+    normed = (wide_ref[...].astype(full) - vec_ref[0:1]) * vec_ref[1:2]
+    value = normed * vec_ref[2:3] + vec_ref[3:4] + source_ref[...].astype(full)
+    valid = mask_ref[:, 1:2]
+    dbefore = combined * (silu_slope(value) * valid)
+    dbefore_ref[...] = dbefore.astype(low)
+    dwide = (dbefore - vec_ref[5:6] - normed * vec_ref[4:5]) * vec_ref[6:7] * valid
+    dwide = dwide.astype(low)
+    dweight_ref[...] = lax.dot_general(
+        hidden_ref[...], dwide, (((0,), (0,)), ((), ())), preferred_element_type=full
+    ).astype(low)
+    part = lax.dot_general(
+        dwide, w_ref[...], (((1,), (1,)), ((), ())), preferred_element_type=full
+    )
+
+    @pl.when(at == 0)
+    def _():
+        total_ref[...] = part
+
+    @pl.when(at > 0)
+    def _():
+        total_ref[...] += part
+
+    @pl.when(at == blocks - 1)
+    def _():
+        mid = (mid_ref[...] - mid_vec_ref[0:1]) * mid_vec_ref[1:2]
+        dout = total_ref[...] * silu_slope(mid * mid_vec_ref[2:3] + mid_vec_ref[3:4]) * valid
+        dout_ref[...] = dout
+        sums_ref[...] = jnp.zeros_like(sums_ref)
+        sums_ref[0, :] = jnp.sum(dout * mid, axis=0)
+        sums_ref[1, :] = jnp.sum(dout, axis=0)
+
+
+def expand_back(task_weights, grads, wide, source, vecs, masks, hidden, weight, mid, mid_vecs, block):
+    pixels, depth = wide.shape
+    width = hidden.shape[1]
+    tasks = len(grads)
+    column = lambda j, w: (0, j)
+    fixed = lambda j, w: (0, 0)
+    blocks = depth // block
+    return pl.pallas_call(
+        lambda *refs: expand_back_kernel(tasks, blocks, *refs),
+        out_shape=[
+            jax.ShapeDtypeStruct((pixels, depth), low),
+            jax.ShapeDtypeStruct((width, depth), low),
+            jax.ShapeDtypeStruct((pixels, width), full),
+            jax.ShapeDtypeStruct((8, width), full),
+        ],
+        grid_spec=pltpu.PrefetchScalarGridSpec(
+            num_scalar_prefetch=1,
+            grid=(blocks,),
+            in_specs=[spec((pixels, block), column)] * (tasks + 2)
+            + [
+                spec((8, block), column),
+                spec(masks.shape, fixed),
+                spec((pixels, width), fixed),
+                spec((width, block), column),
+                spec((pixels, width), fixed),
+                spec((8, width), fixed),
+            ],
+            out_specs=[
+                spec((pixels, block), column),
+                spec((width, block), column),
+                spec((pixels, width), fixed),
+                spec((8, width), fixed),
+            ],
+            scratch_shapes=[pltpu.VMEM((pixels, width), full)],
+        ),
+        compiler_params=params(),
+        cost_estimate=cost(4 * pixels * depth * width, 14 * pixels * depth),
+    )(task_weights, *grads, wide, source, vecs, masks, hidden, weight, mid, mid_vecs)
+
+
+def weight_grad_kernel(slot_ref, x_ref, other_ref, dy_ref, dy_other_ref, out_ref, turned_ref):
+    at = pl.program_id(0)
+    pixels = x_ref.shape[0]
+
+    @pl.when(at == 0)
+    def _():
+        turned_ref[:, :pixels] = x_ref[...].T
+        turned_ref[:, pixels:] = other_ref[...].T
+
+    @pl.when(slot_ref[at] >= 0)
+    def _():
+        total = jnp.dot(turned_ref[:, :pixels], dy_ref[...], preferred_element_type=full)
+        total += jnp.dot(turned_ref[:, pixels:], dy_other_ref[...], preferred_element_type=full)
+        out_ref[...] = total.astype(low)
+
+    @pl.when(slot_ref[at] < 0)
+    def _():
+        out_ref[...] = jnp.zeros_like(out_ref)
+
+
+def weight_grad(x, other, dys, dys_other, slot_of, three):
+    pixels, depth = x.shape
+    parts = slot_of.shape[0]
+    fixed = lambda g, s: (0, 0)
+    picked = lambda g, s: (0, jnp.maximum(s[g], 0))
+    return pl.pallas_call(
+        weight_grad_kernel,
+        out_shape=jax.ShapeDtypeStruct((depth, parts * three), low),
+        grid_spec=pltpu.PrefetchScalarGridSpec(
+            num_scalar_prefetch=1,
+            grid=(parts,),
+            in_specs=[
+                spec(x.shape, fixed),
+                spec(other.shape, fixed),
+                spec((pixels, three), picked),
+                spec((pixels, three), picked),
+            ],
+            out_specs=spec((depth, three), lambda g, s: (0, g)),
+            scratch_shapes=[pltpu.VMEM((depth, 2 * pixels), low)],
+        ),
+        compiler_params=params(),
+        cost_estimate=cost(
+            4 * pixels * depth * dys.shape[1], 2 * depth * parts * three + 4 * pixels * dys.shape[1]
+        ),
+    )(slot_of, x, other, dys, dys_other)
+
+
+def place_kernel(part_ref, core_ref, mine_ref, other_ref, out_ref):
+    at = pl.program_id(0)
+    half = mine_ref.shape[0]
+
+    @pl.when(part_ref[at] >= 0)
+    def _():
+        core = core_ref[0]
+        out_ref[0, pl.ds(pl.multiple_of(core * half, half), half), :] = mine_ref[...].astype(full)
+        out_ref[0, pl.ds(pl.multiple_of((1 - core) * half, half), half), :] = other_ref[
+            ...
+        ].astype(full)
+
+    @pl.when(part_ref[at] < 0)
+    def _():
+        out_ref[...] = jnp.zeros_like(out_ref)
+
+
+def place_rows(mine, other, part_of, core, head):
+    half = mine.shape[0]
+    taps = part_of.shape[0]
+    picked = lambda i, p, c: (0, jnp.maximum(p[i], 0))
+    return pl.pallas_call(
+        place_kernel,
+        out_shape=jax.ShapeDtypeStruct((taps, 2 * half, head), full),
+        grid_spec=pltpu.PrefetchScalarGridSpec(
+            num_scalar_prefetch=2,
+            grid=(taps,),
+            in_specs=[spec((half, head), picked), spec((half, head), picked)],
+            out_specs=spec((1, 2 * half, head), lambda i, p, c: (i, 0, 0)),
+        ),
+        compiler_params=params(),
+        cost_estimate=cost(0, 12 * taps * half * head),
+    )(part_of, core, mine, other)
 
 
 def on_device(
@@ -222,24 +546,42 @@
     count = jnp.sum(crop_scale).astype(full) * float(W_UNIT * rows * line)
     crops = float(crop_scale.shape[0])
 
-    red_all = gather_rows(w_reduce, 0).reshape(depth, width)
-    mid_own = w_middle.reshape(-1, 3, 3, width).transpose(1, 0, 2, 3).reshape(3, -1, 3 * width)
-    mid_all = gather_rows(mid_own, 1)
-    mid_all = mid_all.transpose(1, 0, 2, 3, 4).reshape(3 * width, 3 * width)
-    exp_all = gather_rows(w_expand, 0).reshape(width, depth)
+    core = lax.axis_index("c")
+    ratio = depth // width
+    red_rows, mid_rows, exp_rows = (w.shape[0] // 2 for w in (w_reduce, w_middle, w_expand))
+    mid_own = half_of(w_middle.transpose(1, 0, 2), 1, core).reshape(9 * mid_rows, width)
+    exp_own = half_of(w_expand, 0, core).reshape(exp_rows, ratio, width).transpose(1, 0, 2)
+    block_own = jnp.concatenate(
+        [half_of(w_reduce, 0, core), mid_own, exp_own.reshape(ratio * exp_rows, width)], axis=0
+    )
+    block_mine = lax.all_gather(block_own, LINE, axis=0, tiled=False)
+    block_all = both_halves(block_mine, flip(block_mine, [("c", 1)]), core, 1)
+    cuts = np.cumsum([0, red_rows, 9 * mid_rows, ratio * exp_rows])
+    red_all, mid_all, exp_all = (block_all[:, :, cuts[i] : cuts[i + 1]] for i in range(3))
+    red_all = red_all.reshape(depth, width)
+    mid_all = mid_all.reshape(line, 2, 3, 3, mid_rows, width).transpose(2, 0, 1, 4, 3, 5)
+    mid_all = mid_all.reshape(3 * width, 3 * width)
+    exp_all = exp_all.reshape(line, 2, ratio, exp_rows, width).transpose(0, 1, 3, 2, 4)
+    exp_all = exp_all.reshape(width, depth)
     terms, table = head_plan(rows)
     slots = table.shape[0]
+    three = 3 * head
     by_term = w_heads.reshape(own, tasks, 3, 3, head).transpose(1, 2, 0, 3, 4)
-    by_term = by_term.reshape(tasks, 3, own, 3 * head)
+    by_term = by_term.reshape(tasks, 3, own, three)
     parts = [by_term[t, 1] for t in range(tasks)] + [by_term[t, s + 1] for t, s, _ in terms]
-    heads_all = gather_rows(jnp.stack(parts), 1)
-    heads_all = heads_all.transpose(1, 0, 2, 3, 4).reshape(len(parts), depth, 3 * head)
-    picked_term = [jnp.asarray(table[s])[place] for s in range(slots)]
-
-    def slot_weight(s):
-        if (table[s] == table[s][0]).all():
-            return heads_all[tasks + int(table[s][0])]
-        return lax.dynamic_index_in_dim(heads_all, tasks + picked_term[s], 0, keepdims=False)
+    quarter = own // lax.axis_size(("x", "c"))
+    heads_own = jnp.concatenate(
+        [lax.dynamic_slice_in_dim(part, group * quarter, quarter, axis=0) for part in parts], axis=1
+    )
+    heads_own, block_mine = lax.optimization_barrier((heads_own, block_mine))
+    heads_all = lax.all_gather(heads_own, AXES, axis=0, tiled=True)
+    term_tasks = np.array([task for task, _, _ in terms], np.int32)
+    picked_term = jnp.asarray(table)[:, place]
+    slot_tasks = [sorted({int(term_tasks[e]) for e in table[s]}) for s in range(slots)]
+    side_task = jnp.asarray(term_tasks)[picked_term]
+    centers = jnp.arange(tasks, dtype=jnp.int32)
+    all_tasks = jnp.concatenate([centers, side_task])
+    all_picked = jnp.concatenate([centers, tasks + picked_term])
 
     source = features.reshape(pixels, depth) * valid.astype(low)
     reduced = dot(source, red_all)
@@ -270,39 +612,31 @@
     before = normed3 * gain_expand + bias_expand + source.astype(full)
     grid = (jax.nn.silu(before) * valid).astype(low)
 
-    masks = [[same((k - 1) * rate) for k in range(3)] for rate in head_rates]
-
-    def gathered(spread, task):
-        rate = head_rates[task]
-        return sum(
-            along(spread[:, k * head : (k + 1) * head], (k - 1) * rate, 0) * masks[task][k]
+    def mask_table(group):
+        inside = crop_table(crop_scale, crop_group, group, W_UNIT, cols)
+        columns = [
+            jnp.sum(inside * along(inside, (k - 1) * rate, 0), axis=1)
+            for rate in head_rates
             for k in range(3)
-        )
-
-    def choose(s, by_task):
-        tasks_of = [terms[e][0] for e in table[s]]
-        chosen = by_task(tasks_of[0])
-        for task in sorted(set(tasks_of) - {tasks_of[0]}):
-            here = jnp.asarray(np.array([t == task for t in tasks_of]))[place]
-            chosen = jnp.where(here, by_task(task), chosen)
-        return chosen
-
-    side_terms = []
-    for s in range(slots):
-        spread = dot(grid, slot_weight(s))
-        side_terms.append(choose(s, lambda task: gathered(spread, task)).astype(low))
+        ]
+        table = jnp.pad(jnp.stack(columns, axis=1), ((0, 0), (0, 128 - 3 * tasks)))
+        return jnp.tile(table, (rows, 1))
+
+    masks = mask_table(group)
+    side_terms = head_terms(grid, heads_all, masks, tasks + picked_term, side_task, head, low)
     moved = [None] * tasks
     for e, (task, side, hop) in enumerate(terms):
         pairs = [(f, f - side * hop) for f in range(line) if 0 <= f - side * hop < line]
         using = [s for s in range(slots) if any(table[s, f] == e for f, _ in pairs)]
-        sent = side_terms[using[0]]
+        sent = side_terms[:, using[0] * head : (using[0] + 1) * head]
         for s in using[1:]:
-            sent = jnp.where(picked_term[s] == e, side_terms[s], sent)
+            sent = jnp.where(picked_term[s] == e, side_terms[:, s * head : (s + 1) * head], sent)
         got = rows_to(sent, pairs).astype(full)
         moved[task] = got if moved[task] is None else moved[task] + got
+    middle_terms = head_terms(grid, heads_all, masks, centers, centers, head, full)
     mixed = []
     for task in range(tasks):
-        center = gathered(dot(grid, heads_all[task]), task)
+        center = middle_terms[:, task * head : (task + 1) * head]
         mixed.append(center if moved[task] is None else center + moved[task])
     mixed = jnp.concatenate(mixed, axis=1)
     gain_h, bias_h = gain_heads.reshape(-1), bias_heads.reshape(-1)
@@ -317,7 +651,7 @@
         logits = dot(act, w_class[task]) + b_class[task]
         onehot = (marks[task][:, None] == jnp.arange(classes, dtype=jnp.int32)[None, :]).astype(full)
         dlogits = ((jax.nn.softmax(logits, axis=-1) - onehot) * valid / crops).astype(low)
-        class_part.append(dot_tn(act, dlogits))
+        class_part.append(dot_tn(dlogits, act))
         class_bias_part.append(jnp.sum(dlogits.astype(full), axis=0))
         dactiv.append(dot_nt(dlogits, w_class[task]))
     dout_h = jnp.concatenate(dactiv, axis=1) * valid * silu_slope(out_h)
@@ -326,75 +660,63 @@
     dmixed = valid * (gain_h * scale_h) * (dout_h - dbias_h / count - normed_h * (dgain_h / count))
     dmixed = dmixed.astype(low)
 
-    def spread_back(grad, task):
-        rate = head_rates[task]
-        return jnp.concatenate(
-            [along(grad * masks[task][k].astype(low), -(k - 1) * rate, 0) for k in range(3)], axis=1
-        )
-
     back = []
     for task, side, hop in terms:
         pairs = [(f, f + side * hop) for f in range(line) if 0 <= f + side * hop < line]
         back.append(rows_to(dmixed[:, task * head : (task + 1) * head], pairs))
-    shared_grads, head_parts = [], [None] * len(parts)
-    for task in range(tasks):
-        dspread = spread_back(dmixed[:, task * head : (task + 1) * head], task)
-        shared_grads.append(dot_nt(dspread, heads_all[task]))
-        head_parts[task] = dot_tn(grid, dspread).astype(low)
+    dsides = []
     for s in range(slots):
         dside = back[table[s][0]]
         for e in sorted(set(table[s].tolist()) - {int(table[s][0])}):
             dside = jnp.where(picked_term[s] == e, back[e], dside)
-        dspread = choose(s, lambda task: spread_back(dside, task))
-        dshared = dot_nt(dspread, slot_weight(s))
-        dweight = dot_tn(grid, dspread).astype(low)
-        tasks_of = np.array([terms[e][0] for e in table[s]])
-        for task in sorted(set(tasks_of.tolist())):
-            here = jnp.asarray((tasks_of == task).astype(np.float32))[place]
-            shared_grads[task] = shared_grads[task] + here * dshared
-        for e in sorted(set(table[s].tolist())):
-            here = jnp.asarray((table[s] == e).astype(np.float32))[place].astype(low)
-            part = here * dweight
-            held = head_parts[tasks + e]
-            head_parts[tasks + e] = part if held is None else held + part
-    slope3 = valid * silu_slope(before)
-    sums = []
-    for task in range(tasks):
-        part = shared_grads[task] * slope3
-        sums += [jnp.sum(part * normed3, axis=0), jnp.sum(part, axis=0)]
-    gram_part = jnp.stack(
-        [jnp.sum(shared_grads[t] * shared_grads[u]) for t in range(tasks) for u in range(tasks)]
-    )
-    class_part = jnp.stack(class_part).reshape(-1)
-    class_bias_part = jnp.stack(class_bias_part).reshape(-1)
-    small = jnp.concatenate([class_part, class_bias_part, gram_part])
-    short = -small.shape[0] % depth
-    small = jnp.pad(small, (0, short)).reshape(-1, depth)
-    summed = all_sum(jnp.concatenate([jnp.stack(sums), small], axis=0))
+        dsides.append(dside)
+    dterms = jnp.concatenate([dmixed] + dsides, axis=1)
+    dys = spread_back(dterms, masks, all_tasks, head)
+    half = own // 2
+
+    def half_columns(which):
+        cuts = [f * own + which * half for f in range(line)]
+        return jnp.concatenate(
+            [lax.dynamic_slice_in_dim(grid, cut, half, axis=1) for cut in cuts], axis=1
+        )
+
+    grid_other = flip(half_columns(1 - core), [("c", 1)])
+    dterms_other = flip(dterms, [("c", 1)])
+    dys_other = spread_back(dterms_other, mask_table(group ^ 1), all_tasks, head)
+    slot_of = jnp.full((len(terms),), -1, jnp.int32)
+    for s in range(slots):
+        slot_of = jnp.where(jnp.arange(len(terms)) == picked_term[s], tasks + s, slot_of)
+    slot_of = jnp.concatenate([centers, slot_of])
+    core_at = core.reshape(1).astype(jnp.int32)
+    head_half = weight_grad(half_columns(core), grid_other, dys, dys_other, slot_of, three)
+    dys, head_half = lax.optimization_barrier((dys, head_half))
+    head_own, head_other = scatter_halves(head_half.reshape(line, half, len(parts) * three))
+
+    here = (side_task[:, None] == centers[None, :]).astype(full).reshape(-1)
+    vec_rows = [mean3, scale3, gain_expand, bias_expand]
+    vecs = jnp.pad(jnp.stack(vec_rows), ((0, 4), (0, 0)))
+    *shared_grads, sums = shared_back(
+        dys, heads_all, all_picked, here, slot_tasks, tasks, expanded, source, vecs, masks, 256
+    )
+    gram_part = jnp.sum(sums[2 * tasks : 4 * tasks], axis=1)
+    gram_row = jnp.pad(gram_part, (0, depth - gram_part.shape[0]))[None, :]
+    summed = all_sum(jnp.concatenate([sums[: 2 * tasks], gram_row], axis=0))
     sums3 = summed[: 2 * tasks].reshape(tasks, 2, depth)
-    small = summed[2 * tasks :].reshape(-1)
-    size = tasks * head * classes
-    grad_class = small[:size].reshape(tasks, head, classes)
-    grad_class_bias = small[size : size + tasks * classes].reshape(tasks, classes)
-    gram = small[size + tasks * classes :][: tasks * tasks].reshape(tasks, tasks)
-    task_weights = task_scales(gram)
-    head_full = jnp.stack(head_parts).reshape(len(parts), line, own, 3 * head).transpose(1, 0, 2, 3)
-    head_own = scatter_rows(head_full, 1)
-
-    combined = sum(task_weights[t] * shared_grads[t] for t in range(tasks))
+    weight_list = task_scales([summed[2 * tasks, i] for i in range(6)])
+    task_weights = jnp.stack(weight_list)
+
     dgain3, dbias3 = (
-        sum(task_weights[t] * sums3[t, j] for t in range(tasks)) for j in range(2)
-    )
-    dbefore = combined * slope3
-    dexpanded = valid * (gain_expand * scale3) * (
-        dbefore - dbias3 / count - normed3 * (dgain3 / count)
-    )
-    dexpanded = dexpanded.astype(low)
-    dhidden2 = dot_nt(dexpanded, exp_all)
-    dout2 = dhidden2 * valid * silu_slope(out2)
-    sums2 = all_sum(jnp.stack([jnp.sum(dout2 * normed2, axis=0), jnp.sum(dout2, axis=0)]))
+        sum(weight_list[t] * sums3[t, j] for t in range(tasks)) for j in range(2)
+    )
+    vec_rows += [dgain3 / count, dbias3 / count, gain_expand * scale3]
+    vecs = jnp.pad(jnp.stack(vec_rows), ((0, 1), (0, 0)))
+    mid_vecs = jnp.pad(jnp.stack([mean2, scale2, gain_middle, bias_middle]), ((0, 4), (0, 0)))
+    dbefore, exp_part, dout2, sums2 = expand_back(
+        task_weights, shared_grads, expanded, source, vecs, masks, hidden2, exp_all, middled,
+        mid_vecs, 256,
+    )
+    sums2 = all_sum(sums2[:2])
     dgain2, dbias2 = sums2[0], sums2[1]
-    exp_own = scatter_rows(dot_tn(hidden2, dexpanded).astype(low).reshape(line, -1, depth), 0)
     dmiddled = valid * (gain_middle * scale2) * (
         dout2 - dbias2 / count - normed2 * (dgain2 / count)
     )
@@ -414,28 +736,48 @@
     dout1 = dhidden1 * valid * silu_slope(out1)
     sums1 = all_sum(jnp.stack([jnp.sum(dout1 * normed1, axis=0), jnp.sum(dout1, axis=0)]))
     dgain1, dbias1 = sums1[0], sums1[1]
-    mid_part = dot_tn(wide1, dspread).astype(low).reshape(3, line, -1, 3 * width)
-    mid_sum = scatter_rows(mid_part.transpose(1, 0, 2, 3), 1)
-    mid_sum = mid_sum.reshape(3, -1, 3, width).transpose(1, 0, 2, 3).reshape(w_middle.shape)
+    class_sums = jnp.concatenate(
+        [jnp.concatenate(class_part, axis=0), jnp.pad(jnp.stack(class_bias_part), ((0, 0), (0, head - classes)))],
+        axis=0,
+    )
+    class_sums, sums1 = lax.optimization_barrier((class_sums, sums1))
+    class_sums = all_sum(class_sums)
+    grad_class = class_sums[: tasks * classes].reshape(tasks, classes, head).transpose(0, 2, 1)
+    grad_class_bias = class_sums[tasks * classes :, :classes]
     dreduced = valid * (gain_reduce * scale1) * (
         dout1 - dbias1 / count - normed1 * (dgain1 / count)
     )
     dreduced = dreduced.astype(low)
-    red_own = scatter_rows(dot_tn(source, dreduced).astype(low).reshape(line, -1, width), 0)
-    dfeatures = dbefore + dot_nt(dreduced, red_all)
-
-    zero = jnp.zeros((own, 3 * head), full)
-    ordered = [[zero, head_own[t], zero] for t in range(tasks)]
+    dfeatures = dbefore.astype(full) + dot_nt(dreduced, red_all)
+
+    mid_part = dot_tn(wide1, dspread).astype(low).reshape(3, line, -1, 3, width)
+    mid_part = mid_part.transpose(1, 2, 0, 3, 4).reshape(line, 2 * mid_rows, 9, width)
+    exp_part = exp_part.reshape(line, 2 * exp_rows, ratio, width)
+    later = jnp.concatenate([mid_part.reshape(line, 2 * mid_rows, -1, width), exp_part], axis=2)
+    later = between_cores(later)
+    wide_rows = 9 + ratio
+    later_own, later_other = scatter_halves(later.reshape(line, mid_rows * wide_rows, width))
+    later_sum = both_halves(later_own, later_other, core, 0).astype(full)
+    later_sum = later_sum.reshape(2 * mid_rows, wide_rows, width)
+    mid_sum = later_sum[:, :9]
+    exp_sum = later_sum[:, 9:].reshape(2 * exp_rows, depth)
+    red_part = dot_tn(source, dreduced).astype(low).reshape(line, -1, width)
+    red_sum = both_halves(*scatter_few(between_cores(red_part)), core, 0).astype(full)
+    part_of = np.full((tasks, 3, 3), -1, np.int32)
+    for task in range(tasks):
+        part_of[task, 1] = 3 * task + np.arange(3)
     for e, (task, side, _) in enumerate(terms):
-        ordered[task][side + 1] = head_own[tasks + e]
-    heads_out = jnp.stack([part for row in ordered for part in row])
-    heads_out = heads_out.reshape(tasks, 3, own, 3, head).transpose(2, 0, 1, 3, 4)
+        part_of[task, side + 1] = 3 * (tasks + e) + np.arange(3)
+    heads_out = place_rows(
+        head_own, head_other, jnp.asarray(part_of.reshape(-1)), core_at, head
+    )
+    heads_out = heads_out.reshape(tasks, 9, own, head).transpose(2, 0, 1, 3)
     return (
         dfeatures.reshape(1, rows, cols, depth),
-        red_own,
+        red_sum.reshape(w_reduce.shape),
         mid_sum,
-        exp_own,
-        heads_out.reshape(w_heads.shape),
+        exp_sum,
+        heads_out,
         dgain1,
         dbias1,
         dgain2,

time: 1150 us -> 757 us (0.66)
  waiting for transfers between devices: 632 us -> 288 us
  Pallas kernels: 0 us -> 119 us
  matrix products: 128 us -> 37.7 us
  other arithmetic: 108 us -> 60.3 us
  local copies, waits for them, and re-layouts: 113 us -> 81.8 us
  starting transfers between devices: 111 us -> 137 us
  between operations: 48.2 us -> 24.4 us
    reduce_scatter x4 -> x2, waiting for transfers between devices: 275 us -> 33.8 us  [scatter_halves(): lax.psum_scatter(summed, LINE, scatter_dimension=0, tiled=False)]
    all_gather x4 -> x2, waiting for transfers between devices: 246 us -> 103 us  [the longest x1 70.5 us: on_device(): block_mine = lax.all_gather(block_own, LINE, axis=0, tiled=False)]
    pallas_call x0 -> x8, Pallas kernels: none -> 119 us  [the longest x1 25.8 us: shared_back(): pl.pallas_call(lambda *refs: shared_back_kernel(tasks, side_tasks, *refs)...]
    dot_general x11 -> x5, matrix products: 64.9 us -> 14 us  [dot_nt(): lax.dot_general(a, b, (((1,), (1,)), ((), ())), preferred_element_type=full)]
    convert_element_type x18 -> x9, other arithmetic: 43.7 us -> 9.1 us  [the longest x3 3.32 us: over_groups(): own = (own.astype(full) + flip(own, [('x', bit)]).astype(full)).astype(low)]
    ppermute x72 -> x74, starting transfers between devices: 72.1 us -> 104 us  [flip(): return lax.ppermute(value, names, pairs)]
    ppermute x72 -> x74, waiting for transfers between devices: 80.8 us -> 111 us  [flip(): return lax.ppermute(value, names, pairs)]
    unnamed x250 -> x121, local copies, waits for them, and re-layouts: 53.4 us -> 23.9 us
  transfers between devices with their start and end apart: 92 -> 91, of which waited for: 58 -> 57; matrix products, arithmetic and copies ran while one was open for 19% -> 21% of each run, Pallas kernels for 0% -> 9%
where the time goes in v2:
time: 757 us; the launch traced here: 749 us
  waiting for transfers between devices  288 us (38%)
  starting transfers between devices  137 us (18%)
  Pallas kernels  119 us (16%)
  local copies, waits for them, and re-layouts  81.8 us (11%)
  other arithmetic  60.3 us (8%)
  matrix products  37.7 us (5%)
  between operations  24.4 us (3%)
    ppermute x74, waiting for transfers between devices, flip(): return lax.ppermute(value, names, pairs)  111 us
    ppermute x74, starting transfers between devices, flip(): return lax.ppermute(value, names, pairs)  104 us
    all_gather x1, waiting for transfers between devices, on_device(): block_mine = lax.all_gather(block_own, LINE, axis=0, tiled=False)  70.5 us
    ppermute x12, waiting for transfers between devices, rows_to(): return lax.ppermute(value, LINE, pairs)  39.9 us
    reduce_scatter x2, waiting for transfers between devices, scatter_halves(): lax.psum_scatter(summed, LINE, scatter_dimension=0, tiled=False)  33.8 us
    all_gather x1, waiting for transfers between devices, on_device(): heads_all = lax.all_gather(heads_own, AXES, axis=0, tiled=True)  32.7 us
    ppermute x12, starting transfers between devices, rows_to(): return lax.ppermute(value, LINE, pairs)  29.8 us
    pallas_call x1, Pallas kernels, shared_back(): pl.pallas_call(lambda *refs: shared_back_kernel(tasks, side_tasks, *refs)...  25.8 us
  transfers between devices with their start and end apart: 91, of which 57 were waited for; matrix products, arithmetic and copies ran while one was open for 21% of the time, Pallas kernels for 9%

profile of v2, /device:TPU:0, one launch (start us, length us, event | category | flops | bytes accessed | tf_op | source)
XLA Modules:
  0.0 748.9 jit_solution(3530976904577259652)
XLA Ops:
  10.2 5.7 copy.109
  19.6 70.5 %all-gather.6.cloned.1.call-done = bf16[4352,512]{1,0:T(8,128)(2,1)} async-done(((bf16[544,512]{1,0:T(8,128)(2,1)}), bf16[4352,512]{1,0:T(8,128)(2,1)}) %all-gather.6.cloned.1.call-update) | async-done | bytes 4456464 | tf_op jit(solution)/shard_map/all_gather | solution.py:557
  91.7 3.8 broadcast_multiply_fusion
  98.2 4.9 select_bitcast_fusion
  125.1 4.1 collective-permute-start.8
  130.8 4.0 fusion
  134.9 7.0 copy.107
  143.9 7.1 collective-permute-done.8
  151.0 4.9 fusion.24
  172.2 4.0 copy.108
  177.6 4.5 fusion.65
  200.2 7.5 %multiply_convert_fusion = (bf16[768,2048]{1,0:T(8,128)(2,1)}, bf16[768,2048]{1,0:T(8,128)(2,1)}) fusion(f32[768,2048]{1,0:T(8,128)} %get-tuple-element.255.refs_8_.refs_4_, f32[768]{0:T(1024)S(1)} %mul.642, f32[2048]{0:T(1024)S(1)} %copy-done.29, f32[2048]{0:T(1024)S(1)} %copy-done.28, f32[2048]{0:T(1024)S(1)} %bitcast.236, f32[2048]{0:T(1024)S(1)} %bitcast.240, ...), kind=kLoop, calls=%fused_computation.10 | loop fusion | flops 20447232 | bytes 15766016 | tf_op jit(solution)/shard_map/convert_element_type | solution.py:613
  207.8 32.7 %all-gather.4.cloned.1.call-done.w_ref.refs_3_.refs_4_.refs_5_.refs_6_.refs_7_ = bf16[2048,5376]{1,0:T(8,128)(2,1)} async-done(((bf16[64,5376]{1,0:T(8,128)(2,1)}), bf16[2048,5376]{1,0:T(8,128)(2,1)}) %all-gather.4.cloned.1.call-update) | async-done | bytes 22020112 | tf_op jit(solution)/shard_map/all_gather | solution.py:577
  241.2 10.3 %shard_map.325 = bf16[768,512]{1,0:T(8,128)(2,1)} custom-call(s32[2]{0:T(128)} %get-tuple-element.240.picked_ref, s32[2]{0:T(128)} %gather_fusion, bf16[768,2048]{1,0:T(8,128)(2,1)} %get-tuple-element.154.x_ref, bf16[2048,5376]{1,0:T(8,128)(2,1)} %all-gather.4.cloned.1.call-done.w_ref.refs_3_.refs_4_.refs_5_.refs_6_.refs_7_, f32[768,128]{1,0:T(8,128)} %bitcast.204), custom_call_target="tpu_custom_call" | custom-call | flops 4831838208 | bytes 9437184 | tf_op jit(solution)/shard_map/pallas_call | solution.py:217
  260.5 13.6 %shard_map.324 = f32[768,768]{1,0:T(8,128)} custom-call(s32[3]{0:T(128)} %iota.34.picked_ref.task_ref, s32[3]{0:T(128)} %iota.34.picked_ref.task_ref, bf16[768,2048]{1,0:T(8,128)(2,1)} %get-tuple-element.154.x_ref, bf16[2048,5376]{1,0:T(8,128)(2,1)} %all-gather.4.cloned.1.call-done.w_ref.refs_3_.refs_4_.refs_5_.refs_6_.refs_7_, f32[768,128]{1,0:T(8,128)} %bitcast.205), custom_call_target="tpu_custom_call" | custom-call | flops 7247757312 | bytes 12582912 | tf_op jit(solution)/shard_map/pallas_call | solution.py:217
  274.1 3.6 collective-permute-done.24
  283.7 8.9 %collective-permute-start.29 = (f32[2,768]{1,0:T(2,128)S(1)}, f32[2,768]{1,0:T(2,128)S(1)}, u32[]{:S(2)}, u32[]{:S(2)}) collective-permute-start(f32[2,768]{1,0:T(2,128)S(1)} %fusion.60), channel_id=1, source_target_pairs={{0,4},{4,0},{1,5},{5,1},{2,6},{6,2},{3,7},{7,3},{8,12},{12,8},{9,1... | collective-permute-start | bytes 18440 | tf_op jit(solution)/shard_map/ppermute | solution.py:37
  298.8 4.3 collective-permute-start.34
  317.7 3.8 collective-permute-start.40
  323.1 3.8 collective-permute-done.41
  332.4 6.8 collective-permute-start.44
  346.5 8.8 %collective-permute-done.45 = bf16[768,256]{1,0:T(8,128)(2,1)S(1)} collective-permute-done((bf16[768,256]{1,0:T(8,128)(2,1)S(1)}, bf16[768,256]{1,0:T(8,128)(2,1)S(1)}, u32[]{:S(2)}, u32[]{:S(2)}) %collective-permute-start.45) | collective-permute-done | bytes 393248 | tf_op jit(solution)/shard_map/ppermute | solution.py:63
  363.0 6.4 shard_map.326.dy_ref.refs_2_
  370.1 6.5 shard_map.327.dy_other_ref
  376.7 21.9 %shard_map.328 = bf16[1024,5376]{1,0:T(8,128)(2,1)} custom-call(s32[7]{0:T(128)} %pad_add_fusion.2.slot_ref, bf16[768,1024]{1,0:T(8,128)(2,1)} %copy-done.35, bf16[768,1024]{1,0:T(8,128)(2,1)} %collective-permute-done.46.other_ref, bf16[768,3840]{1,0:T(8,128)(2,1)} %shard_map.326.dy_ref.refs_2_, bf16[768,3840]{1,0:T(8,128)(2,1)} %shard_map.327.dy_other_ref), custom_call_target="tpu_custom_call" | custom-call | flops 12079595520 | bytes 22806528 | tf_op jit(solution)/shard_map/pallas_call | solution.py:451
  400.0 25.8 %shard_map.329 = (bf16[768,2048]{1,0:T(8,128)(2,1)}, bf16[768,2048]{1,0:T(8,128)(2,1)}, bf16[768,2048]{1,0:T(8,128)(2,1)}, f32[16,2048]{1,0:T(8,128)}) custom-call(s32[5]{0:T(128)} %get-tuple-element.253.refs_0_, f32[6]{0:T(128)} %reshape.416.refs_1_, bf16[768,3840]{1,0:T(8,128)(2,1)} %shard_map.326.dy_ref.refs_2_, ...), custom_call_target="tpu_custom_call" | custom-call | flops 12079595520 | bytes 34603008 | tf_op jit(solution)/shard_map/pallas_call | solution.py:319
  428.4 6.2 collective-permute-start.49
  441.4 4.2 collective-permute-start.54
  446.2 3.5 collective-permute-done.52
  461.8 18.4 %shard_map.330 = (bf16[768,2048]{1,0:T(8,128)(2,1)}, bf16[512,2048]{1,0:T(8,128)(2,1)}, f32[768,512]{1,0:T(8,128)}, f32[8,512]{1,0:T(8,128)}) custom-call(f32[3]{0:T(128)} %pad_maximum_fusion.19.refs_0_, bf16[768,2048]{1,0:T(8,128)(2,1)} %get-tuple-element.31.refs_1_, bf16[768,2048]{1,0:T(8,128)(2,1)} %get-tuple-element.32.refs_2_, ...), custom_call_target="tpu_custom_call" | custom-call | flops 3221225472 | bytes 22020096 | tf_op jit(solution)/shard_map/pallas_call | solution.py:393
  489.9 5.4 collective-permute-start.59
  497.8 4.5 reshape.409
  507.4 7.2 convolution_convert_fusion
  514.6 12.3 %reshape.407 = bf16[3,8,64,3,512]{4,3,2,1,0:T(4,128)(2,1)} reshape(bf16[1536,1536]{1,0:T(8,128)(2,1)} %convolution_convert_fusion) | data formatting | bytes 9437184 | tf_op jit(solution)/shard_map/reshape | solution.py:753
  526.9 4.3 copy.122
  531.6 6.0 collective-permute-done.74
  546.1 5.8 fusion.90
  553.2 4.7 collective-permute-start.63
  558.1 11.8 %collective-permute-done.62 = bf16[384,512]{1,0:T(8,128)(2,1)S(1)} collective-permute-done((bf16[384,512]{1,0:T(8,128)(2,1)S(1)}, bf16[384,512]{1,0:T(8,128)(2,1)S(1)}, u32[]{:S(2)}, u32[]{:S(2)}) %collective-permute-start.62) | collective-permute-done | bytes 393248 | tf_op jit(solution)/shard_map/ppermute | solution.py:63
  576.8 11.8 %collective-permute-start.65 = (f32[2,512]{1,0:T(2,128)S(1)}, f32[2,512]{1,0:T(2,128)S(1)}, u32[]{:S(2)}, u32[]{:S(2)}) collective-permute-start(f32[2,512]{1,0:T(2,128)S(1)} %fusion.56), channel_id=1, source_target_pairs={{0,4},{4,0},{1,5},{5,1},{2,6},{6,2},{3,7},{7,3},{8,12},{12,8},{9,1... | collective-permute-start | bytes 12296 | tf_op jit(solution)/shard_map/ppermute | solution.py:37
  600.7 3.7 collective-permute-done.70
  606.9 4.0 convolution_convert_fusion.1
  615.0 3.6 all-to-all-start
  626.6 27.3 %collective-permute-done.81 = f32[66,256]{1,0:T(8,128)S(1)} collective-permute-done((f32[66,256]{1,0:T(8,128)S(1)}, f32[66,256]{1,0:T(8,128)S(1)}, u32[]{:S(2)}, u32[]{:S(2)}) %collective-permute-start.81) | collective-permute-done | bytes 67616 | tf_op jit(solution)/shard_map/ppermute | solution.py:37
  660.4 7.4 convert_add_fusion
  673.2 33.8 %reduce-scatter.3.cloned.1.call-done = bf16[1,416,512]{2,1,0:T(8,128)(2,1)} async-done(((bf16[8,416,512]{2,1,0:T(8,128)(2,1)}), bf16[1,416,512]{2,1,0:T(8,128)(2,1)}) %reduce-scatter.3.cloned.1.call-update) | async-done | bytes 426000 | tf_op jit(solution)/shard_map/reduce_scatter | solution.py:97
  712.3 6.1 collective-permute-done.75
  726.1 16.1 %shard_map.331 = f32[27,256,256]{2,1,0:T(8,128)} custom-call(s32[27]{0:T(128)} %constant.148.clone.part_ref, s32[1]{0:T(128)} %bitcast.103.core_ref, bf16[128,5376]{1,0:T(8,128)(2,1)} %add_convert_fusion.1.mine_ref, bf16[128,5376]{1,0:T(8,128)(2,1)} %collective-permute-done.78.other_ref), custom_call_target="tpu_custom_call" | custom-call | bytes 10616832 | tf_op jit(solution)/shard_map/pallas_call | solution.py:494
  (468 shorter events, 230.8 us)
Async XLA Ops:
  7.2 83.0 %all-gather.6.cloned.1.call-start = ((), (), s32[]{:S(2)}) async-start(), calls=%async_computation.6 | async-start | bytes 5013504 | tf_op jit(solution)/shard_map/all_gather | solution.py:557
  10.2 230.3 %all-gather.4.cloned.1.call-start = ((), (), s32[]{:S(2)}) async-start(), calls=%async_computation.3 | async-start | bytes 22708224 | tf_op jit(solution)/shard_map/all_gather | solution.py:577
  90.2 528.8 %reduce-scatter.5.cloned.1.call-start = ((), (), s32[]{:S(2)}) async-start(), calls=%async_computation.5 | async-start | bytes 12386304 | tf_op jit(solution)/shard_map/reduce_scatter | solution.py:97
  90.3 7.9 %collective-permute-start = (bf16[8,544,512]{2,1,0:T(8,128)(2,1)}, bf16[8,544,512]{2,1,0:T(8,128)(2,1)}, u32[]{:S(2)}, u32[]{:S(2)}) collective-permute-start(bf16[8,544,512]{2,1,0:T(8,128)(2,1)} %bitcast.220), channel_id=1, source_target_pairs={{0,1},{1,0},{2,3},{3,2},{4,5},{5,4},{6,7},{7,6},{8,9},{9,8},{10,11... | collective-permute-start | bytes 13369352 | tf_op jit(solution)/shard_map/ppermute | solution.py:37
  125.1 25.9 %collective-permute-start.8 = (bf16[384,512]{1,0:T(8,128)(2,1)S(1)}, bf16[384,512]{1,0:T(8,128)(2,1)}, u32[]{:S(2)}, u32[]{:S(2)}) collective-permute-start(bf16[384,512]{1,0:T(8,128)(2,1)S(1)} %get-tuple-element.208), channel_id=1, source_target_pairs={{0,4},{4,8},{8,12},{12,16},{16,20},{20,24},{24,28},{1,5},{5,9},{9,... | collective-permute-start | bytes 1179656 | tf_op jit(solution)/shard_map/ppermute | solution.py:63
  129.2 21.8 %collective-permute-start.9 = (bf16[384,512]{1,0:T(8,128)(2,1)S(1)}, bf16[384,512]{1,0:T(8,128)(2,1)}, u32[]{:S(2)}, u32[]{:S(2)}) collective-permute-start(bf16[384,512]{1,0:T(8,128)(2,1)S(1)} %get-tuple-element.209), channel_id=1, source_target_pairs={{4,0},{8,4},{12,8},{16,12},{20,16},{24,20},{28,24},{5,1},{9,5},{13... | collective-permute-start | bytes 1179656 | tf_op jit(solution)/shard_map/ppermute | solution.py:63
  167.8 9.1 %collective-permute-start.14 = (f32[2,512]{1,0:T(2,128)S(1)}, f32[2,512]{1,0:T(2,128)S(1)}, u32[]{:S(2)}, u32[]{:S(2)}) collective-permute-start(f32[2,512]{1,0:T(2,128)S(1)} %add_add_fusion.15), channel_id=1, source_target_pairs={{0,8},{8,0},{16,24},{24,16},{1,9},{9,1},{17,25},{25,17},{2,10},{10... | collective-permute-start | bytes 12296 | tf_op jit(solution)/shard_map/ppermute | solution.py:37
  169.2 7.7 %collective-permute-start.15 = (f32[2,512]{1,0:T(2,128)S(1)}, f32[2,512]{1,0:T(2,128)S(1)}, u32[]{:S(2)}, u32[]{:S(2)}) collective-permute-start(f32[2,512]{1,0:T(2,128)S(1)} %add_add_fusion.15), channel_id=1, source_target_pairs={{0,16},{8,24},{16,0},{24,8},{1,17},{9,25},{17,1},{25,9},{2,18},{10... | collective-permute-start | bytes 12296 | tf_op jit(solution)/shard_map/ppermute | solution.py:37
  170.9 6.0 collective-permute-start.16
  190.8 6.5 collective-permute-start.21
  190.9 6.4 collective-permute-start.22
  194.3 5.9 collective-permute-start.23
  252.7 27.4 %collective-permute-start.26 = (bf16[768,256]{1,0:T(8,128)(2,1)S(1)}, bf16[768,256]{1,0:T(8,128)(2,1)S(1)}, u32[]{:S(2)}, u32[]{:S(2)}) collective-permute-start(bf16[768,256]{1,0:T(8,128)(2,1)S(1)} %get-tuple-element.207), channel_id=1, source_target_pairs={{0,24},{4,28},{1,25},{5,29},{2,26},{6,30},{3,27},{7,31}} | collective-permute-start | bytes 1179656 | tf_op jit(solution)/shard_map/ppermute | solution.py:63
  256.1 24.1 %collective-permute-start.27 = (bf16[768,256]{1,0:T(8,128)(2,1)S(1)}, bf16[768,256]{1,0:T(8,128)(2,1)S(1)}, u32[]{:S(2)}, u32[]{:S(2)}) collective-permute-start(bf16[768,256]{1,0:T(8,128)(2,1)S(1)} %get-tuple-element.207), channel_id=1, source_target_pairs={{24,0},{28,4},{25,1},{29,5},{26,2},{30,6},{27,3},{31,7}} | collective-permute-start | bytes 1179656 | tf_op jit(solution)/shard_map/ppermute | solution.py:63
  257.4 20.3 %collective-permute-start.24 = (bf16[768,256]{1,0:T(8,128)(2,1)S(1)}, bf16[768,256]{1,0:T(8,128)(2,1)S(1)}, u32[]{:S(2)}, u32[]{:S(2)}) collective-permute-start(bf16[768,256]{1,0:T(8,128)(2,1)S(1)} %get-tuple-element.205), channel_id=1, source_target_pairs={{0,12},{4,16},{8,20},{12,24},{16,28},{1,13},{5,17},{9,21},{13,25},... | collective-permute-start | bytes 1179656 | tf_op jit(solution)/shard_map/ppermute | solution.py:63
  258.7 21.5 %collective-permute-start.25 = (bf16[768,256]{1,0:T(8,128)(2,1)S(1)}, bf16[768,256]{1,0:T(8,128)(2,1)S(1)}, u32[]{:S(2)}, u32[]{:S(2)}) collective-permute-start(bf16[768,256]{1,0:T(8,128)(2,1)S(1)} %get-tuple-element.206), channel_id=1, source_target_pairs={{12,0},{16,4},{20,8},{24,12},{28,16},{13,1},{17,5},{21,9},{25,13},... | collective-permute-start | bytes 1179656 | tf_op jit(solution)/shard_map/ppermute | solution.py:63
  283.7 10.6 %collective-permute-start.29 = (f32[2,768]{1,0:T(2,128)S(1)}, f32[2,768]{1,0:T(2,128)S(1)}, u32[]{:S(2)}, u32[]{:S(2)}) collective-permute-start(f32[2,768]{1,0:T(2,128)S(1)} %fusion.60), channel_id=1, source_target_pairs={{0,4},{4,0},{1,5},{5,1},{2,6},{6,2},{3,7},{7,3},{8,12},{12,8},{9,1... | collective-permute-start | bytes 18440 | tf_op jit(solution)/shard_map/ppermute | solution.py:37
  298.8 6.0 collective-permute-start.34
  317.1 5.8 collective-permute-start.39
  329.5 14.2 %collective-permute-start.42 = (bf16[768,256]{1,0:T(8,128)(2,1)S(1)}, bf16[768,256]{1,0:T(8,128)(2,1)S(1)}, u32[]{:S(2)}, u32[]{:S(2)}) collective-permute-start(bf16[768,256]{1,0:T(8,128)(2,1)S(1)} %get-tuple-element.199), channel_id=1, source_target_pairs={{0,12},{4,16},{8,20},{12,24},{16,28},{1,13},{5,17},{9,21},{13,25},... | collective-permute-start | bytes 1179656 | tf_op jit(solution)/shard_map/ppermute | solution.py:63
  331.1 12.6 %collective-permute-start.43 = (bf16[768,256]{1,0:T(8,128)(2,1)S(1)}, bf16[768,256]{1,0:T(8,128)(2,1)S(1)}, u32[]{:S(2)}, u32[]{:S(2)}) collective-permute-start(bf16[768,256]{1,0:T(8,128)(2,1)S(1)} %get-tuple-element.199), channel_id=1, source_target_pairs={{12,0},{16,4},{20,8},{24,12},{28,16},{13,1},{17,5},{21,9},{25,13},... | collective-permute-start | bytes 1179656 | tf_op jit(solution)/shard_map/ppermute | solution.py:63
  332.4 14.1 %collective-permute-start.44 = (bf16[768,256]{1,0:T(8,128)(2,1)S(1)}, bf16[768,256]{1,0:T(8,128)(2,1)S(1)}, u32[]{:S(2)}, u32[]{:S(2)}) collective-permute-start(bf16[768,256]{1,0:T(8,128)(2,1)S(1)} %get-tuple-element.200), channel_id=1, source_target_pairs={{0,24},{4,28},{1,25},{5,29},{2,26},{6,30},{3,27},{7,31}} | collective-permute-start | bytes 1179656 | tf_op jit(solution)/shard_map/ppermute | solution.py:63
  339.2 16.2 %collective-permute-start.45 = (bf16[768,256]{1,0:T(8,128)(2,1)S(1)}, bf16[768,256]{1,0:T(8,128)(2,1)S(1)}, u32[]{:S(2)}, u32[]{:S(2)}) collective-permute-start(bf16[768,256]{1,0:T(8,128)(2,1)S(1)} %get-tuple-element.200), channel_id=1, source_target_pairs={{24,0},{28,4},{25,1},{29,5},{26,2},{30,6},{27,3},{31,7}} | collective-permute-start | bytes 1179656 | tf_op jit(solution)/shard_map/ppermute | solution.py:63
  355.6 13.8 %collective-permute-start.47 = (bf16[768,1280]{1,0:T(8,128)(2,1)S(1)}, bf16[768,1280]{1,0:T(8,128)(2,1)}, u32[]{:S(2)}, u32[]{:S(2)}) collective-permute-start(bf16[768,1280]{1,0:T(8,128)(2,1)S(1)} %pad_maximum_fusion.6.d_ref), channel_id=1, source_target_pairs={{0,1},{1,0},{2,3},{3,2},{4,5},{5,4},{6,7},{7,6},{8,9},{9,8},{10,11... | collective-permute-start | bytes 5898248 | tf_op jit(solution)/shard_map/ppermute | solution.py:37
  359.1 17.6 %collective-permute-start.46 = (bf16[768,1024]{1,0:T(8,128)(2,1)}, bf16[768,1024]{1,0:T(8,128)(2,1)}, u32[]{:S(2)}, u32[]{:S(2)}) collective-permute-start(bf16[768,1024]{1,0:T(8,128)(2,1)} %get-tuple-element.178), channel_id=1, source_target_pairs={{0,1},{1,0},{2,3},{3,2},{4,5},{5,4},{6,7},{7,6},{8,9},{9,8},{10,11... | collective-permute-start | bytes 4718600 | tf_op jit(solution)/shard_map/ppermute | solution.py:37
  398.6 308.4 %reduce-scatter.3.cloned.1.call-start = ((), (), s32[]{:S(2)}) async-start(), calls=%async_computation.4 | async-start | bytes 3833856 | tf_op jit(solution)/shard_map/reduce_scatter | solution.py:97
  428.4 8.9 %collective-permute-start.49 = (f32[7,2048]{1,0:T(8,128)S(1)}, f32[7,2048]{1,0:T(8,128)S(1)}, u32[]{:S(2)}, u32[]{:S(2)}) collective-permute-start(f32[7,2048]{1,0:T(8,128)S(1)} %fusion.107), channel_id=1, source_target_pairs={{0,4},{4,0},{1,5},{5,1},{2,6},{6,2},{3,7},{7,3},{8,12},{12,8},{9,1... | collective-permute-start | bytes 172040 | tf_op jit(solution)/shard_map/ppermute | solution.py:37
  441.2 8.6 %collective-permute-start.52 = (f32[7,2048]{1,0:T(8,128)S(1)}, f32[7,2048]{1,0:T(8,128)S(1)}, u32[]{:S(2)}, u32[]{:S(2)}) collective-permute-start(f32[7,2048]{1,0:T(8,128)S(1)} %add_add_fusion.3), channel_id=1, source_target_pairs={{0,8},{8,0},{16,24},{24,16},{1,9},{9,1},{17,25},{25,17},{2,10},{10... | collective-permute-start | bytes 172040 | tf_op jit(solution)/shard_map/ppermute | solution.py:37
  441.2 11.8 %collective-permute-start.53 = (f32[7,2048]{1,0:T(8,128)S(1)}, f32[7,2048]{1,0:T(8,128)S(1)}, u32[]{:S(2)}, u32[]{:S(2)}) collective-permute-start(f32[7,2048]{1,0:T(8,128)S(1)} %add_add_fusion.3), channel_id=1, source_target_pairs={{0,16},{8,24},{16,0},{24,8},{1,17},{9,25},{17,1},{25,9},{2,18},{10... | collective-permute-start | bytes 172040 | tf_op jit(solution)/shard_map/ppermute | solution.py:37
  441.4 11.6 %collective-permute-start.54 = (f32[7,2048]{1,0:T(8,128)S(1)}, f32[7,2048]{1,0:T(8,128)S(1)}, u32[]{:S(2)}, u32[]{:S(2)}) collective-permute-start(f32[7,2048]{1,0:T(8,128)S(1)} %add_add_fusion.3), channel_id=1, source_target_pairs={{0,24},{8,16},{16,8},{24,0},{1,25},{9,17},{17,9},{25,1},{2,26},{10... | collective-permute-start | bytes 172040 | tf_op jit(solution)/shard_map/ppermute | solution.py:37
  489.9 14.7 %collective-permute-start.59 = (f32[2,512]{1,0:T(2,128)S(1)}, f32[2,512]{1,0:T(2,128)S(1)}, u32[]{:S(2)}, u32[]{:S(2)}) collective-permute-start(f32[2,512]{1,0:T(2,128)S(1)} %add_add_fusion.13), channel_id=1, source_target_pairs={{0,8},{8,0},{16,24},{24,16},{1,9},{9,1},{17,25},{25,17},{2,10},{10... | collective-permute-start | bytes 12296 | tf_op jit(solution)/shard_map/ppermute | solution.py:37
  495.3 9.3 %collective-permute-start.60 = (f32[2,512]{1,0:T(2,128)S(1)}, f32[2,512]{1,0:T(2,128)S(1)}, u32[]{:S(2)}, u32[]{:S(2)}) collective-permute-start(f32[2,512]{1,0:T(2,128)S(1)} %add_add_fusion.13), channel_id=1, source_target_pairs={{0,16},{8,24},{16,0},{24,8},{1,17},{9,25},{17,1},{25,9},{2,18},{10... | collective-permute-start | bytes 12296 | tf_op jit(solution)/shard_map/ppermute | solution.py:37
  495.3 9.3 %collective-permute-start.61 = (f32[2,512]{1,0:T(2,128)S(1)}, f32[2,512]{1,0:T(2,128)S(1)}, u32[]{:S(2)}, u32[]{:S(2)}) collective-permute-start(f32[2,512]{1,0:T(2,128)S(1)} %add_add_fusion.13), channel_id=1, source_target_pairs={{0,24},{8,16},{16,8},{24,0},{1,25},{9,17},{17,9},{25,1},{2,26},{10... | collective-permute-start | bytes 12296 | tf_op jit(solution)/shard_map/ppermute | solution.py:37
  531.5 6.1 collective-permute-start.74
  551.9 18.0 %collective-permute-start.62 = (bf16[384,512]{1,0:T(8,128)(2,1)S(1)}, bf16[384,512]{1,0:T(8,128)(2,1)S(1)}, u32[]{:S(2)}, u32[]{:S(2)}) collective-permute-start(bf16[384,512]{1,0:T(8,128)(2,1)S(1)} %get-tuple-element.194), channel_id=1, source_target_pairs={{4,0},{8,4},{12,8},{16,12},{20,16},{24,20},{28,24},{5,1},{9,5},{13... | collective-permute-start | bytes 1179656 | tf_op jit(solution)/shard_map/ppermute | solution.py:63
  553.2 20.0 %collective-permute-start.63 = (bf16[384,512]{1,0:T(8,128)(2,1)S(1)}, bf16[384,512]{1,0:T(8,128)(2,1)S(1)}, u32[]{:S(2)}, u32[]{:S(2)}) collective-permute-start(bf16[384,512]{1,0:T(8,128)(2,1)S(1)} %get-tuple-element.195), channel_id=1, source_target_pairs={{0,4},{4,8},{8,12},{12,16},{16,20},{20,24},{24,28},{1,5},{5,9},{9,... | collective-permute-start | bytes 1179656 | tf_op jit(solution)/shard_map/ppermute | solution.py:63
  576.8 13.8 %collective-permute-start.65 = (f32[2,512]{1,0:T(2,128)S(1)}, f32[2,512]{1,0:T(2,128)S(1)}, u32[]{:S(2)}, u32[]{:S(2)}) collective-permute-start(f32[2,512]{1,0:T(2,128)S(1)} %fusion.56), channel_id=1, source_target_pairs={{0,4},{4,0},{1,5},{5,1},{2,6},{6,2},{3,7},{7,3},{8,12},{12,8},{9,1... | collective-permute-start | bytes 12296 | tf_op jit(solution)/shard_map/ppermute | solution.py:37
  615.0 56.4 %all-to-all-start = ((bf16[8,128,512]{2,1,0:T(8,128)(2,1)}), bf16[8,128,512]{2,1,0:T(8,128)(2,1)S(1)}, u32[]{:S(2)}, u32[]{:S(2)}) async-start(bf16[8,128,512]{2,1,0:T(8,128)(2,1)} %add_convert_fusion.2), calls=%async_computation | async-start | bytes 2097152 | tf_op jit(solution)/shard_map/all_to_all | solution.py:101
  619.0 89.6 %collective-permute-start.77 = (bf16[128,5376]{1,0:T(8,128)(2,1)}, bf16[128,5376]{1,0:T(8,128)(2,1)}, u32[]{:S(2)}, u32[]{:S(2)}) collective-permute-start(bf16[128,5376]{1,0:T(8,128)(2,1)} %bitcast.229), channel_id=1, source_target_pairs={{0,2},{2,0},{1,3},{3,1},{4,6},{6,4},{5,7},{7,5},{8,10},{10,8},{9,1... | collective-permute-start | bytes 4128776 | tf_op jit(solution)/shard_map/ppermute | solution.py:37
  623.4 30.5 %collective-permute-start.81 = (f32[66,256]{1,0:T(8,128)S(1)}, f32[66,256]{1,0:T(8,128)S(1)}, u32[]{:S(2)}, u32[]{:S(2)}) collective-permute-start(f32[66,256]{1,0:T(8,128)S(1)} %add.829), channel_id=1, source_target_pairs={{0,2},{2,0},{1,3},{3,1},{4,6},{6,4},{5,7},{7,5},{8,10},{10,8},{9,1... | collective-permute-start | bytes 202760 | tf_op jit(solution)/shard_map/ppermute | solution.py:37
  624.4 31.5 %collective-permute-start.82 = (f32[66,256]{1,0:T(8,128)S(1)}, f32[66,256]{1,0:T(8,128)S(1)}, u32[]{:S(2)}, u32[]{:S(2)}) collective-permute-start(f32[66,256]{1,0:T(8,128)S(1)} %add.829), channel_id=1, source_target_pairs={{0,6},{2,4},{4,2},{6,0},{1,7},{3,5},{5,3},{7,1},{8,14},{10,12},{12... | collective-permute-start | bytes 202760 | tf_op jit(solution)/shard_map/ppermute | solution.py:37
  656.0 11.8 %collective-permute-start.83 = (f32[66,256]{1,0:T(8,128)S(1)}, f32[66,256]{1,0:T(8,128)S(1)}, u32[]{:S(2)}, u32[]{:S(2)}) collective-permute-start(f32[66,256]{1,0:T(8,128)S(1)} %add_add_fusion.1), channel_id=1, source_target_pairs={{0,8},{8,0},{16,24},{24,16},{1,9},{9,1},{17,25},{25,17},{2,10},{10... | collective-permute-start | bytes 202760 | tf_op jit(solution)/shard_map/ppermute | solution.py:37
  657.3 12.9 %collective-permute-start.84 = (f32[66,256]{1,0:T(8,128)S(1)}, f32[66,256]{1,0:T(8,128)S(1)}, u32[]{:S(2)}, u32[]{:S(2)}) collective-permute-start(f32[66,256]{1,0:T(8,128)S(1)} %add_add_fusion.1), channel_id=1, source_target_pairs={{0,16},{8,24},{16,0},{24,8},{1,17},{9,25},{17,1},{25,9},{2,18},{10... | collective-permute-start | bytes 202760 | tf_op jit(solution)/shard_map/ppermute | solution.py:37
  659.7 10.6 %collective-permute-start.85 = (f32[66,256]{1,0:T(8,128)S(1)}, f32[66,256]{1,0:T(8,128)S(1)}, u32[]{:S(2)}, u32[]{:S(2)}) collective-permute-start(f32[66,256]{1,0:T(8,128)S(1)} %add_add_fusion.1), channel_id=1, source_target_pairs={{0,24},{8,16},{16,8},{24,0},{1,25},{9,17},{17,9},{25,1},{2,26},{10... | collective-permute-start | bytes 202760 | tf_op jit(solution)/shard_map/ppermute | solution.py:37
  671.6 40.1 %collective-permute-start.72 = (bf16[128,512]{1,0:T(8,128)(2,1)S(1)}, bf16[128,512]{1,0:T(8,128)(2,1)S(1)}, u32[]{:S(2)}, u32[]{:S(2)}) collective-permute-start(bf16[128,512]{1,0:T(8,128)(2,1)S(1)} %reduce_sum.393), channel_id=1, source_target_pairs={{0,2},{2,0},{1,3},{3,1},{4,6},{6,4},{5,7},{7,5},{8,10},{10,8},{9,1... | collective-permute-start | bytes 393224 | tf_op jit(solution)/shard_map/ppermute | solution.py:37
  707.0 11.4 %collective-permute-start.75 = (bf16[416,512]{1,0:T(8,128)(2,1)}, bf16[416,512]{1,0:T(8,128)(2,1)S(1)}, u32[]{:S(2)}, u32[]{:S(2)}) collective-permute-start(bf16[416,512]{1,0:T(8,128)(2,1)} %bitcast.234), channel_id=1, source_target_pairs={{0,2},{2,0},{1,3},{3,1},{4,6},{6,4},{5,7},{7,5},{8,10},{10,8},{9,1... | collective-permute-start | bytes 1277960 | tf_op jit(solution)/shard_map/ppermute | solution.py:37
  711.7 14.3 %collective-permute-start.78 = (bf16[128,5376]{1,0:T(8,128)(2,1)}, bf16[128,5376]{1,0:T(8,128)(2,1)}, u32[]{:S(2)}, u32[]{:S(2)}) collective-permute-start(bf16[128,5376]{1,0:T(8,128)(2,1)} %add_convert_fusion.1.mine_ref), channel_id=1, source_target_pairs={{0,1},{1,0},{2,3},{3,2},{4,5},{5,4},{6,7},{7,6},{8,9},{9,8},{10,11... | collective-permute-start | bytes 4128776 | tf_op jit(solution)/shard_map/ppermute | solution.py:37
  711.8 6.9 collective-permute-start.73
  (93 other events, 862.5 us)
Sparse Core Ops, SparseCore 0:
  10.8 79.3 all-gather.5
  93.7 146.7 all-gather.3
  398.8 203.3 reduce-scatter.4
  606.2 100.7 reduce-scatter.2

commit v3 on v2

--- a/solution.py
+++ b/solution.py
@@ -26,7 +26,7 @@
 
 
 def flip(value, moves):
-    moves = sorted(moves, key=lambda move: AXES.index(move[0]))
+    moves = sorted([m for m in moves if m[1]], key=lambda move: AXES.index(move[0]))
     names = tuple(name for name, _ in moves)
     places = coords(names)
     index = {place: i for i, place in enumerate(places)}
@@ -57,6 +57,14 @@
     return value
 
 
+def sum_along(value, name):
+    bit = 1
+    while bit < lax.axis_size(name):
+        value = value + flip(value, [(name, bit)])
+        bit *= 2
+    return value
+
+
 def rows_to(value, pairs):
     if not pairs:
         return jnp.zeros_like(value)
@@ -93,13 +101,21 @@
     return own, flip(own, [("c", 1)])
 
 
-def scatter_halves(summed):
-    return over_groups(lax.psum_scatter(summed, LINE, scatter_dimension=0, tiled=False))
-
-
-def scatter_few(summed):
-    arrived = lax.all_to_all(summed, LINE, 0, 0, tiled=True)
-    return over_groups(jnp.sum(arrived.astype(full), axis=0).astype(low))
+def scatter_y(partial):
+    parts = partial.reshape(-1, 2, *partial.shape[1:])
+    here = lax.axis_index("y")
+    mine = lax.dynamic_index_in_dim(parts, here, 1, keepdims=False)
+    other = lax.dynamic_index_in_dim(parts, 1 - here, 1, keepdims=False)
+    return (mine.astype(full) + flip(other, [("y", 1)]).astype(full)).astype(low)
+
+
+def scatter_z(parts):
+    here = lax.axis_index("z")
+    total = lax.dynamic_index_in_dim(parts, here, 0, keepdims=False).astype(full)
+    for m in range(1, lax.axis_size("z")):
+        part = lax.dynamic_index_in_dim(parts, here ^ m, 0, keepdims=False)
+        total = total + flip(part, [("z", m)]).astype(full)
+    return total.astype(low)
 
 
 def along(value, offset, axis):
@@ -123,9 +139,13 @@
     return ((column >= starts[None, :]) & (column < ends[None, :])).astype(full)
 
 
+def silu(value):
+    return value * (0.5 + 0.5 * jnp.tanh(0.5 * value))
+
+
 def silu_slope(value):
-    sigma = jax.nn.sigmoid(value)
-    return sigma * (1.0 + value * (1.0 - sigma))
+    turn = jnp.tanh(0.5 * value)
+    return 0.5 + 0.5 * turn + 0.25 * value * (1.0 - turn * turn)
 
 
 def norm_scale(value, count):
@@ -159,6 +179,20 @@
     return terms, table
 
 
+def row_moves(terms, line):
+    moves = []
+    for e, (task, side, hop) in enumerate(terms):
+        pairs = [(f, f - side * hop) for f in range(line) if 0 <= f - side * hop < line]
+        last = moves[-1] if moves else None
+        if last and last[0] == task and not {t for _, t in last[1]} & {t for _, t in pairs}:
+            if not {f for f, _ in last[1]} & {f for f, _ in pairs}:
+                last[1].extend(pairs)
+                last[2].append((e, [f for f, _ in pairs]))
+                continue
+        moves.append((task, pairs, [(e, [f for f, _ in pairs])]))
+    return moves
+
+
 def task_scales(products):
     g00, g01, g02, g11, g12, g22 = products
     n0, n1, n2 = (jnp.sqrt(g + 1e-12) for g in (g00, g11, g22))
@@ -198,17 +232,21 @@
 
 def terms_kernel(picked_ref, task_ref, x_ref, w_ref, mask_ref, out_ref):
     at = pl.program_id(0)
-    spread = jnp.dot(x_ref[...], w_ref[...], preferred_element_type=full)
     pixels, head = out_ref.shape
+
+    def product(k):
+        return jnp.dot(
+            x_ref[...], w_ref[:, k * head : (k + 1) * head], preferred_element_type=full
+        )
+
     for task, rate in enumerate(head_rates):
 
         @pl.when(task_ref[at] == task)
         def _():
-            total = spread[:, head : 2 * head]
-            for k, shift in ((0, rate), (2, pixels - rate)):
-                piece = pltpu.roll(spread[:, k * head : (k + 1) * head], shift, 0)
-                total = total + piece * mask_ref[:, 3 * task + k : 3 * task + k + 1]
-            out_ref[...] = total.astype(out_ref.dtype)
+            left = pltpu.roll(product(0), rate, 0) * mask_ref[:, 3 * task : 3 * task + 1]
+            right = pltpu.roll(product(2), pixels - rate, 0)
+            right = right * mask_ref[:, 3 * task + 2 : 3 * task + 3]
+            out_ref[...] = (product(1) + left + right).astype(out_ref.dtype)
 
 
 def head_terms(grid, heads_all, masks, picked, task_of, head, dtype):
@@ -235,7 +273,7 @@
 
 
 def spread_kernel(task_ref, d_ref, mask_ref, out_ref):
-    at = pl.program_id(0)
+    at = pl.program_id(1)
     pixels, head = d_ref.shape
     for task, rate in enumerate(head_rates):
 
@@ -248,23 +286,23 @@
                 out_ref[:, k * head : (k + 1) * head] = pltpu.roll(piece, shift, 0).astype(low)
 
 
-def spread_back(grads, masks, task_of, head):
-    pixels = grads.shape[0]
+def spread_back(grads, masks, task_of, head, pixels):
+    rows = grads.shape[0]
     items = grads.shape[1] // head
     return pl.pallas_call(
         spread_kernel,
-        out_shape=jax.ShapeDtypeStruct((pixels, 3 * head * items), low),
+        out_shape=jax.ShapeDtypeStruct((rows, 3 * head * items), low),
         grid_spec=pltpu.PrefetchScalarGridSpec(
             num_scalar_prefetch=1,
-            grid=(items,),
+            grid=(rows // pixels, items),
             in_specs=[
-                spec((pixels, head), lambda i, t: (0, i)),
-                spec(masks.shape, lambda i, t: (0, 0)),
+                spec((pixels, head), lambda j, i, t: (j, i)),
+                spec((pixels, masks.shape[1]), lambda j, i, t: (j, 0)),
             ],
-            out_specs=spec((pixels, 3 * head), lambda i, t: (0, i)),
+            out_specs=spec((pixels, 3 * head), lambda j, i, t: (j, i)),
         ),
         compiler_params=params(),
-        cost_estimate=cost(10 * pixels * head * items * 3, 8 * pixels * head * items),
+        cost_estimate=cost(30 * rows * head * items, 8 * rows * head * items),
     )(task_of, grads, masks)
 
 
@@ -274,8 +312,8 @@
     dy_ref = refs[2]
     w_refs = refs[3 : 3 + tasks + slots]
     wide_ref, source_ref, vec_ref, mask_ref = refs[3 + tasks + slots : 7 + tasks + slots]
-    out_refs = refs[7 + tasks + slots : -1]
-    sums_ref = refs[-1]
+    out_refs = refs[7 + tasks + slots : -3]
+    slope_ref, normed_ref, sums_ref = refs[-3:]
     three = w_refs[0].shape[1]
 
     def back(i):
@@ -294,6 +332,8 @@
     normed = (wide_ref[...].astype(full) - vec_ref[0:1]) * vec_ref[1:2]
     value = normed * vec_ref[2:3] + vec_ref[3:4] + source_ref[...].astype(full)
     slope = silu_slope(value) * mask_ref[:, 1:2]
+    slope_ref[...] = slope.astype(low)
+    normed_ref[...] = normed.astype(low)
     rows = []
     for t in range(tasks):
         out_refs[t][...] = grads[t].astype(low)
@@ -318,7 +358,7 @@
     column = lambda j, p, h: (0, j)
     return pl.pallas_call(
         lambda *refs: shared_back_kernel(tasks, side_tasks, *refs),
-        out_shape=[jax.ShapeDtypeStruct((pixels, depth), low)] * tasks
+        out_shape=[jax.ShapeDtypeStruct((pixels, depth), low)] * (tasks + 2)
         + [jax.ShapeDtypeStruct((16, depth), full)],
         grid_spec=pltpu.PrefetchScalarGridSpec(
             num_scalar_prefetch=2,
@@ -331,7 +371,7 @@
                 spec((8, block), column),
                 spec(masks.shape, lambda j, p, h: (0, 0)),
             ],
-            out_specs=[spec((pixels, block), column)] * tasks + [spec((16, block), column)],
+            out_specs=[spec((pixels, block), column)] * (tasks + 2) + [spec((16, block), column)],
         ),
         compiler_params=params(),
         cost_estimate=cost(
@@ -341,26 +381,35 @@
 
 
 def expand_back_kernel(tasks, blocks, *refs):
-    weight_ref = refs[0]
+    gram_ref, sum_ref = refs[0], refs[1 + tasks]
     grad_refs = refs[1 : 1 + tasks]
-    wide_ref, source_ref, vec_ref, mask_ref, hidden_ref, w_ref, mid_ref, mid_vec_ref = refs[
-        1 + tasks : 9 + tasks
+    slope_ref, normed_ref, vec_ref, mask_ref, hidden_ref, w_ref, mid_ref, mid_vec_ref = refs[
+        2 + tasks : 10 + tasks
     ]
-    dbefore_ref, dweight_ref, dout_ref, sums_ref, total_ref = refs[9 + tasks :]
+    dbefore_ref, dweight_ref, dout_ref, sums_ref, total_ref, turned_ref = refs[10 + tasks :]
     at = pl.program_id(0)
-    combined = grad_refs[0][...].astype(full) * weight_ref[0]
+
+    @pl.when(at == 0)
+    def _():
+        turned_ref[...] = hidden_ref[...].T
+
+    gram = 2 * tasks
+    weights = task_scales([gram_ref[gram : gram + 1, i : i + 1] for i in range(6)])
+    combined = grad_refs[0][...].astype(full) * weights[0]
+    dgain = sum_ref[0:1] * weights[0]
+    dbias = sum_ref[1:2] * weights[0]
     for t in range(1, tasks):
-        combined = combined + grad_refs[t][...].astype(full) * weight_ref[t]
-    normed = (wide_ref[...].astype(full) - vec_ref[0:1]) * vec_ref[1:2]
-    value = normed * vec_ref[2:3] + vec_ref[3:4] + source_ref[...].astype(full)
+        combined = combined + grad_refs[t][...].astype(full) * weights[t]
+        dgain = dgain + sum_ref[2 * t : 2 * t + 1] * weights[t]
+        dbias = dbias + sum_ref[2 * t + 1 : 2 * t + 2] * weights[t]
+    normed = normed_ref[...].astype(full)
     valid = mask_ref[:, 1:2]
-    dbefore = combined * (silu_slope(value) * valid)
+    dbefore = combined * slope_ref[...].astype(full)
     dbefore_ref[...] = dbefore.astype(low)
-    dwide = (dbefore - vec_ref[5:6] - normed * vec_ref[4:5]) * vec_ref[6:7] * valid
+    per = vec_ref[1:2]
+    dwide = (dbefore - dbias * per - normed * (dgain * per)) * vec_ref[0:1] * valid
     dwide = dwide.astype(low)
-    dweight_ref[...] = lax.dot_general(
-        hidden_ref[...], dwide, (((0,), (0,)), ((), ())), preferred_element_type=full
-    ).astype(low)
+    dweight_ref[...] = jnp.dot(turned_ref[...], dwide, preferred_element_type=full).astype(low)
     part = lax.dot_general(
         dwide, w_ref[...], (((1,), (1,)), ((), ())), preferred_element_type=full
     )
@@ -383,12 +432,12 @@
         sums_ref[1, :] = jnp.sum(dout, axis=0)
 
 
-def expand_back(task_weights, grads, wide, source, vecs, masks, hidden, weight, mid, mid_vecs, block):
-    pixels, depth = wide.shape
+def expand_back(summed, grads, slope, normed, vecs, masks, hidden, weight, mid, mid_vecs, block):
+    pixels, depth = slope.shape
     width = hidden.shape[1]
     tasks = len(grads)
-    column = lambda j, w: (0, j)
-    fixed = lambda j, w: (0, 0)
+    column = lambda j: (0, j)
+    fixed = lambda j: (0, 0)
     blocks = depth // block
     return pl.pallas_call(
         lambda *refs: expand_back_kernel(tasks, blocks, *refs),
@@ -399,9 +448,12 @@
             jax.ShapeDtypeStruct((8, width), full),
         ],
         grid_spec=pltpu.PrefetchScalarGridSpec(
-            num_scalar_prefetch=1,
+            num_scalar_prefetch=0,
             grid=(blocks,),
-            in_specs=[spec((pixels, block), column)] * (tasks + 2)
+            in_specs=[spec((summed.shape[0], 128), fixed)]
+            + [spec((pixels, block), column)] * tasks
+            + [spec((summed.shape[0], block), column)]
+            + [spec((pixels, block), column)] * 2
             + [
                 spec((8, block), column),
                 spec(masks.shape, fixed),
@@ -416,93 +468,237 @@
                 spec((pixels, width), fixed),
                 spec((8, width), fixed),
             ],
-            scratch_shapes=[pltpu.VMEM((pixels, width), full)],
+            scratch_shapes=[pltpu.VMEM((pixels, width), full), pltpu.VMEM((width, pixels), low)],
         ),
         compiler_params=params(),
-        cost_estimate=cost(4 * pixels * depth * width, 14 * pixels * depth),
-    )(task_weights, *grads, wide, source, vecs, masks, hidden, weight, mid, mid_vecs)
-
-
-def weight_grad_kernel(slot_ref, x_ref, other_ref, dy_ref, dy_other_ref, out_ref, turned_ref):
-    at = pl.program_id(0)
-    pixels = x_ref.shape[0]
-
-    @pl.when(at == 0)
+        cost_estimate=cost(4 * pixels * width, 14 * pixels),
+    )(summed, *grads, summed, slope, normed, vecs, masks, hidden, weight, mid, mid_vecs)
+
+
+def turn_kernel(*refs):
+    out_ref = refs[-1]
+    pixels = refs[0].shape[0]
+    for i, ref in enumerate(refs[:-1]):
+        out_ref[:, i * pixels : (i + 1) * pixels] = ref[...].T
+
+
+def turn(pieces):
+    pixels, depth = pieces[0].shape
+    block = min(depth, 512)
+    return pl.pallas_call(
+        turn_kernel,
+        out_shape=jax.ShapeDtypeStruct((depth, len(pieces) * pixels), low),
+        grid=(depth // block,),
+        in_specs=[spec((pixels, block), lambda i: (0, i))] * len(pieces),
+        out_specs=spec((block, len(pieces) * pixels), lambda i: (i, 0)),
+        compiler_params=params(),
+        cost_estimate=cost(0, 4 * len(pieces) * pixels * depth),
+    )(*pieces)
+
+
+def weight_grad_kernel(members, side_tasks, tasks, groups, *refs):
+    slot_ref, task_ref, x_ref = refs[:3]
+    chips = groups // 2
+    center_refs, side_refs = refs[3 : 3 + chips], refs[3 + chips : 3 + groups]
+    mask_refs = refs[3 + groups : 3 + 2 * groups]
+    out_ref, dy_ref, total_ref = refs[3 + 2 * groups :]
+    pixels = center_refs[0].shape[0]
+    lane = center_refs[0].shape[1] // (2 * tasks)
+    slots = len(side_tasks)
+    three = 3 * lane
+
+    def spread(j, i, grad_ref, at, task):
+        rows = slice(j * pixels, (j + 1) * pixels)
+        held = grad_ref[:, at * lane : (at + 1) * lane]
+        dy_ref[rows, i * three + lane : i * three + 2 * lane] = held
+        rate = head_rates[task]
+        for k, shift in ((0, pixels - rate), (2, rate)):
+            piece = held.astype(full) * mask_refs[j][:, 3 * task + k : 3 * task + k + 1]
+            columns = slice(i * three + k * lane, i * three + (k + 1) * lane)
+            dy_ref[rows, columns] = pltpu.roll(piece, shift, 0).astype(low)
+
+    @pl.when(pl.program_id(0) == 0)
     def _():
-        turned_ref[:, :pixels] = x_ref[...].T
-        turned_ref[:, pixels:] = other_ref[...].T
-
-    @pl.when(slot_ref[at] >= 0)
-    def _():
-        total = jnp.dot(turned_ref[:, :pixels], dy_ref[...], preferred_element_type=full)
-        total += jnp.dot(turned_ref[:, pixels:], dy_other_ref[...], preferred_element_type=full)
-        out_ref[...] = total.astype(low)
-
-    @pl.when(slot_ref[at] < 0)
-    def _():
-        out_ref[...] = jnp.zeros_like(out_ref)
-
-
-def weight_grad(x, other, dys, dys_other, slot_of, three):
-    pixels, depth = x.shape
+        for j in range(groups):
+            for i, item in enumerate(members):
+                if item < tasks:
+                    spread(j, i, center_refs[j // 2], j % 2 * tasks + item, item)
+                    continue
+                at = item - tasks
+                for task in side_tasks[at]:
+                    move = lambda j=j, i=i, at=at, task=task: spread(
+                        j, i, side_refs[j // 2], j % 2 * slots + at, task
+                    )
+                    if len(side_tasks[at]) == 1:
+                        move()
+                    else:
+                        pl.when(task_ref[at] == task)(move)
+
+    total_ref[...] = jnp.dot(x_ref[...], dy_ref[...], preferred_element_type=full)
+    for g in range(out_ref.shape[1] // three):
+        columns = slice(g * three, (g + 1) * three)
+
+        @pl.when(slot_ref[g] >= 0)
+        def _():
+            start = pl.multiple_of(slot_ref[g] * three, 128)
+            out_ref[:, columns] = total_ref[:, pl.ds(start, three)].astype(low)
+
+        @pl.when(slot_ref[g] < 0)
+        def _():
+            out_ref[:, columns] = jnp.zeros((out_ref.shape[0], three), low)
+
+
+def weight_grad(turned, centers, sides, masks, slot_of, side_task, side_tasks, tasks):
+    three = 3 * centers[0].shape[1] // (2 * tasks)
+    items = tasks + len(side_tasks)
+    few = max(1, 2**24 // (turned.shape[1] * three * 2))
+    total = None
+    for start in range(0, items, few):
+        members = list(range(start, min(start + few, items)))
+        here = (slot_of >= start) & (slot_of < start + few)
+        slots = jnp.where(here, slot_of - start, -1)
+        part = some_weight_grad(
+            turned, centers, sides, masks, slots, side_task, side_tasks, tasks, members
+        )
+        total = part if total is None else total + part
+    return total
+
+
+def some_weight_grad(
+    turned, centers, sides, masks, slot_of, side_task, side_tasks, tasks, members
+):
+    depth, pixels = turned.shape
+    groups = len(masks)
     parts = slot_of.shape[0]
-    fixed = lambda g, s: (0, 0)
-    picked = lambda g, s: (0, jnp.maximum(s[g], 0))
+    three = 3 * centers[0].shape[1] // (2 * tasks)
+    items = len(members)
+    block = min(depth, 512)
+    fixed = lambda g, s, t: (0, 0)
     return pl.pallas_call(
-        weight_grad_kernel,
+        lambda *refs: weight_grad_kernel(members, side_tasks, tasks, groups, *refs),
         out_shape=jax.ShapeDtypeStruct((depth, parts * three), low),
         grid_spec=pltpu.PrefetchScalarGridSpec(
-            num_scalar_prefetch=1,
-            grid=(parts,),
-            in_specs=[
-                spec(x.shape, fixed),
-                spec(other.shape, fixed),
-                spec((pixels, three), picked),
-                spec((pixels, three), picked),
+            num_scalar_prefetch=2,
+            grid=(depth // block,),
+            in_specs=[spec((block, pixels), lambda g, s, t: (g, 0))]
+            + [spec(array.shape, fixed) for array in (*centers, *sides, *masks)],
+            out_specs=spec((block, parts * three), lambda g, s, t: (g, 0)),
+            scratch_shapes=[
+                pltpu.VMEM((pixels, items * three), low),
+                pltpu.VMEM((block, items * three), full),
             ],
-            out_specs=spec((depth, three), lambda g, s: (0, g)),
-            scratch_shapes=[pltpu.VMEM((depth, 2 * pixels), low)],
         ),
         compiler_params=params(),
         cost_estimate=cost(
-            4 * pixels * depth * dys.shape[1], 2 * depth * parts * three + 4 * pixels * dys.shape[1]
+            2 * pixels * depth * items * three, 2 * depth * (pixels + parts * three)
         ),
-    )(slot_of, x, other, dys, dys_other)
-
-
-def place_kernel(part_ref, core_ref, mine_ref, other_ref, out_ref):
+    )(slot_of, side_task, turned, *centers, *sides, *masks)
+
+
+def place_halves_kernel(core_ref, mine_ref, other_ref, out_ref):
+    parts, half, _ = mine_ref.shape
+    for i in range(parts):
+        for ref, which in ((mine_ref, core_ref[0]), (other_ref, 1 - core_ref[0])):
+            row = pl.multiple_of((2 * i + which) * half, half)
+            out_ref[pl.ds(row, half), :] = ref[i]
+
+
+def place_halves(mine, other, core, half):
+    parts, _, width = mine.shape
+    fixed = lambda i, c: (0, 0, 0)
+    return pl.pallas_call(
+        place_halves_kernel,
+        out_shape=jax.ShapeDtypeStruct((parts * 2 * half, width), low),
+        grid_spec=pltpu.PrefetchScalarGridSpec(
+            num_scalar_prefetch=1,
+            grid=(1,),
+            in_specs=[spec((parts, half, width), fixed)] * 2,
+            out_specs=spec((parts * 2 * half, width), lambda i, c: (0, 0)),
+        ),
+        compiler_params=params(),
+        cost_estimate=cost(0, 8 * parts * half * width),
+    )(core, mine, other)
+
+
+def place_block_kernel(
+    red_rows, mid_rows, exp_rows, ratio, core_ref, mine_ref, other_ref, mid_ref, exp_ref
+):
+    width = mid_ref.shape[0] // 3
+    for i in range(mine_ref.shape[0]):
+        for ref, which in ((mine_ref, core_ref[0]), (other_ref, 1 - core_ref[0])):
+            row = pl.multiple_of((2 * i + which) * mid_rows, mid_rows)
+            for tap in range(9):
+                ir, ic = divmod(tap, 3)
+                at = red_rows + tap * mid_rows
+                mid_ref[pl.ds(ir * width + row, mid_rows), ic * width : (ic + 1) * width] = ref[
+                    i, at : at + mid_rows
+                ]
+            row = pl.multiple_of((2 * i + which) * exp_rows, exp_rows)
+            for part in range(ratio):
+                at = red_rows + 9 * mid_rows + part * exp_rows
+                exp_ref[pl.ds(row, exp_rows), part * width : (part + 1) * width] = ref[
+                    i, at : at + exp_rows
+                ]
+
+
+def place_block(mine, other, core, red_rows, mid_rows, exp_rows, ratio):
+    width = mine.shape[2]
+    fixed = lambda i, c: (0, 0, 0)
+    flat = lambda i, c: (0, 0)
+    shapes = [(3 * width, 3 * width), (width, ratio * width)]
+    return pl.pallas_call(
+        lambda *refs: place_block_kernel(red_rows, mid_rows, exp_rows, ratio, *refs),
+        out_shape=[jax.ShapeDtypeStruct(shape, low) for shape in shapes],
+        grid_spec=pltpu.PrefetchScalarGridSpec(
+            num_scalar_prefetch=1,
+            grid=(1,),
+            in_specs=[spec(mine.shape, fixed)] * 2,
+            out_specs=[spec(shape, flat) for shape in shapes],
+        ),
+        compiler_params=params(),
+        cost_estimate=cost(0, 8 * mine.size),
+    )(core, mine, other)
+
+
+def place_kernel(chips, part_ref, at_ref, *refs):
     at = pl.program_id(0)
-    half = mine_ref.shape[0]
+    out_ref = refs[-1]
+    taps, _, head = out_ref.shape
+    share, lane = refs[0].shape[0], head // 2
 
     @pl.when(part_ref[at] >= 0)
     def _():
-        core = core_ref[0]
-        out_ref[0, pl.ds(pl.multiple_of(core * half, half), half), :] = mine_ref[...].astype(full)
-        out_ref[0, pl.ds(pl.multiple_of((1 - core) * half, half), half), :] = other_ref[
-            ...
-        ].astype(full)
+        for m in range(chips):
+            row = pl.multiple_of((at_ref[0] ^ m) * share, share)
+            for ref, core in ((refs[m], at_ref[1]), (refs[chips + m], 1 - at_ref[1])):
+                column = pl.multiple_of(core * lane, lane)
+                for k in range(taps):
+                    out_ref[k, pl.ds(row, share), pl.ds(column, lane)] = ref[
+                        :, k * lane : (k + 1) * lane
+                    ].astype(full)
 
     @pl.when(part_ref[at] < 0)
     def _():
         out_ref[...] = jnp.zeros_like(out_ref)
 
 
-def place_rows(mine, other, part_of, core, head):
-    half = mine.shape[0]
-    taps = part_of.shape[0]
+def place_shares(mine, other, part_of, at, head):
+    chips = len(mine)
+    share = mine[0].shape[0]
+    steps = part_of.shape[0]
     picked = lambda i, p, c: (0, jnp.maximum(p[i], 0))
     return pl.pallas_call(
-        place_kernel,
-        out_shape=jax.ShapeDtypeStruct((taps, 2 * half, head), full),
+        lambda *refs: place_kernel(chips, *refs),
+        out_shape=jax.ShapeDtypeStruct((3 * steps, chips * share, head), full),
         grid_spec=pltpu.PrefetchScalarGridSpec(
             num_scalar_prefetch=2,
-            grid=(taps,),
-            in_specs=[spec((half, head), picked), spec((half, head), picked)],
-            out_specs=spec((1, 2 * half, head), lambda i, p, c: (i, 0, 0)),
+            grid=(steps,),
+            in_specs=[spec((share, 3 * head // 2), picked)] * (2 * chips),
+            out_specs=spec((3, chips * share, head), lambda i, p, c: (i, 0, 0)),
         ),
         compiler_params=params(),
-        cost_estimate=cost(0, 12 * taps * half * head),
-    )(part_of, core, mine, other)
+        cost_estimate=cost(0, 36 * steps * chips * share * head // 2),
+    )(part_of, at, *mine, *other)
 
 
 def on_device(
@@ -547,22 +743,32 @@
     crops = float(crop_scale.shape[0])
 
     core = lax.axis_index("c")
+    core_at = core.reshape(1).astype(jnp.int32)
     ratio = depth // width
     red_rows, mid_rows, exp_rows = (w.shape[0] // 2 for w in (w_reduce, w_middle, w_expand))
+    red_own = half_of(w_reduce, 0, core)
     mid_own = half_of(w_middle.transpose(1, 0, 2), 1, core).reshape(9 * mid_rows, width)
     exp_own = half_of(w_expand, 0, core).reshape(exp_rows, ratio, width).transpose(1, 0, 2)
-    block_own = jnp.concatenate(
-        [half_of(w_reduce, 0, core), mid_own, exp_own.reshape(ratio * exp_rows, width)], axis=0
-    )
+    rest_own = jnp.concatenate([mid_own, exp_own.reshape(ratio * exp_rows, width)], axis=0)
+    block_own = jnp.concatenate([red_own, rest_own], axis=0)
+    source = features.reshape(pixels, depth) * valid.astype(low)
     block_mine = lax.all_gather(block_own, LINE, axis=0, tiled=False)
-    block_all = both_halves(block_mine, flip(block_mine, [("c", 1)]), core, 1)
-    cuts = np.cumsum([0, red_rows, 9 * mid_rows, ratio * exp_rows])
-    red_all, mid_all, exp_all = (block_all[:, :, cuts[i] : cuts[i + 1]] for i in range(3))
-    red_all = red_all.reshape(depth, width)
-    mid_all = mid_all.reshape(line, 2, 3, 3, mid_rows, width).transpose(2, 0, 1, 4, 3, 5)
-    mid_all = mid_all.reshape(3 * width, 3 * width)
-    exp_all = exp_all.reshape(line, 2, ratio, exp_rows, width).transpose(0, 1, 3, 2, 4)
-    exp_all = exp_all.reshape(width, depth)
+    block_mine, source = lax.optimization_barrier((block_mine, source))
+    block_other = flip(block_mine, [("c", 1)])
+    if mid_rows % 16 == 0 and red_rows % 16 == 0:
+        red_all = place_halves(block_mine, block_other, core_at, red_rows)
+        mid_all, exp_all = place_block(
+            block_mine, block_other, core_at, red_rows, mid_rows, exp_rows, ratio
+        )
+    else:
+        block_all = both_halves(block_mine, block_other, core, 1)
+        cuts = np.cumsum([0, red_rows, 9 * mid_rows, ratio * exp_rows])
+        red_all, mid_all, exp_all = (block_all[:, :, cuts[i] : cuts[i + 1]] for i in range(3))
+        red_all = red_all.reshape(depth, width)
+        mid_all = mid_all.reshape(line, 2, 3, 3, mid_rows, width).transpose(2, 0, 1, 4, 3, 5)
+        mid_all = mid_all.reshape(3 * width, 3 * width)
+        exp_all = exp_all.reshape(line, 2, ratio, exp_rows, width).transpose(0, 1, 3, 2, 4)
+        exp_all = exp_all.reshape(width, depth)
     terms, table = head_plan(rows)
     slots = table.shape[0]
     three = 3 * head
@@ -583,12 +789,11 @@
     all_tasks = jnp.concatenate([centers, side_task])
     all_picked = jnp.concatenate([centers, tasks + picked_term])
 
-    source = features.reshape(pixels, depth) * valid.astype(low)
     reduced = dot(source, red_all)
     mean1, scale1 = norm_scale(reduced, count)
     normed1 = (reduced - mean1) * scale1
     out1 = normed1 * gain_reduce + bias_reduce
-    hidden1 = (jax.nn.silu(out1) * valid).astype(low)
+    hidden1 = (silu(out1) * valid).astype(low)
     edge = mid_rate * cols
     down = [(i, i + 1) for i in range(line - 1)]
     up = [(i + 1, i) for i in range(line - 1)]
@@ -605,12 +810,28 @@
     mean2, scale2 = norm_scale(middled, count)
     normed2 = (middled - mean2) * scale2
     out2 = normed2 * gain_middle + bias_middle
-    hidden2 = (jax.nn.silu(out2) * valid).astype(low)
+    hidden2 = (silu(out2) * valid).astype(low)
     expanded = dot(hidden2, exp_all)
     mean3, scale3 = norm_scale(expanded, count)
     normed3 = (expanded - mean3) * scale3
     before = normed3 * gain_expand + bias_expand + source.astype(full)
-    grid = (jax.nn.silu(before) * valid).astype(low)
+    grid = (silu(before) * valid).astype(low)
+
+    chips = lax.axis_size("x")
+    chip = lax.axis_index("x")
+    share = own // chips
+
+    def share_columns(which):
+        cuts = [f * own + which * share for f in range(line)]
+        return jnp.concatenate(
+            [lax.dynamic_slice_in_dim(grid, cut, share, axis=1) for cut in cuts], axis=1
+        )
+
+    grid_pieces = []
+    for m in range(chips):
+        piece = share_columns(chip ^ m)
+        piece = flip(piece, [("x", m)]) if m else piece
+        grid_pieces += [piece, flip(piece, [("c", 1)])]
 
     def mask_table(group):
         inside = crop_table(crop_scale, crop_group, group, W_UNIT, cols)
@@ -623,17 +844,20 @@
         return jnp.tile(table, (rows, 1))
 
     masks = mask_table(group)
+    moves = row_moves(terms, line)
     side_terms = head_terms(grid, heads_all, masks, tasks + picked_term, side_task, head, low)
     moved = [None] * tasks
-    for e, (task, side, hop) in enumerate(terms):
-        pairs = [(f, f - side * hop) for f in range(line) if 0 <= f - side * hop < line]
-        using = [s for s in range(slots) if any(table[s, f] == e for f, _ in pairs)]
-        sent = side_terms[:, using[0] * head : (using[0] + 1) * head]
-        for s in using[1:]:
-            sent = jnp.where(picked_term[s] == e, side_terms[:, s * head : (s + 1) * head], sent)
+    for task, pairs, members in moves:
+        sends = {f: s for e, froms in members for f in froms for s in range(slots) if table[s, f] == e}
+        sent = None
+        for s in sorted(set(sends.values())):
+            part = side_terms[:, s * head : (s + 1) * head]
+            here = jnp.asarray(np.array([sends.get(f) == s for f in range(line)]))[place]
+            sent = part if sent is None else jnp.where(here, part, sent)
         got = rows_to(sent, pairs).astype(full)
         moved[task] = got if moved[task] is None else moved[task] + got
     middle_terms = head_terms(grid, heads_all, masks, centers, centers, head, full)
+    middle_terms, grid_pieces = lax.optimization_barrier((middle_terms, grid_pieces))
     mixed = []
     for task in range(tasks):
         center = middle_terms[:, task * head : (task + 1) * head]
@@ -643,7 +867,7 @@
     mean_h, scale_h = norm_scale(mixed, count)
     normed_h = (mixed - mean_h) * scale_h
     out_h = normed_h * gain_h + bias_h
-    activ = (jax.nn.silu(out_h) * valid).astype(low)
+    activ = (silu(out_h) * valid).astype(low)
     marks = labels.reshape(tasks, pixels)
     class_part, class_bias_part, dactiv = [], [], []
     for task in range(tasks):
@@ -660,44 +884,59 @@
     dmixed = valid * (gain_h * scale_h) * (dout_h - dbias_h / count - normed_h * (dgain_h / count))
     dmixed = dmixed.astype(low)
 
-    back = []
-    for task, side, hop in terms:
-        pairs = [(f, f + side * hop) for f in range(line) if 0 <= f + side * hop < line]
-        back.append(rows_to(dmixed[:, task * head : (task + 1) * head], pairs))
+    class_sums = jnp.concatenate(
+        [jnp.concatenate(class_part, axis=0), jnp.pad(jnp.stack(class_bias_part), ((0, 0), (0, head - classes)))],
+        axis=0,
+    )
+    class_sums = class_sums + flip(class_sums, [("c", 1)])
+    class_sums = sum_along(class_sums, "y")
+    lane = head // 2
+    tap_half = 3 * lane
+
+    def half_taps(grads, which):
+        cuts = [i * head + which * lane for i in range(grads.shape[1] // head)]
+        return jnp.concatenate(
+            [lax.dynamic_slice_in_dim(grads, cut, lane, axis=1) for cut in cuts], axis=1
+        )
+
+    def from_groups(grads):
+        halves = [half_taps(grads, core), flip(half_taps(grads, 1 - core), [("c", 1)])]
+        halves = jnp.concatenate(halves, axis=1)
+        return [halves] + [flip(halves, [("x", m)]) for m in range(1, chips)]
+
+    center_halves = from_groups(dmixed)
+    all_masks = [masks, mask_table(group ^ 1)]
+    for m in range(1, chips):
+        all_masks += [mask_table((chip ^ m) * 2 + core), mask_table((chip ^ m) * 2 + 1 - core)]
+    back = [None] * len(terms)
+    for task, pairs, members in moves:
+        got = rows_to(dmixed[:, task * head : (task + 1) * head], [(t, f) for f, t in pairs])
+        for e, froms in members:
+            here = jnp.asarray(np.array([f in froms for f in range(line)]))[place]
+            back[e] = got if len(members) == 1 else jnp.where(here, got, jnp.zeros_like(got))
     dsides = []
     for s in range(slots):
         dside = back[table[s][0]]
         for e in sorted(set(table[s].tolist()) - {int(table[s][0])}):
             dside = jnp.where(picked_term[s] == e, back[e], dside)
         dsides.append(dside)
-    dterms = jnp.concatenate([dmixed] + dsides, axis=1)
-    dys = spread_back(dterms, masks, all_tasks, head)
-    half = own // 2
-
-    def half_columns(which):
-        cuts = [f * own + which * half for f in range(line)]
-        return jnp.concatenate(
-            [lax.dynamic_slice_in_dim(grid, cut, half, axis=1) for cut in cuts], axis=1
-        )
-
-    grid_other = flip(half_columns(1 - core), [("c", 1)])
-    dterms_other = flip(dterms, [("c", 1)])
-    dys_other = spread_back(dterms_other, mask_table(group ^ 1), all_tasks, head)
-    slot_of = jnp.full((len(terms),), -1, jnp.int32)
-    for s in range(slots):
-        slot_of = jnp.where(jnp.arange(len(terms)) == picked_term[s], tasks + s, slot_of)
-    slot_of = jnp.concatenate([centers, slot_of])
-    core_at = core.reshape(1).astype(jnp.int32)
-    head_half = weight_grad(half_columns(core), grid_other, dys, dys_other, slot_of, three)
-    dys, head_half = lax.optimization_barrier((dys, head_half))
-    head_own, head_other = scatter_halves(head_half.reshape(line, half, len(parts) * three))
-
+    turned, dsides, center_halves, class_sums = lax.optimization_barrier(
+        (turn(grid_pieces), jnp.concatenate(dsides, axis=1), center_halves, class_sums)
+    )
+    class_sums = sum_along(class_sums, "z")
+    side_halves = from_groups(dsides)
+    dterms = jnp.concatenate([dmixed, dsides], axis=1)
+    dys = spread_back(dterms, masks, all_tasks, head, pixels)
     here = (side_task[:, None] == centers[None, :]).astype(full).reshape(-1)
     vec_rows = [mean3, scale3, gain_expand, bias_expand]
     vecs = jnp.pad(jnp.stack(vec_rows), ((0, 4), (0, 0)))
-    *shared_grads, sums = shared_back(
+    *shared_grads, slope3, normed3, sums = shared_back(
         dys, heads_all, all_picked, here, slot_tasks, tasks, expanded, source, vecs, masks, 256
     )
+    sums, center_halves, side_halves, class_sums = lax.optimization_barrier(
+        (sums, center_halves, side_halves, class_sums)
+    )
+    class_sums = sum_along(class_sums, "x")
     gram_part = jnp.sum(sums[2 * tasks : 4 * tasks], axis=1)
     gram_row = jnp.pad(gram_part, (0, depth - gram_part.shape[0]))[None, :]
     summed = all_sum(jnp.concatenate([sums[: 2 * tasks], gram_row], axis=0))
@@ -705,14 +944,25 @@
     weight_list = task_scales([summed[2 * tasks, i] for i in range(6)])
     task_weights = jnp.stack(weight_list)
 
+    slot_of = jnp.full((len(terms),), -1, jnp.int32)
+    for s in range(slots):
+        slot_of = jnp.where(jnp.arange(len(terms)) == picked_term[s], tasks + s, slot_of)
+    slot_of = jnp.concatenate([centers, slot_of])
+    head_part = weight_grad(
+        turned, center_halves, side_halves, all_masks, slot_of, side_task, slot_tasks, tasks
+    )
+    shared_grads, head_part = lax.optimization_barrier((shared_grads, head_part))
+    head_part = head_part.reshape(line, share, len(parts) * tap_half)
+    head_own = lax.psum_scatter(head_part, LINE, scatter_dimension=0, tiled=False)
+
     dgain3, dbias3 = (
         sum(weight_list[t] * sums3[t, j] for t in range(tasks)) for j in range(2)
     )
-    vec_rows += [dgain3 / count, dbias3 / count, gain_expand * scale3]
-    vecs = jnp.pad(jnp.stack(vec_rows), ((0, 1), (0, 0)))
+    vec_rows = [gain_expand * scale3, jnp.broadcast_to(1.0 / count, (depth,))]
+    vecs = jnp.pad(jnp.stack(vec_rows), ((0, 6), (0, 0)))
     mid_vecs = jnp.pad(jnp.stack([mean2, scale2, gain_middle, bias_middle]), ((0, 4), (0, 0)))
     dbefore, exp_part, dout2, sums2 = expand_back(
-        task_weights, shared_grads, expanded, source, vecs, masks, hidden2, exp_all, middled,
+        summed, shared_grads, slope3, normed3, vecs, masks, hidden2, exp_all, middled,
         mid_vecs, 256,
     )
     sums2 = all_sum(sums2[:2])
@@ -728,6 +978,21 @@
     dwide = dot_nt(dspread, mid_all)
     from_below = rows_to(dwide[:edge, :width].astype(low), up).astype(full)
     from_above = rows_to(dwide[pixels - edge :, 2 * width :].astype(low), down).astype(full)
+    dspread, exp_part, dwide = lax.optimization_barrier((dspread, exp_part, dwide))
+    mid_part = dot_tn(wide1, dspread).astype(low).reshape(3, line, 2, mid_rows, 3 * width)
+    exp_part = exp_part.reshape(line, 2, exp_rows, depth)
+
+    def later_half(which):
+        mid_half = lax.dynamic_index_in_dim(mid_part, which, 2, keepdims=False)
+        exp_half = lax.dynamic_index_in_dim(exp_part, which, 1, keepdims=False)
+        pieces = [
+            mid_half[i, :, :, k * width : (k + 1) * width] for i in range(3) for k in range(3)
+        ]
+        pieces += [exp_half[:, :, k * width : (k + 1) * width] for k in range(ratio)]
+        return jnp.concatenate(pieces, axis=1)
+
+    later_other = flip(later_half(1 - core), [("c", 1)])
+    later = (later_half(core).astype(full) + later_other.astype(full)).astype(low)
     dhidden1 = (
         dwide[:, width : 2 * width]
         + jnp.concatenate([dwide[edge:, :width], from_below], axis=0)
@@ -735,43 +1000,41 @@
     )
     dout1 = dhidden1 * valid * silu_slope(out1)
     sums1 = all_sum(jnp.stack([jnp.sum(dout1 * normed1, axis=0), jnp.sum(dout1, axis=0)]))
+    sums1, later = lax.optimization_barrier((sums1, later))
+    cut = later.shape[1] // 2
+    later_own = jnp.concatenate(
+        [scatter_z(scatter_y(piece)) for piece in (later[:, :cut], later[:, cut:])], axis=0
+    )
     dgain1, dbias1 = sums1[0], sums1[1]
-    class_sums = jnp.concatenate(
-        [jnp.concatenate(class_part, axis=0), jnp.pad(jnp.stack(class_bias_part), ((0, 0), (0, head - classes)))],
-        axis=0,
-    )
-    class_sums, sums1 = lax.optimization_barrier((class_sums, sums1))
-    class_sums = all_sum(class_sums)
+    dreduced = valid * (gain_reduce * scale1) * (
+        dout1 - dbias1 / count - normed1 * (dgain1 / count)
+    )
+    dreduced = dreduced.astype(low)
+    dfeatures = dbefore.astype(full) + dot_nt(dreduced, red_all)
+
+    red_part = dot_tn(source, dreduced).astype(low).reshape(line, -1, width)
+    red_sum = over_groups(scatter_z(scatter_y(between_cores(red_part))))
+    red_sum = both_halves(*red_sum, core, 0).astype(full)
+    part_of = np.full((tasks, 3), -1, np.int32)
+    part_of[:, 1] = np.arange(tasks)
+    for e, (task, side, _) in enumerate(terms):
+        part_of[task, side + 1] = tasks + e
+    head_shares = [head_own] + [flip(head_own, [("x", m)]) for m in range(1, chips)]
+    head_others = [flip(part, [("c", 1)]) for part in head_shares]
+    at = jnp.stack([chip, core]).astype(jnp.int32)
+    heads_out = place_shares(head_shares, head_others, jnp.asarray(part_of.reshape(-1)), at, head)
+    heads_out = heads_out.reshape(tasks, 9, own, head).transpose(2, 0, 1, 3)
+    later_own, later_other = over_groups(later_own)
+    later_sum = both_halves(
+        later_own.reshape(9 + ratio, mid_rows, width),
+        later_other.reshape(9 + ratio, mid_rows, width),
+        core,
+        1,
+    ).reshape(9 + ratio, 2 * mid_rows, width)
+    mid_sum = later_sum[:9].transpose(1, 0, 2).astype(full)
+    exp_sum = later_sum[9:].transpose(1, 0, 2).reshape(2 * exp_rows, depth).astype(full)
     grad_class = class_sums[: tasks * classes].reshape(tasks, classes, head).transpose(0, 2, 1)
     grad_class_bias = class_sums[tasks * classes :, :classes]
-    dreduced = valid * (gain_reduce * scale1) * (
-        dout1 - dbias1 / count - normed1 * (dgain1 / count)
-    )
-    dreduced = dreduced.astype(low)
-    dfeatures = dbefore.astype(full) + dot_nt(dreduced, red_all)
-
-    mid_part = dot_tn(wide1, dspread).astype(low).reshape(3, line, -1, 3, width)
-    mid_part = mid_part.transpose(1, 2, 0, 3, 4).reshape(line, 2 * mid_rows, 9, width)
-    exp_part = exp_part.reshape(line, 2 * exp_rows, ratio, width)
-    later = jnp.concatenate([mid_part.reshape(line, 2 * mid_rows, -1, width), exp_part], axis=2)
-    later = between_cores(later)
-    wide_rows = 9 + ratio
-    later_own, later_other = scatter_halves(later.reshape(line, mid_rows * wide_rows, width))
-    later_sum = both_halves(later_own, later_other, core, 0).astype(full)
-    later_sum = later_sum.reshape(2 * mid_rows, wide_rows, width)
-    mid_sum = later_sum[:, :9]
-    exp_sum = later_sum[:, 9:].reshape(2 * exp_rows, depth)
-    red_part = dot_tn(source, dreduced).astype(low).reshape(line, -1, width)
-    red_sum = both_halves(*scatter_few(between_cores(red_part)), core, 0).astype(full)
-    part_of = np.full((tasks, 3, 3), -1, np.int32)
-    for task in range(tasks):
-        part_of[task, 1] = 3 * task + np.arange(3)
-    for e, (task, side, _) in enumerate(terms):
-        part_of[task, side + 1] = 3 * (tasks + e) + np.arange(3)
-    heads_out = place_rows(
-        head_own, head_other, jnp.asarray(part_of.reshape(-1)), core_at, head
-    )
-    heads_out = heads_out.reshape(tasks, 9, own, head).transpose(2, 0, 1, 3)
     return (
         dfeatures.reshape(1, rows, cols, depth),
         red_sum.reshape(w_reduce.shape),

time: 757 us -> 701 us (0.926)
  local copies, waits for them, and re-layouts: 81.8 us -> 43.5 us
  other arithmetic: 60.3 us -> 50.2 us
    ppermute x74 -> x90, waiting for transfers between devices: 111 us -> 183 us  [flip(): return lax.ppermute(value, names, pairs)]
    reduce_scatter x2 -> x1, waiting for transfers between devices: 33.8 us -> 0.02 us  [on_device(): lax.psum_scatter(head_part, LINE, scatter_dimension=0, tiled=False)]
    all_gather x1, waiting for transfers between devices: 32.7 us -> 0.01 us  [on_device(): heads_all = lax.all_gather(heads_own, AXES, axis=0, tiled=True)]
    reshape x5 -> x0, local copies, waits for them, and re-layouts: 29 us -> none  [the longest x1 12.3 us: on_device(): mid_part = dot_tn(wide1, dspread).astype(low).reshape(3, line, -1, 3, width)]
    another operation x6 -> x4, other arithmetic: 10.6 us -> 0.14 us  [both_halves(): return jnp.stack([first, second], axis=axis)]
    transpose x2 -> x0, local copies, waits for them, and re-layouts: 8.32 us -> none  [the longest x1 4.33 us: on_device(): mid_part.transpose(1, 2, 0, 3, 4).reshape(line, 2 * mid_rows, 9, width)]
    pallas_call x4 -> x6, Pallas kernels: 50.9 us -> 55.7 us  [the longest x1 24.9 us: some_weight_grad(): pl.pallas_call(lambda *refs: weight_grad_kernel(members, side_tasks, task...]
    unnamed x121 -> x163, local copies, waits for them, and re-layouts: 23.9 us -> 20.6 us
  transfers between devices with their start and end apart: 91 -> 103, of which waited for: 57 -> 56; matrix products, arithmetic and copies ran while one was open for 21% -> 15% of each run, Pallas kernels for 9% -> 14%
where the time goes in v3:
time: 701 us; the launch traced here: 694 us
  waiting for transfers between devices  286 us (41%)
  starting transfers between devices  133 us (19%)
  Pallas kernels  124 us (18%)
  other arithmetic  50.2 us (7%)
  local copies, waits for them, and re-layouts  43.5 us (6%)
  matrix products  31.7 us (5%)
  between operations  25.2 us (4%)
    ppermute x90, waiting for transfers between devices, flip(): return lax.ppermute(value, names, pairs)  183 us
    ppermute x90, starting transfers between devices, flip(): return lax.ppermute(value, names, pairs)  101 us
    all_gather x1, waiting for transfers between devices, on_device(): block_mine = lax.all_gather(block_own, LINE, axis=0, tiled=False)  64.1 us
    ppermute x10, waiting for transfers between devices, rows_to(): return lax.ppermute(value, LINE, pairs)  38.6 us
    ppermute x10, starting transfers between devices, rows_to(): return lax.ppermute(value, LINE, pairs)  32.4 us
    pallas_call x1, Pallas kernels, shared_back(): pl.pallas_call(lambda *refs: shared_back_kernel(tasks, side_tasks, *refs)...  26 us
    pallas_call x1, Pallas kernels, some_weight_grad(): pl.pallas_call(lambda *refs: weight_grad_kernel(members, side_tasks, task...  24.9 us
    pallas_call x2, Pallas kernels, head_terms(): pl.pallas_call(terms_kernel, out_shape=jax.ShapeDtypeStruct((pixels, item...  22.7 us
  transfers between devices with their start and end apart: 103, of which 56 were waited for; matrix products, arithmetic and copies ran while one was open for 15% of the time, Pallas kernels for 14%

profile of v3, /device:TPU:0, one launch (start us, length us, event | category | flops | bytes accessed | tf_op | source)
XLA Modules:
  0.0 693.9 jit_solution(5642338310883284819)
XLA Ops:
  12.6 5.7 copy.106
  21.9 4.1 bitcast_multiply_fusion.refs_9_
  26.1 64.1 %all-gather.6.cloned.1.call-done = bf16[4352,512]{1,0:T(8,128)(2,1)} async-done(((bf16[544,512]{1,0:T(8,128)(2,1)}), bf16[4352,512]{1,0:T(8,128)(2,1)}) %all-gather.6.cloned.1.call-update) | async-done | bytes 4456464 | tf_op jit(solution)/shard_map/all_gather | solution.py:755
  90.3 7.7 %collective-permute-done.other_ref.refs_2_ = bf16[8,544,512]{2,1,0:T(8,128)(2,1)S(1)} collective-permute-done((bf16[8,544,512]{2,1,0:T(8,128)(2,1)}, bf16[8,544,512]{2,1,0:T(8,128)(2,1)S(1)}, u32[]{:S(2)}, u32[]{:S(2)}) %collective-permute-start) | collective-permute-done | bytes 4456480 | tf_op jit(solution)/shard_map/ppermute | solution.py:37
  100.2 3.3 shard_map.351
  103.4 3.4 fusion.100
  123.3 5.4 collective-permute-start.8
  128.9 6.8 shard_map.352
  135.7 5.6 collective-permute-done.9
  141.3 8.7 %collective-permute-done.8 = bf16[384,512]{1,0:T(8,128)(2,1)} collective-permute-done((bf16[384,512]{1,0:T(8,128)(2,1)S(1)}, bf16[384,512]{1,0:T(8,128)(2,1)}, u32[]{:S(2)}, u32[]{:S(2)}) %collective-permute-start.8) | collective-permute-done | bytes 393248 | tf_op jit(solution)/shard_map/ppermute | solution.py:71
  150.0 6.4 fusion.51
  171.3 3.4 collective-permute-done.16
  175.4 4.5 fusion.98
  195.9 5.3 multiply_convert_fusion.x_ref
  212.7 33.8 %collective-permute-done.25.refs_2_ = bf16[768,1024]{1,0:T(8,128)(2,1)} collective-permute-done((bf16[768,1024]{1,0:T(8,128)(2,1)}, bf16[768,1024]{1,0:T(8,128)(2,1)}, u32[]{:S(2)}, u32[]{:S(2)}) %collective-permute-start.25) | collective-permute-done | bytes 1572896 | tf_op jit(solution)/shard_map/ppermute | solution.py:37
  247.4 10.0 %shard_map.354 = bf16[768,512]{1,0:T(8,128)(2,1)} custom-call(s32[2]{0:T(128)} %get-tuple-element.257.picked_ref, s32[2]{0:T(128)} %gather_fusion, bf16[768,2048]{1,0:T(8,128)(2,1)} %copy-done.3, bf16[2048,5376]{1,0:T(8,128)(2,1)} %all-gather.4.cloned.1.call-done.w_ref.refs_3_.refs_4_.refs_5_.refs_6_.refs_7_, f32[768,128]{1,0:T(8,128)} %bitcast.343), custom_call_target="tpu_custom_call" | custom-call | flops 4831838208 | bytes 9437184 | tf_op jit(solution)/shard_map/pallas_call | solution.py:255
  260.5 5.5 collective-permute-start.27
  266.0 3.1 collective-permute-start.29
  269.6 12.7 %shard_map.353 = f32[768,768]{1,0:T(8,128)} custom-call(s32[3]{0:T(128)} %iota.36.picked_ref.task_ref, s32[3]{0:T(128)} %iota.36.picked_ref.task_ref, bf16[768,2048]{1,0:T(8,128)(2,1)} %copy-done.3, bf16[2048,5376]{1,0:T(8,128)(2,1)} %all-gather.4.cloned.1.call-done.w_ref.refs_3_.refs_4_.refs_5_.refs_6_.refs_7_, f32[768,128]{1,0:T(8,128)} %bitcast.344), custom_call_target="tpu_custom_call" | custom-call | flops 7247757312 | bytes 12582912 | tf_op jit(solution)/shard_map/pallas_call | solution.py:255
  282.6 7.7 %collective-permute-done.29 = bf16[768,256]{1,0:T(8,128)(2,1)S(1)} collective-permute-done((bf16[768,256]{1,0:T(8,128)(2,1)S(1)}, bf16[768,256]{1,0:T(8,128)(2,1)S(1)}, u32[]{:S(2)}, u32[]{:S(2)}) %collective-permute-start.29) | collective-permute-done | bytes 393248 | tf_op jit(solution)/shard_map/ppermute | solution.py:71
  294.5 3.3 collective-permute-start.33
  301.5 5.0 collective-permute-start.36
  313.1 3.3 multiply_reduce_fusion.1
  329.4 2.8 collective-permute-done.43
  342.1 8.2 %collective-permute-start.46 = (bf16[768,256]{1,0:T(8,128)(2,1)S(1)}, bf16[768,256]{1,0:T(8,128)(2,1)S(1)}, u32[]{:S(2)}, u32[]{:S(2)}) collective-permute-start(bf16[768,256]{1,0:T(8,128)(2,1)S(1)} %get-tuple-element.207), channel_id=1, source_target_pairs={{24,0},{28,4},{0,24},{4,28},{25,1},{29,5},{1,25},{5,29},{26,2},{30... | collective-permute-start | bytes 1179656 | tf_op jit(solution)/shard_map/ppermute | solution.py:71
  356.7 5.5 shard_map.355.refs_2_
  362.2 6.6 collective-permute-done.46
  372.8 6.4 shard_map.356.refs_2_
  379.3 4.2 collective-permute-start.54
  385.1 26.0 %shard_map.357 = (bf16[768,2048]{1,0:T(8,128)(2,1)}, bf16[768,2048]{1,0:T(8,128)(2,1)}, bf16[768,2048]{1,0:T(8,128)(2,1)}, bf16[768,2048]{1,0:T(8,128)(2,1)}, bf...) custom-call(s32[5]{0:T(128)} %get-tuple-element.278.refs_0_, f32[6]{0:T(128)} %reshape.408.refs_1_, ...), custom_call_target="tpu_custom_call" | custom-call | flops 12079595520 | bytes 34603008 | tf_op jit(solution)/shard_map/pallas_call | solution.py:359
  421.8 3.0 collective-permute-start.60
  428.9 24.9 %shard_map.358 = bf16[1024,2688]{1,0:T(8,128)(2,1)} custom-call(s32[7]{0:T(128)} %and_select_fusion.refs_0_, s32[2]{0:T(128)} %gather_fusion, bf16[1024,3072]{1,0:T(8,128)(2,1)} %shard_map.355.refs_2_, bf16[768,768]{1,0:T(8,128)(2,1)} %copy-done.22, bf16[768,768]{1,0:T(8,128)(2,1)} %collective-permute-done.48.refs_4_, bf16[768,512]{1,0:T(8,128)(2,1)} %copy-done.25, ...), custom_call_target="tpu_custom_call" | custom-call | flops 12079595520 | bytes 11796480 | tf_op jit(solution)/shard_map/pallas_call | solution.py:577
  454.5 19.6 %shard_map.359 = (bf16[768,2048]{1,0:T(8,128)(2,1)}, bf16[512,2048]{1,0:T(8,128)(2,1)}, f32[768,512]{1,0:T(8,128)}, f32[8,512]{1,0:T(8,128)}) custom-call(f32[7,2048]{1,0:T(8,128)} %add_add_fusion.1.refs_0_.refs_4_, bf16[768,2048]{1,0:T(8,128)(2,1)} %get-tuple-element.80.refs_1_, bf16[768,2048]{1,0:T(8,128)(2,1)} %get-tuple-element.81.refs_2_, ...), custom_call_target="tpu_custom_call" | custom-call | flops 1572864 | bytes 10752 | tf_op jit(solution)/shard_map/pallas_call | solution.py:442
  498.3 3.8 fusion.122
  506.5 5.0 convolution_convert_fusion
  514.5 5.9 collective-permute-done.70
  520.5 3.9 collective-permute-done.69
  527.8 11.6 %collective-permute-start.74 = (f32[2,512]{1,0:T(2,128)S(1)}, f32[2,512]{1,0:T(2,128)S(1)}, u32[]{:S(2)}, u32[]{:S(2)}) collective-permute-start(f32[2,512]{1,0:T(2,128)S(1)} %fusion.86), channel_id=1, source_target_pairs={{0,6},{2,4},{4,2},{6,0},{1,7},{3,5},{5,3},{7,1},{8,14},{10,12},{12... | collective-permute-start | bytes 12296 | tf_op jit(solution)/shard_map/ppermute | solution.py:37
  558.0 20.9 %collective-permute-done.90 = bf16[4,208,512]{2,1,0:T(8,128)(2,1)S(1)} collective-permute-done((bf16[4,208,512]{2,1,0:T(8,128)(2,1)S(1)}, bf16[4,208,512]{2,1,0:T(8,128)(2,1)S(1)}, u32[]{:S(2)}, u32[]{:S(2)}) %collective-permute-start.90) | collective-permute-done | bytes 852000 | tf_op jit(solution)/shard_map/ppermute | solution.py:37
  583.7 19.2 %collective-permute-done.86 = bf16[4,208,512]{2,1,0:T(8,128)(2,1)S(1)} collective-permute-done((bf16[4,208,512]{2,1,0:T(8,128)(2,1)S(1)}, bf16[4,208,512]{2,1,0:T(8,128)(2,1)S(1)}, u32[]{:S(2)}, u32[]{:S(2)}) %collective-permute-start.86) | collective-permute-done | bytes 852000 | tf_op jit(solution)/shard_map/ppermute | solution.py:37
  608.1 20.0 %collective-permute-done.92 = bf16[208,512]{1,0:T(8,128)(2,1)S(1)} collective-permute-done((bf16[208,512]{1,0:T(8,128)(2,1)S(1)}, bf16[208,512]{1,0:T(8,128)(2,1)S(1)}, u32[]{:S(2)}, u32[]{:S(2)}) %collective-permute-start.92) | collective-permute-done | bytes 213024 | tf_op jit(solution)/shard_map/ppermute | solution.py:37
  629.7 7.1 %collective-permute-done.88 = bf16[208,512]{1,0:T(8,128)(2,1)S(1)} collective-permute-done((bf16[208,512]{1,0:T(8,128)(2,1)S(1)}, bf16[208,512]{1,0:T(8,128)(2,1)S(1)}, u32[]{:S(2)}, u32[]{:S(2)}) %collective-permute-start.88) | collective-permute-done | bytes 213024 | tf_op jit(solution)/shard_map/ppermute | solution.py:37
  640.3 3.0 collective-permute-start.81
  643.3 3.0 collective-permute-done.94
  646.5 3.8 collective-permute-done.82
  651.5 4.6 convert_add_fusion
  658.8 15.5 %collective-permute-done.96.refs_3_ = bf16[128,2688]{1,0:T(8,128)(2,1)S(1)} collective-permute-done((bf16[128,2688]{1,0:T(8,128)(2,1)}, bf16[128,2688]{1,0:T(8,128)(2,1)S(1)}, u32[]{:S(2)}, u32[]{:S(2)}) %collective-permute-start.96) | collective-permute-done | bytes 688160 | tf_op jit(solution)/shard_map/ppermute | solution.py:37
  678.0 8.8 %shard_map.360 = f32[27,256,256]{2,1,0:T(8,128)} custom-call(s32[9]{0:T(128)} %constant.244.clone.refs_0_, s32[2]{0:T(128)} %pad_add_fusion.2.refs_1_, bf16[128,2688]{1,0:T(8,128)(2,1)} %bitcast.369, bf16[128,2688]{1,0:T(8,128)(2,1)} %copy-done.27, bf16[128,2688]{1,0:T(8,128)(2,1)} %copy-done.28, bf16[128,2688]{1,0:T(8,128)(2,1)} %copy-done.29), custom_call_target="tpu_custom_call" | custom-call | bytes 10616832 | tf_op jit(solution)/shard_map/pallas_call | solution.py:690
  (565 shorter events, 206.4 us)
Async XLA Ops:
  7.2 83.0 %all-gather.6.cloned.1.call-start = ((), (), s32[]{:S(2)}) async-start(), calls=%async_computation.3 | async-start | bytes 5013504 | tf_op jit(solution)/shard_map/all_gather | solution.py:755
  10.2 236.4 %all-gather.4.cloned.1.call-start = ((), (), s32[]{:S(2)}) async-start(), calls=%async_computation.1 | async-start | bytes 22708224 | tf_op jit(solution)/shard_map/all_gather | solution.py:783
  90.2 566.0 %reduce-scatter.2.cloned.1.call-start = ((), (), s32[]{:S(2)}) async-start(), calls=%async_computation.2 | async-start | bytes 6193152 | tf_op jit(solution)/shard_map/reduce_scatter | solution.py:956
  90.3 7.8 %collective-permute-start = (bf16[8,544,512]{2,1,0:T(8,128)(2,1)}, bf16[8,544,512]{2,1,0:T(8,128)(2,1)S(1)}, u32[]{:S(2)}, u32[]{:S(2)}) collective-permute-start(bf16[8,544,512]{2,1,0:T(8,128)(2,1)} %bitcast.340), channel_id=1, source_target_pairs={{0,1},{1,0},{2,3},{3,2},{4,5},{5,4},{6,7},{7,6},{8,9},{9,8},{10,11... | collective-permute-start | bytes 13369352 | tf_op jit(solution)/shard_map/ppermute | solution.py:37
  122.0 19.3 %collective-permute-start.9 = (bf16[384,512]{1,0:T(8,128)(2,1)S(1)}, bf16[384,512]{1,0:T(8,128)(2,1)}, u32[]{:S(2)}, u32[]{:S(2)}) collective-permute-start(bf16[384,512]{1,0:T(8,128)(2,1)S(1)} %get-tuple-element.227), channel_id=1, source_target_pairs={{4,0},{8,4},{12,8},{16,12},{20,16},{24,20},{28,24},{5,1},{9,5},{13... | collective-permute-start | bytes 1179656 | tf_op jit(solution)/shard_map/ppermute | solution.py:71
  123.3 26.7 %collective-permute-start.8 = (bf16[384,512]{1,0:T(8,128)(2,1)S(1)}, bf16[384,512]{1,0:T(8,128)(2,1)}, u32[]{:S(2)}, u32[]{:S(2)}) collective-permute-start(bf16[384,512]{1,0:T(8,128)(2,1)S(1)} %get-tuple-element.226), channel_id=1, source_target_pairs={{0,4},{4,8},{8,12},{12,16},{16,20},{20,24},{24,28},{1,5},{5,9},{9,... | collective-permute-start | bytes 1179656 | tf_op jit(solution)/shard_map/ppermute | solution.py:71
  208.0 38.6 %collective-permute-start.25 = (bf16[768,1024]{1,0:T(8,128)(2,1)}, bf16[768,1024]{1,0:T(8,128)(2,1)}, u32[]{:S(2)}, u32[]{:S(2)}) collective-permute-start(bf16[768,1024]{1,0:T(8,128)(2,1)} %get-tuple-element.178), channel_id=1, source_target_pairs={{0,2},{2,0},{1,3},{3,1},{4,6},{6,4},{5,7},{7,5},{8,10},{10,8},{9,1... | collective-permute-start | bytes 4718600 | tf_op jit(solution)/shard_map/ppermute | solution.py:37
  212.6 69.7 %collective-permute-start.24 = (bf16[768,1024]{1,0:T(8,128)(2,1)S(1)}, bf16[768,1024]{1,0:T(8,128)(2,1)}, u32[]{:S(2)}, u32[]{:S(2)}) collective-permute-start(bf16[768,1024]{1,0:T(8,128)(2,1)S(1)} %get-tuple-element.62.refs_0_), channel_id=1, source_target_pairs={{0,1},{1,0},{2,3},{3,2},{4,5},{5,4},{6,7},{7,6},{8,9},{9,8},{10,11... | collective-permute-start | bytes 4718600 | tf_op jit(solution)/shard_map/ppermute | solution.py:37
  246.5 35.8 %collective-permute-start.26 = (bf16[768,1024]{1,0:T(8,128)(2,1)}, bf16[768,1024]{1,0:T(8,128)(2,1)}, u32[]{:S(2)}, u32[]{:S(2)}) collective-permute-start(bf16[768,1024]{1,0:T(8,128)(2,1)} %collective-permute-done.25.refs_2_), channel_id=1, source_target_pairs={{0,1},{1,0},{2,3},{3,2},{4,5},{5,4},{6,7},{7,6},{8,9},{9,8},{10,11... | collective-permute-start | bytes 4718600 | tf_op jit(solution)/shard_map/ppermute | solution.py:37
  259.2 23.2 %collective-permute-start.28 = (bf16[768,256]{1,0:T(8,128)(2,1)S(1)}, bf16[768,256]{1,0:T(8,128)(2,1)S(1)}, u32[]{:S(2)}, u32[]{:S(2)}) collective-permute-start(bf16[768,256]{1,0:T(8,128)(2,1)S(1)} %get-tuple-element.224), channel_id=1, source_target_pairs={{12,0},{16,4},{20,8},{24,12},{28,16},{13,1},{17,5},{21,9},{25,13},... | collective-permute-start | bytes 1179656 | tf_op jit(solution)/shard_map/ppermute | solution.py:71
  260.5 22.1 %collective-permute-start.27 = (bf16[768,256]{1,0:T(8,128)(2,1)S(1)}, bf16[768,256]{1,0:T(8,128)(2,1)S(1)}, u32[]{:S(2)}, u32[]{:S(2)}) collective-permute-start(bf16[768,256]{1,0:T(8,128)(2,1)S(1)} %get-tuple-element.223), channel_id=1, source_target_pairs={{0,12},{4,16},{8,20},{12,24},{16,28},{1,13},{5,17},{9,21},{13,25},... | collective-permute-start | bytes 1179656 | tf_op jit(solution)/shard_map/ppermute | solution.py:71
  266.0 24.4 %collective-permute-start.29 = (bf16[768,256]{1,0:T(8,128)(2,1)S(1)}, bf16[768,256]{1,0:T(8,128)(2,1)S(1)}, u32[]{:S(2)}, u32[]{:S(2)}) collective-permute-start(bf16[768,256]{1,0:T(8,128)(2,1)S(1)} %get-tuple-element.225), channel_id=1, source_target_pairs={{0,24},{4,28},{24,0},{28,4},{1,25},{5,29},{25,1},{29,5},{2,26},{6,... | collective-permute-start | bytes 1179656 | tf_op jit(solution)/shard_map/ppermute | solution.py:71
  337.2 33.1 %collective-permute-start.48 = (bf16[768,768]{1,0:T(8,128)(2,1)S(1)}, bf16[768,768]{1,0:T(8,128)(2,1)}, u32[]{:S(2)}, u32[]{:S(2)}) collective-permute-start(bf16[768,768]{1,0:T(8,128)(2,1)S(1)} %pad_maximum_fusion.5.refs_3_), channel_id=1, source_target_pairs={{0,2},{2,0},{1,3},{3,1},{4,6},{6,4},{5,7},{7,5},{8,10},{10,8},{9,1... | collective-permute-start | bytes 3538952 | tf_op jit(solution)/shard_map/ppermute | solution.py:37
  337.8 18.1 %collective-permute-start.49 = (f32[66,256]{1,0:T(8,128)S(1)}, f32[66,256]{1,0:T(8,128)S(1)}, u32[]{:S(2)}, u32[]{:S(2)}) collective-permute-start(f32[66,256]{1,0:T(8,128)S(1)} %pad_maximum_fusion.14), channel_id=1, source_target_pairs={{0,1},{1,0},{2,3},{3,2},{4,5},{5,4},{6,7},{7,6},{8,9},{9,8},{10,11... | collective-permute-start | bytes 202760 | tf_op jit(solution)/shard_map/ppermute | solution.py:37
  338.7 23.5 %collective-permute-start.44 = (bf16[768,256]{1,0:T(8,128)(2,1)}, bf16[768,256]{1,0:T(8,128)(2,1)S(1)}, u32[]{:S(2)}, u32[]{:S(2)}) collective-permute-start(bf16[768,256]{1,0:T(8,128)(2,1)} %get-tuple-element.208), channel_id=1, source_target_pairs={{0,12},{4,16},{8,20},{12,24},{16,28},{1,13},{5,17},{9,21},{13,25},... | collective-permute-start | bytes 1179656 | tf_op jit(solution)/shard_map/ppermute | solution.py:71
  340.8 21.4 %collective-permute-start.45 = (bf16[768,256]{1,0:T(8,128)(2,1)}, bf16[768,256]{1,0:T(8,128)(2,1)S(1)}, u32[]{:S(2)}, u32[]{:S(2)}) collective-permute-start(bf16[768,256]{1,0:T(8,128)(2,1)} %get-tuple-element.208), channel_id=1, source_target_pairs={{12,0},{16,4},{20,8},{24,12},{28,16},{13,1},{17,5},{21,9},{25,13},... | collective-permute-start | bytes 1179656 | tf_op jit(solution)/shard_map/ppermute | solution.py:71
  342.1 26.7 %collective-permute-start.46 = (bf16[768,256]{1,0:T(8,128)(2,1)S(1)}, bf16[768,256]{1,0:T(8,128)(2,1)S(1)}, u32[]{:S(2)}, u32[]{:S(2)}) collective-permute-start(bf16[768,256]{1,0:T(8,128)(2,1)S(1)} %get-tuple-element.207), channel_id=1, source_target_pairs={{24,0},{28,4},{0,24},{4,28},{25,1},{29,5},{1,25},{5,29},{26,2},{30... | collective-permute-start | bytes 1179656 | tf_op jit(solution)/shard_map/ppermute | solution.py:71
  370.4 13.1 %collective-permute-start.51 = (bf16[768,256]{1,0:T(8,128)(2,1)S(1)}, bf16[768,256]{1,0:T(8,128)(2,1)S(1)}, u32[]{:S(2)}, u32[]{:S(2)}) collective-permute-start(bf16[768,256]{1,0:T(8,128)(2,1)S(1)} %pad_maximum_fusion.11), channel_id=1, source_target_pairs={{0,1},{1,0},{2,3},{3,2},{4,5},{5,4},{6,7},{7,6},{8,9},{9,8},{10,11... | collective-permute-start | bytes 1179656 | tf_op jit(solution)/shard_map/ppermute | solution.py:37
  371.2 8.1 %collective-permute-start.53 = (f32[66,256]{1,0:T(8,128)S(1)}, f32[66,256]{1,0:T(8,128)S(1)}, u32[]{:S(2)}, u32[]{:S(2)}) collective-permute-start(f32[66,256]{1,0:T(8,128)S(1)} %add.899), channel_id=1, source_target_pairs={{0,8},{8,0},{16,24},{24,16},{1,9},{9,1},{17,25},{25,17},{2,10},{10... | collective-permute-start | bytes 202760 | tf_op jit(solution)/shard_map/ppermute | solution.py:37
  379.3 31.8 %collective-permute-start.54 = (f32[66,256]{1,0:T(8,128)S(1)}, f32[66,256]{1,0:T(8,128)S(1)}, u32[]{:S(2)}, u32[]{:S(2)}) collective-permute-start(f32[66,256]{1,0:T(8,128)S(1)} %add.900), channel_id=1, source_target_pairs={{0,16},{8,24},{16,0},{24,8},{1,17},{9,25},{17,1},{25,9},{2,18},{10... | collective-permute-start | bytes 202760 | tf_op jit(solution)/shard_map/ppermute | solution.py:37
  383.6 27.6 %collective-permute-start.52 = (bf16[768,512]{1,0:T(8,128)(2,1)S(1)}, bf16[768,512]{1,0:T(8,128)(2,1)S(1)}, u32[]{:S(2)}, u32[]{:S(2)}) collective-permute-start(bf16[768,512]{1,0:T(8,128)(2,1)S(1)} %pad_maximum_fusion.7.refs_5_), channel_id=1, source_target_pairs={{0,2},{2,0},{1,3},{3,1},{4,6},{6,4},{5,7},{7,5},{8,10},{10,8},{9,1... | collective-permute-start | bytes 2359304 | tf_op jit(solution)/shard_map/ppermute | solution.py:37
  421.8 32.1 %collective-permute-start.60 = (f32[7,2048]{1,0:T(8,128)S(1)}, f32[7,2048]{1,0:T(8,128)S(1)}, u32[]{:S(2)}, u32[]{:S(2)}) collective-permute-start(f32[7,2048]{1,0:T(8,128)S(1)} %add_add_fusion.2), channel_id=1, source_target_pairs={{0,16},{8,24},{16,0},{24,8},{1,17},{9,25},{17,1},{25,9},{2,18},{10... | collective-permute-start | bytes 172040 | tf_op jit(solution)/shard_map/ppermute | solution.py:37
  424.7 29.1 %collective-permute-start.61 = (f32[7,2048]{1,0:T(8,128)S(1)}, f32[7,2048]{1,0:T(8,128)S(1)}, u32[]{:S(2)}, u32[]{:S(2)}) collective-permute-start(f32[7,2048]{1,0:T(8,128)S(1)} %add_add_fusion.2), channel_id=1, source_target_pairs={{0,24},{8,16},{16,8},{24,0},{1,25},{9,17},{17,9},{25,1},{2,26},{10... | collective-permute-start | bytes 172040 | tf_op jit(solution)/shard_map/ppermute | solution.py:37
  426.1 27.8 %collective-permute-start.59 = (f32[7,2048]{1,0:T(8,128)S(1)}, f32[7,2048]{1,0:T(8,128)S(1)}, u32[]{:S(2)}, u32[]{:S(2)}) collective-permute-start(f32[7,2048]{1,0:T(8,128)S(1)} %add_add_fusion.2), channel_id=1, source_target_pairs={{0,8},{8,0},{16,24},{24,16},{1,9},{9,1},{17,25},{25,17},{2,10},{10... | collective-permute-start | bytes 172040 | tf_op jit(solution)/shard_map/ppermute | solution.py:37
  483.4 10.8 %collective-permute-start.67 = (f32[2,512]{1,0:T(2,128)S(1)}, f32[2,512]{1,0:T(2,128)S(1)}, u32[]{:S(2)}, u32[]{:S(2)}) collective-permute-start(f32[2,512]{1,0:T(2,128)S(1)} %add_add_fusion.12), channel_id=1, source_target_pairs={{0,16},{8,24},{16,0},{24,8},{1,17},{9,25},{17,1},{25,9},{2,18},{10... | collective-permute-start | bytes 12296 | tf_op jit(solution)/shard_map/ppermute | solution.py:37
  486.0 8.2 %collective-permute-start.68 = (f32[2,512]{1,0:T(2,128)S(1)}, f32[2,512]{1,0:T(2,128)S(1)}, u32[]{:S(2)}, u32[]{:S(2)}) collective-permute-start(f32[2,512]{1,0:T(2,128)S(1)} %add_add_fusion.12), channel_id=1, source_target_pairs={{0,24},{8,16},{16,8},{24,0},{1,25},{9,17},{17,9},{25,1},{2,26},{10... | collective-permute-start | bytes 12296 | tf_op jit(solution)/shard_map/ppermute | solution.py:37
  502.2 18.2 %collective-permute-start.70 = (bf16[384,512]{1,0:T(8,128)(2,1)S(1)}, bf16[384,512]{1,0:T(8,128)(2,1)S(1)}, u32[]{:S(2)}, u32[]{:S(2)}) collective-permute-start(bf16[384,512]{1,0:T(8,128)(2,1)S(1)} %get-tuple-element.195), channel_id=1, source_target_pairs={{0,4},{4,8},{8,12},{12,16},{16,20},{20,24},{24,28},{1,5},{5,9},{9,... | collective-permute-start | bytes 1179656 | tf_op jit(solution)/shard_map/ppermute | solution.py:71
  504.9 19.5 %collective-permute-start.69 = (bf16[384,512]{1,0:T(8,128)(2,1)S(1)}, bf16[384,512]{1,0:T(8,128)(2,1)S(1)}, u32[]{:S(2)}, u32[]{:S(2)}) collective-permute-start(bf16[384,512]{1,0:T(8,128)(2,1)S(1)} %get-tuple-element.194), channel_id=1, source_target_pairs={{4,0},{8,4},{12,8},{16,12},{20,16},{24,20},{28,24},{5,1},{9,5},{13... | collective-permute-start | bytes 1179656 | tf_op jit(solution)/shard_map/ppermute | solution.py:71
  514.0 36.1 %collective-permute-start.78 = (bf16[8,416,512]{2,1,0:T(8,128)(2,1)S(1)}, bf16[8,416,512]{2,1,0:T(8,128)(2,1)S(1)}, u32[]{:S(2)}, u32[]{:S(2)}) collective-permute-start(bf16[8,416,512]{2,1,0:T(8,128)(2,1)S(1)} %slice_dynamic-update-slice_fusion), channel_id=1, source_target_pairs={{0,1},{1,0},{2,3},{3,2},{4,5},{5,4},{6,7},{7,6},{8,9},{9,8},{10,11... | collective-permute-start | bytes 10223624 | tf_op jit(solution)/shard_map/ppermute | solution.py:37
  526.8 12.7 %collective-permute-start.73 = (f32[2,512]{1,0:T(2,128)S(1)}, f32[2,512]{1,0:T(2,128)S(1)}, u32[]{:S(2)}, u32[]{:S(2)}) collective-permute-start(f32[2,512]{1,0:T(2,128)S(1)} %fusion.86), channel_id=1, source_target_pairs={{0,2},{2,0},{1,3},{3,1},{4,6},{6,4},{5,7},{7,5},{8,10},{10,8},{9,1... | collective-permute-start | bytes 12296 | tf_op jit(solution)/shard_map/ppermute | solution.py:37
  527.8 13.3 %collective-permute-start.74 = (f32[2,512]{1,0:T(2,128)S(1)}, f32[2,512]{1,0:T(2,128)S(1)}, u32[]{:S(2)}, u32[]{:S(2)}) collective-permute-start(f32[2,512]{1,0:T(2,128)S(1)} %fusion.86), channel_id=1, source_target_pairs={{0,6},{2,4},{4,2},{6,0},{1,7},{3,5},{5,3},{7,1},{8,14},{10,12},{12... | collective-permute-start | bytes 12296 | tf_op jit(solution)/shard_map/ppermute | solution.py:37
  551.6 27.4 %collective-permute-start.90 = (bf16[4,208,512]{2,1,0:T(8,128)(2,1)S(1)}, bf16[4,208,512]{2,1,0:T(8,128)(2,1)S(1)}, u32[]{:S(2)}, u32[]{:S(2)}) collective-permute-start(bf16[4,208,512]{2,1,0:T(8,128)(2,1)S(1)} %dynamic-slice_bitcast_fusion.4), channel_id=1, source_target_pairs={{0,4},{4,0},{1,5},{5,1},{2,6},{6,2},{3,7},{7,3},{8,12},{12,8},{9,1... | collective-permute-start | bytes 2555912 | tf_op jit(solution)/shard_map/ppermute | solution.py:37
  553.4 49.5 %collective-permute-start.86 = (bf16[4,208,512]{2,1,0:T(8,128)(2,1)S(1)}, bf16[4,208,512]{2,1,0:T(8,128)(2,1)S(1)}, u32[]{:S(2)}, u32[]{:S(2)}) collective-permute-start(bf16[4,208,512]{2,1,0:T(8,128)(2,1)S(1)} %dynamic-slice_bitcast_fusion.5), channel_id=1, source_target_pairs={{0,4},{4,0},{1,5},{5,1},{2,6},{6,2},{3,7},{7,3},{8,12},{12,8},{9,1... | collective-permute-start | bytes 2555912 | tf_op jit(solution)/shard_map/ppermute | solution.py:37
  557.3 48.1 %collective-permute-start.79 = (bf16[8,128,512]{2,1,0:T(8,128)(2,1)S(1)}, bf16[8,128,512]{2,1,0:T(8,128)(2,1)S(1)}, u32[]{:S(2)}, u32[]{:S(2)}) collective-permute-start(bf16[8,128,512]{2,1,0:T(8,128)(2,1)S(1)} %constant_dynamic-slice_fusion), channel_id=1, source_target_pairs={{0,1},{1,0},{2,3},{3,2},{4,5},{5,4},{6,7},{7,6},{8,9},{9,8},{10,11... | collective-permute-start | bytes 3145736 | tf_op jit(solution)/shard_map/ppermute | solution.py:37
  579.3 26.5 %collective-permute-start.93 = (bf16[208,512]{1,0:T(8,128)(2,1)S(1)}, bf16[208,512]{1,0:T(8,128)(2,1)S(1)}, u32[]{:S(2)}, u32[]{:S(2)}) collective-permute-start(bf16[208,512]{1,0:T(8,128)(2,1)S(1)} %get-tuple-element.215), channel_id=1, source_target_pairs={{0,24},{8,16},{16,8},{24,0},{1,25},{9,17},{17,9},{25,1},{2,26},{10... | collective-permute-start | bytes 638984 | tf_op jit(solution)/shard_map/ppermute | solution.py:37
  581.8 46.3 %collective-permute-start.92 = (bf16[208,512]{1,0:T(8,128)(2,1)S(1)}, bf16[208,512]{1,0:T(8,128)(2,1)S(1)}, u32[]{:S(2)}, u32[]{:S(2)}) collective-permute-start(bf16[208,512]{1,0:T(8,128)(2,1)S(1)} %get-tuple-element.216), channel_id=1, source_target_pairs={{0,16},{8,24},{16,0},{24,8},{1,17},{9,25},{17,1},{25,9},{2,18},{10... | collective-permute-start | bytes 638984 | tf_op jit(solution)/shard_map/ppermute | solution.py:37
  581.8 47.8 %collective-permute-start.91 = (bf16[208,512]{1,0:T(8,128)(2,1)S(1)}, bf16[208,512]{1,0:T(8,128)(2,1)S(1)}, u32[]{:S(2)}, u32[]{:S(2)}) collective-permute-start(bf16[208,512]{1,0:T(8,128)(2,1)S(1)} %get-tuple-element.214), channel_id=1, source_target_pairs={{0,8},{8,0},{16,24},{24,16},{1,9},{9,1},{17,25},{25,17},{2,10},{10... | collective-permute-start | bytes 638984 | tf_op jit(solution)/shard_map/ppermute | solution.py:37
  603.2 26.5 %collective-permute-start.89 = (bf16[208,512]{1,0:T(8,128)(2,1)S(1)}, bf16[208,512]{1,0:T(8,128)(2,1)S(1)}, u32[]{:S(2)}, u32[]{:S(2)}) collective-permute-start(bf16[208,512]{1,0:T(8,128)(2,1)S(1)} %get-tuple-element.212), channel_id=1, source_target_pairs={{0,24},{8,16},{16,8},{24,0},{1,25},{9,17},{17,9},{25,1},{2,26},{10... | collective-permute-start | bytes 638984 | tf_op jit(solution)/shard_map/ppermute | solution.py:37
  605.4 31.4 %collective-permute-start.88 = (bf16[208,512]{1,0:T(8,128)(2,1)S(1)}, bf16[208,512]{1,0:T(8,128)(2,1)S(1)}, u32[]{:S(2)}, u32[]{:S(2)}) collective-permute-start(bf16[208,512]{1,0:T(8,128)(2,1)S(1)} %get-tuple-element.213), channel_id=1, source_target_pairs={{0,16},{8,24},{16,0},{24,8},{1,17},{9,25},{17,1},{25,9},{2,18},{10... | collective-permute-start | bytes 638984 | tf_op jit(solution)/shard_map/ppermute | solution.py:37
  605.8 31.1 %collective-permute-start.87 = (bf16[208,512]{1,0:T(8,128)(2,1)S(1)}, bf16[208,512]{1,0:T(8,128)(2,1)S(1)}, u32[]{:S(2)}, u32[]{:S(2)}) collective-permute-start(bf16[208,512]{1,0:T(8,128)(2,1)S(1)} %get-tuple-element.211), channel_id=1, source_target_pairs={{0,8},{8,0},{16,24},{24,16},{1,9},{9,1},{17,25},{25,17},{2,10},{10... | collective-permute-start | bytes 638984 | tf_op jit(solution)/shard_map/ppermute | solution.py:37
  628.1 10.6 %collective-permute-start.80 = (bf16[4,128,512]{2,1,0:T(8,128)(2,1)S(1)}, bf16[4,128,512]{2,1,0:T(8,128)(2,1)S(1)}, u32[]{:S(2)}, u32[]{:S(2)}) collective-permute-start(bf16[4,128,512]{2,1,0:T(8,128)(2,1)S(1)} %dynamic-slice_bitcast_fusion.6), channel_id=1, source_target_pairs={{0,4},{4,0},{1,5},{5,1},{2,6},{6,2},{3,7},{7,3},{8,12},{12,8},{9,1... | collective-permute-start | bytes 1572872 | tf_op jit(solution)/shard_map/ppermute | solution.py:37
  637.0 9.3 %collective-permute-start.94 = (bf16[416,512]{1,0:T(8,128)(2,1)S(1)}, bf16[416,512]{1,0:T(8,128)(2,1)S(1)}, u32[]{:S(2)}, u32[]{:S(2)}) collective-permute-start(bf16[416,512]{1,0:T(8,128)(2,1)S(1)} %pad_maximum_fusion.10), channel_id=1, source_target_pairs={{0,2},{2,0},{1,3},{3,1},{4,6},{6,4},{5,7},{7,5},{8,10},{10,8},{9,1... | collective-permute-start | bytes 1277960 | tf_op jit(solution)/shard_map/ppermute | solution.py:37
  640.3 10.0 %collective-permute-start.82 = (bf16[128,512]{1,0:T(8,128)(2,1)S(1)}, bf16[128,512]{1,0:T(8,128)(2,1)S(1)}, u32[]{:S(2)}, u32[]{:S(2)}) collective-permute-start(bf16[128,512]{1,0:T(8,128)(2,1)S(1)} %get-tuple-element.230), channel_id=1, source_target_pairs={{0,16},{8,24},{16,0},{24,8},{1,17},{9,25},{17,1},{25,9},{2,18},{10... | collective-permute-start | bytes 393224 | tf_op jit(solution)/shard_map/ppermute | solution.py:37
  640.3 10.0 %collective-permute-start.81 = (bf16[128,512]{1,0:T(8,128)(2,1)S(1)}, bf16[128,512]{1,0:T(8,128)(2,1)S(1)}, u32[]{:S(2)}, u32[]{:S(2)}) collective-permute-start(bf16[128,512]{1,0:T(8,128)(2,1)S(1)} %get-tuple-element.228), channel_id=1, source_target_pairs={{0,8},{8,0},{16,24},{24,16},{1,9},{9,1},{17,25},{25,17},{2,10},{10... | collective-permute-start | bytes 393224 | tf_op jit(solution)/shard_map/ppermute | solution.py:37
  646.4 10.9 %collective-permute-start.95 = (bf16[416,512]{1,0:T(8,128)(2,1)S(1)}, bf16[416,512]{1,0:T(8,128)(2,1)S(1)}, u32[]{:S(2)}, u32[]{:S(2)}) collective-permute-start(bf16[416,512]{1,0:T(8,128)(2,1)S(1)} %add_convert_fusion.2), channel_id=1, source_target_pairs={{0,1},{1,0},{2,3},{3,2},{4,5},{5,4},{6,7},{7,6},{8,9},{9,8},{10,11... | collective-permute-start | bytes 1277960 | tf_op jit(solution)/shard_map/ppermute | solution.py:37
  656.2 19.2 %collective-permute-start.85 = (bf16[128,512]{1,0:T(8,128)(2,1)S(1)}, bf16[128,512]{1,0:T(8,128)(2,1)S(1)}, u32[]{:S(2)}, u32[]{:S(2)}) collective-permute-start(bf16[128,512]{1,0:T(8,128)(2,1)S(1)} %add_convert_fusion.3), channel_id=1, source_target_pairs={{0,1},{1,0},{2,3},{3,2},{4,5},{5,4},{6,7},{7,6},{8,9},{9,8},{10,11... | collective-permute-start | bytes 393224 | tf_op jit(solution)/shard_map/ppermute | solution.py:37
  656.3 18.0 %collective-permute-start.96 = (bf16[128,2688]{1,0:T(8,128)(2,1)}, bf16[128,2688]{1,0:T(8,128)(2,1)S(1)}, u32[]{:S(2)}, u32[]{:S(2)}) collective-permute-start(bf16[128,2688]{1,0:T(8,128)(2,1)} %bitcast.368), channel_id=1, source_target_pairs={{0,2},{2,0},{1,3},{3,1},{4,6},{6,4},{5,7},{7,5},{8,10},{10,8},{9,1... | collective-permute-start | bytes 2064392 | tf_op jit(solution)/shard_map/ppermute | solution.py:37
  658.7 17.6 %collective-permute-start.97 = (bf16[128,2688]{1,0:T(8,128)(2,1)S(1)}, bf16[128,2688]{1,0:T(8,128)(2,1)S(1)}, u32[]{:S(2)}, u32[]{:S(2)}) collective-permute-start(bf16[128,2688]{1,0:T(8,128)(2,1)S(1)} %bitcast.370), channel_id=1, source_target_pairs={{0,1},{1,0},{2,3},{3,2},{4,5},{5,4},{6,7},{7,6},{8,9},{9,8},{10,11... | collective-permute-start | bytes 2064392 | tf_op jit(solution)/shard_map/ppermute | solution.py:37
  (115 other events, 919.5 us)
Sparse Core Ops, SparseCore 0:
  10.8 79.3 all-gather.5
  93.7 150.0 all-gather.3
  482.2 150.7 reduce-scatter.1

commit v4 on v3

--- a/solution.py
+++ b/solution.py
@@ -107,6 +107,23 @@
     mine = lax.dynamic_index_in_dim(parts, here, 1, keepdims=False)
     other = lax.dynamic_index_in_dim(parts, 1 - here, 1, keepdims=False)
     return (mine.astype(full) + flip(other, [("y", 1)]).astype(full)).astype(low)
+
+
+def scatter_x(partial, axis):
+    chips, here = lax.axis_size("x"), lax.axis_index("x")
+    size = partial.shape[axis] // chips
+    total = lax.dynamic_slice_in_dim(partial, here * size, size, axis).astype(full)
+    for m in range(1, chips):
+        part = lax.dynamic_slice_in_dim(partial, (here ^ m) * size, size, axis)
+        total = total + flip(part, [("x", m)]).astype(full)
+    return total.astype(low)
+
+
+def gather_x(own):
+    chips, here = lax.axis_size("x"), lax.axis_index("x")
+    parts = jnp.stack([own] + [flip(own, [("x", m)]) for m in range(1, chips)])
+    ordered = [lax.dynamic_index_in_dim(parts, here ^ m, 0, keepdims=False) for m in range(chips)]
+    return jnp.concatenate(ordered, axis=0)
 
 
 def scatter_z(parts):
@@ -306,78 +323,110 @@
     )(task_of, grads, masks)
 
 
-def shared_back_kernel(tasks, side_tasks, *refs):
+def center_back_kernel(tasks, *refs):
+    dy_ref = refs[0]
+    w_refs = refs[1 : 1 + tasks]
+    wide_ref, source_ref, vec_ref, mask_ref = refs[1 + tasks : 5 + tasks]
+    out_refs = refs[5 + tasks : -2]
+    slope_ref, normed_ref = refs[-2:]
+    three = w_refs[0].shape[1]
+    pixels = dy_ref.shape[0]
+    for at in range(0, pixels, pixels // 3):
+        rows = slice(at, at + pixels // 3)
+        for t in range(tasks):
+            out_refs[t][rows, :] = lax.dot_general(
+                dy_ref[rows, t * three : (t + 1) * three],
+                w_refs[t][...],
+                (((1,), (1,)), ((), ())),
+                preferred_element_type=full,
+            ).astype(low)
+        normed = (wide_ref[rows, :].astype(full) - vec_ref[0:1]) * vec_ref[1:2]
+        value = normed * vec_ref[2:3] + vec_ref[3:4] + source_ref[rows, :].astype(full)
+        slope_ref[rows, :] = (silu_slope(value) * mask_ref[rows, 1:2]).astype(low)
+        normed_ref[rows, :] = normed.astype(low)
+
+
+def center_back(dys, heads_all, tasks, wide, source, vecs, masks, block):
+    pixels, depth = wide.shape
+    three = dys.shape[1] // tasks
+    column = lambda j: (0, j)
+    fixed = lambda j: (0, 0)
+    return pl.pallas_call(
+        lambda *refs: center_back_kernel(tasks, *refs),
+        out_shape=[jax.ShapeDtypeStruct((pixels, depth), low)] * (tasks + 2),
+        grid=(depth // block,),
+        in_specs=[spec(dys.shape, fixed)]
+        + [spec((block, three), lambda j, i=i: (j, i)) for i in range(tasks)]
+        + [spec((pixels, block), column)] * 2
+        + [spec((8, block), column), spec(masks.shape, fixed)],
+        out_specs=[spec((pixels, block), column)] * (tasks + 2),
+        compiler_params=params(),
+        cost_estimate=cost(2 * pixels * depth * three * tasks, 16 * pixels * depth),
+    )(dys, *([heads_all] * tasks), wide, source, vecs, masks)
+
+
+def side_back_kernel(tasks, side_tasks, touched, *refs):
     slots = len(side_tasks)
-    picked_ref, here_ref = refs[:2]
-    dy_ref = refs[2]
-    w_refs = refs[3 : 3 + tasks + slots]
-    wide_ref, source_ref, vec_ref, mask_ref = refs[3 + tasks + slots : 7 + tasks + slots]
-    out_refs = refs[7 + tasks + slots : -3]
-    slope_ref, normed_ref, sums_ref = refs[-3:]
-    three = w_refs[0].shape[1]
-
-    def back(i):
-        return lax.dot_general(
-            dy_ref[:, i * three : (i + 1) * three],
-            w_refs[i][...],
-            (((1,), (1,)), ((), ())),
-            preferred_element_type=full,
-        )
-
-    grads = [back(t) for t in range(tasks)]
-    for s, choices in enumerate(side_tasks):
-        side = back(tasks + s)
-        for t in choices:
-            grads[t] = grads[t] + (side if len(choices) == 1 else side * here_ref[s * tasks + t])
-    normed = (wide_ref[...].astype(full) - vec_ref[0:1]) * vec_ref[1:2]
-    value = normed * vec_ref[2:3] + vec_ref[3:4] + source_ref[...].astype(full)
-    slope = silu_slope(value) * mask_ref[:, 1:2]
-    slope_ref[...] = slope.astype(low)
-    normed_ref[...] = normed.astype(low)
-    rows = []
-    for t in range(tasks):
-        out_refs[t][...] = grads[t].astype(low)
-        part = grads[t] * slope
-        rows += [jnp.sum(part * normed, axis=0), jnp.sum(part, axis=0)]
-    for t in range(tasks):
-        for u in range(t, tasks):
-            rows.append(jnp.sum(grads[t] * grads[u], axis=0))
+    here_ref, dy_ref = refs[1:3]
+    w_refs = refs[3 : 3 + slots]
+    held_refs = refs[3 + slots : 3 + slots + tasks]
+    slope_ref, normed_ref = refs[3 + slots + tasks : 5 + slots + tasks]
+    out_refs = refs[5 + slots + tasks : -1]
+    sums_ref = refs[-1]
+    pixels = dy_ref.shape[0]
+    totals = None
+    for at in range(0, pixels, pixels // 3):
+        rows = slice(at, at + pixels // 3)
+        grads = [ref[rows, :].astype(full) for ref in held_refs]
+        for s, choices in enumerate(side_tasks):
+            three = w_refs[s].shape[1]
+            side = lax.dot_general(
+                dy_ref[rows, s * three : (s + 1) * three],
+                w_refs[s][...],
+                (((1,), (1,)), ((), ())),
+                preferred_element_type=full,
+            )
+            for t in choices:
+                more = side if len(choices) == 1 else side * here_ref[s * tasks + t]
+                grads[t] = grads[t] + more
+        slope, normed = slope_ref[rows, :].astype(full), normed_ref[rows, :].astype(full)
+        parts = []
+        for t in range(tasks):
+            part = grads[t] * slope
+            parts += [jnp.sum(part * normed, axis=0), jnp.sum(part, axis=0)]
+        for t in range(tasks):
+            for u in range(t, tasks):
+                parts.append(jnp.sum(grads[t] * grads[u], axis=0))
+        for i, t in enumerate(touched):
+            out_refs[i][rows, :] = grads[t].astype(low)
+        totals = parts if totals is None else [a + b for a, b in zip(totals, parts)]
     sums_ref[...] = jnp.zeros_like(sums_ref)
-    for i, row in enumerate(rows):
+    for i, row in enumerate(totals):
         sums_ref[i, :] = row
 
 
-def shared_back(dys, heads_all, picked, here, side_tasks, tasks, wide, source, vecs, masks, block):
-    pixels, depth = wide.shape
-    items = tasks + len(side_tasks)
-    three = dys.shape[1] // items
-    weights = [
-        spec((block, three), (lambda j, p, h, i=i: (j, i)) if i < tasks else (lambda j, p, h, i=i: (j, p[i])))
-        for i in range(items)
-    ]
+def side_back(dys, heads_all, picked, here, side_tasks, tasks, held, slope, normed, block):
+    pixels, depth = slope.shape
+    slots = len(side_tasks)
+    three = dys.shape[1] // slots
+    touched = sorted({t for choices in side_tasks for t in choices})
     column = lambda j, p, h: (0, j)
-    return pl.pallas_call(
-        lambda *refs: shared_back_kernel(tasks, side_tasks, *refs),
-        out_shape=[jax.ShapeDtypeStruct((pixels, depth), low)] * (tasks + 2)
+    *outs, sums = pl.pallas_call(
+        lambda *refs: side_back_kernel(tasks, side_tasks, touched, *refs),
+        out_shape=[jax.ShapeDtypeStruct((pixels, depth), low)] * len(touched)
         + [jax.ShapeDtypeStruct((16, depth), full)],
         grid_spec=pltpu.PrefetchScalarGridSpec(
             num_scalar_prefetch=2,
             grid=(depth // block,),
             in_specs=[spec(dys.shape, lambda j, p, h: (0, 0))]
-            + weights
-            + [
-                spec((pixels, block), column),
-                spec((pixels, block), column),
-                spec((8, block), column),
-                spec(masks.shape, lambda j, p, h: (0, 0)),
-            ],
-            out_specs=[spec((pixels, block), column)] * (tasks + 2) + [spec((16, block), column)],
+            + [spec((block, three), lambda j, p, h, i=i: (j, p[i])) for i in range(slots)]
+            + [spec((pixels, block), column)] * (tasks + 2),
+            out_specs=[spec((pixels, block), column)] * len(touched) + [spec((16, block), column)],
         ),
         compiler_params=params(),
-        cost_estimate=cost(
-            2 * pixels * depth * three * items, 2 * items * depth * three + 12 * pixels * depth
-        ),
-    )(picked, here, dys, *([heads_all] * items), wide, source, vecs, masks)
+        cost_estimate=cost(2 * pixels * depth * three * slots, 14 * pixels * depth),
+    )(picked, here, dys, *([heads_all] * slots), *held, slope, normed)
+    return [outs[touched.index(t)] if t in touched else held[t] for t in range(tasks)], sums
 
 
 def expand_back_kernel(tasks, blocks, *refs):
@@ -386,15 +435,20 @@
     slope_ref, normed_ref, vec_ref, mask_ref, hidden_ref, w_ref, mid_ref, mid_vec_ref = refs[
         2 + tasks : 10 + tasks
     ]
-    dbefore_ref, dweight_ref, dout_ref, sums_ref, total_ref, turned_ref = refs[10 + tasks :]
+    dbefore_ref, dweight_ref, dout_ref, sums_ref, total_ref, turned_ref, scale_ref = refs[
+        10 + tasks :
+    ]
     at = pl.program_id(0)
 
     @pl.when(at == 0)
     def _():
         turned_ref[...] = hidden_ref[...].T
-
-    gram = 2 * tasks
-    weights = task_scales([gram_ref[gram : gram + 1, i : i + 1] for i in range(6)])
+        gram = 2 * tasks
+        scales = task_scales([gram_ref[gram : gram + 1, i : i + 1] for i in range(6)])
+        for t in range(tasks):
+            scale_ref[t : t + 1, :] = jnp.broadcast_to(scales[t], (1, scale_ref.shape[1]))
+
+    weights = [scale_ref[t : t + 1, :] for t in range(tasks)]
     combined = grad_refs[0][...].astype(full) * weights[0]
     dgain = sum_ref[0:1] * weights[0]
     dbias = sum_ref[1:2] * weights[0]
@@ -468,7 +522,11 @@
                 spec((pixels, width), fixed),
                 spec((8, width), fixed),
             ],
-            scratch_shapes=[pltpu.VMEM((pixels, width), full), pltpu.VMEM((width, pixels), low)],
+            scratch_shapes=[
+                pltpu.VMEM((pixels, width), full),
+                pltpu.VMEM((width, pixels), low),
+                pltpu.VMEM((8, block), full),
+            ],
         ),
         compiler_params=params(),
         cost_estimate=cost(4 * pixels * width, 14 * pixels),
@@ -920,18 +978,30 @@
         for e in sorted(set(table[s].tolist()) - {int(table[s][0])}):
             dside = jnp.where(picked_term[s] == e, back[e], dside)
         dsides.append(dside)
-    turned, dsides, center_halves, class_sums = lax.optimization_barrier(
-        (turn(grid_pieces), jnp.concatenate(dsides, axis=1), center_halves, class_sums)
+    vecs = jnp.pad(jnp.stack([mean3, scale3, gain_expand, bias_expand]), ((0, 4), (0, 0)))
+    dys = spread_back(dmixed, masks, centers, head, pixels)
+    *center_grads, slope3, normed3 = center_back(
+        dys, heads_all, tasks, expanded, source, vecs, masks, 256
+    )
+    center_grads, slope3, normed3, turned, dsides, center_halves, class_sums = (
+        lax.optimization_barrier(
+            (
+                center_grads,
+                slope3,
+                normed3,
+                turn(grid_pieces),
+                jnp.concatenate(dsides, axis=1),
+                center_halves,
+                class_sums,
+            )
+        )
     )
     class_sums = sum_along(class_sums, "z")
     side_halves = from_groups(dsides)
-    dterms = jnp.concatenate([dmixed, dsides], axis=1)
-    dys = spread_back(dterms, masks, all_tasks, head, pixels)
+    dys = spread_back(dsides, masks, side_task, head, pixels)
     here = (side_task[:, None] == centers[None, :]).astype(full).reshape(-1)
-    vec_rows = [mean3, scale3, gain_expand, bias_expand]
-    vecs = jnp.pad(jnp.stack(vec_rows), ((0, 4), (0, 0)))
-    *shared_grads, slope3, normed3, sums = shared_back(
-        dys, heads_all, all_picked, here, slot_tasks, tasks, expanded, source, vecs, masks, 256
+    shared_grads, sums = side_back(
+        dys, heads_all, tasks + picked_term, here, slot_tasks, tasks, center_grads, slope3, normed3, 256
     )
     sums, center_halves, side_halves, class_sums = lax.optimization_barrier(
         (sums, center_halves, side_halves, class_sums)
@@ -1001,10 +1071,12 @@
     dout1 = dhidden1 * valid * silu_slope(out1)
     sums1 = all_sum(jnp.stack([jnp.sum(dout1 * normed1, axis=0), jnp.sum(dout1, axis=0)]))
     sums1, later = lax.optimization_barrier((sums1, later))
-    cut = later.shape[1] // 2
-    later_own = jnp.concatenate(
-        [scatter_z(scatter_y(piece)) for piece in (later[:, :cut], later[:, cut:])], axis=0
-    )
+    cut = later.shape[1] // 64 * 32
+    first, second = scatter_x(later[:, :cut], 1), scatter_x(later[:, cut:], 1)
+    second, head_own = lax.optimization_barrier((second, head_own))
+    head_shares = [head_own] + [flip(head_own, [("x", m)]) for m in range(1, chips)]
+    head_others = [flip(part, [("c", 1)]) for part in head_shares]
+    later_own = [scatter_z(scatter_y(piece)) for piece in (first, second)]
     dgain1, dbias1 = sums1[0], sums1[1]
     dreduced = valid * (gain_reduce * scale1) * (
         dout1 - dbias1 / count - normed1 * (dgain1 / count)
@@ -1019,12 +1091,14 @@
     part_of[:, 1] = np.arange(tasks)
     for e, (task, side, _) in enumerate(terms):
         part_of[task, side + 1] = tasks + e
-    head_shares = [head_own] + [flip(head_own, [("x", m)]) for m in range(1, chips)]
-    head_others = [flip(part, [("c", 1)]) for part in head_shares]
+    head_shares, head_others, later_own = lax.optimization_barrier(
+        (head_shares, head_others, later_own)
+    )
     at = jnp.stack([chip, core]).astype(jnp.int32)
     heads_out = place_shares(head_shares, head_others, jnp.asarray(part_of.reshape(-1)), at, head)
     heads_out = heads_out.reshape(tasks, 9, own, head).transpose(2, 0, 1, 3)
-    later_own, later_other = over_groups(later_own)
+    later_own = jnp.concatenate([gather_x(piece) for piece in later_own], axis=0)
+    later_other = flip(later_own, [("c", 1)])
     later_sum = both_halves(
         later_own.reshape(9 + ratio, mid_rows, width),
         later_other.reshape(9 + ratio, mid_rows, width),

time: 701 us -> 653 us (0.932)
  waiting for transfers between devices: 286 us -> 241 us
  Pallas kernels: 124 us -> 133 us
    ppermute x90 -> x93, waiting for transfers between devices: 183 us -> 139 us  [flip(): return lax.ppermute(value, names, pairs)]
    pallas_call x1 -> x2, Pallas kernels: 26 us -> 35.6 us  [the longest x1 18.4 us: center_back(): pl.pallas_call(lambda *refs: center_back_kernel(tasks, *refs), out_shape=...]
    ppermute x90 -> x93, starting transfers between devices: 101 us -> 95.4 us  [flip(): return lax.ppermute(value, names, pairs)]
    unnamed x163 -> x150, local copies, waits for them, and re-layouts: 20.6 us -> 19 us
  transfers between devices with their start and end apart: 103 -> 106, of which waited for: 56 -> 59; matrix products, arithmetic and copies ran while one was open for 15% -> 15% of each run, Pallas kernels for 14% -> 21%
where the time goes in v4:
time: 653 us; the launch traced here: 646 us
  waiting for transfers between devices  241 us (37%)
  Pallas kernels  133 us (20%)
  starting transfers between devices  127 us (19%)
  other arithmetic  45.1 us (7%)
  local copies, waits for them, and re-layouts  42 us (6%)
  matrix products  31.7 us (5%)
  between operations  25 us (4%)
    ppermute x93, waiting for transfers between devices, flip(): return lax.ppermute(value, names, pairs)  139 us
    ppermute x93, starting transfers between devices, flip(): return lax.ppermute(value, names, pairs)  95.4 us
    all_gather x1, waiting for transfers between devices, on_device(): block_mine = lax.all_gather(block_own, LINE, axis=0, tiled=False)  64.1 us
    ppermute x10, waiting for transfers between devices, rows_to(): return lax.ppermute(value, LINE, pairs)  37.6 us
    ppermute x10, starting transfers between devices, rows_to(): return lax.ppermute(value, LINE, pairs)  31.9 us
    pallas_call x1, Pallas kernels, some_weight_grad(): pl.pallas_call(lambda *refs: weight_grad_kernel(members, side_tasks, task...  25 us
    pallas_call x2, Pallas kernels, head_terms(): pl.pallas_call(terms_kernel, out_shape=jax.ShapeDtypeStruct((pixels, item...  22.9 us
    unnamed x150, local copies, waits for them, and re-layouts  19 us
  transfers between devices with their start and end apart: 106, of which 59 were waited for; matrix products, arithmetic and copies ran while one was open for 15% of the time, Pallas kernels for 21%

profile of v4, /device:TPU:0, one launch (start us, length us, event | category | flops | bytes accessed | tf_op | source)
XLA Modules:
  0.0 646.0 jit_solution(10487311403518459809)
XLA Ops:
  12.5 5.7 copy.82
  21.9 4.1 bitcast_multiply_fusion.refs_5_
  26.0 64.1 %all-gather.6.cloned.1.call-done = bf16[4352,512]{1,0:T(8,128)(2,1)} async-done(((bf16[544,512]{1,0:T(8,128)(2,1)}), bf16[4352,512]{1,0:T(8,128)(2,1)}) %all-gather.6.cloned.1.call-update) | async-done | bytes 4456464 | tf_op jit(solution)/shard_map/all_gather | solution.py:813
  90.3 7.7 %collective-permute-done.other_ref.refs_2_ = bf16[8,544,512]{2,1,0:T(8,128)(2,1)S(1)} collective-permute-done((bf16[8,544,512]{2,1,0:T(8,128)(2,1)}, bf16[8,544,512]{2,1,0:T(8,128)(2,1)S(1)}, u32[]{:S(2)}, u32[]{:S(2)}) %collective-permute-start) | collective-permute-done | bytes 4456480 | tf_op jit(solution)/shard_map/ppermute | solution.py:37
  100.2 3.2 shard_map.351
  103.4 3.4 fusion.109
  111.8 2.4 collective-permute-done.4
  123.3 5.5 collective-permute-start.8
  128.9 6.8 %shard_map.352 = (bf16[1536,1536]{1,0:T(8,128)(2,1)}, bf16[512,2048]{1,0:T(8,128)(2,1)}) custom-call(s32[1]{0:T(128)} %bitcast.10.core_ref.refs_0_, bf16[8,544,512]{2,1,0:T(8,128)(2,1)} %bitcast.353, bf16[8,544,512]{2,1,0:T(8,128)(2,1)} %copy-done.8), custom_call_target="tpu_custom_call" | custom-call | bytes 17825792 | tf_op jit(solution)/shard_map/pallas_call | solution.py:707
  135.8 5.5 collective-permute-done.9
  141.3 8.7 %collective-permute-done.8 = bf16[384,512]{1,0:T(8,128)(2,1)} collective-permute-done((bf16[384,512]{1,0:T(8,128)(2,1)S(1)}, bf16[384,512]{1,0:T(8,128)(2,1)}, u32[]{:S(2)}, u32[]{:S(2)}) %collective-permute-start.8) | collective-permute-done | bytes 393248 | tf_op jit(solution)/shard_map/ppermute | solution.py:71
  149.9 6.4 fusion.46
  160.3 2.8 collective-permute-start.13
  171.3 3.4 collective-permute-done.16
  175.4 4.5 fusion.107
  195.9 5.3 multiply_convert_fusion.x_ref
  212.6 34.0 %collective-permute-done.25.refs_2_ = bf16[768,1024]{1,0:T(8,128)(2,1)} collective-permute-done((bf16[768,1024]{1,0:T(8,128)(2,1)}, bf16[768,1024]{1,0:T(8,128)(2,1)}, u32[]{:S(2)}, u32[]{:S(2)}) %collective-permute-start.25) | collective-permute-done | bytes 1572896 | tf_op jit(solution)/shard_map/ppermute | solution.py:37
  247.4 9.9 %shard_map.354 = bf16[768,512]{1,0:T(8,128)(2,1)} custom-call(s32[2]{0:T(128)} %get-tuple-element.289.picked_ref.refs_0_, s32[2]{0:T(128)} %gather_fusion, bf16[768,2048]{1,0:T(8,128)(2,1)} %copy-done.3, bf16[2048,5376]{1,0:T(8,128)(2,1)} %all-gather.4.cloned.1.call-done.w_ref.refs_1_.refs_2_.refs_3_.refs_4_, f32[768,128]{1,0:T(8,128)} %bitcast.344), custom_call_target="tpu_custom_call" | custom-call | flops 4831838208 | bytes 9437184 | tf_op jit(solution)/shard_map/pallas_call | solution.py:272
  260.5 5.5 collective-permute-start.27
  266.0 3.1 collective-permute-start.29
  269.6 13.0 %shard_map.353 = f32[768,768]{1,0:T(8,128)} custom-call(s32[3]{0:T(128)} %iota.33.picked_ref.task_ref, s32[3]{0:T(128)} %iota.33.picked_ref.task_ref, bf16[768,2048]{1,0:T(8,128)(2,1)} %copy-done.3, bf16[2048,5376]{1,0:T(8,128)(2,1)} %all-gather.4.cloned.1.call-done.w_ref.refs_1_.refs_2_.refs_3_.refs_4_, f32[768,128]{1,0:T(8,128)} %bitcast.345), custom_call_target="tpu_custom_call" | custom-call | flops 7247757312 | bytes 12582912 | tf_op jit(solution)/shard_map/pallas_call | solution.py:272
  282.6 7.7 %collective-permute-done.29 = bf16[768,256]{1,0:T(8,128)(2,1)S(1)} collective-permute-done((bf16[768,256]{1,0:T(8,128)(2,1)S(1)}, bf16[768,256]{1,0:T(8,128)(2,1)S(1)}, u32[]{:S(2)}, u32[]{:S(2)}) %collective-permute-start.29) | collective-permute-done | bytes 393248 | tf_op jit(solution)/shard_map/ppermute | solution.py:71
  294.4 3.3 collective-permute-start.33
  302.0 6.9 %collective-permute-start.36 = (f32[2,768]{1,0:T(2,128)S(1)}, f32[2,768]{1,0:T(2,128)S(1)}, u32[]{:S(2)}, u32[]{:S(2)}) collective-permute-start(f32[2,768]{1,0:T(2,128)S(1)} %add_add_fusion.8), channel_id=1, source_target_pairs={{0,24},{8,16},{16,8},{24,0},{1,25},{9,17},{17,9},{25,1},{2,26},{10... | collective-permute-start | bytes 18440 | tf_op jit(solution)/shard_map/ppermute | solution.py:37
  310.1 5.5 shard_map.357.refs_2_
  328.6 2.4 collective-permute-start.43
  336.6 3.4 collective-permute-start.44
  341.3 6.7 %collective-permute-start.46 = (bf16[768,256]{1,0:T(8,128)(2,1)S(1)}, bf16[768,256]{1,0:T(8,128)(2,1)S(1)}, u32[]{:S(2)}, u32[]{:S(2)}) collective-permute-start(bf16[768,256]{1,0:T(8,128)(2,1)S(1)} %get-tuple-element.235), channel_id=1, source_target_pairs={{24,0},{28,4},{0,24},{4,28},{25,1},{29,5},{1,25},{5,29},{26,2},{30... | collective-permute-start | bytes 1179656 | tf_op jit(solution)/shard_map/ppermute | solution.py:71
  348.5 4.8 shard_map.355.refs_0_
  355.2 18.4 %shard_map.356 = (bf16[768,2048]{1,0:T(8,128)(2,1)}, bf16[768,2048]{1,0:T(8,128)(2,1)}, bf16[768,2048]{1,0:T(8,128)(2,1)}, bf16[768,2048]{1,0:T(8,128)(2,1)}, bf16[768,2048]{1,0:T(8,128)(2,1)}) custom-call(bf16[768,2304]{1,0:T(8,128)(2,1)} %shard_map.355.refs_0_, bf16[2048,5376]{1,0:T(8,128)(2,1)} %all-gather.4.cloned.1.call-done.w_ref.refs_1_.refs_2_.refs_3_.refs_4_, ...), custom_call_target="tpu_custom_call" | custom-call | flops 7247757312 | bytes 25165824 | tf_op jit(solution)/shard_map/pallas_call | solution.py:354
  375.2 5.4 collective-permute-done.48.refs_4_
  387.1 3.5 shard_map.358.refs_2_
  391.5 17.1 %shard_map.359 = (bf16[768,2048]{1,0:T(8,128)(2,1)}, bf16[768,2048]{1,0:T(8,128)(2,1)}, f32[16,2048]{1,0:T(8,128)}) custom-call(s32[2]{0:T(128)} %get-tuple-element.289.picked_ref.refs_0_, f32[6]{0:T(128)} %reshape.408.refs_1_, bf16[768,1536]{1,0:T(8,128)(2,1)} %shard_map.358.refs_2_, ...), custom_call_target="tpu_custom_call" | custom-call | flops 4831838208 | bytes 22020096 | tf_op jit(solution)/shard_map/pallas_call | solution.py:414
  424.8 25.0 %shard_map.360 = bf16[1024,2688]{1,0:T(8,128)(2,1)} custom-call(s32[7]{0:T(128)} %and_select_fusion.refs_0_, s32[2]{0:T(128)} %gather_fusion, bf16[1024,3072]{1,0:T(8,128)(2,1)} %shard_map.357.refs_2_, bf16[768,768]{1,0:T(8,128)(2,1)} %copy-done.20, bf16[768,768]{1,0:T(8,128)(2,1)} %copy-done.46, bf16[768,512]{1,0:T(8,128)(2,1)} %copy-done.23, ...), custom_call_target="tpu_custom_call" | custom-call | flops 12079595520 | bytes 11796480 | tf_op jit(solution)/shard_map/pallas_call | solution.py:635
  451.7 17.4 %shard_map.361 = (bf16[768,2048]{1,0:T(8,128)(2,1)}, bf16[512,2048]{1,0:T(8,128)(2,1)}, f32[768,512]{1,0:T(8,128)}, f32[8,512]{1,0:T(8,128)}) custom-call(f32[7,2048]{1,0:T(8,128)} %add_add_fusion.1.refs_0_.refs_4_, bf16[768,2048]{1,0:T(8,128)(2,1)} %get-tuple-element.104.refs_1_, bf16[768,2048]{1,0:T(8,128)(2,1)} %get-tuple-element.105.refs_2_, ...), custom_call_target="tpu_custom_call" | custom-call | flops 1572864 | bytes 10752 | tf_op jit(solution)/shard_map/pallas_call | solution.py:496
  484.0 2.6 collective-permute-start.67
  489.2 3.1 collective-permute-done.68
  496.6 3.8 fusion.130
  504.4 5.0 convolution_convert_fusion
  512.4 15.7 %collective-permute-done.70 = bf16[384,512]{1,0:T(8,128)(2,1)S(1)} collective-permute-done((bf16[384,512]{1,0:T(8,128)(2,1)S(1)}, bf16[384,512]{1,0:T(8,128)(2,1)S(1)}, u32[]{:S(2)}, u32[]{:S(2)}) %collective-permute-start.70) | collective-permute-done | bytes 393248 | tf_op jit(solution)/shard_map/ppermute | solution.py:71
  532.0 2.7 collective-permute-start.74
  551.2 4.6 convert_add_fusion
  555.8 10.2 %collective-permute-done.90 = bf16[8,96,512]{2,1,0:T(8,128)(2,1)S(1)} collective-permute-done((bf16[8,96,512]{2,1,0:T(8,128)(2,1)S(1)}, bf16[8,96,512]{2,1,0:T(8,128)(2,1)S(1)}, u32[]{:S(2)}, u32[]{:S(2)}) %collective-permute-start.90) | collective-permute-done | bytes 786464 | tf_op jit(solution)/shard_map/ppermute | solution.py:37
  568.0 13.9 %collective-permute-done.86 = bf16[8,112,512]{2,1,0:T(8,128)(2,1)S(1)} collective-permute-done((bf16[8,112,512]{2,1,0:T(8,128)(2,1)S(1)}, bf16[8,112,512]{2,1,0:T(8,128)(2,1)S(1)}, u32[]{:S(2)}, u32[]{:S(2)}) %collective-permute-start.86) | collective-permute-done | bytes 917536 | tf_op jit(solution)/shard_map/ppermute | solution.py:37
  592.0 5.1 collective-permute-done.93
  607.7 5.2 collective-permute-done.82
  624.1 2.5 collective-permute-done.100
  627.8 8.7 %shard_map.362 = f32[27,256,256]{2,1,0:T(8,128)} custom-call(s32[9]{0:T(128)} %constant.268.clone.refs_0_, s32[2]{0:T(128)} %pad_add_fusion.refs_1_, bf16[128,2688]{1,0:T(8,128)(2,1)} %bitcast.375, bf16[128,2688]{1,0:T(8,128)(2,1)} %copy-done.25, bf16[128,2688]{1,0:T(8,128)(2,1)} %copy-done.26, bf16[128,2688]{1,0:T(8,128)(2,1)} %copy-done.27), custom_call_target="tpu_custom_call" | custom-call | bytes 10616832 | tf_op jit(solution)/shard_map/pallas_call | solution.py:748
  (563 shorter events, 205.0 us)
Async XLA Ops:
  7.2 83.0 %all-gather.6.cloned.1.call-start = ((), (), s32[]{:S(2)}) async-start(), calls=%async_computation.3 | async-start | bytes 5013504 | tf_op jit(solution)/shard_map/all_gather | solution.py:813
  10.2 236.4 %all-gather.4.cloned.1.call-start = ((), (), s32[]{:S(2)}) async-start(), calls=%async_computation.1 | async-start | bytes 22708224 | tf_op jit(solution)/shard_map/all_gather | solution.py:841
  90.2 498.9 %reduce-scatter.2.cloned.1.call-start = ((), (), s32[]{:S(2)}) async-start(), calls=%async_computation.2 | async-start | bytes 6193152 | tf_op jit(solution)/shard_map/reduce_scatter | solution.py:1026
  90.3 7.8 %collective-permute-start = (bf16[8,544,512]{2,1,0:T(8,128)(2,1)}, bf16[8,544,512]{2,1,0:T(8,128)(2,1)S(1)}, u32[]{:S(2)}, u32[]{:S(2)}) collective-permute-start(bf16[8,544,512]{2,1,0:T(8,128)(2,1)} %bitcast.351), channel_id=1, source_target_pairs={{0,1},{1,0},{2,3},{3,2},{4,5},{5,4},{6,7},{7,6},{8,9},{9,8},{10,11... | collective-permute-start | bytes 13369352 | tf_op jit(solution)/shard_map/ppermute | solution.py:37
  122.0 19.3 %collective-permute-start.9 = (bf16[384,512]{1,0:T(8,128)(2,1)S(1)}, bf16[384,512]{1,0:T(8,128)(2,1)}, u32[]{:S(2)}, u32[]{:S(2)}) collective-permute-start(bf16[384,512]{1,0:T(8,128)(2,1)S(1)} %get-tuple-element.249), channel_id=1, source_target_pairs={{4,0},{8,4},{12,8},{16,12},{20,16},{24,20},{28,24},{5,1},{9,5},{13... | collective-permute-start | bytes 1179656 | tf_op jit(solution)/shard_map/ppermute | solution.py:71
  123.3 26.7 %collective-permute-start.8 = (bf16[384,512]{1,0:T(8,128)(2,1)S(1)}, bf16[384,512]{1,0:T(8,128)(2,1)}, u32[]{:S(2)}, u32[]{:S(2)}) collective-permute-start(bf16[384,512]{1,0:T(8,128)(2,1)S(1)} %get-tuple-element.248), channel_id=1, source_target_pairs={{0,4},{4,8},{8,12},{12,16},{16,20},{20,24},{24,28},{1,5},{5,9},{9,... | collective-permute-start | bytes 1179656 | tf_op jit(solution)/shard_map/ppermute | solution.py:71
  207.8 38.7 %collective-permute-start.25 = (bf16[768,1024]{1,0:T(8,128)(2,1)}, bf16[768,1024]{1,0:T(8,128)(2,1)}, u32[]{:S(2)}, u32[]{:S(2)}) collective-permute-start(bf16[768,1024]{1,0:T(8,128)(2,1)} %get-tuple-element.206), channel_id=1, source_target_pairs={{0,2},{2,0},{1,3},{3,1},{4,6},{6,4},{5,7},{7,5},{8,10},{10,8},{9,1... | collective-permute-start | bytes 4718600 | tf_op jit(solution)/shard_map/ppermute | solution.py:37
  212.5 70.1 %collective-permute-start.24 = (bf16[768,1024]{1,0:T(8,128)(2,1)S(1)}, bf16[768,1024]{1,0:T(8,128)(2,1)}, u32[]{:S(2)}, u32[]{:S(2)}) collective-permute-start(bf16[768,1024]{1,0:T(8,128)(2,1)S(1)} %get-tuple-element.82.refs_0_), channel_id=1, source_target_pairs={{0,1},{1,0},{2,3},{3,2},{4,5},{5,4},{6,7},{7,6},{8,9},{9,8},{10,11... | collective-permute-start | bytes 4718600 | tf_op jit(solution)/shard_map/ppermute | solution.py:37
  246.5 36.0 %collective-permute-start.26 = (bf16[768,1024]{1,0:T(8,128)(2,1)}, bf16[768,1024]{1,0:T(8,128)(2,1)}, u32[]{:S(2)}, u32[]{:S(2)}) collective-permute-start(bf16[768,1024]{1,0:T(8,128)(2,1)} %collective-permute-done.25.refs_2_), channel_id=1, source_target_pairs={{0,1},{1,0},{2,3},{3,2},{4,5},{5,4},{6,7},{7,6},{8,9},{9,8},{10,11... | collective-permute-start | bytes 4718600 | tf_op jit(solution)/shard_map/ppermute | solution.py:37
  259.2 23.4 %collective-permute-start.28 = (bf16[768,256]{1,0:T(8,128)(2,1)S(1)}, bf16[768,256]{1,0:T(8,128)(2,1)S(1)}, u32[]{:S(2)}, u32[]{:S(2)}) collective-permute-start(bf16[768,256]{1,0:T(8,128)(2,1)S(1)} %get-tuple-element.246), channel_id=1, source_target_pairs={{12,0},{16,4},{20,8},{24,12},{28,16},{13,1},{17,5},{21,9},{25,13},... | collective-permute-start | bytes 1179656 | tf_op jit(solution)/shard_map/ppermute | solution.py:71
  260.5 22.1 %collective-permute-start.27 = (bf16[768,256]{1,0:T(8,128)(2,1)S(1)}, bf16[768,256]{1,0:T(8,128)(2,1)S(1)}, u32[]{:S(2)}, u32[]{:S(2)}) collective-permute-start(bf16[768,256]{1,0:T(8,128)(2,1)S(1)} %get-tuple-element.245), channel_id=1, source_target_pairs={{0,12},{4,16},{8,20},{12,24},{16,28},{1,13},{5,17},{9,21},{13,25},... | collective-permute-start | bytes 1179656 | tf_op jit(solution)/shard_map/ppermute | solution.py:71
  266.0 24.4 %collective-permute-start.29 = (bf16[768,256]{1,0:T(8,128)(2,1)S(1)}, bf16[768,256]{1,0:T(8,128)(2,1)S(1)}, u32[]{:S(2)}, u32[]{:S(2)}) collective-permute-start(bf16[768,256]{1,0:T(8,128)(2,1)S(1)} %get-tuple-element.247), channel_id=1, source_target_pairs={{0,24},{4,28},{24,0},{28,4},{1,25},{5,29},{25,1},{29,5},{2,26},{6,... | collective-permute-start | bytes 1179656 | tf_op jit(solution)/shard_map/ppermute | solution.py:71
  293.8 8.0 %collective-permute-start.32 = (f32[2,768]{1,0:T(2,128)S(1)}, f32[2,768]{1,0:T(2,128)S(1)}, u32[]{:S(2)}, u32[]{:S(2)}) collective-permute-start(f32[2,768]{1,0:T(2,128)S(1)} %fusion.99), channel_id=1, source_target_pairs={{0,2},{2,0},{1,3},{3,1},{4,6},{6,4},{5,7},{7,5},{8,10},{10,8},{9,1... | collective-permute-start | bytes 18440 | tf_op jit(solution)/shard_map/ppermute | solution.py:37
  294.4 7.4 %collective-permute-start.33 = (f32[2,768]{1,0:T(2,128)S(1)}, f32[2,768]{1,0:T(2,128)S(1)}, u32[]{:S(2)}, u32[]{:S(2)}) collective-permute-start(f32[2,768]{1,0:T(2,128)S(1)} %fusion.99), channel_id=1, source_target_pairs={{0,6},{2,4},{4,2},{6,0},{1,7},{3,5},{5,3},{7,1},{8,14},{10,12},{12... | collective-permute-start | bytes 18440 | tf_op jit(solution)/shard_map/ppermute | solution.py:37
  301.8 13.7 %collective-permute-start.35 = (f32[2,768]{1,0:T(2,128)S(1)}, f32[2,768]{1,0:T(2,128)S(1)}, u32[]{:S(2)}, u32[]{:S(2)}) collective-permute-start(f32[2,768]{1,0:T(2,128)S(1)} %add_add_fusion.8), channel_id=1, source_target_pairs={{0,16},{8,24},{16,0},{24,8},{1,17},{9,25},{17,1},{25,9},{2,18},{10... | collective-permute-start | bytes 18440 | tf_op jit(solution)/shard_map/ppermute | solution.py:37
  302.0 13.5 %collective-permute-start.36 = (f32[2,768]{1,0:T(2,128)S(1)}, f32[2,768]{1,0:T(2,128)S(1)}, u32[]{:S(2)}, u32[]{:S(2)}) collective-permute-start(f32[2,768]{1,0:T(2,128)S(1)} %add_add_fusion.8), channel_id=1, source_target_pairs={{0,24},{8,16},{16,8},{24,0},{1,25},{9,17},{17,9},{25,1},{2,26},{10... | collective-permute-start | bytes 18440 | tf_op jit(solution)/shard_map/ppermute | solution.py:37
  335.7 17.6 %collective-permute-start.47 = (bf16[768,384]{1,0:T(8,128)(2,1)S(1)}, bf16[768,384]{1,0:T(8,128)(2,1)S(1)}, u32[]{:S(2)}, u32[]{:S(2)}) collective-permute-start(bf16[768,384]{1,0:T(8,128)(2,1)S(1)} %pad_maximum_fusion.7), channel_id=1, source_target_pairs={{0,1},{1,0},{2,3},{3,2},{4,5},{5,4},{6,7},{7,6},{8,9},{9,8},{10,11... | collective-permute-start | bytes 1769480 | tf_op jit(solution)/shard_map/ppermute | solution.py:37
  336.0 19.0 %collective-permute-start.49 = (f32[66,256]{1,0:T(8,128)S(1)}, f32[66,256]{1,0:T(8,128)S(1)}, u32[]{:S(2)}, u32[]{:S(2)}) collective-permute-start(f32[66,256]{1,0:T(8,128)S(1)} %pad_maximum_fusion.13), channel_id=1, source_target_pairs={{0,1},{1,0},{2,3},{3,2},{4,5},{5,4},{6,7},{7,6},{8,9},{9,8},{10,11... | collective-permute-start | bytes 202760 | tf_op jit(solution)/shard_map/ppermute | solution.py:37
  336.6 37.1 %collective-permute-start.44 = (bf16[768,256]{1,0:T(8,128)(2,1)S(1)}, bf16[768,256]{1,0:T(8,128)(2,1)S(1)}, u32[]{:S(2)}, u32[]{:S(2)}) collective-permute-start(bf16[768,256]{1,0:T(8,128)(2,1)S(1)} %get-tuple-element.236), channel_id=1, source_target_pairs={{0,12},{4,16},{8,20},{12,24},{16,28},{1,13},{5,17},{9,21},{13,25},... | collective-permute-start | bytes 1179656 | tf_op jit(solution)/shard_map/ppermute | solution.py:71
  340.0 33.7 %collective-permute-start.45 = (bf16[768,256]{1,0:T(8,128)(2,1)S(1)}, bf16[768,256]{1,0:T(8,128)(2,1)S(1)}, u32[]{:S(2)}, u32[]{:S(2)}) collective-permute-start(bf16[768,256]{1,0:T(8,128)(2,1)S(1)} %get-tuple-element.236), channel_id=1, source_target_pairs={{12,0},{16,4},{20,8},{24,12},{28,16},{13,1},{17,5},{21,9},{25,13},... | collective-permute-start | bytes 1179656 | tf_op jit(solution)/shard_map/ppermute | solution.py:71
  341.3 32.5 %collective-permute-start.46 = (bf16[768,256]{1,0:T(8,128)(2,1)S(1)}, bf16[768,256]{1,0:T(8,128)(2,1)S(1)}, u32[]{:S(2)}, u32[]{:S(2)}) collective-permute-start(bf16[768,256]{1,0:T(8,128)(2,1)S(1)} %get-tuple-element.235), channel_id=1, source_target_pairs={{24,0},{28,4},{0,24},{4,28},{25,1},{29,5},{1,25},{5,29},{26,2},{30... | collective-permute-start | bytes 1179656 | tf_op jit(solution)/shard_map/ppermute | solution.py:71
  353.4 27.1 %collective-permute-start.48 = (bf16[768,768]{1,0:T(8,128)(2,1)S(1)}, bf16[768,768]{1,0:T(8,128)(2,1)S(1)}, u32[]{:S(2)}, u32[]{:S(2)}) collective-permute-start(bf16[768,768]{1,0:T(8,128)(2,1)S(1)} %pad_maximum_fusion.4.refs_3_), channel_id=1, source_target_pairs={{0,2},{2,0},{1,3},{3,1},{4,6},{6,4},{5,7},{7,5},{8,10},{10,8},{9,1... | collective-permute-start | bytes 3538952 | tf_op jit(solution)/shard_map/ppermute | solution.py:37
  354.9 18.8 %collective-permute-start.50 = (f32[66,256]{1,0:T(8,128)S(1)}, f32[66,256]{1,0:T(8,128)S(1)}, u32[]{:S(2)}, u32[]{:S(2)}) collective-permute-start(f32[66,256]{1,0:T(8,128)S(1)} %fusion.149), channel_id=1, source_target_pairs={{0,4},{4,0},{1,5},{5,1},{2,6},{6,2},{3,7},{7,3},{8,12},{12,8},{9,1... | collective-permute-start | bytes 202760 | tf_op jit(solution)/shard_map/ppermute | solution.py:37
  383.1 25.7 %collective-permute-start.52 = (bf16[768,512]{1,0:T(8,128)(2,1)S(1)}, bf16[768,512]{1,0:T(8,128)(2,1)S(1)}, u32[]{:S(2)}, u32[]{:S(2)}) collective-permute-start(bf16[768,512]{1,0:T(8,128)(2,1)S(1)} %pad_maximum_fusion.6.refs_5_), channel_id=1, source_target_pairs={{0,2},{2,0},{1,3},{3,1},{4,6},{6,4},{5,7},{7,5},{8,10},{10,8},{9,1... | collective-permute-start | bytes 2359304 | tf_op jit(solution)/shard_map/ppermute | solution.py:37
  390.9 17.8 %collective-permute-start.54 = (f32[66,256]{1,0:T(8,128)S(1)}, f32[66,256]{1,0:T(8,128)S(1)}, u32[]{:S(2)}, u32[]{:S(2)}) collective-permute-start(f32[66,256]{1,0:T(8,128)S(1)} %add.927), channel_id=1, source_target_pairs={{0,16},{8,24},{16,0},{24,8},{1,17},{9,25},{17,1},{25,9},{2,18},{10... | collective-permute-start | bytes 202760 | tf_op jit(solution)/shard_map/ppermute | solution.py:37
  416.8 33.0 %collective-permute-start.102 = (f32[66,256]{1,0:T(8,128)S(1)}, f32[66,256]{1,0:T(8,128)S(1)}, u32[]{:S(2)}, u32[]{:S(2)}) collective-permute-start(f32[66,256]{1,0:T(8,128)S(1)} %add.928), channel_id=1, source_target_pairs={{0,2},{2,0},{1,3},{3,1},{4,6},{6,4},{5,7},{7,5},{8,10},{10,8},{9,1... | collective-permute-start | bytes 202760 | tf_op jit(solution)/shard_map/ppermute | solution.py:37
  418.2 32.8 %collective-permute-start.60 = (f32[7,2048]{1,0:T(8,128)S(1)}, f32[7,2048]{1,0:T(8,128)S(1)}, u32[]{:S(2)}, u32[]{:S(2)}) collective-permute-start(f32[7,2048]{1,0:T(8,128)S(1)} %add_add_fusion.2), channel_id=1, source_target_pairs={{0,16},{8,24},{16,0},{24,8},{1,17},{9,25},{17,1},{25,9},{2,18},{10... | collective-permute-start | bytes 172040 | tf_op jit(solution)/shard_map/ppermute | solution.py:37
  420.6 30.4 %collective-permute-start.61 = (f32[7,2048]{1,0:T(8,128)S(1)}, f32[7,2048]{1,0:T(8,128)S(1)}, u32[]{:S(2)}, u32[]{:S(2)}) collective-permute-start(f32[7,2048]{1,0:T(8,128)S(1)} %add_add_fusion.2), channel_id=1, source_target_pairs={{0,24},{8,16},{16,8},{24,0},{1,25},{9,17},{17,9},{25,1},{2,26},{10... | collective-permute-start | bytes 172040 | tf_op jit(solution)/shard_map/ppermute | solution.py:37
  421.9 29.1 %collective-permute-start.59 = (f32[7,2048]{1,0:T(8,128)S(1)}, f32[7,2048]{1,0:T(8,128)S(1)}, u32[]{:S(2)}, u32[]{:S(2)}) collective-permute-start(f32[7,2048]{1,0:T(8,128)S(1)} %add_add_fusion.2), channel_id=1, source_target_pairs={{0,8},{8,0},{16,24},{24,16},{1,9},{9,1},{17,25},{25,17},{2,10},{10... | collective-permute-start | bytes 172040 | tf_op jit(solution)/shard_map/ppermute | solution.py:37
  500.5 27.6 %collective-permute-start.70 = (bf16[384,512]{1,0:T(8,128)(2,1)S(1)}, bf16[384,512]{1,0:T(8,128)(2,1)S(1)}, u32[]{:S(2)}, u32[]{:S(2)}) collective-permute-start(bf16[384,512]{1,0:T(8,128)(2,1)S(1)} %get-tuple-element.223), channel_id=1, source_target_pairs={{0,4},{4,8},{8,12},{12,16},{16,20},{20,24},{24,28},{1,5},{5,9},{9,... | collective-permute-start | bytes 1179656 | tf_op jit(solution)/shard_map/ppermute | solution.py:71
  502.9 25.3 %collective-permute-start.69 = (bf16[384,512]{1,0:T(8,128)(2,1)S(1)}, bf16[384,512]{1,0:T(8,128)(2,1)S(1)}, u32[]{:S(2)}, u32[]{:S(2)}) collective-permute-start(bf16[384,512]{1,0:T(8,128)(2,1)S(1)} %get-tuple-element.222), channel_id=1, source_target_pairs={{4,0},{8,4},{12,8},{16,12},{20,16},{24,20},{28,24},{5,1},{9,5},{13... | collective-permute-start | bytes 1179656 | tf_op jit(solution)/shard_map/ppermute | solution.py:71
  511.9 32.1 %collective-permute-start.78 = (bf16[8,416,512]{2,1,0:T(8,128)(2,1)S(1)}, bf16[8,416,512]{2,1,0:T(8,128)(2,1)S(1)}, u32[]{:S(2)}, u32[]{:S(2)}) collective-permute-start(bf16[8,416,512]{2,1,0:T(8,128)(2,1)S(1)} %slice_dynamic-update-slice_fusion), channel_id=1, source_target_pairs={{0,1},{1,0},{2,3},{3,2},{4,5},{5,4},{6,7},{7,6},{8,9},{9,8},{10,11... | collective-permute-start | bytes 10223624 | tf_op jit(solution)/shard_map/ppermute | solution.py:37
  545.4 20.5 %collective-permute-start.90 = (bf16[8,96,512]{2,1,0:T(8,128)(2,1)S(1)}, bf16[8,96,512]{2,1,0:T(8,128)(2,1)S(1)}, u32[]{:S(2)}, u32[]{:S(2)}) collective-permute-start(bf16[8,96,512]{2,1,0:T(8,128)(2,1)S(1)} %constant_dynamic-slice_fusion), channel_id=1, source_target_pairs={{0,2},{2,0},{1,3},{3,1},{4,6},{6,4},{5,7},{7,5},{8,10},{10,8},{9,1... | collective-permute-start | bytes 2359304 | tf_op jit(solution)/shard_map/ppermute | solution.py:37
  549.7 32.5 %collective-permute-start.79 = (bf16[8,128,512]{2,1,0:T(8,128)(2,1)S(1)}, bf16[8,128,512]{2,1,0:T(8,128)(2,1)S(1)}, u32[]{:S(2)}, u32[]{:S(2)}) collective-permute-start(bf16[8,128,512]{2,1,0:T(8,128)(2,1)S(1)} %constant_dynamic-slice_fusion.2), channel_id=1, source_target_pairs={{0,1},{1,0},{2,3},{3,2},{4,5},{5,4},{6,7},{7,6},{8,9},{9,8},{10,11... | collective-permute-start | bytes 3145736 | tf_op jit(solution)/shard_map/ppermute | solution.py:37
  549.8 32.1 %collective-permute-start.86 = (bf16[8,112,512]{2,1,0:T(8,128)(2,1)S(1)}, bf16[8,112,512]{2,1,0:T(8,128)(2,1)S(1)}, u32[]{:S(2)}, u32[]{:S(2)}) collective-permute-start(bf16[8,112,512]{2,1,0:T(8,128)(2,1)S(1)} %constant_dynamic-slice_fusion.1), channel_id=1, source_target_pairs={{0,2},{2,0},{1,3},{3,1},{4,6},{6,4},{5,7},{7,5},{8,10},{10,8},{9,1... | collective-permute-start | bytes 2752520 | tf_op jit(solution)/shard_map/ppermute | solution.py:37
  566.5 18.1 %collective-permute-start.91 = (bf16[4,96,512]{2,1,0:T(8,128)(2,1)S(1)}, bf16[4,96,512]{2,1,0:T(8,128)(2,1)S(1)}, u32[]{:S(2)}, u32[]{:S(2)}) collective-permute-start(bf16[4,96,512]{2,1,0:T(8,128)(2,1)S(1)} %dynamic-slice_bitcast_fusion.6), channel_id=1, source_target_pairs={{0,4},{4,0},{1,5},{5,1},{2,6},{6,2},{3,7},{7,3},{8,12},{12,8},{9,1... | collective-permute-start | bytes 1179656 | tf_op jit(solution)/shard_map/ppermute | solution.py:37
  583.3 15.1 %collective-permute-start.80 = (bf16[4,128,512]{2,1,0:T(8,128)(2,1)}, bf16[4,128,512]{2,1,0:T(8,128)(2,1)S(1)}, u32[]{:S(2)}, u32[]{:S(2)}) collective-permute-start(bf16[4,128,512]{2,1,0:T(8,128)(2,1)} %dynamic-slice_bitcast_fusion.4), channel_id=1, source_target_pairs={{0,4},{4,0},{1,5},{5,1},{2,6},{6,2},{3,7},{7,3},{8,12},{12,8},{9,1... | collective-permute-start | bytes 1572872 | tf_op jit(solution)/shard_map/ppermute | solution.py:37
  586.9 10.2 %collective-permute-start.93 = (bf16[96,512]{1,0:T(8,128)(2,1)S(1)}, bf16[96,512]{1,0:T(8,128)(2,1)S(1)}, u32[]{:S(2)}, u32[]{:S(2)}) collective-permute-start(bf16[96,512]{1,0:T(8,128)(2,1)S(1)} %get-tuple-element.258), channel_id=1, source_target_pairs={{0,16},{8,24},{16,0},{24,8},{1,17},{9,25},{17,1},{25,9},{2,18},{10... | collective-permute-start | bytes 294920 | tf_op jit(solution)/shard_map/ppermute | solution.py:37
  586.9 10.2 %collective-permute-start.92 = (bf16[96,512]{1,0:T(8,128)(2,1)S(1)}, bf16[96,512]{1,0:T(8,128)(2,1)S(1)}, u32[]{:S(2)}, u32[]{:S(2)}) collective-permute-start(bf16[96,512]{1,0:T(8,128)(2,1)S(1)} %get-tuple-element.256), channel_id=1, source_target_pairs={{0,8},{8,0},{16,24},{24,16},{1,9},{9,1},{17,25},{25,17},{2,10},{10... | collective-permute-start | bytes 294920 | tf_op jit(solution)/shard_map/ppermute | solution.py:37
  589.2 14.4 %collective-permute-start.87 = (bf16[128,2688]{1,0:T(8,128)(2,1)}, bf16[128,2688]{1,0:T(8,128)(2,1)S(1)}, u32[]{:S(2)}, u32[]{:S(2)}) collective-permute-start(bf16[128,2688]{1,0:T(8,128)(2,1)} %bitcast.374), channel_id=1, source_target_pairs={{0,2},{2,0},{1,3},{3,1},{4,6},{6,4},{5,7},{7,5},{8,10},{10,8},{9,1... | collective-permute-start | bytes 2064392 | tf_op jit(solution)/shard_map/ppermute | solution.py:37
  591.2 12.3 %collective-permute-start.95 = (bf16[4,112,512]{2,1,0:T(8,128)(2,1)S(1)}, bf16[4,112,512]{2,1,0:T(8,128)(2,1)S(1)}, u32[]{:S(2)}, u32[]{:S(2)}) collective-permute-start(bf16[4,112,512]{2,1,0:T(8,128)(2,1)S(1)} %dynamic-slice_bitcast_fusion.5), channel_id=1, source_target_pairs={{0,4},{4,0},{1,5},{5,1},{2,6},{6,2},{3,7},{7,3},{8,12},{12,8},{9,1... | collective-permute-start | bytes 1376264 | tf_op jit(solution)/shard_map/ppermute | solution.py:37
  598.6 7.0 %collective-permute-start.83 = (bf16[128,512]{1,0:T(8,128)(2,1)S(1)}, bf16[128,512]{1,0:T(8,128)(2,1)S(1)}, u32[]{:S(2)}, u32[]{:S(2)}) collective-permute-start(bf16[128,512]{1,0:T(8,128)(2,1)S(1)} %get-tuple-element.251), channel_id=1, source_target_pairs={{0,24},{8,16},{16,8},{24,0},{1,25},{9,17},{17,9},{25,1},{2,26},{10... | collective-permute-start | bytes 393224 | tf_op jit(solution)/shard_map/ppermute | solution.py:37
  600.7 12.2 %collective-permute-start.82 = (bf16[128,512]{1,0:T(8,128)(2,1)S(1)}, bf16[128,512]{1,0:T(8,128)(2,1)S(1)}, u32[]{:S(2)}, u32[]{:S(2)}) collective-permute-start(bf16[128,512]{1,0:T(8,128)(2,1)S(1)} %get-tuple-element.252), channel_id=1, source_target_pairs={{0,16},{8,24},{16,0},{24,8},{1,17},{9,25},{17,1},{25,9},{2,18},{10... | collective-permute-start | bytes 393224 | tf_op jit(solution)/shard_map/ppermute | solution.py:37
  601.4 11.6 %collective-permute-start.81 = (bf16[128,512]{1,0:T(8,128)(2,1)S(1)}, bf16[128,512]{1,0:T(8,128)(2,1)S(1)}, u32[]{:S(2)}, u32[]{:S(2)}) collective-permute-start(bf16[128,512]{1,0:T(8,128)(2,1)S(1)} %get-tuple-element.250), channel_id=1, source_target_pairs={{0,8},{8,0},{16,24},{24,16},{1,9},{9,1},{17,25},{25,17},{2,10},{10... | collective-permute-start | bytes 393224 | tf_op jit(solution)/shard_map/ppermute | solution.py:37
  603.6 15.7 %collective-permute-start.88 = (bf16[128,2688]{1,0:T(8,128)(2,1)S(1)}, bf16[128,2688]{1,0:T(8,128)(2,1)S(1)}, u32[]{:S(2)}, u32[]{:S(2)}) collective-permute-start(bf16[128,2688]{1,0:T(8,128)(2,1)S(1)} %bitcast.376), channel_id=1, source_target_pairs={{0,1},{1,0},{2,3},{3,2},{4,5},{5,4},{6,7},{7,6},{8,9},{9,8},{10,11... | collective-permute-start | bytes 2064392 | tf_op jit(solution)/shard_map/ppermute | solution.py:37
  603.6 15.7 %collective-permute-start.89 = (bf16[128,2688]{1,0:T(8,128)(2,1)S(1)}, bf16[128,2688]{1,0:T(8,128)(2,1)S(1)}, u32[]{:S(2)}, u32[]{:S(2)}) collective-permute-start(bf16[128,2688]{1,0:T(8,128)(2,1)S(1)} %collective-permute-done.87.refs_3_), channel_id=1, source_target_pairs={{0,1},{1,0},{2,3},{3,2},{4,5},{5,4},{6,7},{7,6},{8,9},{9,8},{10,11... | collective-permute-start | bytes 2064392 | tf_op jit(solution)/shard_map/ppermute | solution.py:37
  605.6 9.7 %collective-permute-start.98 = (bf16[112,512]{1,0:T(8,128)(2,1)S(1)}, bf16[112,512]{1,0:T(8,128)(2,1)S(1)}, u32[]{:S(2)}, u32[]{:S(2)}) collective-permute-start(bf16[112,512]{1,0:T(8,128)(2,1)S(1)} %get-tuple-element.254), channel_id=1, source_target_pairs={{0,24},{8,16},{16,8},{24,0},{1,25},{9,17},{17,9},{25,1},{2,26},{10... | collective-permute-start | bytes 344072 | tf_op jit(solution)/shard_map/ppermute | solution.py:37
  626.8 9.7 %collective-permute-start.101 = (bf16[416,512]{1,0:T(8,128)(2,1)S(1)}, bf16[416,512]{1,0:T(8,128)(2,1)S(1)}, u32[]{:S(2)}, u32[]{:S(2)}) collective-permute-start(bf16[416,512]{1,0:T(8,128)(2,1)S(1)} %pad_maximum_fusion.9), channel_id=1, source_target_pairs={{0,1},{1,0},{2,3},{3,2},{4,5},{5,4},{6,7},{7,6},{8,9},{9,8},{10,11... | collective-permute-start | bytes 1277960 | tf_op jit(solution)/shard_map/ppermute | solution.py:37
  (111 other events, 833.7 us)
Sparse Core Ops, SparseCore 0:
  10.8 79.3 all-gather.5
  93.7 150.2 all-gather.3
  449.9 119.4 reduce-scatter.1

commit v5 on v4

--- a/solution.py
+++ b/solution.py
@@ -902,6 +902,22 @@
         return jnp.tile(table, (rows, 1))
 
     masks = mask_table(group)
+    all_masks = [masks, mask_table(group ^ 1)]
+    for m in range(1, chips):
+        all_masks += [mask_table((chip ^ m) * 2 + core), mask_table((chip ^ m) * 2 + 1 - core)]
+    slot_of = jnp.full((len(terms),), -1, jnp.int32)
+    for s in range(slots):
+        slot_of = jnp.where(jnp.arange(len(terms)) == picked_term[s], tasks + s, slot_of)
+    slot_of = jnp.concatenate([centers, slot_of])
+    side_here = (side_task[:, None] == centers[None, :]).astype(full).reshape(-1)
+    vecs = jnp.pad(jnp.stack([mean3, scale3, gain_expand, bias_expand]), ((0, 4), (0, 0)))
+    side_picked = tasks + picked_term
+    grid, all_masks, slot_of, side_here, vecs, side_picked, side_task, picked_term = (
+        lax.optimization_barrier(
+            (grid, all_masks, slot_of, side_here, vecs, side_picked, side_task, picked_term)
+        )
+    )
+    masks = all_masks[0]
     moves = row_moves(terms, line)
     side_terms = head_terms(grid, heads_all, masks, tasks + picked_term, side_task, head, low)
     moved = [None] * tasks
@@ -963,9 +979,6 @@
         return [halves] + [flip(halves, [("x", m)]) for m in range(1, chips)]
 
     center_halves = from_groups(dmixed)
-    all_masks = [masks, mask_table(group ^ 1)]
-    for m in range(1, chips):
-        all_masks += [mask_table((chip ^ m) * 2 + core), mask_table((chip ^ m) * 2 + 1 - core)]
     back = [None] * len(terms)
     for task, pairs, members in moves:
         got = rows_to(dmixed[:, task * head : (task + 1) * head], [(t, f) for f, t in pairs])
@@ -978,10 +991,9 @@
         for e in sorted(set(table[s].tolist()) - {int(table[s][0])}):
             dside = jnp.where(picked_term[s] == e, back[e], dside)
         dsides.append(dside)
-    vecs = jnp.pad(jnp.stack([mean3, scale3, gain_expand, bias_expand]), ((0, 4), (0, 0)))
     dys = spread_back(dmixed, masks, centers, head, pixels)
     *center_grads, slope3, normed3 = center_back(
-        dys, heads_all, tasks, expanded, source, vecs, masks, 256
+        dys, heads_all, tasks, expanded, source, vecs, masks, 512
     )
     center_grads, slope3, normed3, turned, dsides, center_halves, class_sums = (
         lax.optimization_barrier(
@@ -999,9 +1011,8 @@
     class_sums = sum_along(class_sums, "z")
     side_halves = from_groups(dsides)
     dys = spread_back(dsides, masks, side_task, head, pixels)
-    here = (side_task[:, None] == centers[None, :]).astype(full).reshape(-1)
     shared_grads, sums = side_back(
-        dys, heads_all, tasks + picked_term, here, slot_tasks, tasks, center_grads, slope3, normed3, 256
+        dys, heads_all, side_picked, side_here, slot_tasks, tasks, center_grads, slope3, normed3, 512
     )
     sums, center_halves, side_halves, class_sums = lax.optimization_barrier(
         (sums, center_halves, side_halves, class_sums)
@@ -1014,10 +1025,6 @@
     weight_list = task_scales([summed[2 * tasks, i] for i in range(6)])
     task_weights = jnp.stack(weight_list)
 
-    slot_of = jnp.full((len(terms),), -1, jnp.int32)
-    for s in range(slots):
-        slot_of = jnp.where(jnp.arange(len(terms)) == picked_term[s], tasks + s, slot_of)
-    slot_of = jnp.concatenate([centers, slot_of])
     head_part = weight_grad(
         turned, center_halves, side_halves, all_masks, slot_of, side_task, slot_tasks, tasks
     )
@@ -1033,7 +1040,7 @@
     mid_vecs = jnp.pad(jnp.stack([mean2, scale2, gain_middle, bias_middle]), ((0, 4), (0, 0)))
     dbefore, exp_part, dout2, sums2 = expand_back(
         summed, shared_grads, slope3, normed3, vecs, masks, hidden2, exp_all, middled,
-        mid_vecs, 256,
+        mid_vecs, 512,
     )
     sums2 = all_sum(sums2[:2])
     dgain2, dbias2 = sums2[0], sums2[1]
@@ -1091,13 +1098,11 @@
     part_of[:, 1] = np.arange(tasks)
     for e, (task, side, _) in enumerate(terms):
         part_of[task, side + 1] = tasks + e
-    head_shares, head_others, later_own = lax.optimization_barrier(
-        (head_shares, head_others, later_own)
-    )
     at = jnp.stack([chip, core]).astype(jnp.int32)
     heads_out = place_shares(head_shares, head_others, jnp.asarray(part_of.reshape(-1)), at, head)
     heads_out = heads_out.reshape(tasks, 9, own, head).transpose(2, 0, 1, 3)
     later_own = jnp.concatenate([gather_x(piece) for piece in later_own], axis=0)
+    heads_out, later_own = lax.optimization_barrier((heads_out, later_own))
     later_other = flip(later_own, [("c", 1)])
     later_sum = both_halves(
         later_own.reshape(9 + ratio, mid_rows, width),

time: 653 us -> 639 us (0.979)
  waiting for transfers between devices: 241 us -> 229 us
    ppermute x93, waiting for transfers between devices: 139 us -> 128 us  [flip(): return lax.ppermute(value, names, pairs)]
    unnamed x150 -> x144, local copies, waits for them, and re-layouts: 19 us -> 19.8 us
  transfers between devices with their start and end apart: 106 -> 106, of which waited for: 59 -> 61; matrix products, arithmetic and copies ran while one was open for 15% -> 16% of each run, Pallas kernels for 21% -> 21%
where the time goes in v5:
time: 639 us; the launch traced here: 632 us
  waiting for transfers between devices  229 us (36%)
  Pallas kernels  132 us (21%)
  starting transfers between devices  126 us (20%)
  other arithmetic  45.8 us (7%)
  local copies, waits for them, and re-layouts  42.7 us (7%)
  matrix products  31.7 us (5%)
  between operations  24.9 us (4%)
    ppermute x93, waiting for transfers between devices, flip(): return lax.ppermute(value, names, pairs)  128 us
    ppermute x93, starting transfers between devices, flip(): return lax.ppermute(value, names, pairs)  93.1 us
    all_gather x1, waiting for transfers between devices, on_device(): block_mine = lax.all_gather(block_own, LINE, axis=0, tiled=False)  64.6 us
    ppermute x10, waiting for transfers between devices, rows_to(): return lax.ppermute(value, LINE, pairs)  36.7 us
    ppermute x10, starting transfers between devices, rows_to(): return lax.ppermute(value, LINE, pairs)  32.6 us
    pallas_call x1, Pallas kernels, some_weight_grad(): pl.pallas_call(lambda *refs: weight_grad_kernel(members, side_tasks, task...  25 us
    pallas_call x2, Pallas kernels, head_terms(): pl.pallas_call(terms_kernel, out_shape=jax.ShapeDtypeStruct((pixels, item...  22.9 us
    unnamed x144, local copies, waits for them, and re-layouts  19.8 us
  transfers between devices with their start and end apart: 106, of which 61 were waited for; matrix products, arithmetic and copies ran while one was open for 16% of the time, Pallas kernels for 21%

profile of v5, /device:TPU:0, one launch (start us, length us, event | category | flops | bytes accessed | tf_op | source)
XLA Modules:
  0.0 632.3 jit_solution(7179426484858817053)
XLA Ops:
  12.0 5.7 copy.86
  21.4 4.2 bitcast_multiply_fusion.refs_5_
  25.6 64.6 %all-gather.6.cloned.1.call-done = bf16[4352,512]{1,0:T(8,128)(2,1)} async-done(((bf16[544,512]{1,0:T(8,128)(2,1)}), bf16[4352,512]{1,0:T(8,128)(2,1)}) %all-gather.6.cloned.1.call-update) | async-done | bytes 4456464 | tf_op jit(solution)/shard_map/all_gather | solution.py:813
  90.3 7.7 %collective-permute-done.other_ref.refs_2_ = bf16[8,544,512]{2,1,0:T(8,128)(2,1)S(1)} collective-permute-done((bf16[8,544,512]{2,1,0:T(8,128)(2,1)}, bf16[8,544,512]{2,1,0:T(8,128)(2,1)S(1)}, u32[]{:S(2)}, u32[]{:S(2)}) %collective-permute-start) | collective-permute-done | bytes 4456480 | tf_op jit(solution)/shard_map/ppermute | solution.py:37
  100.2 3.2 shard_map.351
  103.4 3.4 fusion.110
  123.3 5.5 collective-permute-start.8
  128.9 6.9 %shard_map.352 = (bf16[1536,1536]{1,0:T(8,128)(2,1)}, bf16[512,2048]{1,0:T(8,128)(2,1)}) custom-call(s32[1]{0:T(128)} %bitcast.8.core_ref.refs_0_, bf16[8,544,512]{2,1,0:T(8,128)(2,1)} %bitcast.357, bf16[8,544,512]{2,1,0:T(8,128)(2,1)} %copy-done.8), custom_call_target="tpu_custom_call" | custom-call | bytes 17825792 | tf_op jit(solution)/shard_map/pallas_call | solution.py:707
  135.9 5.4 collective-permute-done.9
  141.3 8.7 %collective-permute-done.8 = bf16[384,512]{1,0:T(8,128)(2,1)} collective-permute-done((bf16[384,512]{1,0:T(8,128)(2,1)S(1)}, bf16[384,512]{1,0:T(8,128)(2,1)}, u32[]{:S(2)}, u32[]{:S(2)}) %collective-permute-start.8) | collective-permute-done | bytes 393248 | tf_op jit(solution)/shard_map/ppermute | solution.py:71
  149.9 6.4 %fusion.46 = f32[768,1536]{1,0:T(8,128)S(1)} fusion(bf16[1536,1536]{1,0:T(8,128)(2,1)} %get-tuple-element.80, bf16[384,512]{1,0:T(8,128)(2,1)} %collective-permute-done.9, bf16[768,512]{1,0:T(8,128)(2,1)S(1)} %multiply_convert_fusion.6, bf16[384,512]{1,0:T(8,128)(2,1)} %collective-permute-done.8), kind=kOutput, calls=%fused_computation.155 | convolution fusion | flops 3635675136 | bytes 11010048 | tf_op jit(solution)/shard_map/dot_general | solution.py:227
  160.3 2.8 collective-permute-start.13
  171.3 3.4 collective-permute-done.16
  175.4 4.5 fusion.108
  195.9 5.3 multiply_convert_fusion.x_ref
  219.8 26.7 %collective-permute-done.25.refs_2_ = bf16[768,1024]{1,0:T(8,128)(2,1)} collective-permute-done((bf16[768,1024]{1,0:T(8,128)(2,1)}, bf16[768,1024]{1,0:T(8,128)(2,1)}, u32[]{:S(2)}, u32[]{:S(2)}) %collective-permute-start.25) | collective-permute-done | bytes 1572896 | tf_op jit(solution)/shard_map/ppermute | solution.py:37
  247.1 9.9 %shard_map.354 = bf16[768,512]{1,0:T(8,128)(2,1)} custom-call(s32[2]{0:T(128)} %broadcast_add_fusion.picked_ref, s32[2]{0:T(128)} %copy-done.37, bf16[768,2048]{1,0:T(8,128)(2,1)} %copy-done.3, bf16[2048,5376]{1,0:T(8,128)(2,1)} %all-gather.4.cloned.1.call-done.w_ref.refs_1_.refs_2_.refs_3_.refs_4_, f32[768,128]{1,0:T(8,128)} %bitcast.348), custom_call_target="tpu_custom_call" | custom-call | flops 4831838208 | bytes 9437184 | tf_op jit(solution)/shard_map/pallas_call | solution.py:272
  260.2 5.5 collective-permute-start.27
  265.6 3.1 collective-permute-start.29
  269.3 12.9 %shard_map.353 = f32[768,768]{1,0:T(8,128)} custom-call(s32[3]{0:T(128)} %iota.36.picked_ref.task_ref, s32[3]{0:T(128)} %iota.36.picked_ref.task_ref, bf16[768,2048]{1,0:T(8,128)(2,1)} %copy-done.3, bf16[2048,5376]{1,0:T(8,128)(2,1)} %all-gather.4.cloned.1.call-done.w_ref.refs_1_.refs_2_.refs_3_.refs_4_, f32[768,128]{1,0:T(8,128)} %bitcast.349), custom_call_target="tpu_custom_call" | custom-call | flops 7247757312 | bytes 12582912 | tf_op jit(solution)/shard_map/pallas_call | solution.py:272
  282.3 7.7 %collective-permute-done.29 = bf16[768,256]{1,0:T(8,128)(2,1)S(1)} collective-permute-done((bf16[768,256]{1,0:T(8,128)(2,1)S(1)}, bf16[768,256]{1,0:T(8,128)(2,1)S(1)}, u32[]{:S(2)}, u32[]{:S(2)}) %collective-permute-start.29) | collective-permute-done | bytes 393248 | tf_op jit(solution)/shard_map/ppermute | solution.py:71
  294.1 3.3 collective-permute-start.33
  301.2 5.0 collective-permute-start.36
  309.2 5.5 shard_map.357.refs_2_
  340.5 8.6 %collective-permute-start.46 = (bf16[768,256]{1,0:T(8,128)(2,1)S(1)}, bf16[768,256]{1,0:T(8,128)(2,1)S(1)}, u32[]{:S(2)}, u32[]{:S(2)}) collective-permute-start(bf16[768,256]{1,0:T(8,128)(2,1)S(1)} %get-tuple-element.249), channel_id=1, source_target_pairs={{24,0},{28,4},{0,24},{4,28},{25,1},{29,5},{1,25},{5,29},{26,2},{30... | collective-permute-start | bytes 1179656 | tf_op jit(solution)/shard_map/ppermute | solution.py:71
  349.6 4.9 shard_map.355.refs_0_
  355.4 18.0 %shard_map.356 = (bf16[768,2048]{1,0:T(8,128)(2,1)}, bf16[768,2048]{1,0:T(8,128)(2,1)}, bf16[768,2048]{1,0:T(8,128)(2,1)}, bf16[768,2048]{1,0:T(8,128)(2,1)}, bf16[768,2048]{1,0:T(8,128)(2,1)}) custom-call(bf16[768,2304]{1,0:T(8,128)(2,1)} %shard_map.355.refs_0_, bf16[2048,5376]{1,0:T(8,128)(2,1)} %all-gather.4.cloned.1.call-done.w_ref.refs_1_.refs_2_.refs_3_.refs_4_, ...), custom_call_target="tpu_custom_call" | custom-call | flops 7247757312 | bytes 25165824 | tf_op jit(solution)/shard_map/pallas_call | solution.py:354
  374.9 6.8 %collective-permute-done.48.refs_4_ = bf16[768,768]{1,0:T(8,128)(2,1)S(1)} collective-permute-done((bf16[768,768]{1,0:T(8,128)(2,1)S(1)}, bf16[768,768]{1,0:T(8,128)(2,1)S(1)}, u32[]{:S(2)}, u32[]{:S(2)}) %collective-permute-start.48) | collective-permute-done | bytes 1179680 | tf_op jit(solution)/shard_map/ppermute | solution.py:37
  385.8 3.6 shard_map.358.refs_2_
  390.3 16.6 %shard_map.359 = (bf16[768,2048]{1,0:T(8,128)(2,1)}, bf16[768,2048]{1,0:T(8,128)(2,1)}, f32[16,2048]{1,0:T(8,128)}) custom-call(s32[2]{0:T(128)} %broadcast_add_fusion.1.refs_0_, f32[6]{0:T(128)} %reshape.412.refs_1_, bf16[768,1536]{1,0:T(8,128)(2,1)} %shard_map.358.refs_2_, ...), custom_call_target="tpu_custom_call" | custom-call | flops 4831838208 | bytes 22020096 | tf_op jit(solution)/shard_map/pallas_call | solution.py:414
  420.8 25.0 %shard_map.360 = bf16[1024,2688]{1,0:T(8,128)(2,1)} custom-call(s32[7]{0:T(128)} %and_select_fusion.refs_0_, s32[2]{0:T(128)} %copy-done.37, bf16[1024,3072]{1,0:T(8,128)(2,1)} %shard_map.357.refs_2_, bf16[768,768]{1,0:T(8,128)(2,1)} %copy-done.20, bf16[768,768]{1,0:T(8,128)(2,1)} %copy-done.43, bf16[768,512]{1,0:T(8,128)(2,1)} %copy-done.23, ...), custom_call_target="tpu_custom_call" | custom-call | flops 12079595520 | bytes 11796480 | tf_op jit(solution)/shard_map/pallas_call | solution.py:635
  447.8 16.5 %shard_map.361 = (bf16[768,2048]{1,0:T(8,128)(2,1)}, bf16[512,2048]{1,0:T(8,128)(2,1)}, f32[768,512]{1,0:T(8,128)}, f32[8,512]{1,0:T(8,128)}) custom-call(f32[7,2048]{1,0:T(8,128)} %add_add_fusion.1.refs_0_.refs_4_, bf16[768,2048]{1,0:T(8,128)(2,1)} %get-tuple-element.122.refs_1_, bf16[768,2048]{1,0:T(8,128)(2,1)} %get-tuple-element.123.refs_2_, ...), custom_call_target="tpu_custom_call" | custom-call | flops 1572864 | bytes 10752 | tf_op jit(solution)/shard_map/pallas_call | solution.py:496
  478.8 2.6 collective-permute-start.67
  484.0 3.0 collective-permute-done.68
  491.4 3.8 fusion.132
  495.3 3.1 collective-permute-start.70
  499.9 5.0 convolution_convert_fusion
  507.9 14.9 %collective-permute-done.70 = bf16[384,512]{1,0:T(8,128)(2,1)S(1)} collective-permute-done((bf16[384,512]{1,0:T(8,128)(2,1)S(1)}, bf16[384,512]{1,0:T(8,128)(2,1)S(1)}, u32[]{:S(2)}, u32[]{:S(2)}) %collective-permute-start.70) | collective-permute-done | bytes 393248 | tf_op jit(solution)/shard_map/ppermute | solution.py:71
  526.4 2.9 collective-permute-start.74
  533.0 3.4 collective-permute-start.77
  546.9 4.6 convert_add_fusion
  551.5 10.6 %collective-permute-done.90 = bf16[8,96,512]{2,1,0:T(8,128)(2,1)S(1)} collective-permute-done((bf16[8,96,512]{2,1,0:T(8,128)(2,1)S(1)}, bf16[8,96,512]{2,1,0:T(8,128)(2,1)S(1)}, u32[]{:S(2)}, u32[]{:S(2)}) %collective-permute-start.90) | collective-permute-done | bytes 786464 | tf_op jit(solution)/shard_map/ppermute | solution.py:37
  565.8 6.8 %collective-permute-done.91 = bf16[4,96,512]{2,1,0:T(8,128)(2,1)S(1)} collective-permute-done((bf16[4,96,512]{2,1,0:T(8,128)(2,1)S(1)}, bf16[4,96,512]{2,1,0:T(8,128)(2,1)S(1)}, u32[]{:S(2)}, u32[]{:S(2)}) %collective-permute-start.91) | collective-permute-done | bytes 393248 | tf_op jit(solution)/shard_map/ppermute | solution.py:37
  574.6 2.6 collective-permute-start.92
  583.6 3.6 collective-permute-done.95
  595.3 3.1 collective-permute-start.98
  607.1 3.4 collective-permute-done.100
  612.4 8.7 %shard_map.362 = f32[27,256,256]{2,1,0:T(8,128)} custom-call(s32[9]{0:T(128)} %constant.273.clone.refs_0_, s32[2]{0:T(128)} %pad_add_fusion.1.refs_1_, bf16[128,2688]{1,0:T(8,128)(2,1)} %bitcast.378, bf16[128,2688]{1,0:T(8,128)(2,1)} %copy-done.25, bf16[128,2688]{1,0:T(8,128)(2,1)} %copy-done.26, bf16[128,2688]{1,0:T(8,128)(2,1)} %copy-done.27), custom_call_target="tpu_custom_call" | custom-call | bytes 10616832 | tf_op jit(solution)/shard_map/pallas_call | solution.py:748
  (561 shorter events, 207.8 us)
Async XLA Ops:
  7.2 83.0 %all-gather.6.cloned.1.call-start = ((), (), s32[]{:S(2)}) async-start(), calls=%async_computation.3 | async-start | bytes 5013504 | tf_op jit(solution)/shard_map/all_gather | solution.py:813
  10.2 236.9 %all-gather.4.cloned.1.call-start = ((), (), s32[]{:S(2)}) async-start(), calls=%async_computation.1 | async-start | bytes 22708224 | tf_op jit(solution)/shard_map/all_gather | solution.py:841
  90.2 492.0 %reduce-scatter.2.cloned.1.call-start = ((), (), s32[]{:S(2)}) async-start(), calls=%async_computation.2 | async-start | bytes 6193152 | tf_op jit(solution)/shard_map/reduce_scatter | solution.py:1033
  90.3 7.8 %collective-permute-start = (bf16[8,544,512]{2,1,0:T(8,128)(2,1)}, bf16[8,544,512]{2,1,0:T(8,128)(2,1)S(1)}, u32[]{:S(2)}, u32[]{:S(2)}) collective-permute-start(bf16[8,544,512]{2,1,0:T(8,128)(2,1)} %bitcast.355), channel_id=1, source_target_pairs={{0,1},{1,0},{2,3},{3,2},{4,5},{5,4},{6,7},{7,6},{8,9},{9,8},{10,11... | collective-permute-start | bytes 13369352 | tf_op jit(solution)/shard_map/ppermute | solution.py:37
  122.0 19.3 %collective-permute-start.9 = (bf16[384,512]{1,0:T(8,128)(2,1)S(1)}, bf16[384,512]{1,0:T(8,128)(2,1)}, u32[]{:S(2)}, u32[]{:S(2)}) collective-permute-start(bf16[384,512]{1,0:T(8,128)(2,1)S(1)} %get-tuple-element.263), channel_id=1, source_target_pairs={{4,0},{8,4},{12,8},{16,12},{20,16},{24,20},{28,24},{5,1},{9,5},{13... | collective-permute-start | bytes 1179656 | tf_op jit(solution)/shard_map/ppermute | solution.py:71
  123.3 26.7 %collective-permute-start.8 = (bf16[384,512]{1,0:T(8,128)(2,1)S(1)}, bf16[384,512]{1,0:T(8,128)(2,1)}, u32[]{:S(2)}, u32[]{:S(2)}) collective-permute-start(bf16[384,512]{1,0:T(8,128)(2,1)S(1)} %get-tuple-element.262), channel_id=1, source_target_pairs={{0,4},{4,8},{8,12},{12,16},{16,20},{20,24},{24,28},{1,5},{5,9},{9,... | collective-permute-start | bytes 1179656 | tf_op jit(solution)/shard_map/ppermute | solution.py:71
  207.8 38.8 %collective-permute-start.25 = (bf16[768,1024]{1,0:T(8,128)(2,1)}, bf16[768,1024]{1,0:T(8,128)(2,1)}, u32[]{:S(2)}, u32[]{:S(2)}) collective-permute-start(bf16[768,1024]{1,0:T(8,128)(2,1)} %get-tuple-element.220), channel_id=1, source_target_pairs={{0,2},{2,0},{1,3},{3,1},{4,6},{6,4},{5,7},{7,5},{8,10},{10,8},{9,1... | collective-permute-start | bytes 4718600 | tf_op jit(solution)/shard_map/ppermute | solution.py:37
  219.8 62.4 %collective-permute-start.24 = (bf16[768,1024]{1,0:T(8,128)(2,1)S(1)}, bf16[768,1024]{1,0:T(8,128)(2,1)}, u32[]{:S(2)}, u32[]{:S(2)}) collective-permute-start(bf16[768,1024]{1,0:T(8,128)(2,1)S(1)} %get-tuple-element.96.refs_0_), channel_id=1, source_target_pairs={{0,1},{1,0},{2,3},{3,2},{4,5},{5,4},{6,7},{7,6},{8,9},{9,8},{10,11... | collective-permute-start | bytes 4718600 | tf_op jit(solution)/shard_map/ppermute | solution.py:37
  246.5 35.7 %collective-permute-start.26 = (bf16[768,1024]{1,0:T(8,128)(2,1)}, bf16[768,1024]{1,0:T(8,128)(2,1)}, u32[]{:S(2)}, u32[]{:S(2)}) collective-permute-start(bf16[768,1024]{1,0:T(8,128)(2,1)} %collective-permute-done.25.refs_2_), channel_id=1, source_target_pairs={{0,1},{1,0},{2,3},{3,2},{4,5},{5,4},{6,7},{7,6},{8,9},{9,8},{10,11... | collective-permute-start | bytes 4718600 | tf_op jit(solution)/shard_map/ppermute | solution.py:37
  258.9 23.4 %collective-permute-start.28 = (bf16[768,256]{1,0:T(8,128)(2,1)S(1)}, bf16[768,256]{1,0:T(8,128)(2,1)S(1)}, u32[]{:S(2)}, u32[]{:S(2)}) collective-permute-start(bf16[768,256]{1,0:T(8,128)(2,1)S(1)} %get-tuple-element.260), channel_id=1, source_target_pairs={{12,0},{16,4},{20,8},{24,12},{28,16},{13,1},{17,5},{21,9},{25,13},... | collective-permute-start | bytes 1179656 | tf_op jit(solution)/shard_map/ppermute | solution.py:71
  260.2 22.1 %collective-permute-start.27 = (bf16[768,256]{1,0:T(8,128)(2,1)S(1)}, bf16[768,256]{1,0:T(8,128)(2,1)S(1)}, u32[]{:S(2)}, u32[]{:S(2)}) collective-permute-start(bf16[768,256]{1,0:T(8,128)(2,1)S(1)} %get-tuple-element.259), channel_id=1, source_target_pairs={{0,12},{4,16},{8,20},{12,24},{16,28},{1,13},{5,17},{9,21},{13,25},... | collective-permute-start | bytes 1179656 | tf_op jit(solution)/shard_map/ppermute | solution.py:71
  265.6 24.4 %collective-permute-start.29 = (bf16[768,256]{1,0:T(8,128)(2,1)S(1)}, bf16[768,256]{1,0:T(8,128)(2,1)S(1)}, u32[]{:S(2)}, u32[]{:S(2)}) collective-permute-start(bf16[768,256]{1,0:T(8,128)(2,1)S(1)} %get-tuple-element.261), channel_id=1, source_target_pairs={{0,24},{4,28},{24,0},{28,4},{1,25},{5,29},{25,1},{29,5},{2,26},{6,... | collective-permute-start | bytes 1179656 | tf_op jit(solution)/shard_map/ppermute | solution.py:71
  301.1 13.6 %collective-permute-start.35 = (f32[2,768]{1,0:T(2,128)S(1)}, f32[2,768]{1,0:T(2,128)S(1)}, u32[]{:S(2)}, u32[]{:S(2)}) collective-permute-start(f32[2,768]{1,0:T(2,128)S(1)} %add_add_fusion.8), channel_id=1, source_target_pairs={{0,16},{8,24},{16,0},{24,8},{1,17},{9,25},{17,1},{25,9},{2,18},{10... | collective-permute-start | bytes 18440 | tf_op jit(solution)/shard_map/ppermute | solution.py:37
  301.2 13.5 %collective-permute-start.36 = (f32[2,768]{1,0:T(2,128)S(1)}, f32[2,768]{1,0:T(2,128)S(1)}, u32[]{:S(2)}, u32[]{:S(2)}) collective-permute-start(f32[2,768]{1,0:T(2,128)S(1)} %add_add_fusion.8), channel_id=1, source_target_pairs={{0,24},{8,16},{16,8},{24,0},{1,25},{9,17},{17,9},{25,1},{2,26},{10... | collective-permute-start | bytes 18440 | tf_op jit(solution)/shard_map/ppermute | solution.py:37
  306.2 8.5 %collective-permute-start.34 = (f32[2,768]{1,0:T(2,128)S(1)}, f32[2,768]{1,0:T(2,128)S(1)}, u32[]{:S(2)}, u32[]{:S(2)}) collective-permute-start(f32[2,768]{1,0:T(2,128)S(1)} %add_add_fusion.8), channel_id=1, source_target_pairs={{0,8},{8,0},{16,24},{24,16},{1,9},{9,1},{17,25},{25,17},{2,10},{10... | collective-permute-start | bytes 18440 | tf_op jit(solution)/shard_map/ppermute | solution.py:37
  336.7 17.7 %collective-permute-start.47 = (bf16[768,384]{1,0:T(8,128)(2,1)S(1)}, bf16[768,384]{1,0:T(8,128)(2,1)S(1)}, u32[]{:S(2)}, u32[]{:S(2)}) collective-permute-start(bf16[768,384]{1,0:T(8,128)(2,1)S(1)} %pad_maximum_fusion.7), channel_id=1, source_target_pairs={{0,1},{1,0},{2,3},{3,2},{4,5},{5,4},{6,7},{7,6},{8,9},{9,8},{10,11... | collective-permute-start | bytes 1769480 | tf_op jit(solution)/shard_map/ppermute | solution.py:37
  337.0 18.2 %collective-permute-start.49 = (f32[66,256]{1,0:T(8,128)S(1)}, f32[66,256]{1,0:T(8,128)S(1)}, u32[]{:S(2)}, u32[]{:S(2)}) collective-permute-start(f32[66,256]{1,0:T(8,128)S(1)} %pad_maximum_fusion.13), channel_id=1, source_target_pairs={{0,1},{1,0},{2,3},{3,2},{4,5},{5,4},{6,7},{7,6},{8,9},{9,8},{10,11... | collective-permute-start | bytes 202760 | tf_op jit(solution)/shard_map/ppermute | solution.py:37
  337.7 35.7 %collective-permute-start.44 = (bf16[768,256]{1,0:T(8,128)(2,1)S(1)}, bf16[768,256]{1,0:T(8,128)(2,1)S(1)}, u32[]{:S(2)}, u32[]{:S(2)}) collective-permute-start(bf16[768,256]{1,0:T(8,128)(2,1)S(1)} %get-tuple-element.250), channel_id=1, source_target_pairs={{0,12},{4,16},{8,20},{12,24},{16,28},{1,13},{5,17},{9,21},{13,25},... | collective-permute-start | bytes 1179656 | tf_op jit(solution)/shard_map/ppermute | solution.py:71
  339.2 34.3 %collective-permute-start.45 = (bf16[768,256]{1,0:T(8,128)(2,1)S(1)}, bf16[768,256]{1,0:T(8,128)(2,1)S(1)}, u32[]{:S(2)}, u32[]{:S(2)}) collective-permute-start(bf16[768,256]{1,0:T(8,128)(2,1)S(1)} %get-tuple-element.250), channel_id=1, source_target_pairs={{12,0},{16,4},{20,8},{24,12},{28,16},{13,1},{17,5},{21,9},{25,13},... | collective-permute-start | bytes 1179656 | tf_op jit(solution)/shard_map/ppermute | solution.py:71
  340.5 33.0 %collective-permute-start.46 = (bf16[768,256]{1,0:T(8,128)(2,1)S(1)}, bf16[768,256]{1,0:T(8,128)(2,1)S(1)}, u32[]{:S(2)}, u32[]{:S(2)}) collective-permute-start(bf16[768,256]{1,0:T(8,128)(2,1)S(1)} %get-tuple-element.249), channel_id=1, source_target_pairs={{24,0},{28,4},{0,24},{4,28},{25,1},{29,5},{1,25},{5,29},{26,2},{30... | collective-permute-start | bytes 1179656 | tf_op jit(solution)/shard_map/ppermute | solution.py:71
  354.6 27.1 %collective-permute-start.48 = (bf16[768,768]{1,0:T(8,128)(2,1)S(1)}, bf16[768,768]{1,0:T(8,128)(2,1)S(1)}, u32[]{:S(2)}, u32[]{:S(2)}) collective-permute-start(bf16[768,768]{1,0:T(8,128)(2,1)S(1)} %pad_maximum_fusion.4.refs_3_), channel_id=1, source_target_pairs={{0,2},{2,0},{1,3},{3,1},{4,6},{6,4},{5,7},{7,5},{8,10},{10,8},{9,1... | collective-permute-start | bytes 3538952 | tf_op jit(solution)/shard_map/ppermute | solution.py:37
  355.2 18.1 %collective-permute-start.50 = (f32[66,256]{1,0:T(8,128)S(1)}, f32[66,256]{1,0:T(8,128)S(1)}, u32[]{:S(2)}, u32[]{:S(2)}) collective-permute-start(f32[66,256]{1,0:T(8,128)S(1)} %fusion.151), channel_id=1, source_target_pairs={{0,4},{4,0},{1,5},{5,1},{2,6},{6,2},{3,7},{7,3},{8,12},{12,8},{9,1... | collective-permute-start | bytes 202760 | tf_op jit(solution)/shard_map/ppermute | solution.py:37
  383.8 23.2 %collective-permute-start.52 = (bf16[768,512]{1,0:T(8,128)(2,1)S(1)}, bf16[768,512]{1,0:T(8,128)(2,1)S(1)}, u32[]{:S(2)}, u32[]{:S(2)}) collective-permute-start(bf16[768,512]{1,0:T(8,128)(2,1)S(1)} %pad_maximum_fusion.6.refs_5_), channel_id=1, source_target_pairs={{0,2},{2,0},{1,3},{3,1},{4,6},{6,4},{5,7},{7,5},{8,10},{10,8},{9,1... | collective-permute-start | bytes 2359304 | tf_op jit(solution)/shard_map/ppermute | solution.py:37
  389.5 17.4 %collective-permute-start.54 = (f32[66,256]{1,0:T(8,128)S(1)}, f32[66,256]{1,0:T(8,128)S(1)}, u32[]{:S(2)}, u32[]{:S(2)}) collective-permute-start(f32[66,256]{1,0:T(8,128)S(1)} %add.929), channel_id=1, source_target_pairs={{0,16},{8,24},{16,0},{24,8},{1,17},{9,25},{17,1},{25,9},{2,18},{10... | collective-permute-start | bytes 202760 | tf_op jit(solution)/shard_map/ppermute | solution.py:37
  409.6 6.7 %collective-permute-start.57 = (f32[7,2048]{1,0:T(8,128)S(1)}, f32[7,2048]{1,0:T(8,128)S(1)}, u32[]{:S(2)}, u32[]{:S(2)}) collective-permute-start(f32[7,2048]{1,0:T(8,128)S(1)} %fusion.150), channel_id=1, source_target_pairs={{0,2},{2,0},{1,3},{3,1},{4,6},{6,4},{5,7},{7,5},{8,10},{10,8},{9,1... | collective-permute-start | bytes 172040 | tf_op jit(solution)/shard_map/ppermute | solution.py:37
  414.9 30.9 %collective-permute-start.102 = (f32[66,256]{1,0:T(8,128)S(1)}, f32[66,256]{1,0:T(8,128)S(1)}, u32[]{:S(2)}, u32[]{:S(2)}) collective-permute-start(f32[66,256]{1,0:T(8,128)S(1)} %add.930), channel_id=1, source_target_pairs={{0,2},{2,0},{1,3},{3,1},{4,6},{6,4},{5,7},{7,5},{8,10},{10,8},{9,1... | collective-permute-start | bytes 202760 | tf_op jit(solution)/shard_map/ppermute | solution.py:37
  416.7 30.4 %collective-permute-start.60 = (f32[7,2048]{1,0:T(8,128)S(1)}, f32[7,2048]{1,0:T(8,128)S(1)}, u32[]{:S(2)}, u32[]{:S(2)}) collective-permute-start(f32[7,2048]{1,0:T(8,128)S(1)} %add_add_fusion.2), channel_id=1, source_target_pairs={{0,16},{8,24},{16,0},{24,8},{1,17},{9,25},{17,1},{25,9},{2,18},{10... | collective-permute-start | bytes 172040 | tf_op jit(solution)/shard_map/ppermute | solution.py:37
  418.9 28.1 %collective-permute-start.61 = (f32[7,2048]{1,0:T(8,128)S(1)}, f32[7,2048]{1,0:T(8,128)S(1)}, u32[]{:S(2)}, u32[]{:S(2)}) collective-permute-start(f32[7,2048]{1,0:T(8,128)S(1)} %add_add_fusion.2), channel_id=1, source_target_pairs={{0,24},{8,16},{16,8},{24,0},{1,25},{9,17},{17,9},{25,1},{2,26},{10... | collective-permute-start | bytes 172040 | tf_op jit(solution)/shard_map/ppermute | solution.py:37
  420.3 26.8 %collective-permute-start.59 = (f32[7,2048]{1,0:T(8,128)S(1)}, f32[7,2048]{1,0:T(8,128)S(1)}, u32[]{:S(2)}, u32[]{:S(2)}) collective-permute-start(f32[7,2048]{1,0:T(8,128)S(1)} %add_add_fusion.2), channel_id=1, source_target_pairs={{0,8},{8,0},{16,24},{24,16},{1,9},{9,1},{17,25},{25,17},{2,10},{10... | collective-permute-start | bytes 172040 | tf_op jit(solution)/shard_map/ppermute | solution.py:37
  465.0 6.8 %collective-permute-start.62 = (f32[2,512]{1,0:T(2,128)S(1)}, f32[2,512]{1,0:T(2,128)S(1)}, u32[]{:S(2)}, u32[]{:S(2)}) collective-permute-start(f32[2,512]{1,0:T(2,128)S(1)} %slice.497), channel_id=1, source_target_pairs={{0,1},{1,0},{2,3},{3,2},{4,5},{5,4},{6,7},{7,6},{8,9},{9,8},{10,11... | collective-permute-start | bytes 12296 | tf_op jit(solution)/shard_map/ppermute | solution.py:37
  495.3 27.4 %collective-permute-start.70 = (bf16[384,512]{1,0:T(8,128)(2,1)S(1)}, bf16[384,512]{1,0:T(8,128)(2,1)S(1)}, u32[]{:S(2)}, u32[]{:S(2)}) collective-permute-start(bf16[384,512]{1,0:T(8,128)(2,1)S(1)} %get-tuple-element.237), channel_id=1, source_target_pairs={{0,4},{4,8},{8,12},{12,16},{16,20},{20,24},{24,28},{1,5},{5,9},{9,... | collective-permute-start | bytes 1179656 | tf_op jit(solution)/shard_map/ppermute | solution.py:71
  498.4 24.4 %collective-permute-start.69 = (bf16[384,512]{1,0:T(8,128)(2,1)S(1)}, bf16[384,512]{1,0:T(8,128)(2,1)S(1)}, u32[]{:S(2)}, u32[]{:S(2)}) collective-permute-start(bf16[384,512]{1,0:T(8,128)(2,1)S(1)} %get-tuple-element.236), channel_id=1, source_target_pairs={{4,0},{8,4},{12,8},{16,12},{20,16},{24,20},{28,24},{5,1},{9,5},{13... | collective-permute-start | bytes 1179656 | tf_op jit(solution)/shard_map/ppermute | solution.py:71
  507.4 32.7 %collective-permute-start.78 = (bf16[8,416,512]{2,1,0:T(8,128)(2,1)S(1)}, bf16[8,416,512]{2,1,0:T(8,128)(2,1)S(1)}, u32[]{:S(2)}, u32[]{:S(2)}) collective-permute-start(bf16[8,416,512]{2,1,0:T(8,128)(2,1)S(1)} %slice_dynamic-update-slice_fusion), channel_id=1, source_target_pairs={{0,1},{1,0},{2,3},{3,2},{4,5},{5,4},{6,7},{7,6},{8,9},{9,8},{10,11... | collective-permute-start | bytes 10223624 | tf_op jit(solution)/shard_map/ppermute | solution.py:37
  541.5 20.5 %collective-permute-start.90 = (bf16[8,96,512]{2,1,0:T(8,128)(2,1)S(1)}, bf16[8,96,512]{2,1,0:T(8,128)(2,1)S(1)}, u32[]{:S(2)}, u32[]{:S(2)}) collective-permute-start(bf16[8,96,512]{2,1,0:T(8,128)(2,1)S(1)} %constant_dynamic-slice_fusion), channel_id=1, source_target_pairs={{0,2},{2,0},{1,3},{3,1},{4,6},{6,4},{5,7},{7,5},{8,10},{10,8},{9,1... | collective-permute-start | bytes 2359304 | tf_op jit(solution)/shard_map/ppermute | solution.py:37
  545.4 18.5 %collective-permute-start.79 = (bf16[8,128,512]{2,1,0:T(8,128)(2,1)S(1)}, bf16[8,128,512]{2,1,0:T(8,128)(2,1)S(1)}, u32[]{:S(2)}, u32[]{:S(2)}) collective-permute-start(bf16[8,128,512]{2,1,0:T(8,128)(2,1)S(1)} %constant_dynamic-slice_fusion.2), channel_id=1, source_target_pairs={{0,1},{1,0},{2,3},{3,2},{4,5},{5,4},{6,7},{7,6},{8,9},{9,8},{10,11... | collective-permute-start | bytes 3145736 | tf_op jit(solution)/shard_map/ppermute | solution.py:37
  545.6 33.0 %collective-permute-start.86 = (bf16[8,112,512]{2,1,0:T(8,128)(2,1)S(1)}, bf16[8,112,512]{2,1,0:T(8,128)(2,1)S(1)}, u32[]{:S(2)}, u32[]{:S(2)}) collective-permute-start(bf16[8,112,512]{2,1,0:T(8,128)(2,1)S(1)} %constant_dynamic-slice_fusion.1), channel_id=1, source_target_pairs={{0,2},{2,0},{1,3},{3,1},{4,6},{6,4},{5,7},{7,5},{8,10},{10,8},{9,1... | collective-permute-start | bytes 2752520 | tf_op jit(solution)/shard_map/ppermute | solution.py:37
  562.5 10.0 %collective-permute-start.91 = (bf16[4,96,512]{2,1,0:T(8,128)(2,1)S(1)}, bf16[4,96,512]{2,1,0:T(8,128)(2,1)S(1)}, u32[]{:S(2)}, u32[]{:S(2)}) collective-permute-start(bf16[4,96,512]{2,1,0:T(8,128)(2,1)S(1)} %dynamic-slice_bitcast_fusion.6), channel_id=1, source_target_pairs={{0,4},{4,0},{1,5},{5,1},{2,6},{6,2},{3,7},{7,3},{8,12},{12,8},{9,1... | collective-permute-start | bytes 1179656 | tf_op jit(solution)/shard_map/ppermute | solution.py:37
  565.0 22.2 %collective-permute-start.80 = (bf16[4,128,512]{2,1,0:T(8,128)(2,1)}, bf16[4,128,512]{2,1,0:T(8,128)(2,1)S(1)}, u32[]{:S(2)}, u32[]{:S(2)}) collective-permute-start(bf16[4,128,512]{2,1,0:T(8,128)(2,1)} %dynamic-slice_bitcast_fusion.4), channel_id=1, source_target_pairs={{0,4},{4,0},{1,5},{5,1},{2,6},{6,2},{3,7},{7,3},{8,12},{12,8},{9,1... | collective-permute-start | bytes 1572872 | tf_op jit(solution)/shard_map/ppermute | solution.py:37
  582.2 10.5 %collective-permute-start.96 = (bf16[4,112,512]{2,1,0:T(8,128)(2,1)S(1)}, bf16[4,112,512]{2,1,0:T(8,128)(2,1)S(1)}, u32[]{:S(2)}, u32[]{:S(2)}) collective-permute-start(bf16[4,112,512]{2,1,0:T(8,128)(2,1)S(1)} %dynamic-slice_bitcast_fusion.5), channel_id=1, source_target_pairs={{0,4},{4,0},{1,5},{5,1},{2,6},{6,2},{3,7},{7,3},{8,12},{12,8},{9,1... | collective-permute-start | bytes 1376264 | tf_op jit(solution)/shard_map/ppermute | solution.py:37
  587.4 14.7 %collective-permute-start.87 = (bf16[128,2688]{1,0:T(8,128)(2,1)S(1)}, bf16[128,2688]{1,0:T(8,128)(2,1)S(1)}, u32[]{:S(2)}, u32[]{:S(2)}) collective-permute-start(bf16[128,2688]{1,0:T(8,128)(2,1)S(1)} %bitcast.379), channel_id=1, source_target_pairs={{0,2},{2,0},{1,3},{3,1},{4,6},{6,4},{5,7},{7,5},{8,10},{10,8},{9,1... | collective-permute-start | bytes 2064392 | tf_op jit(solution)/shard_map/ppermute | solution.py:37
  588.3 7.0 %collective-permute-start.83 = (bf16[128,512]{1,0:T(8,128)(2,1)S(1)}, bf16[128,512]{1,0:T(8,128)(2,1)S(1)}, u32[]{:S(2)}, u32[]{:S(2)}) collective-permute-start(bf16[128,512]{1,0:T(8,128)(2,1)S(1)} %get-tuple-element.265), channel_id=1, source_target_pairs={{0,24},{8,16},{16,8},{24,0},{1,25},{9,17},{17,9},{25,1},{2,26},{10... | collective-permute-start | bytes 393224 | tf_op jit(solution)/shard_map/ppermute | solution.py:37
  590.1 10.6 %collective-permute-start.82 = (bf16[128,512]{1,0:T(8,128)(2,1)S(1)}, bf16[128,512]{1,0:T(8,128)(2,1)S(1)}, u32[]{:S(2)}, u32[]{:S(2)}) collective-permute-start(bf16[128,512]{1,0:T(8,128)(2,1)S(1)} %get-tuple-element.266), channel_id=1, source_target_pairs={{0,16},{8,24},{16,0},{24,8},{1,17},{9,25},{17,1},{25,9},{2,18},{10... | collective-permute-start | bytes 393224 | tf_op jit(solution)/shard_map/ppermute | solution.py:37
  590.3 10.4 %collective-permute-start.81 = (bf16[128,512]{1,0:T(8,128)(2,1)S(1)}, bf16[128,512]{1,0:T(8,128)(2,1)S(1)}, u32[]{:S(2)}, u32[]{:S(2)}) collective-permute-start(bf16[128,512]{1,0:T(8,128)(2,1)S(1)} %get-tuple-element.264), channel_id=1, source_target_pairs={{0,8},{8,0},{16,24},{24,16},{1,9},{9,1},{17,25},{25,17},{2,10},{10... | collective-permute-start | bytes 393224 | tf_op jit(solution)/shard_map/ppermute | solution.py:37
  592.9 9.2 %collective-permute-start.99 = (bf16[112,512]{1,0:T(8,128)(2,1)S(1)}, bf16[112,512]{1,0:T(8,128)(2,1)S(1)}, u32[]{:S(2)}, u32[]{:S(2)}) collective-permute-start(bf16[112,512]{1,0:T(8,128)(2,1)S(1)} %get-tuple-element.268), channel_id=1, source_target_pairs={{0,24},{8,16},{16,8},{24,0},{1,25},{9,17},{17,9},{25,1},{2,26},{10... | collective-permute-start | bytes 344072 | tf_op jit(solution)/shard_map/ppermute | solution.py:37
  595.3 9.1 %collective-permute-start.98 = (bf16[112,512]{1,0:T(8,128)(2,1)S(1)}, bf16[112,512]{1,0:T(8,128)(2,1)S(1)}, u32[]{:S(2)}, u32[]{:S(2)}) collective-permute-start(bf16[112,512]{1,0:T(8,128)(2,1)S(1)} %get-tuple-element.269), channel_id=1, source_target_pairs={{0,16},{8,24},{16,0},{24,8},{1,17},{9,25},{17,1},{25,9},{2,18},{10... | collective-permute-start | bytes 344072 | tf_op jit(solution)/shard_map/ppermute | solution.py:37
  602.1 8.5 %collective-permute-start.88 = (bf16[128,2688]{1,0:T(8,128)(2,1)S(1)}, bf16[128,2688]{1,0:T(8,128)(2,1)S(1)}, u32[]{:S(2)}, u32[]{:S(2)}) collective-permute-start(bf16[128,2688]{1,0:T(8,128)(2,1)S(1)} %bitcast.380), channel_id=1, source_target_pairs={{0,1},{1,0},{2,3},{3,2},{4,5},{5,4},{6,7},{7,6},{8,9},{9,8},{10,11... | collective-permute-start | bytes 2064392 | tf_op jit(solution)/shard_map/ppermute | solution.py:37
  602.2 8.5 %collective-permute-start.89 = (bf16[128,2688]{1,0:T(8,128)(2,1)S(1)}, bf16[128,2688]{1,0:T(8,128)(2,1)S(1)}, u32[]{:S(2)}, u32[]{:S(2)}) collective-permute-start(bf16[128,2688]{1,0:T(8,128)(2,1)S(1)} %collective-permute-done.87.refs_3_), channel_id=1, source_target_pairs={{0,1},{1,0},{2,3},{3,2},{4,5},{5,4},{6,7},{7,6},{8,9},{9,8},{10,11... | collective-permute-start | bytes 2064392 | tf_op jit(solution)/shard_map/ppermute | solution.py:37
  607.1 14.0 %collective-permute-start.85 = (bf16[128,512]{1,0:T(8,128)(2,1)S(1)}, bf16[128,512]{1,0:T(8,128)(2,1)S(1)}, u32[]{:S(2)}, u32[]{:S(2)}) collective-permute-start(bf16[128,512]{1,0:T(8,128)(2,1)S(1)} %add_convert_fusion.4), channel_id=1, source_target_pairs={{0,1},{1,0},{2,3},{3,2},{4,5},{5,4},{6,7},{7,6},{8,9},{9,8},{10,11... | collective-permute-start | bytes 393224 | tf_op jit(solution)/shard_map/ppermute | solution.py:37
  (108 other events, 795.2 us)
Sparse Core Ops, SparseCore 0:
  10.8 79.3 all-gather.5
  93.7 150.2 all-gather.3
  445.9 120.4 reduce-scatter.1

commit v6 on v5

--- a/solution.py
+++ b/solution.py
@@ -1101,8 +1101,9 @@
     at = jnp.stack([chip, core]).astype(jnp.int32)
     heads_out = place_shares(head_shares, head_others, jnp.asarray(part_of.reshape(-1)), at, head)
     heads_out = heads_out.reshape(tasks, 9, own, head).transpose(2, 0, 1, 3)
-    later_own = jnp.concatenate([gather_x(piece) for piece in later_own], axis=0)
-    heads_out, later_own = lax.optimization_barrier((heads_out, later_own))
+    first, second = later_own
+    first, (heads_out, second) = gather_x(first), lax.optimization_barrier((heads_out, second))
+    later_own = jnp.concatenate([first, gather_x(second)], axis=0)
     later_other = flip(later_own, [("c", 1)])
     later_sum = both_halves(
         later_own.reshape(9 + ratio, mid_rows, width),

time: 639 us -> 650 us (1.017)
  waiting for transfers between devices: 229 us -> 243 us
    ppermute x93, waiting for transfers between devices: 128 us -> 142 us  [flip(): return lax.ppermute(value, names, pairs)]
  transfers between devices with their start and end apart: 106 -> 106, of which waited for: 61 -> 60; matrix products, arithmetic and copies ran while one was open for 16% -> 15% of each run, Pallas kernels for 21% -> 20%
where the time goes in v6:
time: 650 us; the launch traced here: 644 us
  waiting for transfers between devices  243 us (37%)
  Pallas kernels  132 us (20%)
  starting transfers between devices  124 us (19%)
  other arithmetic  45.9 us (7%)
  local copies, waits for them, and re-layouts  42.7 us (7%)
  matrix products  31.7 us (5%)
  between operations  25 us (4%)
    ppermute x93, waiting for transfers between devices, flip(): return lax.ppermute(value, names, pairs)  142 us
    ppermute x93, starting transfers between devices, flip(): return lax.ppermute(value, names, pairs)  91.2 us
    all_gather x1, waiting for transfers between devices, on_device(): block_mine = lax.all_gather(block_own, LINE, axis=0, tiled=False)  64.6 us
    ppermute x10, waiting for transfers between devices, rows_to(): return lax.ppermute(value, LINE, pairs)  36.7 us
    ppermute x10, starting transfers between devices, rows_to(): return lax.ppermute(value, LINE, pairs)  32.6 us
    pallas_call x1, Pallas kernels, some_weight_grad(): pl.pallas_call(lambda *refs: weight_grad_kernel(members, side_tasks, task...  25 us
    pallas_call x2, Pallas kernels, head_terms(): pl.pallas_call(terms_kernel, out_shape=jax.ShapeDtypeStruct((pixels, item...  22.9 us
    unnamed x144, local copies, waits for them, and re-layouts  19.8 us
  transfers between devices with their start and end apart: 106, of which 60 were waited for; matrix products, arithmetic and copies ran while one was open for 15% of the time, Pallas kernels for 20%

profile of v6, /device:TPU:0, one launch (start us, length us, event | category | flops | bytes accessed | tf_op | source)
XLA Modules:
  0.0 644.1 jit_solution(6681750536534765115)
XLA Ops:
  12.0 5.7 copy.86
  21.4 4.2 bitcast_multiply_fusion.refs_5_
  25.6 64.6 %all-gather.6.cloned.1.call-done = bf16[4352,512]{1,0:T(8,128)(2,1)} async-done(((bf16[544,512]{1,0:T(8,128)(2,1)}), bf16[4352,512]{1,0:T(8,128)(2,1)}) %all-gather.6.cloned.1.call-update) | async-done | bytes 4456464 | tf_op jit(solution)/shard_map/all_gather | solution.py:813
  90.3 7.7 %collective-permute-done.other_ref.refs_2_ = bf16[8,544,512]{2,1,0:T(8,128)(2,1)S(1)} collective-permute-done((bf16[8,544,512]{2,1,0:T(8,128)(2,1)}, bf16[8,544,512]{2,1,0:T(8,128)(2,1)S(1)}, u32[]{:S(2)}, u32[]{:S(2)}) %collective-permute-start) | collective-permute-done | bytes 4456480 | tf_op jit(solution)/shard_map/ppermute | solution.py:37
  100.2 3.2 shard_map.351
  103.4 3.4 fusion.110
  123.3 5.5 collective-permute-start.8
  128.9 6.9 %shard_map.352 = (bf16[1536,1536]{1,0:T(8,128)(2,1)}, bf16[512,2048]{1,0:T(8,128)(2,1)}) custom-call(s32[1]{0:T(128)} %bitcast.8.core_ref.refs_0_, bf16[8,544,512]{2,1,0:T(8,128)(2,1)} %bitcast.357, bf16[8,544,512]{2,1,0:T(8,128)(2,1)} %copy-done.8), custom_call_target="tpu_custom_call" | custom-call | bytes 17825792 | tf_op jit(solution)/shard_map/pallas_call | solution.py:707
  135.9 5.4 collective-permute-done.9
  141.3 8.7 %collective-permute-done.8 = bf16[384,512]{1,0:T(8,128)(2,1)} collective-permute-done((bf16[384,512]{1,0:T(8,128)(2,1)S(1)}, bf16[384,512]{1,0:T(8,128)(2,1)}, u32[]{:S(2)}, u32[]{:S(2)}) %collective-permute-start.8) | collective-permute-done | bytes 393248 | tf_op jit(solution)/shard_map/ppermute | solution.py:71
  149.9 6.4 fusion.46
  160.3 2.8 collective-permute-start.13
  171.3 3.4 collective-permute-done.16
  175.4 4.5 fusion.108
  195.9 5.3 multiply_convert_fusion.x_ref
  219.8 26.7 %collective-permute-done.25.refs_2_ = bf16[768,1024]{1,0:T(8,128)(2,1)} collective-permute-done((bf16[768,1024]{1,0:T(8,128)(2,1)}, bf16[768,1024]{1,0:T(8,128)(2,1)}, u32[]{:S(2)}, u32[]{:S(2)}) %collective-permute-start.25) | collective-permute-done | bytes 1572896 | tf_op jit(solution)/shard_map/ppermute | solution.py:37
  247.1 9.9 %shard_map.354 = bf16[768,512]{1,0:T(8,128)(2,1)} custom-call(s32[2]{0:T(128)} %broadcast_add_fusion.picked_ref, s32[2]{0:T(128)} %copy-done.37, bf16[768,2048]{1,0:T(8,128)(2,1)} %copy-done.3, bf16[2048,5376]{1,0:T(8,128)(2,1)} %all-gather.4.cloned.1.call-done.w_ref.refs_1_.refs_2_.refs_3_.refs_4_, f32[768,128]{1,0:T(8,128)} %bitcast.348), custom_call_target="tpu_custom_call" | custom-call | flops 4831838208 | bytes 9437184 | tf_op jit(solution)/shard_map/pallas_call | solution.py:272
  260.2 5.5 collective-permute-start.27
  265.6 3.1 collective-permute-start.29
  269.3 12.9 %shard_map.353 = f32[768,768]{1,0:T(8,128)} custom-call(s32[3]{0:T(128)} %iota.36.picked_ref.task_ref, s32[3]{0:T(128)} %iota.36.picked_ref.task_ref, bf16[768,2048]{1,0:T(8,128)(2,1)} %copy-done.3, bf16[2048,5376]{1,0:T(8,128)(2,1)} %all-gather.4.cloned.1.call-done.w_ref.refs_1_.refs_2_.refs_3_.refs_4_, f32[768,128]{1,0:T(8,128)} %bitcast.349), custom_call_target="tpu_custom_call" | custom-call | flops 7247757312 | bytes 12582912 | tf_op jit(solution)/shard_map/pallas_call | solution.py:272
  282.3 7.7 %collective-permute-done.29 = bf16[768,256]{1,0:T(8,128)(2,1)S(1)} collective-permute-done((bf16[768,256]{1,0:T(8,128)(2,1)S(1)}, bf16[768,256]{1,0:T(8,128)(2,1)S(1)}, u32[]{:S(2)}, u32[]{:S(2)}) %collective-permute-start.29) | collective-permute-done | bytes 393248 | tf_op jit(solution)/shard_map/ppermute | solution.py:71
  294.1 3.3 collective-permute-start.33
  301.2 5.0 collective-permute-start.36
  309.2 5.5 shard_map.357.refs_2_
  340.5 8.6 %collective-permute-start.46 = (bf16[768,256]{1,0:T(8,128)(2,1)S(1)}, bf16[768,256]{1,0:T(8,128)(2,1)S(1)}, u32[]{:S(2)}, u32[]{:S(2)}) collective-permute-start(bf16[768,256]{1,0:T(8,128)(2,1)S(1)} %get-tuple-element.249), channel_id=1, source_target_pairs={{24,0},{28,4},{0,24},{4,28},{25,1},{29,5},{1,25},{5,29},{26,2},{30... | collective-permute-start | bytes 1179656 | tf_op jit(solution)/shard_map/ppermute | solution.py:71
  349.6 4.9 shard_map.355.refs_0_
  355.4 18.0 %shard_map.356 = (bf16[768,2048]{1,0:T(8,128)(2,1)}, bf16[768,2048]{1,0:T(8,128)(2,1)}, bf16[768,2048]{1,0:T(8,128)(2,1)}, bf16[768,2048]{1,0:T(8,128)(2,1)}, bf16[768,2048]{1,0:T(8,128)(2,1)}) custom-call(bf16[768,2304]{1,0:T(8,128)(2,1)} %shard_map.355.refs_0_, bf16[2048,5376]{1,0:T(8,128)(2,1)} %all-gather.4.cloned.1.call-done.w_ref.refs_1_.refs_2_.refs_3_.refs_4_, ...), custom_call_target="tpu_custom_call" | custom-call | flops 7247757312 | bytes 25165824 | tf_op jit(solution)/shard_map/pallas_call | solution.py:354
  374.9 6.8 %collective-permute-done.48.refs_4_ = bf16[768,768]{1,0:T(8,128)(2,1)S(1)} collective-permute-done((bf16[768,768]{1,0:T(8,128)(2,1)S(1)}, bf16[768,768]{1,0:T(8,128)(2,1)S(1)}, u32[]{:S(2)}, u32[]{:S(2)}) %collective-permute-start.48) | collective-permute-done | bytes 1179680 | tf_op jit(solution)/shard_map/ppermute | solution.py:37
  385.8 3.6 shard_map.358.refs_2_
  390.3 16.6 %shard_map.359 = (bf16[768,2048]{1,0:T(8,128)(2,1)}, bf16[768,2048]{1,0:T(8,128)(2,1)}, f32[16,2048]{1,0:T(8,128)}) custom-call(s32[2]{0:T(128)} %broadcast_add_fusion.1.refs_0_, f32[6]{0:T(128)} %reshape.412.refs_1_, bf16[768,1536]{1,0:T(8,128)(2,1)} %shard_map.358.refs_2_, ...), custom_call_target="tpu_custom_call" | custom-call | flops 4831838208 | bytes 22020096 | tf_op jit(solution)/shard_map/pallas_call | solution.py:414
  420.8 25.0 %shard_map.360 = bf16[1024,2688]{1,0:T(8,128)(2,1)} custom-call(s32[7]{0:T(128)} %and_select_fusion.refs_0_, s32[2]{0:T(128)} %copy-done.37, bf16[1024,3072]{1,0:T(8,128)(2,1)} %shard_map.357.refs_2_, bf16[768,768]{1,0:T(8,128)(2,1)} %copy-done.20, bf16[768,768]{1,0:T(8,128)(2,1)} %copy-done.43, bf16[768,512]{1,0:T(8,128)(2,1)} %copy-done.23, ...), custom_call_target="tpu_custom_call" | custom-call | flops 12079595520 | bytes 11796480 | tf_op jit(solution)/shard_map/pallas_call | solution.py:635
  447.8 16.5 %shard_map.361 = (bf16[768,2048]{1,0:T(8,128)(2,1)}, bf16[512,2048]{1,0:T(8,128)(2,1)}, f32[768,512]{1,0:T(8,128)}, f32[8,512]{1,0:T(8,128)}) custom-call(f32[7,2048]{1,0:T(8,128)} %add_add_fusion.1.refs_0_.refs_4_, bf16[768,2048]{1,0:T(8,128)(2,1)} %get-tuple-element.122.refs_1_, bf16[768,2048]{1,0:T(8,128)(2,1)} %get-tuple-element.123.refs_2_, ...), custom_call_target="tpu_custom_call" | custom-call | flops 1572864 | bytes 10752 | tf_op jit(solution)/shard_map/pallas_call | solution.py:496
  484.0 3.0 collective-permute-done.68
  491.4 3.8 fusion.132
  495.3 3.1 collective-permute-start.70
  499.9 5.0 convolution_convert_fusion
  507.9 14.9 %collective-permute-done.70 = bf16[384,512]{1,0:T(8,128)(2,1)S(1)} collective-permute-done((bf16[384,512]{1,0:T(8,128)(2,1)S(1)}, bf16[384,512]{1,0:T(8,128)(2,1)S(1)}, u32[]{:S(2)}, u32[]{:S(2)}) %collective-permute-start.70) | collective-permute-done | bytes 393248 | tf_op jit(solution)/shard_map/ppermute | solution.py:71
  526.4 2.9 collective-permute-start.74
  533.0 3.4 collective-permute-start.77
  546.9 4.6 convert_add_fusion
  551.5 10.6 %collective-permute-done.86 = bf16[8,96,512]{2,1,0:T(8,128)(2,1)S(1)} collective-permute-done((bf16[8,96,512]{2,1,0:T(8,128)(2,1)S(1)}, bf16[8,96,512]{2,1,0:T(8,128)(2,1)S(1)}, u32[]{:S(2)}, u32[]{:S(2)}) %collective-permute-start.86) | collective-permute-done | bytes 786464 | tf_op jit(solution)/shard_map/ppermute | solution.py:37
  565.8 6.8 %collective-permute-done.87 = bf16[4,96,512]{2,1,0:T(8,128)(2,1)S(1)} collective-permute-done((bf16[4,96,512]{2,1,0:T(8,128)(2,1)S(1)}, bf16[4,96,512]{2,1,0:T(8,128)(2,1)S(1)}, u32[]{:S(2)}, u32[]{:S(2)}) %collective-permute-start.87) | collective-permute-done | bytes 393248 | tf_op jit(solution)/shard_map/ppermute | solution.py:37
  574.6 2.6 collective-permute-start.88
  583.6 11.6 %collective-permute-done.91 = bf16[96,512]{1,0:T(8,128)(2,1)S(1)} collective-permute-done((bf16[96,512]{1,0:T(8,128)(2,1)S(1)}, bf16[96,512]{1,0:T(8,128)(2,1)S(1)}, u32[]{:S(2)}, u32[]{:S(2)}) %collective-permute-start.91) | collective-permute-done | bytes 98336 | tf_op jit(solution)/shard_map/ppermute | solution.py:37
  604.2 6.6 %collective-permute-done.82 = bf16[128,512]{1,0:T(8,128)(2,1)S(1)} collective-permute-done((bf16[128,512]{1,0:T(8,128)(2,1)S(1)}, bf16[128,512]{1,0:T(8,128)(2,1)S(1)}, u32[]{:S(2)}, u32[]{:S(2)}) %collective-permute-start.82) | collective-permute-done | bytes 131104 | tf_op jit(solution)/shard_map/ppermute | solution.py:37
  614.1 2.7 collective-permute-done.98
  619.1 8.7 %shard_map.362 = f32[27,256,256]{2,1,0:T(8,128)} custom-call(s32[9]{0:T(128)} %constant.273.clone.refs_0_, s32[2]{0:T(128)} %pad_add_fusion.1.refs_1_, bf16[128,2688]{1,0:T(8,128)(2,1)} %bitcast.379, bf16[128,2688]{1,0:T(8,128)(2,1)} %copy-done.25, bf16[128,2688]{1,0:T(8,128)(2,1)} %copy-done.26, bf16[128,2688]{1,0:T(8,128)(2,1)} %copy-done.27), custom_call_target="tpu_custom_call" | custom-call | bytes 10616832 | tf_op jit(solution)/shard_map/pallas_call | solution.py:748
  628.6 4.0 collective-permute-done.100
  (561 shorter events, 207.3 us)
Async XLA Ops:
  7.2 83.0 %all-gather.6.cloned.1.call-start = ((), (), s32[]{:S(2)}) async-start(), calls=%async_computation.3 | async-start | bytes 5013504 | tf_op jit(solution)/shard_map/all_gather | solution.py:813
  10.2 236.9 %all-gather.4.cloned.1.call-start = ((), (), s32[]{:S(2)}) async-start(), calls=%async_computation.1 | async-start | bytes 22708224 | tf_op jit(solution)/shard_map/all_gather | solution.py:841
  90.2 488.4 %reduce-scatter.2.cloned.1.call-start = ((), (), s32[]{:S(2)}) async-start(), calls=%async_computation.2 | async-start | bytes 6193152 | tf_op jit(solution)/shard_map/reduce_scatter | solution.py:1033
  90.3 7.8 %collective-permute-start = (bf16[8,544,512]{2,1,0:T(8,128)(2,1)}, bf16[8,544,512]{2,1,0:T(8,128)(2,1)S(1)}, u32[]{:S(2)}, u32[]{:S(2)}) collective-permute-start(bf16[8,544,512]{2,1,0:T(8,128)(2,1)} %bitcast.355), channel_id=1, source_target_pairs={{0,1},{1,0},{2,3},{3,2},{4,5},{5,4},{6,7},{7,6},{8,9},{9,8},{10,11... | collective-permute-start | bytes 13369352 | tf_op jit(solution)/shard_map/ppermute | solution.py:37
  122.0 19.3 %collective-permute-start.9 = (bf16[384,512]{1,0:T(8,128)(2,1)S(1)}, bf16[384,512]{1,0:T(8,128)(2,1)}, u32[]{:S(2)}, u32[]{:S(2)}) collective-permute-start(bf16[384,512]{1,0:T(8,128)(2,1)S(1)} %get-tuple-element.263), channel_id=1, source_target_pairs={{4,0},{8,4},{12,8},{16,12},{20,16},{24,20},{28,24},{5,1},{9,5},{13... | collective-permute-start | bytes 1179656 | tf_op jit(solution)/shard_map/ppermute | solution.py:71
  123.3 26.7 %collective-permute-start.8 = (bf16[384,512]{1,0:T(8,128)(2,1)S(1)}, bf16[384,512]{1,0:T(8,128)(2,1)}, u32[]{:S(2)}, u32[]{:S(2)}) collective-permute-start(bf16[384,512]{1,0:T(8,128)(2,1)S(1)} %get-tuple-element.262), channel_id=1, source_target_pairs={{0,4},{4,8},{8,12},{12,16},{16,20},{20,24},{24,28},{1,5},{5,9},{9,... | collective-permute-start | bytes 1179656 | tf_op jit(solution)/shard_map/ppermute | solution.py:71
  207.8 38.8 %collective-permute-start.25 = (bf16[768,1024]{1,0:T(8,128)(2,1)}, bf16[768,1024]{1,0:T(8,128)(2,1)}, u32[]{:S(2)}, u32[]{:S(2)}) collective-permute-start(bf16[768,1024]{1,0:T(8,128)(2,1)} %get-tuple-element.220), channel_id=1, source_target_pairs={{0,2},{2,0},{1,3},{3,1},{4,6},{6,4},{5,7},{7,5},{8,10},{10,8},{9,1... | collective-permute-start | bytes 4718600 | tf_op jit(solution)/shard_map/ppermute | solution.py:37
  219.8 62.4 %collective-permute-start.24 = (bf16[768,1024]{1,0:T(8,128)(2,1)S(1)}, bf16[768,1024]{1,0:T(8,128)(2,1)}, u32[]{:S(2)}, u32[]{:S(2)}) collective-permute-start(bf16[768,1024]{1,0:T(8,128)(2,1)S(1)} %get-tuple-element.96.refs_0_), channel_id=1, source_target_pairs={{0,1},{1,0},{2,3},{3,2},{4,5},{5,4},{6,7},{7,6},{8,9},{9,8},{10,11... | collective-permute-start | bytes 4718600 | tf_op jit(solution)/shard_map/ppermute | solution.py:37
  246.5 35.7 %collective-permute-start.26 = (bf16[768,1024]{1,0:T(8,128)(2,1)}, bf16[768,1024]{1,0:T(8,128)(2,1)}, u32[]{:S(2)}, u32[]{:S(2)}) collective-permute-start(bf16[768,1024]{1,0:T(8,128)(2,1)} %collective-permute-done.25.refs_2_), channel_id=1, source_target_pairs={{0,1},{1,0},{2,3},{3,2},{4,5},{5,4},{6,7},{7,6},{8,9},{9,8},{10,11... | collective-permute-start | bytes 4718600 | tf_op jit(solution)/shard_map/ppermute | solution.py:37
  258.9 23.4 %collective-permute-start.28 = (bf16[768,256]{1,0:T(8,128)(2,1)S(1)}, bf16[768,256]{1,0:T(8,128)(2,1)S(1)}, u32[]{:S(2)}, u32[]{:S(2)}) collective-permute-start(bf16[768,256]{1,0:T(8,128)(2,1)S(1)} %get-tuple-element.260), channel_id=1, source_target_pairs={{12,0},{16,4},{20,8},{24,12},{28,16},{13,1},{17,5},{21,9},{25,13},... | collective-permute-start | bytes 1179656 | tf_op jit(solution)/shard_map/ppermute | solution.py:71
  260.2 22.1 %collective-permute-start.27 = (bf16[768,256]{1,0:T(8,128)(2,1)S(1)}, bf16[768,256]{1,0:T(8,128)(2,1)S(1)}, u32[]{:S(2)}, u32[]{:S(2)}) collective-permute-start(bf16[768,256]{1,0:T(8,128)(2,1)S(1)} %get-tuple-element.259), channel_id=1, source_target_pairs={{0,12},{4,16},{8,20},{12,24},{16,28},{1,13},{5,17},{9,21},{13,25},... | collective-permute-start | bytes 1179656 | tf_op jit(solution)/shard_map/ppermute | solution.py:71
  265.6 24.4 %collective-permute-start.29 = (bf16[768,256]{1,0:T(8,128)(2,1)S(1)}, bf16[768,256]{1,0:T(8,128)(2,1)S(1)}, u32[]{:S(2)}, u32[]{:S(2)}) collective-permute-start(bf16[768,256]{1,0:T(8,128)(2,1)S(1)} %get-tuple-element.261), channel_id=1, source_target_pairs={{0,24},{4,28},{24,0},{28,4},{1,25},{5,29},{25,1},{29,5},{2,26},{6,... | collective-permute-start | bytes 1179656 | tf_op jit(solution)/shard_map/ppermute | solution.py:71
  301.1 13.6 %collective-permute-start.35 = (f32[2,768]{1,0:T(2,128)S(1)}, f32[2,768]{1,0:T(2,128)S(1)}, u32[]{:S(2)}, u32[]{:S(2)}) collective-permute-start(f32[2,768]{1,0:T(2,128)S(1)} %add_add_fusion.8), channel_id=1, source_target_pairs={{0,16},{8,24},{16,0},{24,8},{1,17},{9,25},{17,1},{25,9},{2,18},{10... | collective-permute-start | bytes 18440 | tf_op jit(solution)/shard_map/ppermute | solution.py:37
  301.2 13.5 %collective-permute-start.36 = (f32[2,768]{1,0:T(2,128)S(1)}, f32[2,768]{1,0:T(2,128)S(1)}, u32[]{:S(2)}, u32[]{:S(2)}) collective-permute-start(f32[2,768]{1,0:T(2,128)S(1)} %add_add_fusion.8), channel_id=1, source_target_pairs={{0,24},{8,16},{16,8},{24,0},{1,25},{9,17},{17,9},{25,1},{2,26},{10... | collective-permute-start | bytes 18440 | tf_op jit(solution)/shard_map/ppermute | solution.py:37
  306.2 8.5 %collective-permute-start.34 = (f32[2,768]{1,0:T(2,128)S(1)}, f32[2,768]{1,0:T(2,128)S(1)}, u32[]{:S(2)}, u32[]{:S(2)}) collective-permute-start(f32[2,768]{1,0:T(2,128)S(1)} %add_add_fusion.8), channel_id=1, source_target_pairs={{0,8},{8,0},{16,24},{24,16},{1,9},{9,1},{17,25},{25,17},{2,10},{10... | collective-permute-start | bytes 18440 | tf_op jit(solution)/shard_map/ppermute | solution.py:37
  336.7 17.7 %collective-permute-start.47 = (bf16[768,384]{1,0:T(8,128)(2,1)S(1)}, bf16[768,384]{1,0:T(8,128)(2,1)S(1)}, u32[]{:S(2)}, u32[]{:S(2)}) collective-permute-start(bf16[768,384]{1,0:T(8,128)(2,1)S(1)} %pad_maximum_fusion.7), channel_id=1, source_target_pairs={{0,1},{1,0},{2,3},{3,2},{4,5},{5,4},{6,7},{7,6},{8,9},{9,8},{10,11... | collective-permute-start | bytes 1769480 | tf_op jit(solution)/shard_map/ppermute | solution.py:37
  337.0 18.2 %collective-permute-start.49 = (f32[66,256]{1,0:T(8,128)S(1)}, f32[66,256]{1,0:T(8,128)S(1)}, u32[]{:S(2)}, u32[]{:S(2)}) collective-permute-start(f32[66,256]{1,0:T(8,128)S(1)} %pad_maximum_fusion.13), channel_id=1, source_target_pairs={{0,1},{1,0},{2,3},{3,2},{4,5},{5,4},{6,7},{7,6},{8,9},{9,8},{10,11... | collective-permute-start | bytes 202760 | tf_op jit(solution)/shard_map/ppermute | solution.py:37
  337.7 35.7 %collective-permute-start.44 = (bf16[768,256]{1,0:T(8,128)(2,1)S(1)}, bf16[768,256]{1,0:T(8,128)(2,1)S(1)}, u32[]{:S(2)}, u32[]{:S(2)}) collective-permute-start(bf16[768,256]{1,0:T(8,128)(2,1)S(1)} %get-tuple-element.250), channel_id=1, source_target_pairs={{0,12},{4,16},{8,20},{12,24},{16,28},{1,13},{5,17},{9,21},{13,25},... | collective-permute-start | bytes 1179656 | tf_op jit(solution)/shard_map/ppermute | solution.py:71
  339.2 34.3 %collective-permute-start.45 = (bf16[768,256]{1,0:T(8,128)(2,1)S(1)}, bf16[768,256]{1,0:T(8,128)(2,1)S(1)}, u32[]{:S(2)}, u32[]{:S(2)}) collective-permute-start(bf16[768,256]{1,0:T(8,128)(2,1)S(1)} %get-tuple-element.250), channel_id=1, source_target_pairs={{12,0},{16,4},{20,8},{24,12},{28,16},{13,1},{17,5},{21,9},{25,13},... | collective-permute-start | bytes 1179656 | tf_op jit(solution)/shard_map/ppermute | solution.py:71
  340.5 33.0 %collective-permute-start.46 = (bf16[768,256]{1,0:T(8,128)(2,1)S(1)}, bf16[768,256]{1,0:T(8,128)(2,1)S(1)}, u32[]{:S(2)}, u32[]{:S(2)}) collective-permute-start(bf16[768,256]{1,0:T(8,128)(2,1)S(1)} %get-tuple-element.249), channel_id=1, source_target_pairs={{24,0},{28,4},{0,24},{4,28},{25,1},{29,5},{1,25},{5,29},{26,2},{30... | collective-permute-start | bytes 1179656 | tf_op jit(solution)/shard_map/ppermute | solution.py:71
  354.6 27.1 %collective-permute-start.48 = (bf16[768,768]{1,0:T(8,128)(2,1)S(1)}, bf16[768,768]{1,0:T(8,128)(2,1)S(1)}, u32[]{:S(2)}, u32[]{:S(2)}) collective-permute-start(bf16[768,768]{1,0:T(8,128)(2,1)S(1)} %pad_maximum_fusion.4.refs_3_), channel_id=1, source_target_pairs={{0,2},{2,0},{1,3},{3,1},{4,6},{6,4},{5,7},{7,5},{8,10},{10,8},{9,1... | collective-permute-start | bytes 3538952 | tf_op jit(solution)/shard_map/ppermute | solution.py:37
  355.2 18.1 %collective-permute-start.50 = (f32[66,256]{1,0:T(8,128)S(1)}, f32[66,256]{1,0:T(8,128)S(1)}, u32[]{:S(2)}, u32[]{:S(2)}) collective-permute-start(f32[66,256]{1,0:T(8,128)S(1)} %fusion.151), channel_id=1, source_target_pairs={{0,4},{4,0},{1,5},{5,1},{2,6},{6,2},{3,7},{7,3},{8,12},{12,8},{9,1... | collective-permute-start | bytes 202760 | tf_op jit(solution)/shard_map/ppermute | solution.py:37
  383.8 23.2 %collective-permute-start.52 = (bf16[768,512]{1,0:T(8,128)(2,1)S(1)}, bf16[768,512]{1,0:T(8,128)(2,1)S(1)}, u32[]{:S(2)}, u32[]{:S(2)}) collective-permute-start(bf16[768,512]{1,0:T(8,128)(2,1)S(1)} %pad_maximum_fusion.6.refs_5_), channel_id=1, source_target_pairs={{0,2},{2,0},{1,3},{3,1},{4,6},{6,4},{5,7},{7,5},{8,10},{10,8},{9,1... | collective-permute-start | bytes 2359304 | tf_op jit(solution)/shard_map/ppermute | solution.py:37
  389.5 17.4 %collective-permute-start.54 = (f32[66,256]{1,0:T(8,128)S(1)}, f32[66,256]{1,0:T(8,128)S(1)}, u32[]{:S(2)}, u32[]{:S(2)}) collective-permute-start(f32[66,256]{1,0:T(8,128)S(1)} %add.929), channel_id=1, source_target_pairs={{0,16},{8,24},{16,0},{24,8},{1,17},{9,25},{17,1},{25,9},{2,18},{10... | collective-permute-start | bytes 202760 | tf_op jit(solution)/shard_map/ppermute | solution.py:37
  409.6 6.7 %collective-permute-start.57 = (f32[7,2048]{1,0:T(8,128)S(1)}, f32[7,2048]{1,0:T(8,128)S(1)}, u32[]{:S(2)}, u32[]{:S(2)}) collective-permute-start(f32[7,2048]{1,0:T(8,128)S(1)} %fusion.150), channel_id=1, source_target_pairs={{0,2},{2,0},{1,3},{3,1},{4,6},{6,4},{5,7},{7,5},{8,10},{10,8},{9,1... | collective-permute-start | bytes 172040 | tf_op jit(solution)/shard_map/ppermute | solution.py:37
  414.9 30.9 %collective-permute-start.102 = (f32[66,256]{1,0:T(8,128)S(1)}, f32[66,256]{1,0:T(8,128)S(1)}, u32[]{:S(2)}, u32[]{:S(2)}) collective-permute-start(f32[66,256]{1,0:T(8,128)S(1)} %add.930), channel_id=1, source_target_pairs={{0,2},{2,0},{1,3},{3,1},{4,6},{6,4},{5,7},{7,5},{8,10},{10,8},{9,1... | collective-permute-start | bytes 202760 | tf_op jit(solution)/shard_map/ppermute | solution.py:37
  416.7 30.4 %collective-permute-start.60 = (f32[7,2048]{1,0:T(8,128)S(1)}, f32[7,2048]{1,0:T(8,128)S(1)}, u32[]{:S(2)}, u32[]{:S(2)}) collective-permute-start(f32[7,2048]{1,0:T(8,128)S(1)} %add_add_fusion.2), channel_id=1, source_target_pairs={{0,16},{8,24},{16,0},{24,8},{1,17},{9,25},{17,1},{25,9},{2,18},{10... | collective-permute-start | bytes 172040 | tf_op jit(solution)/shard_map/ppermute | solution.py:37
  418.9 28.1 %collective-permute-start.61 = (f32[7,2048]{1,0:T(8,128)S(1)}, f32[7,2048]{1,0:T(8,128)S(1)}, u32[]{:S(2)}, u32[]{:S(2)}) collective-permute-start(f32[7,2048]{1,0:T(8,128)S(1)} %add_add_fusion.2), channel_id=1, source_target_pairs={{0,24},{8,16},{16,8},{24,0},{1,25},{9,17},{17,9},{25,1},{2,26},{10... | collective-permute-start | bytes 172040 | tf_op jit(solution)/shard_map/ppermute | solution.py:37
  420.3 26.8 %collective-permute-start.59 = (f32[7,2048]{1,0:T(8,128)S(1)}, f32[7,2048]{1,0:T(8,128)S(1)}, u32[]{:S(2)}, u32[]{:S(2)}) collective-permute-start(f32[7,2048]{1,0:T(8,128)S(1)} %add_add_fusion.2), channel_id=1, source_target_pairs={{0,8},{8,0},{16,24},{24,16},{1,9},{9,1},{17,25},{25,17},{2,10},{10... | collective-permute-start | bytes 172040 | tf_op jit(solution)/shard_map/ppermute | solution.py:37
  465.0 6.8 %collective-permute-start.62 = (f32[2,512]{1,0:T(2,128)S(1)}, f32[2,512]{1,0:T(2,128)S(1)}, u32[]{:S(2)}, u32[]{:S(2)}) collective-permute-start(f32[2,512]{1,0:T(2,128)S(1)} %slice.497), channel_id=1, source_target_pairs={{0,1},{1,0},{2,3},{3,2},{4,5},{5,4},{6,7},{7,6},{8,9},{9,8},{10,11... | collective-permute-start | bytes 12296 | tf_op jit(solution)/shard_map/ppermute | solution.py:37
  495.3 27.4 %collective-permute-start.70 = (bf16[384,512]{1,0:T(8,128)(2,1)S(1)}, bf16[384,512]{1,0:T(8,128)(2,1)S(1)}, u32[]{:S(2)}, u32[]{:S(2)}) collective-permute-start(bf16[384,512]{1,0:T(8,128)(2,1)S(1)} %get-tuple-element.237), channel_id=1, source_target_pairs={{0,4},{4,8},{8,12},{12,16},{16,20},{20,24},{24,28},{1,5},{5,9},{9,... | collective-permute-start | bytes 1179656 | tf_op jit(solution)/shard_map/ppermute | solution.py:71
  498.4 24.4 %collective-permute-start.69 = (bf16[384,512]{1,0:T(8,128)(2,1)S(1)}, bf16[384,512]{1,0:T(8,128)(2,1)S(1)}, u32[]{:S(2)}, u32[]{:S(2)}) collective-permute-start(bf16[384,512]{1,0:T(8,128)(2,1)S(1)} %get-tuple-element.236), channel_id=1, source_target_pairs={{4,0},{8,4},{12,8},{16,12},{20,16},{24,20},{28,24},{5,1},{9,5},{13... | collective-permute-start | bytes 1179656 | tf_op jit(solution)/shard_map/ppermute | solution.py:71
  507.4 32.7 %collective-permute-start.78 = (bf16[8,416,512]{2,1,0:T(8,128)(2,1)S(1)}, bf16[8,416,512]{2,1,0:T(8,128)(2,1)S(1)}, u32[]{:S(2)}, u32[]{:S(2)}) collective-permute-start(bf16[8,416,512]{2,1,0:T(8,128)(2,1)S(1)} %slice_dynamic-update-slice_fusion), channel_id=1, source_target_pairs={{0,1},{1,0},{2,3},{3,2},{4,5},{5,4},{6,7},{7,6},{8,9},{9,8},{10,11... | collective-permute-start | bytes 10223624 | tf_op jit(solution)/shard_map/ppermute | solution.py:37
  541.5 20.5 %collective-permute-start.86 = (bf16[8,96,512]{2,1,0:T(8,128)(2,1)S(1)}, bf16[8,96,512]{2,1,0:T(8,128)(2,1)S(1)}, u32[]{:S(2)}, u32[]{:S(2)}) collective-permute-start(bf16[8,96,512]{2,1,0:T(8,128)(2,1)S(1)} %constant_dynamic-slice_fusion.1), channel_id=1, source_target_pairs={{0,2},{2,0},{1,3},{3,1},{4,6},{6,4},{5,7},{7,5},{8,10},{10,8},{9,1... | collective-permute-start | bytes 2359304 | tf_op jit(solution)/shard_map/ppermute | solution.py:37
  545.4 18.5 %collective-permute-start.79 = (bf16[8,128,512]{2,1,0:T(8,128)(2,1)S(1)}, bf16[8,128,512]{2,1,0:T(8,128)(2,1)S(1)}, u32[]{:S(2)}, u32[]{:S(2)}) collective-permute-start(bf16[8,128,512]{2,1,0:T(8,128)(2,1)S(1)} %constant_dynamic-slice_fusion.2), channel_id=1, source_target_pairs={{0,1},{1,0},{2,3},{3,2},{4,5},{5,4},{6,7},{7,6},{8,9},{9,8},{10,11... | collective-permute-start | bytes 3145736 | tf_op jit(solution)/shard_map/ppermute | solution.py:37
  545.6 32.8 %collective-permute-start.92 = (bf16[8,112,512]{2,1,0:T(8,128)(2,1)S(1)}, bf16[8,112,512]{2,1,0:T(8,128)(2,1)S(1)}, u32[]{:S(2)}, u32[]{:S(2)}) collective-permute-start(bf16[8,112,512]{2,1,0:T(8,128)(2,1)S(1)} %constant_dynamic-slice_fusion), channel_id=1, source_target_pairs={{0,2},{2,0},{1,3},{3,1},{4,6},{6,4},{5,7},{7,5},{8,10},{10,8},{9,1... | collective-permute-start | bytes 2752520 | tf_op jit(solution)/shard_map/ppermute | solution.py:37
  562.5 10.0 %collective-permute-start.87 = (bf16[4,96,512]{2,1,0:T(8,128)(2,1)S(1)}, bf16[4,96,512]{2,1,0:T(8,128)(2,1)S(1)}, u32[]{:S(2)}, u32[]{:S(2)}) collective-permute-start(bf16[4,96,512]{2,1,0:T(8,128)(2,1)S(1)} %dynamic-slice_bitcast_fusion.6), channel_id=1, source_target_pairs={{0,4},{4,0},{1,5},{5,1},{2,6},{6,2},{3,7},{7,3},{8,12},{12,8},{9,1... | collective-permute-start | bytes 1179656 | tf_op jit(solution)/shard_map/ppermute | solution.py:37
  565.0 30.2 %collective-permute-start.80 = (bf16[4,128,512]{2,1,0:T(8,128)(2,1)}, bf16[4,128,512]{2,1,0:T(8,128)(2,1)S(1)}, u32[]{:S(2)}, u32[]{:S(2)}) collective-permute-start(bf16[4,128,512]{2,1,0:T(8,128)(2,1)} %dynamic-slice_bitcast_fusion.4), channel_id=1, source_target_pairs={{0,4},{4,0},{1,5},{5,1},{2,6},{6,2},{3,7},{7,3},{8,12},{12,8},{9,1... | collective-permute-start | bytes 1572872 | tf_op jit(solution)/shard_map/ppermute | solution.py:37
  578.7 21.2 %collective-permute-start.93 = (bf16[128,2688]{1,0:T(8,128)(2,1)}, bf16[128,2688]{1,0:T(8,128)(2,1)S(1)}, u32[]{:S(2)}, u32[]{:S(2)}) collective-permute-start(bf16[128,2688]{1,0:T(8,128)(2,1)} %bitcast.378), channel_id=1, source_target_pairs={{0,2},{2,0},{1,3},{3,1},{4,6},{6,4},{5,7},{7,5},{8,10},{10,8},{9,1... | collective-permute-start | bytes 2064392 | tf_op jit(solution)/shard_map/ppermute | solution.py:37
  581.4 13.7 %collective-permute-start.91 = (bf16[96,512]{1,0:T(8,128)(2,1)S(1)}, bf16[96,512]{1,0:T(8,128)(2,1)S(1)}, u32[]{:S(2)}, u32[]{:S(2)}) collective-permute-start(bf16[96,512]{1,0:T(8,128)(2,1)S(1)} %fusion.53), channel_id=1, source_target_pairs={{0,2},{2,0},{1,3},{3,1},{4,6},{6,4},{5,7},{7,5},{8,10},{10,8},{9,1... | collective-permute-start | bytes 294920 | tf_op jit(solution)/shard_map/ppermute | solution.py:37
  582.2 17.7 %collective-permute-start.96 = (bf16[4,112,512]{2,1,0:T(8,128)(2,1)S(1)}, bf16[4,112,512]{2,1,0:T(8,128)(2,1)S(1)}, u32[]{:S(2)}, u32[]{:S(2)}) collective-permute-start(bf16[4,112,512]{2,1,0:T(8,128)(2,1)S(1)} %dynamic-slice_bitcast_fusion.5), channel_id=1, source_target_pairs={{0,4},{4,0},{1,5},{5,1},{2,6},{6,2},{3,7},{7,3},{8,12},{12,8},{9,1... | collective-permute-start | bytes 1376264 | tf_op jit(solution)/shard_map/ppermute | solution.py:37
  595.4 7.0 %collective-permute-start.83 = (bf16[128,512]{1,0:T(8,128)(2,1)S(1)}, bf16[128,512]{1,0:T(8,128)(2,1)S(1)}, u32[]{:S(2)}, u32[]{:S(2)}) collective-permute-start(bf16[128,512]{1,0:T(8,128)(2,1)S(1)} %get-tuple-element.265), channel_id=1, source_target_pairs={{0,24},{8,16},{16,8},{24,0},{1,25},{9,17},{17,9},{25,1},{2,26},{10... | collective-permute-start | bytes 393224 | tf_op jit(solution)/shard_map/ppermute | solution.py:37
  597.3 13.5 %collective-permute-start.82 = (bf16[128,512]{1,0:T(8,128)(2,1)S(1)}, bf16[128,512]{1,0:T(8,128)(2,1)S(1)}, u32[]{:S(2)}, u32[]{:S(2)}) collective-permute-start(bf16[128,512]{1,0:T(8,128)(2,1)S(1)} %get-tuple-element.266), channel_id=1, source_target_pairs={{0,16},{8,24},{16,0},{24,8},{1,17},{9,25},{17,1},{25,9},{2,18},{10... | collective-permute-start | bytes 393224 | tf_op jit(solution)/shard_map/ppermute | solution.py:37
  597.3 13.5 %collective-permute-start.81 = (bf16[128,512]{1,0:T(8,128)(2,1)S(1)}, bf16[128,512]{1,0:T(8,128)(2,1)S(1)}, u32[]{:S(2)}, u32[]{:S(2)}) collective-permute-start(bf16[128,512]{1,0:T(8,128)(2,1)S(1)} %get-tuple-element.264), channel_id=1, source_target_pairs={{0,8},{8,0},{16,24},{24,16},{1,9},{9,1},{17,25},{25,17},{2,10},{10... | collective-permute-start | bytes 393224 | tf_op jit(solution)/shard_map/ppermute | solution.py:37
  599.9 17.4 %collective-permute-start.94 = (bf16[128,2688]{1,0:T(8,128)(2,1)S(1)}, bf16[128,2688]{1,0:T(8,128)(2,1)S(1)}, u32[]{:S(2)}, u32[]{:S(2)}) collective-permute-start(bf16[128,2688]{1,0:T(8,128)(2,1)S(1)} %bitcast.380), channel_id=1, source_target_pairs={{0,1},{1,0},{2,3},{3,2},{4,5},{5,4},{6,7},{7,6},{8,9},{9,8},{10,11... | collective-permute-start | bytes 2064392 | tf_op jit(solution)/shard_map/ppermute | solution.py:37
  599.9 17.4 %collective-permute-start.95 = (bf16[128,2688]{1,0:T(8,128)(2,1)S(1)}, bf16[128,2688]{1,0:T(8,128)(2,1)S(1)}, u32[]{:S(2)}, u32[]{:S(2)}) collective-permute-start(bf16[128,2688]{1,0:T(8,128)(2,1)S(1)} %collective-permute-done.93.refs_3_), channel_id=1, source_target_pairs={{0,1},{1,0},{2,3},{3,2},{4,5},{5,4},{6,7},{7,6},{8,9},{9,8},{10,11... | collective-permute-start | bytes 2064392 | tf_op jit(solution)/shard_map/ppermute | solution.py:37
  602.5 10.9 %collective-permute-start.99 = (bf16[112,512]{1,0:T(8,128)(2,1)S(1)}, bf16[112,512]{1,0:T(8,128)(2,1)S(1)}, u32[]{:S(2)}, u32[]{:S(2)}) collective-permute-start(bf16[112,512]{1,0:T(8,128)(2,1)S(1)} %get-tuple-element.268), channel_id=1, source_target_pairs={{0,24},{8,16},{16,8},{24,0},{1,25},{9,17},{17,9},{25,1},{2,26},{10... | collective-permute-start | bytes 344072 | tf_op jit(solution)/shard_map/ppermute | solution.py:37
  613.3 15.1 %collective-permute-start.84 = (bf16[128,512]{1,0:T(8,128)(2,1)S(1)}, bf16[128,512]{1,0:T(8,128)(2,1)S(1)}, u32[]{:S(2)}, u32[]{:S(2)}) collective-permute-start(bf16[128,512]{1,0:T(8,128)(2,1)S(1)} %fusion.44), channel_id=1, source_target_pairs={{0,2},{2,0},{1,3},{3,1},{4,6},{6,4},{5,7},{7,5},{8,10},{10,8},{9,1... | collective-permute-start | bytes 393224 | tf_op jit(solution)/shard_map/ppermute | solution.py:37
  (108 other events, 820.0 us)
Sparse Core Ops, SparseCore 0:
  10.8 79.3 all-gather.5
  93.7 150.2 all-gather.3
  445.9 120.4 reduce-scatter.1
